TPU v7x, 32 devices: a whole 2x2x4 slice. The times are simulated.
32 devices in a mesh: dp: 8 (over z, y), ep: 4 (over x, core).
Axes of the slice: x: 2, y: 2, z: 4, core: 2. Of those that a mesh axis runs over, the one named last changes fastest.
Arguments:
- tokens: bfloat16 [4096, 2048], P(('dp', 'ep')), may hold values from -6 to 6
- dense_weights: bfloat16 [2048, 25088], P(('dp', 'ep')), may hold values from -0.70710678 to 0.70710678
- expert_weights: bfloat16 [2048, 8, 4224], P('dp', 'ep'), may hold values from -1.2060454 to 1.2060454
- gain_attn: bfloat16 [2048], replicated, may hold values from 0.5 to 1.5
- gain_ffn: bfloat16 [2048], replicated, may hold values from 0.5 to 1.5
- qkv_bias: bfloat16 [6144], replicated, may hold values from -1.1953125 to 1.1953125
- router_weight: bfloat16 [2048, 9], replicated, may hold values from -0.0625 to 0.0625
- routes: int32 [4096, 4], P(('dp', 'ep')), may hold values from 0 to 7, all different within a row; in each aligned block of 128 rows (0 to 127, 128 to 255, ...) at most 128 rows name the same one
- doc_ids: int32 [4096], P('dp'), may hold values from 0 to 23, as said below
- out_grad: bfloat16 [4096, 2048], P(('dp', 'ep')), may hold values from -6 to 6
Outputs:
- output: bfloat16 [4096, 2048], P(('dp', 'ep'))
- input_grad: float32 [4096, 2048], P(('dp', 'ep'))
- dense_grad: float32 [2048, 25088], P(('dp', 'ep'))
- expert_grad: float32 [2048, 8, 4224], P('dp', 'ep')
- gain_attn_grad: float32 [2048], replicated
- gain_ffn_grad: float32 [2048], replicated
- bias_grad: float32 [6144], replicated
- router_grad: float32 [2048, 9], replicated
Inputs may be any that keep to these rules, and one draw needn't show every extreme that they name: `routes`: among the 128 rows of one device no expert is named by more than 128 rows, a bound that some block reaches. `doc_ids`: each group of 512 tokens (one index of dp) holds three sequences with ids 3 g, 3 g + 1, 3 g + 2 in order; the middle one begins on the group's first device and ends on its last.
All inputs are finite; a program needn't handle non-finite values.
Results may differ from a plain program's by a relative error of at most 0.034.
Values may be sent and summed in bfloat16 or wider, within the bound.
No kernel may reach another device: no remote copies, remote signals or barrier semaphores. Data moves between devices by JAX's collectives and lax.ppermute only.
A program may use at most 832 MiB of HBM per device.

v0:
```python
import jax
import jax.numpy as jnp
from jax import lax
from jax.sharding import PartitionSpec as P

H = 16
HD = 128
FF = 1408
SFF = 5632


norm_eps = 1e-06
rope_base = 1000000.0
exact_mode = lax.Precision.HIGHEST


def rotate(vectors, cosine_table, sine_table):
    half_width = vectors.shape[-1] // 2
    turned = jnp.concatenate([-vectors[..., half_width:], vectors[..., :half_width]], axis=-1)
    return vectors * cosine_table + turned * sine_table


def unrotate(vectors, cosine_table, sine_table):
    half_width = vectors.shape[-1] // 2
    scaled = vectors * sine_table
    return vectors * cosine_table + jnp.concatenate(
        [scaled[..., half_width:], -scaled[..., :half_width]], axis=-1
    )


def rope_tables(places):
    steps_along = jnp.arange(HD // 2, dtype=jnp.float32) * (2.0 / HD)
    inverse = jnp.power(jnp.float32(rope_base), -steps_along)
    angles = places.astype(jnp.float32)[:, None] * inverse[None, :]
    angles = jnp.concatenate([angles, angles], axis=1)
    return (jnp.cos(angles)[:, None, :], jnp.sin(angles)[:, None, :])


def silu_value(values):
    return values * jax.nn.sigmoid(values)


def silu_slope(values):
    sigmoid_of = jax.nn.sigmoid(values)
    return sigmoid_of * (1.0 + values * (1.0 - sigmoid_of))


def softmax_rows(logits):
    row_max = jnp.max(logits, axis=-1, keepdims=True)
    weights = jnp.exp(logits - row_max)
    return weights / jnp.sum(weights, axis=-1, keepdims=True)


def group_rows(rows):
    return lax.all_gather(rows, "ep", axis=0, tiled=True)


def group_sums(parts):
    return lax.psum_scatter(
        parts.astype(jnp.bfloat16), "ep", scatter_dimension=0, tiled=True
    ).astype(jnp.float32)


def section_widths(model_width):
    return [model_width, model_width, model_width, model_width, SFF, SFF, SFF]


def share_columns(matrix, model_width, owners):
    rows_here = matrix.shape[0]
    pieces = []
    offset = 0
    for section_width in section_widths(model_width):
        pieces.append(
            matrix[:, offset : offset + section_width].reshape(
                rows_here, owners, section_width // owners
            )
        )
        offset = offset + section_width
    return jnp.concatenate(pieces, axis=2)


def unshare_columns(grid, model_width):
    rows_here = grid.shape[0]
    owners = grid.shape[1]
    pieces = []
    offset = 0
    for section_width in section_widths(model_width):
        span_width = section_width // owners
        pieces.append(grid[:, :, offset : offset + span_width].reshape(rows_here, section_width))
        offset = offset + span_width
    return jnp.concatenate(pieces, axis=1)


def body(
    tokens,
    dense_weights,
    expert_weights,
    gain_attn,
    gain_ffn,
    qkv_bias,
    router_weight,
    routes,
    doc_ids,
    out_grad,
):
    row_count, model_width = tokens.shape
    group_len = doc_ids.shape[0]
    top_count = routes.shape[1]
    expert_count = router_weight.shape[1] - 1
    local_experts = expert_weights.shape[1]
    owner_count = expert_count // local_experts
    capacity = max(2, 2 * row_count * top_count // expert_count)
    score_scale = HD ** (-0.5)
    owners = lax.axis_size("ep")
    owner_index = lax.axis_index("ep")
    stream = tokens.astype(jnp.float32)
    gain_one = gain_attn.astype(jnp.float32)
    gain_two = gain_ffn.astype(jnp.float32)
    bias_row = qkv_bias.astype(jnp.float32)
    router = router_weight.astype(jnp.float32)
    before = jnp.sum((doc_ids[None, :] < doc_ids[:, None]).astype(jnp.int32), axis=1)
    group_places = jnp.arange(group_len, dtype=jnp.int32) - before
    key_order = jnp.arange(group_len, dtype=jnp.int32)
    inverse_one = lax.rsqrt(jnp.mean(stream * stream, axis=1, keepdims=True) + norm_eps)
    normed = (stream * inverse_one * gain_one).astype(jnp.bfloat16)
    head_share = H // owners
    share_width = model_width // owners
    unit_share = SFF // owners
    grid = share_columns(dense_weights, model_width, owners)
    arrived_rows = lax.all_to_all(grid, "ep", split_axis=1, concat_axis=0, tiled=True)
    dense_share = lax.all_gather(
        arrived_rows.reshape(arrived_rows.shape[0], arrived_rows.shape[2]), "dp", axis=0, tiled=True
    )
    group_cosine, group_sine = rope_tables(group_places)
    group_allowed = (doc_ids[:, None] == doc_ids[None, :]) & (
        key_order[None, :] <= key_order[:, None]
    )
    bias_share = lax.dynamic_slice_in_dim(
        bias_row.reshape(3, owners, share_width), owner_index, 1, 1
    ).reshape(3 * share_width)
    normed_group = group_rows(normed)
    packed_group = (
        jnp.dot(normed_group, dense_share[:, : 3 * share_width], preferred_element_type=jnp.float32)
        + bias_share
    )
    queries_group = rotate(
        packed_group[:, :share_width].reshape(group_len, head_share, HD), group_cosine, group_sine
    ).astype(jnp.bfloat16)
    keys_group = rotate(
        packed_group[:, share_width : 2 * share_width].reshape(group_len, head_share, HD),
        group_cosine,
        group_sine,
    ).astype(jnp.bfloat16)
    values_group = (
        packed_group[:, 2 * share_width :].astype(jnp.bfloat16).reshape(group_len, head_share, HD)
    )

    def share_scores(query_rows):
        raw = (
            jnp.einsum("qhd,khd->hqk", query_rows, keys_group, preferred_element_type=jnp.float32)
            * score_scale
        )
        return jnp.where(group_allowed[None, :, :], raw, -1e30)

    scores = share_scores(queries_group)
    row_max = jnp.max(scores, axis=2, keepdims=True)
    raw_weights = jnp.exp(scores - row_max)
    row_total = jnp.sum(raw_weights, axis=2, keepdims=True)
    log_total = row_max + jnp.log(row_total)
    attend = (raw_weights / row_total).astype(jnp.bfloat16)
    mixed_group = jnp.einsum(
        "hqk,khd->qhd", attend, values_group, preferred_element_type=jnp.float32
    )
    mixed_group = mixed_group.astype(jnp.bfloat16).reshape(group_len, share_width)
    branch = group_sums(
        jnp.einsum(
            "ti,oi->to",
            mixed_group,
            dense_share[:, 3 * share_width : 4 * share_width],
            preferred_element_type=jnp.float32,
        )
    )
    residual = stream + branch
    inverse_two = lax.rsqrt(jnp.mean(residual * residual, axis=1, keepdims=True) + norm_eps)
    normed_two = (residual * inverse_two * gain_two).astype(jnp.bfloat16)
    logits = jnp.dot(normed_two.astype(jnp.float32), router, precision=exact_mode)
    router_probs = softmax_rows(logits[:, :expert_count])
    shared_gate = jax.nn.sigmoid(logits[:, expert_count:])
    gate_values = jnp.take_along_axis(router_probs, routes, axis=1)
    route_flat = routes.reshape(-1)
    onehot = (route_flat[:, None] == jnp.arange(expert_count, dtype=jnp.int32)[None, :]).astype(
        jnp.int32
    )
    slot_rank = jnp.sum((jnp.cumsum(onehot, axis=0) - onehot) * onehot, axis=1)
    slot_index = route_flat * capacity + slot_rank
    slot_match = (
        slot_index[None, :] == jnp.arange(expert_count * capacity, dtype=jnp.int32)[:, None]
    )
    pick_token = jnp.arange(row_count * top_count, dtype=jnp.int32) // top_count
    slot_token = jnp.sum(jnp.where(slot_match, pick_token[None, :], 0), axis=1)
    slot_live = jnp.any(slot_match, axis=1)
    slot_gate = jnp.sum(jnp.where(slot_match, gate_values.reshape(-1)[None, :], 0.0), axis=1)
    outgoing = jnp.where(slot_live[:, None], normed_two[slot_token], jnp.zeros((), jnp.bfloat16))
    outgoing = outgoing.reshape(owner_count, local_experts, capacity, model_width)
    expert_full = lax.all_gather(expert_weights, "dp", axis=0, tiled=True)
    arrived = lax.all_to_all(outgoing, "ep", split_axis=0, concat_axis=0, tiled=True)
    gate_up = jnp.einsum(
        "secd,def->secf", arrived, expert_full[:, :, : 2 * FF], preferred_element_type=jnp.float32
    )
    hidden = (silu_value(gate_up[..., :FF]) * gate_up[..., FF:]).astype(jnp.bfloat16)
    result = jnp.einsum(
        "secf,def->secd", hidden, expert_full[:, :, 2 * FF :], preferred_element_type=jnp.float32
    )
    expert_out, gate_up, arrived = (result.astype(jnp.bfloat16), gate_up, arrived)
    returned = lax.all_to_all(expert_out, "ep", split_axis=0, concat_axis=0, tiled=True).reshape(
        expert_count * capacity, model_width
    )
    picked = returned[slot_index].reshape(row_count, top_count, model_width).astype(jnp.float32)
    routed = jnp.sum(gate_values[:, :, None] * picked, axis=1)
    normed_two_group = group_rows(normed_two)
    shared_cols = dense_share[:, 4 * share_width : 4 * share_width + 2 * unit_share]
    shared_down = dense_share[:, 4 * share_width + 2 * unit_share :]
    shared_gate_up = jnp.dot(normed_two_group, shared_cols, preferred_element_type=jnp.float32)
    shared_hidden = (
        silu_value(shared_gate_up[:, :unit_share]) * shared_gate_up[:, unit_share:]
    ).astype(jnp.bfloat16)
    shared_out = group_sums(
        jnp.einsum("tf,of->to", shared_hidden, shared_down, preferred_element_type=jnp.float32)
    )
    output = (residual + routed + shared_gate * shared_out).astype(jnp.bfloat16)
    cotangent = out_grad.astype(jnp.float32)
    shared_out_grad = (shared_gate * cotangent).astype(jnp.bfloat16)
    shared_logit_grad = (
        jnp.sum(cotangent * shared_out, axis=1, keepdims=True) * shared_gate * (1.0 - shared_gate)
    )
    shared_out_grad_group = group_rows(shared_out_grad)
    shared_hidden_grad = jnp.dot(
        shared_out_grad_group, shared_down, preferred_element_type=jnp.float32
    )
    shared_g = shared_gate_up[:, :unit_share]
    shared_u = shared_gate_up[:, unit_share:]
    shared_grad = jnp.concatenate(
        [
            shared_hidden_grad * shared_u * silu_slope(shared_g),
            shared_hidden_grad * silu_value(shared_g),
        ],
        axis=1,
    ).astype(jnp.bfloat16)
    normed_two_grad = group_sums(
        jnp.einsum("tf,df->td", shared_grad, shared_cols, preferred_element_type=jnp.float32)
    )
    gate_grad = jnp.sum(cotangent[:, None, :] * picked, axis=2)
    outgoing_grad = jnp.where(slot_live[:, None], slot_gate[:, None] * cotangent[slot_token], 0.0)
    outgoing_grad = outgoing_grad.astype(jnp.bfloat16).reshape(
        owner_count, local_experts, capacity, model_width
    )
    arrived_grad = lax.all_to_all(outgoing_grad, "ep", split_axis=0, concat_axis=0, tiled=True)
    hidden_grad = jnp.einsum(
        "secd,def->secf",
        arrived_grad,
        expert_full[:, :, 2 * FF :],
        preferred_element_type=jnp.float32,
    )
    expert_g = gate_up[..., :FF]
    expert_u = gate_up[..., FF:]
    hidden_again = (silu_value(expert_g) * expert_u).astype(jnp.bfloat16)
    gate_up_grad = jnp.concatenate(
        [hidden_grad * expert_u * silu_slope(expert_g), hidden_grad * silu_value(expert_g)], axis=3
    ).astype(jnp.bfloat16)
    input_rows_grad = jnp.einsum(
        "secf,def->secd",
        gate_up_grad,
        expert_full[:, :, : 2 * FF],
        preferred_element_type=jnp.float32,
    ).astype(jnp.bfloat16)
    returned_grad = lax.all_to_all(
        input_rows_grad, "ep", split_axis=0, concat_axis=0, tiled=True
    ).reshape(expert_count * capacity, model_width)
    normed_two_grad = normed_two_grad + jnp.sum(
        returned_grad[slot_index].reshape(row_count, top_count, model_width).astype(jnp.float32),
        axis=1,
    )
    expert_terms = jnp.concatenate(
        [
            jnp.einsum("secd,secf->def", arrived, gate_up_grad, preferred_element_type=jnp.float32),
            jnp.einsum(
                "secd,secf->def", arrived_grad, hidden_again, preferred_element_type=jnp.float32
            ),
        ],
        axis=2,
    )
    expert_grad = lax.psum_scatter(
        expert_terms.astype(jnp.bfloat16), "dp", scatter_dimension=0, tiled=True
    ).astype(jnp.float32)
    expert_match = routes[:, :, None] == jnp.arange(expert_count, dtype=jnp.int32)[None, None, :]
    probs_grad = jnp.sum(jnp.where(expert_match, gate_grad[:, :, None], 0.0), axis=1)
    expert_logit_grad = router_probs * (
        probs_grad - jnp.sum(router_probs * probs_grad, axis=1, keepdims=True)
    )
    logit_grad = jnp.concatenate([expert_logit_grad, shared_logit_grad], axis=1)
    router_grad = jnp.dot(normed_two.astype(jnp.float32).T, logit_grad, precision=exact_mode)
    normed_two_grad = normed_two_grad + jnp.dot(logit_grad, router.T, precision=exact_mode)
    scaled_two = normed_two_grad * gain_two
    gain_two_grad = jnp.sum(normed_two_grad * residual * inverse_two, axis=0)
    residual_grad = (
        cotangent
        + inverse_two * scaled_two
        - residual * inverse_two**3 * jnp.mean(scaled_two * residual, axis=1, keepdims=True)
    )
    branch_grad = residual_grad.astype(jnp.bfloat16)
    branch_grad_group = group_rows(branch_grad)
    mixed_grad = jnp.dot(
        branch_grad_group,
        dense_share[:, 3 * share_width : 4 * share_width],
        preferred_element_type=jnp.float32,
    ).astype(jnp.bfloat16)
    mixed_heads_grad = mixed_grad.reshape(group_len, head_share, HD)
    soft_again = jnp.exp(share_scores(queries_group) - log_total)
    attend_grad = jnp.einsum(
        "qhd,khd->hqk", mixed_heads_grad, values_group, preferred_element_type=jnp.float32
    )
    scores_grad = (
        soft_again * (attend_grad - jnp.sum(soft_again * attend_grad, axis=2, keepdims=True))
    ).astype(jnp.bfloat16)
    queries_grad = (
        jnp.einsum("hqk,khd->qhd", scores_grad, keys_group, preferred_element_type=jnp.float32)
        * score_scale
    ).astype(jnp.bfloat16)
    keys_grad = (
        jnp.einsum("hqk,qhd->khd", scores_grad, queries_group, preferred_element_type=jnp.float32)
        * score_scale
    ).astype(jnp.bfloat16)
    values_grad = jnp.einsum(
        "hqk,qhd->khd",
        soft_again.astype(jnp.bfloat16),
        mixed_heads_grad,
        preferred_element_type=jnp.float32,
    ).astype(jnp.bfloat16)
    packed_grad = jnp.concatenate(
        [
            unrotate(queries_grad.astype(jnp.float32), group_cosine, group_sine).reshape(
                group_len, share_width
            ),
            unrotate(keys_grad.astype(jnp.float32), group_cosine, group_sine).reshape(
                group_len, share_width
            ),
            values_grad.astype(jnp.float32).reshape(group_len, share_width),
        ],
        axis=1,
    ).astype(jnp.bfloat16)
    bias_share_grad = jnp.sum(packed_grad.astype(jnp.float32), axis=0).reshape(3, 1, share_width)
    bias_grad = lax.dynamic_update_slice_in_dim(
        jnp.zeros((3, owners, share_width), jnp.float32), bias_share_grad, owner_index, 1
    ).reshape(3 * model_width)
    normed_grad = group_sums(
        jnp.einsum(
            "tc,dc->td",
            packed_grad,
            dense_share[:, : 3 * share_width],
            preferred_element_type=jnp.float32,
        )
    )
    scaled_one = normed_grad * gain_one
    gain_one_grad = jnp.sum(normed_grad * stream * inverse_one, axis=0)
    input_grad = (
        residual_grad
        + inverse_one * scaled_one
        - stream * inverse_one**3 * jnp.mean(scaled_one * stream, axis=1, keepdims=True)
    )
    group_block = dense_share.shape[0] // lax.axis_size("dp")
    summed_share = lax.psum_scatter(
        jnp.concatenate(
            [
                jnp.einsum(
                    "tc,tf->cf", normed_group, packed_grad, preferred_element_type=jnp.float32
                ),
                jnp.einsum(
                    "tc,tf->cf", branch_grad_group, mixed_group, preferred_element_type=jnp.float32
                ),
                jnp.einsum(
                    "tc,tf->cf", normed_two_group, shared_grad, preferred_element_type=jnp.float32
                ),
                jnp.einsum(
                    "tc,tf->cf",
                    shared_out_grad_group,
                    shared_hidden,
                    preferred_element_type=jnp.float32,
                ),
            ],
            axis=1,
        ).astype(jnp.bfloat16),
        "dp",
        scatter_dimension=0,
        tiled=True,
    ).astype(jnp.float32)
    summed_share = summed_share.reshape(group_block, 1, summed_share.shape[1])
    returned_share = lax.all_to_all(
        summed_share.astype(jnp.bfloat16), "ep", split_axis=0, concat_axis=1, tiled=True
    ).astype(summed_share.dtype)
    dense_grad = unshare_columns(returned_share, model_width)
    small_sums = lax.psum((gain_one_grad, gain_two_grad, bias_grad, router_grad), ("dp", "ep"))
    return (
        output,
        input_grad,
        dense_grad,
        expert_grad,
        small_sums[0],
        small_sums[1],
        small_sums[2],
        small_sums[3],
    )


def solution(mesh):
    in_specs = (
        P(("dp", "ep"), None),
        P(("dp", "ep"), None),
        P("dp", "ep", None),
        P(),
        P(),
        P(),
        P(),
        P(("dp", "ep"), None),
        P("dp"),
        P(("dp", "ep"), None),
    )
    out_specs = (
        P(("dp", "ep"), None),
        P(("dp", "ep"), None),
        P(("dp", "ep"), None),
        P("dp", "ep", None),
        P(),
        P(),
        P(),
        P(),
    )
    return jax.shard_map(body, mesh=mesh, in_specs=in_specs, out_specs=out_specs, check_vma=False)
```

profile of v0, /device:TPU:0, one launch (start us, length us, event | category | flops | bytes accessed | tf_op | source)
XLA Modules:
  0.0 2794.0 jit_solution(6493054578117160115)
XLA Ops:
  35.3 41.7 %all_to_all.44 = bf16[64,4,6272]{2,0,1:T(8,128)(2,1)} all-to-all(bf16[64,4,6272]{2,0,1:T(8,128)(2,1)S(1)} %copy.275), channel_id=1, replica_groups=mesh['dp'=8,'ep'=4] {'ep'}, dimensions={1} | all-to-all | bytes 6422528 | tf_op jit(solution)/shard_map/all_to_all | solution.py:130
  80.6 487.9 %all-gather.9.cloned.1.call-done = bf16[2048,6272]{1,0:T(8,128)(2,1)} async-done(((bf16[256,6272]{1,0:T(8,128)(2,1)}), bf16[2048,6272]{1,0:T(8,128)(2,1)}) %all-gather.9.cloned.1.call-update) | async-done | bytes 25690128 | tf_op jit(solution)/shard_map/all_gather | solution.py:131
  568.5 6.2 fusion.28
  588.5 31.5 %reduce-scatter.7.cloned.1.call-done = bf16[128,2048]{1,0:T(8,128)(2,1)} async-done(((bf16[512,2048]{1,0:T(8,128)(2,1)}), bf16[128,2048]{1,0:T(8,128)(2,1)}) %reduce-scatter.7.cloned.1.call-update) | async-done | bytes 524304 | tf_op jit(solution)/shard_map/reduce_scatter | solution.py:59
  624.6 22.5 all-gather.13.cloned.1.call-done
  647.1 10.2 fusion.5
  661.8 7.4 fusion.38
  677.1 6.0 gather_fusion
  687.6 5.0 all-to-all-start.1
  693.0 6.7 gather_fusion.2
  703.3 5.3 select_convert_fusion
  709.9 34.8 %all-to-all-done.1 = bf16[4,2,128,2048]{3,2,1,0:T(8,128)(2,1)} async-done(((bf16[4,2,128,2048]{3,2,1,0:T(8,128)(2,1)}), bf16[4,2,128,2048]{3,2,1,0:T(8,128)(2,1)}, u32[]{:S(2)}, u32[]{:S(2)}) %all-to-all-start.1) | async-done | bytes 4194336 | tf_op jit(solution)/shard_map/all_to_all | solution.py:206
  744.7 4.9 all-to-all-start.3
  750.8 613.0 %all-gather.11.cloned.1.call-done = bf16[2048,2,4224]{2,0,1:T(8,128)(2,1)} async-done(((bf16[256,2,4224]{2,0,1:T(8,128)(2,1)}), bf16[2048,2,4224]{2,0,1:T(8,128)(2,1)}) %all-gather.11.cloned.1.call-update) | async-done | bytes 34603024 | tf_op jit(solution)/shard_map/all_gather | solution.py:205
  1363.8 21.6 fusion.10
  1385.4 15.5 fusion.12
  1400.9 17.2 convert_bitcast_fusion.1
  1420.4 4.8 all-to-all-start.4
  1425.7 9.1 multiply_convert_fusion.3
  1436.5 10.0 fusion.35
  1446.5 10.5 convert_bitcast_fusion.2
  1459.3 21.8 all-to-all-done.4
  1481.1 4.8 all-to-all-start.2
  1486.3 8.1 gather_fusion.3
  1499.1 35.1 %all-to-all-done.2 = bf16[4,2,128,2048]{3,2,1,0:T(8,128)(2,1)} async-done(((bf16[4,2,128,2048]{3,2,1,0:T(8,128)(2,1)}), bf16[4,2,128,2048]{3,2,1,0:T(8,128)(2,1)}, u32[]{:S(2)}, u32[]{:S(2)}) %all-to-all-start.2) | async-done | bytes 4194336 | tf_op jit(solution)/shard_map/all_to_all | solution.py:215
  1534.2 8.0 gather_fusion.1
  1546.9 6.7 multiply_reduce_fusion.1
  1553.7 5.9 reduce_sum.195
  1563.6 8.1 convolution_convert_fusion.2
  1571.7 9.3 convolution_convert_fusion
  1596.4 7.1 convolution_convert_fusion.1
  1603.5 8.8 copy.305
  1620.6 17.8 pad_maximum_fusion.1
  1638.5 11.6 fusion.9
  1650.0 7.7 fusion.32
  1657.8 18.4 fusion
  1676.2 24.9 pad_maximum_fusion
  1701.1 348.8 %reduce-scatter.15.cloned.1.call-done = bf16[256,6272]{1,0:T(8,128)(2,1)} async-done(((bf16[2048,6272]{1,0:T(8,128)(2,1)}), bf16[256,6272]{1,0:T(8,128)(2,1)}) %reduce-scatter.15.cloned.1.call-update) | async-done | bytes 3211280 | tf_op jit(solution)/shard_map/reduce_scatter | solution.py:371
  2050.4 5.7 reduce.8
  2056.1 4.9 reshape.501
  2061.0 5.0 all-to-all-start.5
  2068.9 25.2 reduce-scatter.13.cloned.1.call-done
  2095.5 55.3 %all-reduce = (f32[2048]{0:T(1024)}, f32[2048]{0:T(1024)}, f32[6144]{0:T(1024)}) all-reduce(f32[2048]{0:T(1024)S(1)} %get-tuple-element.68, f32[2048]{0:T(1024)S(1)} %get-tuple-element.66, f32[6144]{0:T(1024)S(1)} %bitcast.194), channel_id=1, replica_groups=mesh['dp'=8,'ep'=4] {'dp','ep'}, use_global_device_ids=true, to_apply=%region_29.30 | all-reduce | flops 10240 | bytes 81920 | tf_op jit(solution)/shard_map/psum | solution.py:401
  2154.4 6.2 reshape.502
  2160.6 8.2 convert_bitcast_fusion
  2177.4 480.7 %reduce-scatter.17.cloned.1.call-done = bf16[256,2,4224]{0,2,1:T(8,128)(2,1)} async-done(((bf16[2048,2,4224]{0,2,1:T(8,128)(2,1)}), bf16[256,2,4224]{0,2,1:T(8,128)(2,1)}) %reduce-scatter.17.cloned.1.call-update) | async-done | bytes 4325392 | tf_op jit(solution)/shard_map/reduce_scatter | solution.py:292
  2658.1 12.2 copy.319
  2670.3 115.4 %all-reduce.3.cloned.1.call-done = f32[2048,9]{0,1:T(8,128)} async-done(((f32[2048,9]{0,1:T(8,128)}), f32[2048,9]{0,1:T(8,128)}) %all-reduce.3.cloned.1.call-update) | async-done | bytes 73744 | tf_op jit(solution)/shard_map/psum | solution.py:401
  (296 shorter events, 135.5 us)
Async XLA Ops:
  7.2 692.5 %copy-start = (bf16[2048,9]{0,1:T(8,128)(2,1)S(1)}, bf16[2048,9]{0,1:T(8,128)(2,1)}, u32[]{:S(2)}) copy-start(bf16[2048,9]{0,1:T(8,128)(2,1)} %param.16) | copy-start | bytes 110596
  7.2 7.6 copy-start.16
  7.2 73.4 %all-gather.7.cloned.1.call-start = ((), (), s32[]{:S(2)}) async-start(), calls=%async_computation.12 | async-start | bytes 2621440 | tf_op jit(solution)/shard_map/all_gather | solution.py:55
  12.5 556.0 %all-gather.9.cloned.1.call-start = ((), (), s32[]{:S(2)}) async-start(), calls=%async_computation.13 | async-start | bytes 28901376 | tf_op jit(solution)/shard_map/all_gather | solution.py:131
  35.3 42.4 %copy-start.45 = (bf16[6144]{0:T(1024)(128)(2,1)S(1)}, bf16[6144]{0:T(1024)(128)(2,1)}, u32[]{:S(2)}) copy-start(bf16[6144]{0:T(1024)(128)(2,1)} %param.15) | copy-start | bytes 36868
  35.3 42.5 %copy-start.40 = (s32[512]{0:T(512)S(1)}, s32[512]{0:T(512)}, u32[]{:S(2)}) copy-start(s32[512]{0:T(512)} %param.18) | copy-start | bytes 6148
  77.1 542.8 %reduce-scatter.7.cloned.1.call-start = ((), (), s32[]{:S(2)}) async-start(), calls=%async_computation.14 | async-start | bytes 2621440 | tf_op jit(solution)/shard_map/reduce_scatter | solution.py:59
  79.7 497.7 %copy-start.19 = (f32[512,128]{0,1:T(8,128)}, f32[512,128]{0,1:T(8,128)S(1)}, u32[]{:S(2)}) copy-start(f32[512,128]{0,1:T(8,128)S(1)} %get-tuple-element.113) | copy-start | bytes 786436
  584.1 35.9 %copy-start.7 = (bf16[128,2048]{1,0:T(8,128)(2,1)S(1)}, bf16[128,2048]{1,0:T(8,128)(2,1)}, u32[]{:S(2)}) copy-start(bf16[128,2048]{1,0:T(8,128)(2,1)} %param.10) | copy-start | bytes 1572868
  588.4 58.7 %all-gather.13.cloned.1.call-start = ((), (), s32[]{:S(2)}) async-start(), calls=%async_computation.16 | async-start | bytes 2621440 | tf_op jit(solution)/shard_map/all_gather | solution.py:55
  588.5 68.8 %copy-start.31 = (f32[2048]{0:T(1024)}, f32[2048]{0:T(1024)S(1)}, u32[]{:S(2)}) copy-start(f32[2048]{0:T(1024)S(1)} %convert_element_type.204) | copy-start | bytes 24580
  624.4 84.2 %reduce-scatter.9.cloned.1.call-start = ((), (), s32[]{:S(2)}) async-start(), calls=%async_computation.17 | async-start | bytes 2621440 | tf_op jit(solution)/shard_map/reduce_scatter | solution.py:59
  669.1 694.7 %all-gather.11.cloned.1.call-start = ((), (), s32[]{:S(2)}) async-start(), calls=%async_computation.15 | async-start | bytes 38928384 | tf_op jit(solution)/shard_map/all_gather | solution.py:205
  676.4 6.6 copy-start.41
  687.6 5.2 copy-start.9
  687.6 57.1 %all-to-all-start.1 = ((bf16[4,2,128,2048]{3,2,1,0:T(8,128)(2,1)}), bf16[4,2,128,2048]{3,2,1,0:T(8,128)(2,1)}, u32[]{:S(2)}, u32[]{:S(2)}) async-start(bf16[4,2,128,2048]{3,2,1,0:T(8,128)(2,1)} %broadcast_select_fusion), calls=%async_computation.2 | async-start | bytes 8388608 | tf_op jit(solution)/shard_map/all_to_all | solution.py:206
  692.9 6.7 copy-start.1
  709.8 40.0 %copy-start.52 = (f32[128,1]{0,1:T(1,128)}, f32[128,1]{0,1:T(1,128)S(1)}, u32[]{:S(2)}) copy-start(f32[128,1]{0,1:T(1,128)S(1)} %get-tuple-element.74) | copy-start | bytes 1540
  744.7 640.7 %all-to-all-start.3 = ((bf16[4,2,128,2048]{3,2,1,0:T(8,128)(2,1)}), bf16[4,2,128,2048]{3,2,1,0:T(8,128)(2,1)}, u32[]{:S(2)}, u32[]{:S(2)}) async-start(bf16[4,2,128,2048]{3,2,1,0:T(8,128)(2,1)} %select_convert_fusion), calls=%async_computation.6 | async-start | bytes 8388608 | tf_op jit(solution)/shard_map/all_to_all | solution.py:257
  749.5 676.2 %all-gather.15.cloned.1.call-start = ((), (), s32[]{:S(2)}) async-start(), calls=%async_computation.18 | async-start | bytes 2621440 | tf_op jit(solution)/shard_map/all_gather | solution.py:55
  1420.4 60.7 %all-to-all-start.4 = ((bf16[4,2,128,2048]{3,2,1,0:T(8,128)(2,1)}), bf16[4,2,128,2048]{3,2,1,0:T(8,128)(2,1)}, u32[]{:S(2)}, u32[]{:S(2)}) async-start(bf16[4,2,128,2048]{3,2,1,0:T(8,128)(2,1)} %copy.297), calls=%async_computation.7 | async-start | bytes 8388608 | tf_op jit(solution)/shard_map/all_to_all | solution.py:276
  1425.3 134.5 %reduce-scatter.11.cloned.1.call-start = ((), (), s32[]{:S(2)}) async-start(), calls=%async_computation.19 | async-start | bytes 2621440 | tf_op jit(solution)/shard_map/reduce_scatter | solution.py:59
  1459.3 26.9 copy-start.42
  1481.1 53.1 %all-to-all-start.2 = ((bf16[4,2,128,2048]{3,2,1,0:T(8,128)(2,1)}), bf16[4,2,128,2048]{3,2,1,0:T(8,128)(2,1)}, u32[]{:S(2)}, u32[]{:S(2)}) async-start(bf16[4,2,128,2048]{3,2,1,0:T(8,128)(2,1)} %copy.293), calls=%async_computation.3 | async-start | bytes 8388608 | tf_op jit(solution)/shard_map/all_to_all | solution.py:215
  1486.0 99.3 %all-gather.17.cloned.1.call-start = ((), (), s32[]{:S(2)}) async-start(), calls=%async_computation.20 | async-start | bytes 2621440 | tf_op jit(solution)/shard_map/all_gather | solution.py:55
  1553.6 6.0 copy-start.44
  1553.6 6.0 copy-start.47
  1553.6 6.1 copy-start.8
  1553.6 6.1 copy-start.10
  1553.6 6.1 copy-start.32
  1553.6 6.1 copy-start.49
  1553.7 8.5 copy-start.55
  1563.5 486.4 %reduce-scatter.15.cloned.1.call-start = ((), (), s32[]{:S(2)}) async-start(), calls=%async_computation.22 | async-start | bytes 28901376 | tf_op jit(solution)/shard_map/reduce_scatter | solution.py:371
  1563.6 8.1 copy-start.58
  1563.6 8.1 copy-start.61
  1563.6 8.1 copy-start.63
  1595.6 7.9 copy-start.25
  1638.4 11.7 copy-start.24
  1638.4 455.8 %reduce-scatter.13.cloned.1.call-start = ((), (), s32[]{:S(2)}) async-start(), calls=%async_computation.21 | async-start | bytes 2621440 | tf_op jit(solution)/shard_map/reduce_scatter | solution.py:59
  1638.4 11.6 copy-start.26
  1638.4 11.6 copy-start.28
  1657.7 1000.4 %reduce-scatter.17.cloned.1.call-start = ((), (), s32[]{:S(2)}) async-start(), calls=%async_computation.23 | async-start | bytes 38928384 | tf_op jit(solution)/shard_map/reduce_scatter | solution.py:292
  2061.0 33.1 %copy-start.34 = (f32[2048]{0:T(1024)S(1)}, f32[2048]{0:T(1024)}, u32[]{:S(2)}) copy-start(f32[2048]{0:T(1024)} %copy-done.33) | copy-start | bytes 24580
  2061.0 33.1 %copy-start.51 = (f32[128]{0:T(128)S(1)}, f32[128]{0:T(128)}, u32[]{:S(2)}) copy-start(f32[128]{0:T(128)} %copy-done.50) | copy-start | bytes 1540
  2061.0 89.8 %copy-start.53 = (f32[128,1]{0,1:T(1,128)S(1)}, f32[128,1]{0,1:T(1,128)}, u32[]{:S(2)}) copy-start(f32[128,1]{0,1:T(1,128)} %copy-done.52) | copy-start | bytes 1540
  2061.0 89.8 %copy-start.56 = (f32[128]{0:T(128)S(1)}, f32[128]{0:T(128)}, u32[]{:S(2)}) copy-start(f32[128]{0:T(128)} %get-tuple-element.114) | copy-start | bytes 1540
  2061.0 93.4 %all-to-all-start.5 = ((bf16[4,2,200704]{2,1,0:T(2,128)(2,1)}), bf16[4,2,200704]{2,1,0:T(2,128)(2,1)}, u32[]{:S(2)}, u32[]{:S(2)}) async-start(bf16[4,2,200704]{2,1,0:T(2,128)(2,1)} %reshape.501), calls=%async_computation.10 | async-start | bytes 6422528 | tf_op jit(solution)/shard_map/all_to_all | solution.py:397
  2066.1 719.6 %all-reduce.3.cloned.1.call-start = ((), (), s32[]{:S(2)}) async-start(), calls=%async_computation.24 | async-start | bytes 262144 | tf_op jit(solution)/shard_map/psum | solution.py:401
  (34 other events, 79.1 us)
Sparse Core Ops, SparseCore 0:
  12.6 25.2 all-gather.6
  77.2 491.2 all-gather.8
  588.5 31.3 reduce-scatter.6
  624.5 22.5 all-gather.12
  669.3 35.3 reduce-scatter.8
  706.1 657.7 all-gather.10
  1365.4 22.5 all-gather.14
  1446.6 39.1 reduce-scatter.10
  1563.6 21.6 all-gather.16
  1638.5 411.3 reduce-scatter.14
  2052.4 41.6 reduce-scatter.12
  2098.4 559.6 reduce-scatter.16
  2664.2 121.4 all-reduce.2
where the time goes:
time: 2800 us; the launch traced here: 2790 us
  waiting for transfers between devices  2220 us (79%)
  matrix products  194 us (7%)
  local copies, waits for them, and re-layouts  133 us (5%)
  other arithmetic  107 us (4%)
  blocking collectives  97.1 us (3%)
    all_gather x1, waiting for transfers between devices, body(): expert_full = lax.all_gather(expert_weights, 'dp', axis=0, tiled=True)  613 us
    all_gather x1, waiting for transfers between devices, body(): lax.all_gather(arrived_rows.reshape(arrived_rows.shape[0], arrived_rows.s...  488 us
    reduce_scatter x1, waiting for transfers between devices, body(): lax.psum_scatter(expert_terms.astype(jnp.bfloat16), 'dp', scatter_dimensi...  481 us
    reduce_scatter x1, waiting for transfers between devices, body(): lax.psum_scatter(jnp.concatenate([jnp.einsum('tc,tf->cf', normed_group, p...  349 us
    psum x1, waiting for transfers between devices, body(): lax.psum((gain_one_grad, gain_two_grad, bias_grad, router_grad), ('dp', '...  115 us
    reduce_scatter x4, waiting for transfers between devices, group_sums(): lax.psum_scatter(parts.astype(jnp.bfloat16), 'ep', scatter_dimension=0, t...  56.7 us
  transfers between devices with their start and end apart: 18, of which 12 were waited for; matrix products, arithmetic and copies ran while one was open for 12% of the time, Pallas kernels for 0%

commit v1 on v0

v1 whole, which is shorter than its diff:
```python
import jax
import jax.numpy as jnp
from jax import lax
from jax.sharding import Mesh, PartitionSpec as P

H = 16
HD = 128
FF = 1408
SFF = 5632

norm_eps = 1e-06
rope_base = 1000000.0
AXES = ("ring", "pair", "ep")
PLANE = ("pair", "ep")
f32 = jnp.float32
bf16 = jnp.bfloat16


class Layout:
    def __init__(self, rings):
        self.rings = rings
        self.order = list(range(0, rings, 2)) + list(range(1, rings, 2))[::-1]
        place = {r: i for i, r in enumerate(self.order)}
        self.place = [place[r] for r in range(rings)]
        self.core = self.pairs(lambda r, y, x, c: (r, y, x, 1 - c))
        self.side = self.pairs(lambda r, y, x, c: (r, y, 1 - x, c))
        self.up = self.pairs(lambda r, y, x, c: (r, 1 - y, x, c))
        self.cross = self.pairs(lambda r, y, x, c: (r, 1 - y, 1 - x, c))
        self.onward = self.pairs(lambda r, y, x, c: (self.order[(place[r] + 1) % rings], y, x, c))
        self.backward = self.pairs(lambda r, y, x, c: (self.order[(place[r] - 1) % rings], y, x, c))

    def pairs(self, move):
        found = []
        for r in range(self.rings):
            for y in range(2):
                for x in range(2):
                    for c in range(2):
                        u, v, w, q = move(r, y, x, c)
                        found.append((((r * 2 + y) * 2 + x) * 2 + c, ((u * 2 + v) * 2 + w) * 2 + q))
        return found

    def doubling(self):
        steps = []
        bit = 1
        while bit < self.rings * 8:
            steps.append([(i, i ^ bit) for i in range(self.rings * 8)])
            bit *= 2
        return steps


def permute(rows, pairs):
    return lax.ppermute(rows, AXES, pairs)


def stack(*parts):
    return jnp.concatenate(parts, axis=0)


def plus(a, b):
    return (a.astype(f32) + b.astype(f32)).astype(bf16)


def plane_rows(lay, rows):
    near = (rows, permute(rows, lay.side))
    far = (permute(rows, lay.up), permute(rows, lay.cross))
    near, far = stack(*near), stack(*far)
    return stack(near, permute(near, lay.core), far, permute(far, lay.core))


def plane_sums(lay, parts):
    n = parts.shape[0] // 8
    near = plus(parts[: 2 * n], permute(parts[2 * n : 4 * n], lay.core))
    far = plus(parts[4 * n : 6 * n], permute(parts[6 * n :], lay.core))
    total = near[:n].astype(f32) + permute(near[n:], lay.side).astype(f32)
    total = total + permute(far[:n], lay.up).astype(f32)
    return total + permute(far[n:], lay.cross).astype(f32)


def all_rows(lay, rows):
    blocks = [rows]
    for _ in range(lay.rings - 1):
        blocks.append(permute(blocks[-1], lay.onward))
    return [plane_rows(lay, block) for block in blocks]


def all_sums(lay, parts):
    total = None
    for part in parts[::-1]:
        here = plane_sums(lay, part)
        if total is not None:
            here = here + permute(total.astype(bf16), lay.backward).astype(f32)
        total = here
    return total


def rotate(vectors, cosine_table, sine_table):
    half_width = vectors.shape[-1] // 2
    turned = jnp.concatenate([-vectors[..., half_width:], vectors[..., :half_width]], axis=-1)
    return vectors * cosine_table + turned * sine_table


def unrotate(vectors, cosine_table, sine_table):
    half_width = vectors.shape[-1] // 2
    scaled = vectors * sine_table
    return vectors * cosine_table + jnp.concatenate(
        [scaled[..., half_width:], -scaled[..., :half_width]], axis=-1
    )


def rope_tables(places):
    steps_along = jnp.arange(HD // 2, dtype=f32) * (2.0 / HD)
    inverse = jnp.power(jnp.float32(rope_base), -steps_along)
    angles = places.astype(f32)[..., None] * inverse
    angles = jnp.concatenate([angles, angles], axis=-1)
    return jnp.cos(angles), jnp.sin(angles)


def dot(a, b):
    return jnp.dot(a, b, preferred_element_type=f32)


def dot_t(a, b):
    return jnp.einsum("tf,of->to", a, b, preferred_element_type=f32)


def dot_over(a, b):
    return jnp.einsum("tc,tf->cf", a, b, preferred_element_type=f32)


def ffn_chunk(rows, cots, bits, gate_cols, down_cols, own_expert, units):
    wide = 3 * units
    gate_up = dot(rows, gate_cols)
    g = gate_up[:, :wide]
    u = gate_up[:, wide : 2 * wide]
    logits = gate_up[:, 2 * wide :]
    experts = logits.shape[1] - 1
    expert_logits = logits[:, :experts]
    weights = jnp.exp(expert_logits - jnp.max(expert_logits, axis=1, keepdims=True))
    probs = weights / jnp.sum(weights, axis=1, keepdims=True)
    shared_gate = jax.nn.sigmoid(logits[:, experts:])
    own = (jnp.right_shift(bits[:, None], own_expert + jnp.arange(2, dtype=jnp.int32)[None, :]) & 1).astype(f32)
    own_gates = probs[:, :2] * own
    n = rows.shape[0]

    def spread(a, b, c):
        return jnp.concatenate([jnp.broadcast_to(v, (n, units)) for v in (a, b, c)], axis=1)

    gates = spread(shared_gate, own_gates[:, :1], own_gates[:, 1:])
    hidden_grad = dot(cots, down_cols)
    sig = jax.nn.sigmoid(g)
    silu = g * sig
    hidden = (silu * u).astype(bf16).astype(f32)
    gated = (gates * hidden).astype(bf16)
    gated_grad = hidden_grad * gates
    gate_grad = gated_grad * u * sig * (1.0 + g * (1.0 - sig))
    up_grad = gated_grad * silu
    products = (hidden_grad * hidden).reshape(n, 3, units)
    choice_grad = jnp.sum(products, axis=2)
    own_grad = choice_grad[:, 1:] * own
    weighted = jnp.sum(probs[:, :2] * own_grad, axis=1, keepdims=True)
    probs_grad = jnp.concatenate([own_grad, jnp.zeros((n, experts - 2), f32)], axis=1)
    logit_grad = jnp.concatenate(
        [probs * (probs_grad - weighted), choice_grad[:, :1] * shared_gate * (1.0 - shared_gate)], axis=1
    )
    gate_up_grad = jnp.concatenate([gate_grad, up_grad, logit_grad], axis=1).astype(bf16)
    out_part = dot_t(gated, down_cols).astype(bf16)
    rows_grad = dot_t(gate_up_grad, gate_cols).astype(bf16)
    return out_part, rows_grad, gated, gate_up_grad


def body(lay, tokens, dense_weights, expert_weights, gain_attn, gain_ffn, qkv_bias, router_weight, routes, doc_ids, out_grad):
    row_count, model_width = tokens.shape
    rings = lay.rings
    ring = lax.axis_index("ring")
    pair = lax.axis_index("pair")
    ep = lax.axis_index("ep")
    local_experts = expert_weights.shape[1]
    expert_count = router_weight.shape[1] - 1
    owners = expert_count // local_experts
    dp_count = rings * 2
    score_scale = HD ** (-0.5)
    ring_place = jnp.asarray(lay.place, jnp.int32)[ring]
    behind = [jnp.asarray(lay.order, jnp.int32)[(ring_place - s) % rings] for s in range(rings)]

    stream = tokens.astype(f32)
    gain_one = gain_attn.astype(f32)
    gain_two = gain_ffn.astype(f32)

    heads = H // 8
    share = heads * HD
    mine = dense_weights[:, : 4 * model_width].reshape(dense_weights.shape[0], 4, 8, share)
    mine = mine.transpose(2, 0, 1, 3).reshape(8, dense_weights.shape[0], 4 * share)
    plane_part = lax.all_to_all(mine, PLANE, split_axis=0, concat_axis=0, tiled=True)
    plane_part = plane_part.reshape(1, -1, 4 * share)
    attn_full = jnp.zeros((rings,) + plane_part.shape[1:], bf16)
    moving = plane_part
    for s in range(rings):
        attn_full = lax.dynamic_update_slice(attn_full, moving, (behind[s], 0, 0))
        if s < rings - 1:
            moving = permute(moving, lay.onward)
    attn_full = attn_full.reshape(model_width, 4 * share)
    qkv_cols = attn_full[:, : 3 * share]
    out_cols = attn_full[:, 3 * share :]

    unit_share = SFF // owners
    units = FF // dp_count
    shared = dense_weights[:, 4 * model_width :].reshape(-1, 3, owners, unit_share).transpose(2, 0, 1, 3)
    shared = lax.all_to_all(shared, "ep", split_axis=0, concat_axis=0, tiled=True)
    shared = shared.reshape(-1, 1, 3, dp_count, units)
    routed = expert_weights.reshape(-1, local_experts, 3, dp_count, units)
    ffn = jnp.concatenate([shared, routed], axis=1)
    ffn = ffn.transpose(3, 0, 2, 1, 4).reshape(dp_count, -1, 9 * units)
    ffn = lax.all_to_all(ffn, ("ring", "pair"), split_axis=0, concat_axis=0, tiled=True)
    ffn = ffn.reshape(model_width, 9 * units)
    wide = 3 * units
    own_expert = ep * local_experts
    turn = (own_expert + jnp.arange(expert_count, dtype=jnp.int32)) % expert_count
    router = jnp.concatenate([jnp.take(router_weight, turn, axis=1), router_weight[:, expert_count:]], axis=1)
    gate_cols = jnp.concatenate([ffn[:, : 2 * wide], router], axis=1)
    down_cols = ffn[:, 2 * wide :]

    bits = jnp.sum(jnp.left_shift(jnp.int32(1), routes), axis=1)
    bits = lax.all_gather(bits, AXES, axis=0, tiled=False)
    device_of = []
    for s in range(rings):
        for dy in range(2):
            for dc in range(2):
                for dx in range(2):
                    device_of.append((behind[s] * 2 + (pair ^ dy)) * 4 + (ep ^ (2 * dx + dc)))
    bits = bits[jnp.stack(device_of)].reshape(rings, -1)

    doc_pair = jnp.stack([doc_ids, permute(doc_ids, lay.up)])
    group_len = doc_ids.shape[0]
    before = jnp.sum((doc_pair[:, None, :] < doc_pair[:, :, None]).astype(jnp.int32), axis=2)
    spot = jnp.arange(group_len, dtype=jnp.int32)
    blocks = jnp.stack([ep, ep ^ 2, ep ^ 1, ep ^ 3])

    def in_order(values):
        return values.reshape(2, 4, row_count)[:, blocks].reshape(2, group_len)

    places = in_order(spot[None, :] - before)
    docs = in_order(doc_pair)
    spots = in_order(jnp.stack([spot, spot]))
    cosine, sine = rope_tables(places)
    cosine, sine = cosine[:, :, None, :], sine[:, :, None, :]
    allowed = (docs[:, :, None] == docs[:, None, :]) & (spots[:, None, :] <= spots[:, :, None])
    allowed = allowed[:, None]

    inverse_one = lax.rsqrt(jnp.mean(stream * stream, axis=1, keepdims=True) + norm_eps)
    normed = (stream * inverse_one * gain_one).astype(bf16)
    normed_group = plane_rows(lay, normed)
    slot = pair * 4 + ep
    bias_share = lax.dynamic_slice_in_dim(qkv_bias.astype(f32).reshape(3, 8, share), slot, 1, 1).reshape(3 * share)
    packed = dot(normed_group, qkv_cols) + bias_share

    def split_heads(columns):
        return columns.reshape(2, group_len, heads, HD)

    queries = rotate(split_heads(packed[:, :share]), cosine, sine).astype(bf16)
    keys = rotate(split_heads(packed[:, share : 2 * share]), cosine, sine).astype(bf16)
    values = split_heads(packed[:, 2 * share :].astype(bf16))
    scores = jnp.einsum("gqhd,gkhd->ghqk", queries, keys, preferred_element_type=f32) * score_scale
    scores = jnp.where(allowed, scores, -1e30)
    raw = jnp.exp(scores - jnp.max(scores, axis=3, keepdims=True))
    attend = raw / jnp.sum(raw, axis=3, keepdims=True)
    mixed = jnp.einsum("ghqk,gkhd->gqhd", attend.astype(bf16), values, preferred_element_type=f32)
    mixed = mixed.astype(bf16).reshape(2 * group_len, share)
    branch = plane_sums(lay, dot_t(mixed, out_cols).astype(bf16))
    residual = stream + branch
    inverse_two = lax.rsqrt(jnp.mean(residual * residual, axis=1, keepdims=True) + norm_eps)
    normed_two = (residual * inverse_two * gain_two).astype(bf16)

    cots = all_rows(lay, out_grad)
    rows = all_rows(lay, normed_two)
    chunks = [
        ffn_chunk(rows[s], cots[s], bits[s], gate_cols, down_cols, own_expert, units) for s in range(rings)
    ]
    output_sum = all_sums(lay, [c[0] for c in chunks])
    normed_two_grad = all_sums(lay, [c[1] for c in chunks])
    gate_cols_grad = dot_over(stack(*rows), stack(*[c[3] for c in chunks]))
    down_cols_grad = dot_over(stack(*cots), stack(*[c[2] for c in chunks]))
    output = (residual + output_sum).astype(bf16)

    ffn_grad = jnp.concatenate([gate_cols_grad[:, : 2 * wide].astype(bf16), down_cols_grad.astype(bf16)], axis=1)
    ffn_grad = lax.all_to_all(ffn_grad.reshape(dp_count, -1, 9 * units), ("ring", "pair"), split_axis=0, concat_axis=0, tiled=True)
    ffn_grad = ffn_grad.reshape(dp_count, -1, 3, 3, units).transpose(3, 1, 2, 0, 4)
    expert_grad = ffn_grad[1:].reshape(local_experts, -1, 3 * FF).transpose(1, 0, 2).astype(f32)
    shared_grad = ffn_grad[0].reshape(owners, -1, 3 * unit_share)
    shared_grad = lax.all_to_all(shared_grad, "ep", split_axis=0, concat_axis=0, tiled=True)
    shared_grad = shared_grad.reshape(owners, -1, 3, unit_share).transpose(1, 2, 0, 3).reshape(-1, 3 * SFF)

    router_part = gate_cols_grad[:, 2 * wide :].T
    turn_back = (jnp.arange(expert_count, dtype=jnp.int32) - own_expert) % expert_count
    router_part = jnp.concatenate([jnp.take(router_part[:expert_count], turn_back, axis=0), router_part[expert_count:]], axis=0)

    cotangent = out_grad.astype(f32)
    scaled_two = normed_two_grad * gain_two
    gain_two_grad = jnp.sum(normed_two_grad * residual * inverse_two, axis=0)
    residual_grad = (
        cotangent
        + inverse_two * scaled_two
        - residual * inverse_two**3 * jnp.mean(scaled_two * residual, axis=1, keepdims=True)
    )
    branch_grad = residual_grad.astype(bf16)

    branch_grad_group = plane_rows(lay, branch_grad)
    mixed_grad = dot(branch_grad_group, out_cols).astype(bf16)
    mixed_heads = split_heads(mixed_grad)
    attend_grad = jnp.einsum("gqhd,gkhd->ghqk", mixed_heads, values, preferred_element_type=f32)
    scores_grad = (attend * (attend_grad - jnp.sum(attend * attend_grad, axis=3, keepdims=True))).astype(bf16)
    queries_grad = (jnp.einsum("ghqk,gkhd->gqhd", scores_grad, keys, preferred_element_type=f32) * score_scale).astype(bf16)
    keys_grad = (jnp.einsum("ghqk,gqhd->gkhd", scores_grad, queries, preferred_element_type=f32) * score_scale).astype(bf16)
    values_grad = jnp.einsum("ghqk,gqhd->gkhd", attend.astype(bf16), mixed_heads, preferred_element_type=f32).astype(bf16)
    packed_grad = jnp.concatenate(
        [
            unrotate(queries_grad.astype(f32), cosine, sine).astype(bf16).reshape(2 * group_len, share),
            unrotate(keys_grad.astype(f32), cosine, sine).astype(bf16).reshape(2 * group_len, share),
            values_grad.reshape(2 * group_len, share),
        ],
        axis=1,
    )
    normed_grad = plane_sums(lay, dot_t(packed_grad, qkv_cols).astype(bf16))
    scaled_one = normed_grad * gain_one
    gain_one_grad = jnp.sum(normed_grad * stream * inverse_one, axis=0)
    input_grad = (
        residual_grad
        + inverse_one * scaled_one
        - stream * inverse_one**3 * jnp.mean(scaled_one * stream, axis=1, keepdims=True)
    )
    attn_grad = jnp.concatenate([dot_over(normed_group, packed_grad), dot_over(branch_grad_group, mixed)], axis=1)
    attn_grad = attn_grad.astype(bf16).reshape(rings, -1, 4 * share)
    total = None
    for s in range(rings)[::-1]:
        here = lax.dynamic_index_in_dim(attn_grad, behind[s], 0, keepdims=False).astype(f32)
        if total is not None:
            here = here + permute(total.astype(bf16), lay.backward).astype(f32)
        total = here
    total = total.astype(bf16).reshape(8, -1, 4 * share)
    total = lax.all_to_all(total, PLANE, split_axis=0, concat_axis=0, tiled=True)
    attn_grad = total.reshape(8, -1, 4, share).transpose(1, 2, 0, 3).reshape(-1, 4 * model_width)
    dense_grad = jnp.concatenate([attn_grad, shared_grad], axis=1).astype(f32)

    bias_part = jnp.sum(packed_grad.astype(f32), axis=0).reshape(3, 1, share)
    bias_part = lax.dynamic_update_slice(jnp.zeros((3, 8, share), f32), bias_part, (0, slot, 0))

    def sum_everywhere(values):
        for step in lay.doubling():
            values = values + permute(values, step)
        return values

    early = sum_everywhere(stack(router_part, gain_two_grad[None]))
    late = sum_everywhere(stack(gain_one_grad[None], bias_part.reshape(3, model_width)))
    return (
        output,
        input_grad,
        dense_grad,
        expert_grad,
        late[0],
        early[-1],
        late[1:].reshape(-1),
        early[:-1].T,
    )


def solution(mesh):
    devices = mesh.devices
    lay = Layout(devices.shape[0] // 2)
    inner = Mesh(devices.reshape(lay.rings, 2, devices.shape[1]), AXES)
    rows = P(AXES, None)
    experts = P(("ring", "pair"), "ep", None)
    in_specs = (rows, rows, experts, P(), P(), P(), P(), rows, P(("ring", "pair")), rows)
    out_specs = (rows, rows, rows, experts, P(), P(), P(), P())

    def run(*arguments):
        return body(lay, *arguments)

    return jax.shard_map(run, mesh=inner, in_specs=in_specs, out_specs=out_specs, check_vma=False)
```

time: 2800 us -> 1360 us (0.49)
  waiting for transfers between devices: 2220 us -> 562 us
  starting transfers between devices: 26.4 us -> 147 us
  local copies, waits for them, and re-layouts: 133 us -> 243 us
  blocking collectives: 97.1 us -> 58.4 us
    all_gather x6 -> x0, waiting for transfers between devices: 1130 us -> none  [the longest x1 613 us: body(): expert_full = lax.all_gather(expert_weights, 'dp', axis=0, tiled=True)]
    reduce_scatter x6 -> x0, waiting for transfers between devices: 886 us -> none  [the longest x1 481 us: body(): lax.psum_scatter(expert_terms.astype(jnp.bfloat16), 'dp', scatter_dimensi...]
    ppermute x0 -> x129, waiting for transfers between devices: none -> 562 us  [permute(): return lax.ppermute(rows, AXES, pairs)]
    ppermute x0 -> x129, starting transfers between devices: none -> 121 us  [permute(): return lax.ppermute(rows, AXES, pairs)]
    psum x1 -> x0, waiting for transfers between devices: 115 us -> none  [body(): lax.psum((gain_one_grad, gain_two_grad, bias_grad, router_grad), ('dp', '...]
    all_to_all x5 -> x6, waiting for transfers between devices: 91.6 us -> 0.02 us  [the longest x1 0.01 us: body(): lax.all_to_all(ffn, ('ring', 'pair'), split_axis=0, concat_axis=0, tiled=...]
    unnamed x150 -> x393, local copies, waits for them, and re-layouts: 53 us -> 122 us
    all_gather x0 -> x1, blocking collectives: none -> 58.4 us  [body(): bits = lax.all_gather(bits, AXES, axis=0, tiled=False)]
  transfers between devices with their start and end apart: 18 -> 135, of which waited for: 12 -> 42; matrix products, arithmetic and copies ran while one was open for 12% -> 31% of each run, Pallas kernels for 0% -> 0%
where the time goes in v1:
time: 1360 us; the launch traced here: 1350 us
  waiting for transfers between devices  562 us (41%)
  local copies, waits for them, and re-layouts  243 us (18%)
  matrix products  209 us (15%)
  starting transfers between devices  147 us (11%)
  other arithmetic  113 us (8%)
  blocking collectives  58.4 us (4%)
  between operations  18.2 us (1%)
    ppermute x129, waiting for transfers between devices, permute(): return lax.ppermute(rows, AXES, pairs)  562 us
    unnamed x393, local copies, waits for them, and re-layouts  122 us
    ppermute x129, starting transfers between devices, permute(): return lax.ppermute(rows, AXES, pairs)  121 us
    dot_general x10, matrix products, dot(): return jnp.dot(a, b, preferred_element_type=f32)  70.9 us
    dot_general x4, matrix products, dot_over(): return jnp.einsum('tc,tf->cf', a, b, preferred_element_type=f32)  69.5 us
    all_gather x1, blocking collectives, body(): bits = lax.all_gather(bits, AXES, axis=0, tiled=False)  58.4 us
    dot_general x10, matrix products, dot_t(): return jnp.einsum('tf,of->to', a, b, preferred_element_type=f32)  53.1 us
  transfers between devices with their start and end apart: 135, of which 42 were waited for; matrix products, arithmetic and copies ran while one was open for 31% of the time, Pallas kernels for 0%

profile of v1, /device:TPU:0, one launch (start us, length us, event | category | flops | bytes accessed | tf_op | source)
XLA Modules:
  0.0 1349.9 jit_solution(15680798817855044646)
XLA Ops:
  30.0 58.4 %all-gather.1 = s32[32,1,128]{2,1,0:T(1,128)S(1)} all-gather(s32[1,1,128]{2,1,0:T(1,128)S(1)} %bitcast.294), channel_id=2, replica_groups=mesh['ring'=4,'pair'=2,'ep'=4] {'ring','pair','ep'}, dimensions={0}, use_global_device_ids=true | all-gather | bytes 16896 | tf_op jit(solution)/shard_map/all_gather | solution.py:223
  96.6 11.8 copy.200
  135.7 12.3 collective-permute-done.62
  162.0 8.0 collective-permute-done.73
  187.0 10.5 collective-permute-done.82
  216.5 6.3 reshape.1851
  252.1 60.5 %collective-permute-done.95 = bf16[128,2048]{1,0:T(8,128)(2,1)S(1)} collective-permute-done((bf16[128,2048]{1,0:T(8,128)(2,1)}, bf16[128,2048]{1,0:T(8,128)(2,1)S(1)}, u32[]{:S(2)}, u32[]{:S(2)}) %collective-permute-start.95) | collective-permute-done | bytes 524320 | tf_op jit(solution)/shard_map/ppermute | solution.py:52
  314.3 57.8 %collective-permute-done.6 = bf16[1,512,1024]{2,1,0:T(8,128)(2,1)S(1)} collective-permute-done((bf16[1,512,1024]{2,1,0:T(8,128)(2,1)}, bf16[1,512,1024]{2,1,0:T(8,128)(2,1)S(1)}, u32[]{:S(2)}, u32[]{:S(2)}) %collective-permute-start.6) | collective-permute-done | bytes 1048608 | tf_op jit(solution)/shard_map/ppermute | solution.py:52
  383.8 15.8 %collective-permute-done.7 = bf16[1,512,1024]{2,1,0:T(8,128)(2,1)S(1)} collective-permute-done((bf16[1,512,1024]{2,1,0:T(8,128)(2,1)S(1)}, bf16[1,512,1024]{2,1,0:T(8,128)(2,1)S(1)}, u32[]{:S(2)}, u32[]{:S(2)}) %collective-permute-start.7) | collective-permute-done | bytes 1048608 | tf_op jit(solution)/shard_map/ppermute | solution.py:52
  399.7 6.9 fusion.94
  445.0 8.8 collective-permute-done.13
  453.7 9.5 collective-permute-done.12
  470.2 10.0 collective-permute-start.24
  482.9 9.9 collective-permute-done.24
  498.7 8.9 collective-permute-done.25
  507.8 8.7 collective-permute-done.27
  519.5 11.4 collective-permute-done.36
  534.5 10.8 collective-permute-done.39
  563.2 12.0 collective-permute-done.49
  601.3 8.6 fusion.203
  619.1 7.2 fusion.204
  640.9 9.7 multiply_convert_fusion.2
  653.4 9.7 multiply_convert_fusion.6
  664.5 9.7 multiply_convert_fusion.4
  682.2 6.4 convolution_convert_fusion
  701.4 7.5 convolution_convert_fusion.4
  712.1 6.2 convolution_convert_fusion.5
  721.2 7.2 convolution_convert_fusion.6
  731.3 7.6 convolution_convert_fusion.7
  772.4 6.9 collective-permute-done.102
  779.8 10.7 collective-permute-done.101
  792.0 9.8 collective-permute-done.56
  802.6 21.1 %collective-permute-done.55 = bf16[128,2048]{1,0:T(8,128)(2,1)S(1)} collective-permute-done((bf16[128,2048]{1,0:T(8,128)(2,1)S(1)}, bf16[128,2048]{1,0:T(8,128)(2,1)S(1)}, u32[]{:S(2)}, u32[]{:S(2)}) %collective-permute-start.55) | collective-permute-done | bytes 524320 | tf_op jit(solution)/shard_map/ppermute | solution.py:52
  840.5 17.5 %collective-permute-done.45 = bf16[128,2048]{1,0:T(8,128)(2,1)S(1)} collective-permute-done((bf16[128,2048]{1,0:T(8,128)(2,1)S(1)}, bf16[128,2048]{1,0:T(8,128)(2,1)S(1)}, u32[]{:S(2)}, u32[]{:S(2)}) %collective-permute-start.45) | collective-permute-done | bytes 524320 | tf_op jit(solution)/shard_map/ppermute | solution.py:52
  858.4 10.5 collective-permute-done.44
  888.1 17.8 %collective-permute-done.34 = bf16[128,2048]{1,0:T(8,128)(2,1)S(1)} collective-permute-done((bf16[128,2048]{1,0:T(8,128)(2,1)S(1)}, bf16[128,2048]{1,0:T(8,128)(2,1)S(1)}, u32[]{:S(2)}, u32[]{:S(2)}) %collective-permute-start.34) | collective-permute-done | bytes 524320 | tf_op jit(solution)/shard_map/ppermute | solution.py:52
  907.6 8.5 collective-permute-done.33
  933.6 47.4 %fusion.1 = f32[2048,1065]{0,1:T(8,128)} fusion(bf16[4096,2048]{1,0:T(8,128)(2,1)} %get-tuple-element.136, bf16[1024,1]{0,1:T(2,128)(2,1)S(1)} %copy-done.140, bf16[1024,8]{0,1:T(8,128)(2,1)S(1)} %multiply_convert_fusion.14, bf16[1024,528]{0,1:T(8,128)(2,1)} %get-tuple-element.85, bf16[1024,528]{0,1:T(8,128)(2,1)} %get-tuple-element.84, ...), kind=kOutput, calls=%fused_computation.7 | convolution fusion | flops 18007326720 | bytes 34226176 | tf_op jit(solution)/shard_map/tc,tf->cf/dot_general | solution.py:127
  988.6 12.8 fusion.42
  1001.5 6.2 slice.962
  1015.6 13.1 collective-permute-done.108
  1063.6 6.5 copy.230
  1075.1 5.8 convolution_convert_fusion.10
  1087.1 118.9 %collective-permute-done.116 = bf16[512,1024]{1,0:T(8,128)(2,1)S(1)} collective-permute-done((bf16[512,1024]{1,0:T(8,128)(2,1)S(1)}, bf16[512,1024]{1,0:T(8,128)(2,1)S(1)}, u32[]{:S(2)}, u32[]{:S(2)}) %collective-permute-start.116) | collective-permute-done | bytes 1048608 | tf_op jit(solution)/shard_map/ppermute | solution.py:52
  1218.1 13.9 %collective-permute-done.117 = bf16[512,1024]{1,0:T(8,128)(2,1)S(1)} collective-permute-done((bf16[512,1024]{1,0:T(8,128)(2,1)S(1)}, bf16[512,1024]{1,0:T(8,128)(2,1)S(1)}, u32[]{:S(2)}, u32[]{:S(2)}) %collective-permute-start.117) | collective-permute-done | bytes 1048608 | tf_op jit(solution)/shard_map/ppermute | solution.py:52
  1243.4 15.2 %collective-permute-done.118 = bf16[512,1024]{1,0:T(8,128)(2,1)} collective-permute-done((bf16[512,1024]{1,0:T(8,128)(2,1)}, bf16[512,1024]{1,0:T(8,128)(2,1)}, u32[]{:S(2)}, u32[]{:S(2)}) %collective-permute-start.118) | collective-permute-done | bytes 1048608 | tf_op jit(solution)/shard_map/ppermute | solution.py:52
  1286.4 6.2 reshape_squeeze.3
  1320.2 13.9 %copy.221 = f32[256,2,4224]{2,1,0:T(2,128)} copy(f32[256,2,4224]{0,2,1:T(8,128)} %bitcast.222) | data formatting | bytes 17301504
  (907 shorter events, 550.9 us)
Async XLA Ops:
  5.4 116.4 %collective-permute-start = (bf16[128,2048]{1,0:T(8,128)(2,1)}, bf16[128,2048]{1,0:T(8,128)(2,1)}, u32[]{:S(2)}, u32[]{:S(2)}) collective-permute-start(bf16[128,2048]{1,0:T(8,128)(2,1)} %get-tuple-element.77), channel_id=1, source_target_pairs={{0,2},{1,3},{2,0},{3,1},{4,6},{5,7},{6,4},{7,5},{8,10},{9,11},{10,... | collective-permute-start | bytes 1572872 | tf_op jit(solution)/shard_map/ppermute | solution.py:52
  8.3 118.4 %collective-permute-start.2 = (bf16[128,2048]{1,0:T(8,128)(2,1)}, bf16[128,2048]{1,0:T(8,128)(2,1)}, u32[]{:S(2)}, u32[]{:S(2)}) collective-permute-start(bf16[128,2048]{1,0:T(8,128)(2,1)} %get-tuple-element.77), channel_id=1, source_target_pairs={{0,4},{1,5},{2,6},{3,7},{4,0},{5,1},{6,2},{7,3},{8,12},{9,13},{10,... | collective-permute-start | bytes 1572872 | tf_op jit(solution)/shard_map/ppermute | solution.py:52
  9.9 121.5 %collective-permute-start.3 = (bf16[128,2048]{1,0:T(8,128)(2,1)}, bf16[128,2048]{1,0:T(8,128)(2,1)}, u32[]{:S(2)}, u32[]{:S(2)}) collective-permute-start(bf16[128,2048]{1,0:T(8,128)(2,1)} %get-tuple-element.77), channel_id=1, source_target_pairs={{0,6},{1,7},{2,4},{3,5},{4,2},{5,3},{6,0},{7,1},{8,14},{9,15},{10,... | collective-permute-start | bytes 1572872 | tf_op jit(solution)/shard_map/ppermute | solution.py:52
  12.1 139.7 %all-to-all-start = ((bf16[8,64,1024]{2,1,0:T(8,128)(2,1)}), bf16[8,64,1024]{2,1,0:T(8,128)(2,1)}, u32[]{:S(2)}, u32[]{:S(2)}) async-start(bf16[8,64,1024]{2,1,0:T(8,128)(2,1)} %reshape.1759), calls=%async_computation | async-start | bytes 2097152 | tf_op jit(solution)/shard_map/all_to_all | solution.py:193
  16.4 100.4 %collective-permute-start.8 = (s32[512]{0:T(512)S(1)}, s32[512]{0:T(512)S(1)}, u32[]{:S(2)}, u32[]{:S(2)}) collective-permute-start(s32[512]{0:T(512)S(1)} %copy-done.129), channel_id=1, source_target_pairs={{0,4},{1,5},{2,6},{3,7},{4,0},{5,1},{6,2},{7,3},{8,12},{9,13},{10,... | collective-permute-start | bytes 6152 | tf_op jit(solution)/shard_map/ppermute | solution.py:52
  18.4 106.0 %collective-permute-start.60 = (bf16[128,2048]{1,0:T(8,128)(2,1)}, bf16[128,2048]{1,0:T(8,128)(2,1)}, u32[]{:S(2)}, u32[]{:S(2)}) collective-permute-start(bf16[128,2048]{1,0:T(8,128)(2,1)} %param.24), channel_id=1, source_target_pairs={{0,2},{1,3},{2,0},{3,1},{4,6},{5,7},{6,4},{7,5},{8,10},{9,11},{10,... | collective-permute-start | bytes 1572872 | tf_op jit(solution)/shard_map/ppermute | solution.py:52
  126.7 46.1 %collective-permute-start.61 = (bf16[256,2048]{1,0:T(8,128)(2,1)}, bf16[256,2048]{1,0:T(8,128)(2,1)}, u32[]{:S(2)}, u32[]{:S(2)}) collective-permute-start(bf16[256,2048]{1,0:T(8,128)(2,1)} %pad_maximum_fusion.16), channel_id=1, source_target_pairs={{0,1},{1,0},{2,3},{3,2},{4,5},{5,4},{6,7},{7,6},{8,9},{9,8},{10,11... | collective-permute-start | bytes 3145736 | tf_op jit(solution)/shard_map/ppermute | solution.py:52
  131.3 38.7 %collective-permute-start.73 = (bf16[128,2048]{1,0:T(8,128)(2,1)}, bf16[128,2048]{1,0:T(8,128)(2,1)}, u32[]{:S(2)}, u32[]{:S(2)}) collective-permute-start(bf16[128,2048]{1,0:T(8,128)(2,1)} %collective-permute-done.70), channel_id=1, source_target_pairs={{0,4},{1,5},{2,6},{3,7},{4,0},{5,1},{6,2},{7,3},{8,12},{9,13},{10,... | collective-permute-start | bytes 1572872 | tf_op jit(solution)/shard_map/ppermute | solution.py:52
  151.8 59.3 %all-to-all-start.1 = ((bf16[4,64,3,1408]{3,1,2,0:T(8,128)(2,1)}), bf16[4,64,3,1408]{3,1,2,0:T(8,128)(2,1)S(1)}, u32[]{:S(2)}, u32[]{:S(2)}) async-start(bf16[4,64,3,1408]{3,1,2,0:T(8,128)(2,1)} %copy.198), calls=%async_computation.1 | async-start | bytes 4325376 | tf_op jit(solution)/shard_map/all_to_all | solution.py:208
  172.8 61.1 %collective-permute-start.5 = (bf16[1,512,1024]{2,1,0:T(8,128)(2,1)}, bf16[1,512,1024]{2,1,0:T(8,128)(2,1)}, u32[]{:S(2)}, u32[]{:S(2)}) collective-permute-start(bf16[1,512,1024]{2,1,0:T(8,128)(2,1)} %bitcast.1), channel_id=1, source_target_pairs={{0,16},{1,17},{2,18},{3,19},{4,20},{5,21},{6,22},{7,23},{8,0},{9,1... | collective-permute-start | bytes 3145736 | tf_op jit(solution)/shard_map/ppermute | solution.py:52
  201.8 36.4 %collective-permute-start.72 = (bf16[256,2048]{1,0:T(8,128)(2,1)}, bf16[256,2048]{1,0:T(8,128)(2,1)}, u32[]{:S(2)}, u32[]{:S(2)}) collective-permute-start(bf16[256,2048]{1,0:T(8,128)(2,1)} %pad_maximum_fusion.18), channel_id=1, source_target_pairs={{0,1},{1,0},{2,3},{3,2},{4,5},{5,4},{6,7},{7,6},{8,9},{9,8},{10,11... | collective-permute-start | bytes 3145736 | tf_op jit(solution)/shard_map/ppermute | solution.py:52
  205.1 109.1 %collective-permute-start.75 = (bf16[256,2048]{1,0:T(8,128)(2,1)}, bf16[256,2048]{1,0:T(8,128)(2,1)}, u32[]{:S(2)}, u32[]{:S(2)}) collective-permute-start(bf16[256,2048]{1,0:T(8,128)(2,1)} %pad_maximum_fusion.19), channel_id=1, source_target_pairs={{0,1},{1,0},{2,3},{3,2},{4,5},{5,4},{6,7},{7,6},{8,9},{9,8},{10,11... | collective-permute-start | bytes 3145736 | tf_op jit(solution)/shard_map/ppermute | solution.py:52
  207.8 173.4 %collective-permute-start.83 = (bf16[256,2048]{1,0:T(8,128)(2,1)}, bf16[256,2048]{1,0:T(8,128)(2,1)}, u32[]{:S(2)}, u32[]{:S(2)}) collective-permute-start(bf16[256,2048]{1,0:T(8,128)(2,1)} %pad_maximum_fusion.20), channel_id=1, source_target_pairs={{0,1},{1,0},{2,3},{3,2},{4,5},{5,4},{6,7},{7,6},{8,9},{9,8},{10,11... | collective-permute-start | bytes 3145736 | tf_op jit(solution)/shard_map/ppermute | solution.py:52
  210.0 33.4 %collective-permute-start.93 = (bf16[128,2048]{1,0:T(8,128)(2,1)}, bf16[128,2048]{1,0:T(8,128)(2,1)}, u32[]{:S(2)}, u32[]{:S(2)}) collective-permute-start(bf16[128,2048]{1,0:T(8,128)(2,1)} %collective-permute-done.92), channel_id=1, source_target_pairs={{0,2},{1,3},{2,0},{3,1},{4,6},{5,7},{6,4},{7,5},{8,10},{9,11},{10,... | collective-permute-start | bytes 1572872 | tf_op jit(solution)/shard_map/ppermute | solution.py:52
  228.8 358.6 %all-to-all-start.2 = ((bf16[8,256,1584]{1,2,0:T(8,128)(2,1)}), bf16[8,256,1584]{1,2,0:T(8,128)(2,1)}, u32[]{:S(2)}, u32[]{:S(2)}) async-start(bf16[8,256,1584]{1,2,0:T(8,128)(2,1)} %bitcast.223), calls=%async_computation.2 | async-start | bytes 12976128 | tf_op jit(solution)/shard_map/all_to_all | solution.py:213
  233.9 78.8 %collective-permute-start.95 = (bf16[128,2048]{1,0:T(8,128)(2,1)}, bf16[128,2048]{1,0:T(8,128)(2,1)S(1)}, u32[]{:S(2)}, u32[]{:S(2)}) collective-permute-start(bf16[128,2048]{1,0:T(8,128)(2,1)} %collective-permute-done.92), channel_id=1, source_target_pairs={{0,4},{1,5},{2,6},{3,7},{4,0},{5,1},{6,2},{7,3},{8,12},{9,13},{10,... | collective-permute-start | bytes 1572872 | tf_op jit(solution)/shard_map/ppermute | solution.py:52
  238.2 133.9 %collective-permute-start.6 = (bf16[1,512,1024]{2,1,0:T(8,128)(2,1)}, bf16[1,512,1024]{2,1,0:T(8,128)(2,1)S(1)}, u32[]{:S(2)}, u32[]{:S(2)}) collective-permute-start(bf16[1,512,1024]{2,1,0:T(8,128)(2,1)} %collective-permute-done.5), channel_id=1, source_target_pairs={{0,16},{1,17},{2,18},{3,19},{4,20},{5,21},{6,22},{7,23},{8,0},{9,1... | collective-permute-start | bytes 3145736 | tf_op jit(solution)/shard_map/ppermute | solution.py:52
  243.4 69.2 %collective-permute-start.96 = (bf16[128,2048]{1,0:T(8,128)(2,1)}, bf16[128,2048]{1,0:T(8,128)(2,1)S(1)}, u32[]{:S(2)}, u32[]{:S(2)}) collective-permute-start(bf16[128,2048]{1,0:T(8,128)(2,1)} %collective-permute-done.92), channel_id=1, source_target_pairs={{0,6},{1,7},{2,4},{3,5},{4,2},{5,3},{6,0},{7,1},{8,14},{9,15},{10,... | collective-permute-start | bytes 1572872 | tf_op jit(solution)/shard_map/ppermute | solution.py:52
  312.6 117.7 %collective-permute-start.86 = (bf16[256,2048]{1,0:T(8,128)(2,1)}, bf16[256,2048]{1,0:T(8,128)(2,1)}, u32[]{:S(2)}, u32[]{:S(2)}) collective-permute-start(bf16[256,2048]{1,0:T(8,128)(2,1)} %pad_maximum_fusion.21), channel_id=1, source_target_pairs={{0,1},{1,0},{2,3},{3,2},{4,5},{5,4},{6,7},{7,6},{8,9},{9,8},{10,11... | collective-permute-start | bytes 3145736 | tf_op jit(solution)/shard_map/ppermute | solution.py:52
  312.6 129.0 %collective-permute-start.94 = (bf16[256,2048]{1,0:T(8,128)(2,1)}, bf16[256,2048]{1,0:T(8,128)(2,1)}, u32[]{:S(2)}, u32[]{:S(2)}) collective-permute-start(bf16[256,2048]{1,0:T(8,128)(2,1)} %pad_maximum_fusion.22), channel_id=1, source_target_pairs={{0,1},{1,0},{2,3},{3,2},{4,5},{5,4},{6,7},{7,6},{8,9},{9,8},{10,11... | collective-permute-start | bytes 3145736 | tf_op jit(solution)/shard_map/ppermute | solution.py:52
  314.2 166.0 %collective-permute-start.97 = (bf16[256,2048]{1,0:T(8,128)(2,1)}, bf16[256,2048]{1,0:T(8,128)(2,1)}, u32[]{:S(2)}, u32[]{:S(2)}) collective-permute-start(bf16[256,2048]{1,0:T(8,128)(2,1)} %pad_maximum_fusion.23), channel_id=1, source_target_pairs={{0,1},{1,0},{2,3},{3,2},{4,5},{5,4},{6,7},{7,6},{8,9},{9,8},{10,11... | collective-permute-start | bytes 3145736 | tf_op jit(solution)/shard_map/ppermute | solution.py:52
  482.8 35.4 %collective-permute-start.15 = (bf16[256,2048]{1,0:T(8,128)(2,1)S(1)}, bf16[256,2048]{1,0:T(8,128)(2,1)S(1)}, u32[]{:S(2)}, u32[]{:S(2)}) collective-permute-start(bf16[256,2048]{1,0:T(8,128)(2,1)S(1)} %pad_maximum_fusion.8), channel_id=1, source_target_pairs={{0,1},{1,0},{2,3},{3,2},{4,5},{5,4},{6,7},{7,6},{8,9},{9,8},{10,11... | collective-permute-start | bytes 3145736 | tf_op jit(solution)/shard_map/ppermute | solution.py:52
  507.7 37.8 %collective-permute-start.18 = (bf16[256,2048]{1,0:T(8,128)(2,1)S(1)}, bf16[256,2048]{1,0:T(8,128)(2,1)S(1)}, u32[]{:S(2)}, u32[]{:S(2)}) collective-permute-start(bf16[256,2048]{1,0:T(8,128)(2,1)S(1)} %pad_maximum_fusion.9), channel_id=1, source_target_pairs={{0,1},{1,0},{2,3},{3,2},{4,5},{5,4},{6,7},{7,6},{8,9},{9,8},{10,11... | collective-permute-start | bytes 3145736 | tf_op jit(solution)/shard_map/ppermute | solution.py:52
  516.5 33.9 %collective-permute-start.26 = (bf16[256,2048]{1,0:T(8,128)(2,1)S(1)}, bf16[256,2048]{1,0:T(8,128)(2,1)S(1)}, u32[]{:S(2)}, u32[]{:S(2)}) collective-permute-start(bf16[256,2048]{1,0:T(8,128)(2,1)S(1)} %pad_maximum_fusion.10), channel_id=1, source_target_pairs={{0,1},{1,0},{2,3},{3,2},{4,5},{5,4},{6,7},{7,6},{8,9},{9,8},{10,11... | collective-permute-start | bytes 3145736 | tf_op jit(solution)/shard_map/ppermute | solution.py:52
  517.9 35.8 %collective-permute-start.29 = (bf16[256,2048]{1,0:T(8,128)(2,1)S(1)}, bf16[256,2048]{1,0:T(8,128)(2,1)S(1)}, u32[]{:S(2)}, u32[]{:S(2)}) collective-permute-start(bf16[256,2048]{1,0:T(8,128)(2,1)S(1)} %pad_maximum_fusion.11), channel_id=1, source_target_pairs={{0,1},{1,0},{2,3},{3,2},{4,5},{5,4},{6,7},{7,6},{8,9},{9,8},{10,11... | collective-permute-start | bytes 3145736 | tf_op jit(solution)/shard_map/ppermute | solution.py:52
  545.4 32.9 %collective-permute-start.40 = (bf16[256,2048]{1,0:T(8,128)(2,1)S(1)}, bf16[256,2048]{1,0:T(8,128)(2,1)S(1)}, u32[]{:S(2)}, u32[]{:S(2)}) collective-permute-start(bf16[256,2048]{1,0:T(8,128)(2,1)S(1)} %pad_maximum_fusion.13), channel_id=1, source_target_pairs={{0,1},{1,0},{2,3},{3,2},{4,5},{5,4},{6,7},{7,6},{8,9},{9,8},{10,11... | collective-permute-start | bytes 3145736 | tf_op jit(solution)/shard_map/ppermute | solution.py:52
  710.5 33.1 %collective-permute-start.98 = (bf16[256,2048]{1,0:T(8,128)(2,1)}, bf16[256,2048]{1,0:T(8,128)(2,1)S(1)}, u32[]{:S(2)}, u32[]{:S(2)}) collective-permute-start(bf16[256,2048]{1,0:T(8,128)(2,1)} %get-tuple-element.112), channel_id=1, source_target_pairs={{0,1},{1,0},{2,3},{3,2},{4,5},{5,4},{6,7},{7,6},{8,9},{9,8},{10,11... | collective-permute-start | bytes 3145736 | tf_op jit(solution)/shard_map/ppermute | solution.py:52
  768.9 32.9 %collective-permute-start.56 = (bf16[128,2048]{1,0:T(8,128)(2,1)S(1)}, bf16[128,2048]{1,0:T(8,128)(2,1)S(1)}, u32[]{:S(2)}, u32[]{:S(2)}) collective-permute-start(bf16[128,2048]{1,0:T(8,128)(2,1)S(1)} %get-tuple-element.190), channel_id=1, source_target_pairs={{0,6},{1,7},{2,4},{3,5},{4,2},{5,3},{6,0},{7,1},{8,14},{9,15},{10,... | collective-permute-start | bytes 1572872 | tf_op jit(solution)/shard_map/ppermute | solution.py:52
  769.5 54.2 %collective-permute-start.55 = (bf16[128,2048]{1,0:T(8,128)(2,1)S(1)}, bf16[128,2048]{1,0:T(8,128)(2,1)S(1)}, u32[]{:S(2)}, u32[]{:S(2)}) collective-permute-start(bf16[128,2048]{1,0:T(8,128)(2,1)S(1)} %get-tuple-element.189), channel_id=1, source_target_pairs={{0,4},{1,5},{2,6},{3,7},{4,0},{5,1},{6,2},{7,3},{8,12},{9,13},{10,... | collective-permute-start | bytes 1572872 | tf_op jit(solution)/shard_map/ppermute | solution.py:52
  779.3 50.0 %collective-permute-start.91 = (bf16[128,2048]{1,0:T(8,128)(2,1)S(1)}, bf16[128,2048]{1,0:T(8,128)(2,1)S(1)}, u32[]{:S(2)}, u32[]{:S(2)}) collective-permute-start(bf16[128,2048]{1,0:T(8,128)(2,1)S(1)} %copy-done.82), channel_id=1, source_target_pairs={{0,6},{1,7},{2,4},{3,5},{4,2},{5,3},{6,0},{7,1},{8,14},{9,15},{10,... | collective-permute-start | bytes 1572872 | tf_op jit(solution)/shard_map/ppermute | solution.py:52
  790.6 44.8 %collective-permute-start.90 = (bf16[128,2048]{1,0:T(8,128)(2,1)S(1)}, bf16[128,2048]{1,0:T(8,128)(2,1)S(1)}, u32[]{:S(2)}, u32[]{:S(2)}) collective-permute-start(bf16[128,2048]{1,0:T(8,128)(2,1)S(1)} %copy-done.81), channel_id=1, source_target_pairs={{0,4},{1,5},{2,6},{3,7},{4,0},{5,1},{6,2},{7,3},{8,12},{9,13},{10,... | collective-permute-start | bytes 1572872 | tf_op jit(solution)/shard_map/ppermute | solution.py:52
  790.9 37.5 %collective-permute-start.53 = (bf16[128,2048]{1,0:T(8,128)(2,1)S(1)}, bf16[128,2048]{1,0:T(8,128)(2,1)S(1)}, u32[]{:S(2)}, u32[]{:S(2)}) collective-permute-start(bf16[128,2048]{1,0:T(8,128)(2,1)S(1)} %slice.704), channel_id=1, source_target_pairs={{0,2},{1,3},{2,0},{3,1},{4,6},{5,7},{6,4},{7,5},{8,10},{9,11},{10,... | collective-permute-start | bytes 1572872 | tf_op jit(solution)/shard_map/ppermute | solution.py:52
  801.9 33.8 %collective-permute-start.88 = (bf16[128,2048]{1,0:T(8,128)(2,1)S(1)}, bf16[128,2048]{1,0:T(8,128)(2,1)S(1)}, u32[]{:S(2)}, u32[]{:S(2)}) collective-permute-start(bf16[128,2048]{1,0:T(8,128)(2,1)S(1)} %slice.734), channel_id=1, source_target_pairs={{0,2},{1,3},{2,0},{3,1},{4,6},{5,7},{6,4},{7,5},{8,10},{9,11},{10,... | collective-permute-start | bytes 1572872 | tf_op jit(solution)/shard_map/ppermute | solution.py:52
  828.4 45.2 %collective-permute-start.80 = (bf16[128,2048]{1,0:T(8,128)(2,1)S(1)}, bf16[128,2048]{1,0:T(8,128)(2,1)S(1)}, u32[]{:S(2)}, u32[]{:S(2)}) collective-permute-start(bf16[128,2048]{1,0:T(8,128)(2,1)S(1)} %copy-done.80), channel_id=1, source_target_pairs={{0,6},{1,7},{2,4},{3,5},{4,2},{5,3},{6,0},{7,1},{8,14},{9,15},{10,... | collective-permute-start | bytes 1572872 | tf_op jit(solution)/shard_map/ppermute | solution.py:52
  835.3 33.5 %collective-permute-start.44 = (bf16[128,2048]{1,0:T(8,128)(2,1)S(1)}, bf16[128,2048]{1,0:T(8,128)(2,1)S(1)}, u32[]{:S(2)}, u32[]{:S(2)}) collective-permute-start(bf16[128,2048]{1,0:T(8,128)(2,1)S(1)} %get-tuple-element.187), channel_id=1, source_target_pairs={{0,4},{1,5},{2,6},{3,7},{4,0},{5,1},{6,2},{7,3},{8,12},{9,13},{10,... | collective-permute-start | bytes 1572872 | tf_op jit(solution)/shard_map/ppermute | solution.py:52
  835.7 34.0 %collective-permute-start.42 = (bf16[128,2048]{1,0:T(8,128)(2,1)S(1)}, bf16[128,2048]{1,0:T(8,128)(2,1)S(1)}, u32[]{:S(2)}, u32[]{:S(2)}) collective-permute-start(bf16[128,2048]{1,0:T(8,128)(2,1)S(1)} %slice.688), channel_id=1, source_target_pairs={{0,2},{1,3},{2,0},{3,1},{4,6},{5,7},{6,4},{7,5},{8,10},{9,11},{10,... | collective-permute-start | bytes 1572872 | tf_op jit(solution)/shard_map/ppermute | solution.py:52
  869.7 51.2 %collective-permute-start.69 = (bf16[128,2048]{1,0:T(8,128)(2,1)S(1)}, bf16[128,2048]{1,0:T(8,128)(2,1)S(1)}, u32[]{:S(2)}, u32[]{:S(2)}) collective-permute-start(bf16[128,2048]{1,0:T(8,128)(2,1)S(1)} %get-tuple-element.176), channel_id=1, source_target_pairs={{0,6},{1,7},{2,4},{3,5},{4,2},{5,3},{6,0},{7,1},{8,14},{9,15},{10,... | collective-permute-start | bytes 1572872 | tf_op jit(solution)/shard_map/ppermute | solution.py:52
  880.0 36.2 %collective-permute-start.33 = (bf16[128,2048]{1,0:T(8,128)(2,1)S(1)}, bf16[128,2048]{1,0:T(8,128)(2,1)S(1)}, u32[]{:S(2)}, u32[]{:S(2)}) collective-permute-start(bf16[128,2048]{1,0:T(8,128)(2,1)S(1)} %get-tuple-element.185), channel_id=1, source_target_pairs={{0,4},{1,5},{2,6},{3,7},{4,0},{5,1},{6,2},{7,3},{8,12},{9,13},{10,... | collective-permute-start | bytes 1572872 | tf_op jit(solution)/shard_map/ppermute | solution.py:52
  883.6 33.3 %collective-permute-start.31 = (bf16[128,2048]{1,0:T(8,128)(2,1)S(1)}, bf16[128,2048]{1,0:T(8,128)(2,1)S(1)}, u32[]{:S(2)}, u32[]{:S(2)}) collective-permute-start(bf16[128,2048]{1,0:T(8,128)(2,1)S(1)} %slice.672), channel_id=1, source_target_pairs={{0,2},{1,3},{2,0},{3,1},{4,6},{5,7},{6,4},{7,5},{8,10},{9,11},{10,... | collective-permute-start | bytes 1572872 | tf_op jit(solution)/shard_map/ppermute | solution.py:52
  884.8 33.8 %collective-permute-start.58 = (bf16[128,2048]{1,0:T(8,128)(2,1)S(1)}, bf16[128,2048]{1,0:T(8,128)(2,1)S(1)}, u32[]{:S(2)}, u32[]{:S(2)}) collective-permute-start(bf16[128,2048]{1,0:T(8,128)(2,1)S(1)} %add_convert_fusion.25), channel_id=1, source_target_pairs={{0,8},{1,9},{2,10},{3,11},{4,12},{5,13},{6,14},{7,15},{8,24},{9,25... | collective-permute-start | bytes 1572872 | tf_op jit(solution)/shard_map/ppermute | solution.py:52
  916.9 64.1 %collective-permute-start.23 = (bf16[128,2048]{1,0:T(8,128)(2,1)}, bf16[128,2048]{1,0:T(8,128)(2,1)}, u32[]{:S(2)}, u32[]{:S(2)}) collective-permute-start(bf16[128,2048]{1,0:T(8,128)(2,1)} %get-tuple-element.184), channel_id=1, source_target_pairs={{0,6},{1,7},{2,4},{3,5},{4,2},{5,3},{6,0},{7,1},{8,14},{9,15},{10,... | collective-permute-start | bytes 1572872 | tf_op jit(solution)/shard_map/ppermute | solution.py:52
  918.6 62.4 %collective-permute-start.22 = (bf16[128,2048]{1,0:T(8,128)(2,1)}, bf16[128,2048]{1,0:T(8,128)(2,1)}, u32[]{:S(2)}, u32[]{:S(2)}) collective-permute-start(bf16[128,2048]{1,0:T(8,128)(2,1)} %get-tuple-element.183), channel_id=1, source_target_pairs={{0,4},{1,5},{2,6},{3,7},{4,0},{5,1},{6,2},{7,3},{8,12},{9,13},{10,... | collective-permute-start | bytes 1572872 | tf_op jit(solution)/shard_map/ppermute | solution.py:52
  920.9 60.1 %collective-permute-start.20 = (bf16[128,2048]{1,0:T(8,128)(2,1)}, bf16[128,2048]{1,0:T(8,128)(2,1)}, u32[]{:S(2)}, u32[]{:S(2)}) collective-permute-start(bf16[128,2048]{1,0:T(8,128)(2,1)} %slice.656), channel_id=1, source_target_pairs={{0,2},{1,3},{2,0},{3,1},{4,6},{5,7},{6,4},{7,5},{8,10},{9,11},{10,... | collective-permute-start | bytes 1572872 | tf_op jit(solution)/shard_map/ppermute | solution.py:52
  927.4 53.6 %collective-permute-start.105 = (bf16[128,2048]{1,0:T(8,128)(2,1)}, bf16[128,2048]{1,0:T(8,128)(2,1)}, u32[]{:S(2)}, u32[]{:S(2)}) collective-permute-start(bf16[128,2048]{1,0:T(8,128)(2,1)} %add_convert_fusion.20), channel_id=1, source_target_pairs={{0,8},{1,9},{2,10},{3,11},{4,12},{5,13},{6,14},{7,15},{8,24},{9,25... | collective-permute-start | bytes 1572872 | tf_op jit(solution)/shard_map/ppermute | solution.py:52
  931.0 50.0 %collective-permute-start.59 = (bf16[128,2048]{1,0:T(8,128)(2,1)}, bf16[128,2048]{1,0:T(8,128)(2,1)}, u32[]{:S(2)}, u32[]{:S(2)}) collective-permute-start(bf16[128,2048]{1,0:T(8,128)(2,1)} %add_convert_fusion.24), channel_id=1, source_target_pairs={{0,8},{1,9},{2,10},{3,11},{4,12},{5,13},{6,14},{7,15},{8,24},{9,25... | collective-permute-start | bytes 1572872 | tf_op jit(solution)/shard_map/ppermute | solution.py:52
  1035.0 226.1 %all-to-all-start.4 = ((bf16[8,256,1584]{1,2,0:T(8,128)(2,1)}), bf16[8,256,1584]{1,2,0:T(8,128)(2,1)}, u32[]{:S(2)}, u32[]{:S(2)}) async-start(bf16[8,256,1584]{1,2,0:T(8,128)(2,1)} %bitcast.224), calls=%async_computation.4 | async-start | bytes 12976128 | tf_op jit(solution)/shard_map/all_to_all | solution.py:285
  1081.1 124.8 %collective-permute-start.116 = (bf16[512,1024]{1,0:T(8,128)(2,1)S(1)}, bf16[512,1024]{1,0:T(8,128)(2,1)S(1)}, u32[]{:S(2)}, u32[]{:S(2)}) collective-permute-start(bf16[512,1024]{1,0:T(8,128)(2,1)S(1)} %fusion.114), channel_id=1, source_target_pairs={{0,8},{1,9},{2,10},{3,11},{4,12},{5,13},{6,14},{7,15},{8,24},{9,25... | collective-permute-start | bytes 3145736 | tf_op jit(solution)/shard_map/ppermute | solution.py:52
  1292.6 41.4 %all-to-all-start.5 = ((bf16[4,64,4224]{2,1,0:T(8,128)(2,1)}), bf16[4,64,4224]{2,1,0:T(8,128)(2,1)}, u32[]{:S(2)}, u32[]{:S(2)}) async-start(bf16[4,64,4224]{2,1,0:T(8,128)(2,1)} %reshape_squeeze.3), calls=%async_computation.5 | async-start | bytes 4325376 | tf_op jit(solution)/shard_map/all_to_all | solution.py:289
  (256 other events, 6406.7 us)

commit v2 on v1

v2 whole, which is shorter than its diff:
```python
import functools

import jax
import jax.numpy as jnp
from jax import lax
from jax.experimental import pallas as pl
from jax.experimental.pallas import tpu as pltpu
from jax.sharding import Mesh, PartitionSpec as P

H = 16
HD = 128
FF = 1408
SFF = 5632

norm_eps = 1e-06
rope_base = 1000000.0
AXES = ("ring", "pair", "ep")
PLANE = ("pair", "ep")
f32 = jnp.float32
bf16 = jnp.bfloat16


class Layout:
    def __init__(self, rings):
        self.rings = rings
        self.order = list(range(0, rings, 2)) + list(range(1, rings, 2))[::-1]
        place = {r: i for i, r in enumerate(self.order)}
        self.place = [place[r] for r in range(rings)]
        self.core = self.pairs(lambda r, y, x, c: (r, y, x, 1 - c))
        self.side = self.pairs(lambda r, y, x, c: (r, y, 1 - x, c))
        self.up = self.pairs(lambda r, y, x, c: (r, 1 - y, x, c))
        self.onward = self.pairs(lambda r, y, x, c: (self.order[(place[r] + 1) % rings], y, x, c))
        self.backward = self.pairs(lambda r, y, x, c: (self.order[(place[r] - 1) % rings], y, x, c))

    def pairs(self, move):
        found = []
        for r in range(self.rings):
            for y in range(2):
                for x in range(2):
                    for c in range(2):
                        u, v, w, q = move(r, y, x, c)
                        found.append((((r * 2 + y) * 2 + x) * 2 + c, ((u * 2 + v) * 2 + w) * 2 + q))
        return found

    def doubling(self):
        steps = []
        bit = 1
        while bit < self.rings * 8:
            steps.append([(i, i ^ bit) for i in range(self.rings * 8)])
            bit *= 2
        return steps


def permute(rows, pairs):
    return lax.ppermute(rows, AXES, pairs)


def stack(*parts):
    return jnp.concatenate(parts, axis=0)


def plus(a, b):
    return (a.astype(f32) + b.astype(f32)).astype(bf16)


def plane_rows(lay, rows):
    side = permute(rows, lay.side)
    up = permute(rows, lay.up)
    near, far = stack(rows, side), stack(up, permute(up, lay.side))
    return stack(near, permute(near, lay.core), far, permute(far, lay.core))


def plane_sums(lay, own, other):
    n = own.shape[0] // 4
    here = plus(own, permute(other, lay.core))
    up = plus(here[2 * n : 3 * n], permute(here[3 * n :], lay.side))
    total = here[:n].astype(f32) + permute(here[n : 2 * n], lay.side).astype(f32)
    return total + permute(up, lay.up).astype(f32)


def rope_tables(places):
    steps_along = jnp.arange(HD // 2, dtype=f32) * (2.0 / HD)
    inverse = jnp.power(jnp.float32(rope_base), -steps_along)
    angles = places.astype(f32)[..., None] * inverse
    angles = jnp.concatenate([angles, angles], axis=-1)
    return jnp.cos(angles), jnp.sin(angles)


def dot(a, b):
    return jnp.dot(a, b, preferred_element_type=f32)


def dot_over(a, b):
    return jnp.einsum("tc,tf->cf", a, b, preferred_element_type=f32)


def after(value, *others):
    return lax.optimization_barrier((value,) + others)[0]


def together(*values):
    return lax.optimization_barrier(values)


def dot_nt(a, b):
    return lax.dot_general(a, b, (((1,), (1,)), ((), ())), preferred_element_type=f32)


def dot_tn(a, b):
    return lax.dot_general(a, b, (((0,), (0,)), ((), ())), preferred_element_type=f32)


def joined(refs):
    return jnp.concatenate([ref[0, 0] for ref in refs], axis=0)


def ffn_kernel(units, pad, experts, where_ref, rows_ref, c0, c1, c2, c3, gate_ref, down_ref, *refs):
    out_own_ref, out_far_ref, own_ref, far_ref, hidden_ref, gate_grad_ref = refs[-6:]
    n, width = rows_ref.shape
    wide = 3 * units
    base = wide // 128 * 128
    at = wide - base
    cots = joined((c0, c1, c2, c3))
    gate_up = dot_nt(rows_ref[...], gate_ref[...])
    hidden_grad = dot_nt(cots[:, :width], down_ref[...])
    g, u = gate_up[:, :pad], gate_up[:, pad:]
    logits = g[:, base : base + 128]
    lane = lax.broadcasted_iota(jnp.int32, (n, 128), 1)
    routed = (lane >= at) & (lane < at + experts)
    peak = jnp.max(jnp.where(routed, logits, -jnp.inf), axis=1, keepdims=True)
    weights = jnp.where(routed, jnp.exp(logits - peak), 0.0)
    probs = weights / jnp.sum(weights, axis=1, keepdims=True)
    shared_gate = jax.nn.sigmoid(logits[:, at + experts : at + experts + 1])
    bits = jnp.right_shift(cots[:, width : width + 128].astype(f32).astype(jnp.int32), where_ref[8])
    own = [(jnp.right_shift(bits, i) & 1).astype(f32)[:, :1] for i in range(2)]
    gate = [probs[:, at + i : at + i + 1] * own[i] for i in range(2)]
    spot = lax.broadcasted_iota(jnp.int32, (n, pad), 1)
    gates = jnp.where(spot < units, shared_gate, jnp.where(spot < 2 * units, gate[0], gate[1]))
    sig = jax.nn.sigmoid(g)
    silu = g * sig
    hidden = (silu * u).astype(bf16).astype(f32)
    gated = (gates * hidden).astype(bf16)
    hidden_ref[...] = gated
    gated_grad = hidden_grad * gates
    up_grad = gated_grad * silu
    gate_grad = gated_grad * u * (sig + silu * (1.0 - sig))
    products = hidden_grad * hidden

    def total(k):
        inside = (spot >= k * units) & (spot < (k + 1) * units)
        return jnp.sum(jnp.where(inside, products, 0.0), axis=1, keepdims=True)

    shared_grad = total(0) * shared_gate * (1.0 - shared_gate)
    own_grad = [total(1 + i) * own[i] for i in range(2)]
    weighted = probs[:, at : at + 1] * own_grad[0] + probs[:, at + 1 : at + 2] * own_grad[1]
    probs_grad = jnp.where(lane == at, own_grad[0], jnp.where(lane == at + 1, own_grad[1], 0.0))
    logit_grad = probs * (probs_grad - weighted)
    logit_grad = jnp.where(lane == at + experts, shared_grad, logit_grad)
    tail = jnp.where(lane < at, gate_grad[:, base : base + 128], logit_grad)
    parts = [gate_grad[:, :base], tail]
    if base + 128 < pad:
        parts.append(gate_grad[:, base + 128 :])
    gate_up_grad = jnp.concatenate(parts + [up_grad], axis=1).astype(bf16)
    gate_grad_ref[...] = gate_up_grad
    out_part = dot(gated, down_ref[...]).astype(bf16)
    out_own_ref[...] = out_part[: n // 2]
    out_far_ref[...] = out_part[n // 2 :]
    rows_grad = dot(gate_up_grad, gate_ref[...]).astype(bf16)
    own_ref[...] = rows_grad[: n // 2]
    far_ref[...] = rows_grad[n // 2 :]


def cot_specs(cots, chunk):
    block = (1, 1) + cots.shape[2:]

    def spec(j):
        return pl.BlockSpec(block, lambda i, where: (where[chunk(i)[1] * 4 + j], chunk(i)[0], 0, 0))

    return [spec(j) for j in range(4)]


def ffn_chunks(first, chunks, where, rows, cots, gate_rows, down_rows, kept, units, experts):
    total, width = rows.shape
    steps = chunks * 2
    tile = total // (cots.shape[1] * 2)
    pad = down_rows.shape[0]

    def among(w):
        return pl.BlockSpec((tile, w), lambda i, where: (first * 2 + i, 0))

    def half(w):
        return pl.BlockSpec((tile // 2, w), lambda i, where: (i, 0))

    def whole(r):
        return pl.BlockSpec((r, width), lambda i, where: (0, 0), pipeline_mode=pl.Buffered(1))

    shapes = [(steps * tile // 2, width)] * 4 + [(total, pad), (total, 2 * pad)]
    kept = list(kept)
    return pl.pallas_call(
        functools.partial(ffn_kernel, units, pad, experts),
        grid_spec=pltpu.PrefetchScalarGridSpec(
            num_scalar_prefetch=1,
            grid=(steps,),
            in_specs=[among(width)]
            + cot_specs(cots, lambda i: (first + i // 2, i % 2))
            + [whole(2 * pad), whole(pad)]
            + [pl.BlockSpec(memory_space=pl.ANY)] * len(kept),
            out_specs=[half(width)] * 4 + [among(pad), among(2 * pad)],
        ),
        out_shape=[jax.ShapeDtypeStruct(shape, bf16) for shape in shapes],
        input_output_aliases={8 + i: 4 + i for i in range(len(kept))},
        compiler_params=pltpu.CompilerParams(vmem_limit_bytes=58 * 1024 * 1024),
        cost_estimate=pl.CostEstimate(
            flops=12 * steps * tile * width * pad,
            bytes_accessed=8 * steps * tile * width,
            transcendentals=2 * steps * tile * pad,
        ),
    )(where, rows, cots, cots, cots, cots, gate_rows, down_rows, *kept)


def down_grad_kernel(wide, where_ref, hidden_ref, c0, c1, c2, c3, out_ref, sums):
    step = pl.program_id(0)
    width = sums.shape[1]

    @pl.when(step == 0)
    def _():
        sums[...] = jnp.zeros_like(sums)

    sums[...] += dot_tn(hidden_ref[...], joined((c0, c1, c2, c3))[:, :width])

    @pl.when(step == pl.num_programs(0) - 1)
    def _():
        count, _, block = out_ref.shape
        for d in range(count):
            out_ref[d, :] = sums[:wide, d * block : (d + 1) * block].astype(bf16)


def down_grad(where, hidden, cots, width, wide, count):
    total, pad = hidden.shape
    steps = cots.shape[1] * 2
    shape = (count, wide, width // count)
    if not whole_tiles(wide, width // count):
        rows = jnp.moveaxis(cots[where[:8]], 0, 1).reshape(total, -1)[:, :width]
        return dot_over(hidden, rows)[:wide].reshape(wide, count, -1).transpose(1, 0, 2).astype(bf16)
    return pl.pallas_call(
        functools.partial(down_grad_kernel, wide),
        grid_spec=pltpu.PrefetchScalarGridSpec(
            num_scalar_prefetch=1,
            grid=(steps,),
            in_specs=[pl.BlockSpec((total // steps, pad), lambda i, where: (i, 0))]
            + cot_specs(cots, lambda i: (i // 2, i % 2)),
            out_specs=pl.BlockSpec(shape, lambda i, where: (0, 2, 0)),
            scratch_shapes=[pltpu.VMEM((pad, width), f32)],
        ),
        out_shape=jax.ShapeDtypeStruct((count, 3 * wide, width // count), bf16),
        compiler_params=pltpu.CompilerParams(vmem_limit_bytes=56 * 1024 * 1024),
        cost_estimate=pl.CostEstimate(flops=2 * total * pad * width, bytes_accessed=2 * total * (pad + width), transcendentals=0),
    )(where, hidden, cots, cots, cots, cots)


def gate_grad_kernel(wide, grad_ref, rows_ref, held_ref, out_ref, router_ref, sums):
    step = pl.program_id(0)

    @pl.when(step == 0)
    def _():
        sums[...] = jnp.zeros_like(sums)

    sums[...] += dot_tn(grad_ref[...], rows_ref[...])

    @pl.when(step == pl.num_programs(0) - 1)
    def _():
        count, _, block = out_ref.shape
        pad = sums.shape[0] // 2
        for d in range(count):
            lanes = slice(d * block, (d + 1) * block)
            out_ref[d, :wide] = sums[:wide, lanes].astype(bf16)
            out_ref[d, wide:] = sums[pad : pad + wide, lanes].astype(bf16)
        base = wide // 8 * 8
        router_ref[...] = sums[base : base + router_ref.shape[0]]


def gate_grad(gate_up_grad, rows, held, wide, count):
    total, pads = gate_up_grad.shape
    width = rows.shape[1]
    tile = 512
    shape = (count, 2 * wide, width // count)
    if not whole_tiles(wide, width // count):
        sums = dot_over(gate_up_grad, rows)
        base = wide // 8 * 8
        both = stack(sums[:wide], sums[pads // 2 : pads // 2 + wide])
        both = both.reshape(2 * wide, count, -1).transpose(1, 0, 2).astype(bf16)
        return jnp.concatenate([both, held], axis=1), sums[base : base + 24]
    return pl.pallas_call(
        functools.partial(gate_grad_kernel, wide),
        grid=(total // tile,),
        in_specs=[
            pl.BlockSpec((tile, pads), lambda i: (i, 0)),
            pl.BlockSpec((tile, width), lambda i: (i, 0)),
            pl.BlockSpec(memory_space=pl.ANY),
        ],
        input_output_aliases={2: 0},
        out_specs=[pl.BlockSpec(shape, lambda i: (0, 0, 0)), pl.BlockSpec((24, width), lambda i: (0, 0))],
        out_shape=[jax.ShapeDtypeStruct(held.shape, bf16), jax.ShapeDtypeStruct((24, width), f32)],
        scratch_shapes=[pltpu.VMEM((pads, width), f32)],
        compiler_params=pltpu.CompilerParams(vmem_limit_bytes=56 * 1024 * 1024),
        cost_estimate=pl.CostEstimate(flops=2 * total * pads * width, bytes_accessed=2 * total * (pads + width), transcendentals=0),
    )(gate_up_grad, rows, held)


def whole_tiles(units, rows):
    return units % 16 == 0 and rows % 128 == 0


def turn_kernel(shared_ref, routed_ref, gate_ref, down_ref):
    kind, who = pl.program_id(0), pl.program_id(1)

    def put(out_ref, block):
        count, units, rows = out_ref.shape
        out_ref[...] = block.T.reshape(count, units, rows)

    for last, out_ref in ((False, gate_ref), (True, down_ref)):
        for own, in_ref in ((False, shared_ref), (True, routed_ref)):

            @pl.when(((kind == 2) == last) & ((who > 0) == own))
            def _(out_ref=out_ref, in_ref=in_ref):
                put(out_ref, in_ref[...])


def turn_weights(shared, routed, count):
    rows, columns = shared.shape
    who = 1 + routed.shape[1] // columns
    span = columns // 3
    units = span // count
    if not whole_tiles(units, rows):
        both = jnp.concatenate([shared, routed], axis=1).reshape(rows, who, 3, count, units)
        both = both.transpose(3, 2, 1, 4, 0).reshape(count, -1, rows)
        return both[:, : 2 * who * units], both[:, 2 * who * units :]
    return pl.pallas_call(
        turn_kernel,
        grid=(3, who),
        in_specs=[
            pl.BlockSpec((rows, span), lambda k, w: (0, k)),
            pl.BlockSpec((rows, span), lambda k, w: (0, jnp.maximum(w - 1, 0) * 3 + k)),
        ],
        out_specs=[
            pl.BlockSpec((count, units, rows), lambda k, w: (0, jnp.where(k < 2, k * who + w, 2 * who - 1), 0)),
            pl.BlockSpec((count, units, rows), lambda k, w: (0, jnp.where(k < 2, 0, w), 0)),
        ],
        out_shape=[jax.ShapeDtypeStruct((count, k * who * units, rows), bf16) for k in (2, 1)],
        compiler_params=pltpu.CompilerParams(vmem_limit_bytes=32 * 1024 * 1024),
        cost_estimate=pl.CostEstimate(flops=0, bytes_accessed=4 * who * rows * columns, transcendentals=0),
    )(shared, routed)


def turn_back_kernel(grad_ref, shared_ref, routed_ref):
    count, wide, rows = grad_ref.shape
    who = 1 + routed_ref.shape[1]
    units = wide // who
    for w in range(who):
        block = grad_ref[:, w * units : (w + 1) * units, :].reshape(count * units, rows).T
        if w == 0:
            shared_ref[...] = block
        else:
            routed_ref[:, w - 1, :] = block.astype(f32)


def turn_grads(grad, experts):
    count, wide, rows = grad.shape
    wide = wide // 3
    span = wide // (1 + experts) * count
    if not whole_tiles(span // count, rows):
        both = grad.reshape(count, 3, 1 + experts, -1, rows)
        both = both.transpose(4, 2, 1, 0, 3).reshape(rows, 1 + experts, 3 * span)
        return both[:, 0], both[:, 1:].astype(f32)
    return pl.pallas_call(
        turn_back_kernel,
        grid=(3,),
        in_specs=[pl.BlockSpec((count, wide, rows), lambda k: (0, k, 0))],
        out_specs=[
            pl.BlockSpec((rows, span), lambda k: (0, k)),
            pl.BlockSpec((rows, experts, span), lambda k: (0, 0, k)),
        ],
        out_shape=[
            jax.ShapeDtypeStruct((rows, 3 * span), bf16),
            jax.ShapeDtypeStruct((rows, experts, 3 * span), f32),
        ],
        compiler_params=pltpu.CompilerParams(vmem_limit_bytes=56 * 1024 * 1024),
        cost_estimate=pl.CostEstimate(flops=0, bytes_accessed=6 * count * wide * rows + 10 * rows * span * 3, transcendentals=0),
    )(grad)


def deal_kernel(share, dense_ref, attn_ref, shared_ref):
    width = share * 8
    for o in range(8):
        for k in range(4):
            at = k * width + o * share
            attn_ref[o, :, k * share : (k + 1) * share] = dense_ref[:, at : at + share]
    owners, _, columns = shared_ref.shape
    span = columns // 3
    for o in range(owners):
        for k in range(3):
            at = 4 * width + (k * owners + o) * span
            shared_ref[o, :, k * span : (k + 1) * span] = dense_ref[:, at : at + span]


def deal_columns(dense, share, owners):
    rows, columns = dense.shape
    shapes = [(8, rows, 4 * share), (owners, rows, (columns - 32 * share) // owners)]
    return pl.pallas_call(
        functools.partial(deal_kernel, share),
        out_shape=[jax.ShapeDtypeStruct(shape, bf16) for shape in shapes],
        compiler_params=pltpu.CompilerParams(vmem_limit_bytes=32 * 1024 * 1024),
        cost_estimate=pl.CostEstimate(flops=0, bytes_accessed=4 * rows * columns, transcendentals=0),
    )(dense)


def collect_kernel(share, attn_ref, shared_ref, dense_ref):
    width = share * 8
    for o in range(8):
        for k in range(4):
            at = k * width + o * share
            dense_ref[:, at : at + share] = attn_ref[o, :, k * share : (k + 1) * share].astype(f32)
    owners, _, columns = shared_ref.shape
    span = columns // 3
    for o in range(owners):
        for k in range(3):
            at = 4 * width + (k * owners + o) * span
            dense_ref[:, at : at + span] = shared_ref[o, :, k * span : (k + 1) * span].astype(f32)


def collect_columns(attn, shared, share):
    rows = attn.shape[1]
    columns = 32 * share + shared.shape[0] * shared.shape[2]
    return pl.pallas_call(
        functools.partial(collect_kernel, share),
        out_shape=jax.ShapeDtypeStruct((rows, columns), f32),
        compiler_params=pltpu.CompilerParams(vmem_limit_bytes=32 * 1024 * 1024),
        cost_estimate=pl.CostEstimate(flops=0, bytes_accessed=6 * rows * columns, transcendentals=0),
    )(attn, shared)


def place_kernel(wide, pad, *refs):
    out_ref = refs[-1]
    for k in range(out_ref.shape[0] // pad):
        out_ref[k * pad : k * pad + wide] = refs[0][0, k * wide : (k + 1) * wide]
        if k == 0 and len(refs) > 2:
            out_ref[wide:pad] = refs[1][...]
        else:
            out_ref[k * pad + wide : (k + 1) * pad] = jnp.zeros((pad - wide, out_ref.shape[1]), bf16)


def place_weights(ffn, wide, pad, *router):
    count, units, block = ffn.shape
    width = count * block
    rows = units // wide * pad
    if not whole_tiles(wide, block):
        parts = ffn.transpose(1, 0, 2).reshape(units // wide, wide, width)
        blank = jnp.zeros((pad - wide, width), bf16)
        return stack(*[v for k in range(units // wide) for v in (parts[k], *(router if k == 0 and router else (blank,)))])

    def column(r):
        return pl.BlockSpec((r, block), lambda i: (0, i))

    return pl.pallas_call(
        functools.partial(place_kernel, wide, pad),
        grid=(count,),
        in_specs=[pl.BlockSpec((1, units, block), lambda i: (i, 0, 0))] + [column(pad - wide)] * len(router),
        out_specs=column(rows),
        out_shape=jax.ShapeDtypeStruct((rows, width), bf16),
        compiler_params=pltpu.CompilerParams(vmem_limit_bytes=32 * 1024 * 1024),
        cost_estimate=pl.CostEstimate(flops=0, bytes_accessed=2 * (rows + units) * width, transcendentals=0),
    )(ffn, *router)


def attend_rows(queries, keys, allowed):
    scores = jnp.where(allowed, dot_nt(queries, keys) * HD ** (-0.5), -1e30)
    raw = jnp.exp(scores - jnp.max(scores, axis=1, keepdims=True))
    return raw / jnp.sum(raw, axis=1, keepdims=True)


def allowed_pairs(own_ref, all_ref):
    return (own_ref[:, :1] == all_ref[0, :1]) & (all_ref[0, 1:2] <= own_ref[:, 1:2])


def piece_at(where_ref, s, piece_ref):
    size = piece_ref.shape[0]
    return pl.ds(pl.multiple_of(where_ref[s] * size, size), size)


def attend_kernel(heads, where_ref, rows_ref, bias_ref, cosine_ref, sine_ref, own_ref, all_ref, *refs):
    pieces, (packed_ref, mixed_ref) = refs[:-2], refs[-2:]
    share = heads * HD
    packed = bias_ref[...]
    for s, piece in enumerate(pieces):
        packed = packed + dot(rows_ref[:, piece_at(where_ref, s, piece)], piece[...])
    cosine, sine = cosine_ref[...], sine_ref[...]
    allowed = allowed_pairs(own_ref, all_ref)

    def turned(at):
        v = packed[:, at : at + HD]
        return (v * cosine + pltpu.roll(v, HD // 2, 1) * sine).astype(bf16)

    for h in range(heads):
        queries, keys = turned(h * HD), turned(share + h * HD)
        values = packed[:, 2 * share + h * HD : 2 * share + (h + 1) * HD].astype(bf16)
        attend = attend_rows(queries, keys, allowed)
        mixed_ref[:, h * HD : (h + 1) * HD] = dot(attend.astype(bf16), values).astype(bf16)
        for k, v in enumerate((queries, keys, values)):
            packed_ref[:, k * share + h * HD : k * share + (h + 1) * HD] = v


def project_kernel(where_ref, mixed_ref, *refs):
    pieces, (near_ref, far_ref) = refs[:-2], refs[-2:]
    half = near_ref.shape[0]
    for s, piece in enumerate(pieces):
        rows = dot_nt(mixed_ref[...], piece[...]).astype(bf16)
        columns = piece_at(where_ref, s, piece)
        near_ref[:, columns] = rows[:half]
        far_ref[:, columns] = rows[half:]


def attend_back_kernel(heads, where_ref, grad_ref, packed_ref, cosine_ref, sine_ref, own_ref, all_ref, *refs):
    pieces, (packed_grad_ref, near_ref, far_ref, bias_ref) = refs[:-4], refs[-4:]
    rings = len(pieces) // 2
    share = heads * HD
    scale = HD ** (-0.5)
    mixed_grad = 0.0
    for s, piece in enumerate(pieces[rings:]):
        mixed_grad = mixed_grad + dot(grad_ref[:, piece_at(where_ref, s, piece)], piece[...])
    mixed_grad = mixed_grad.astype(bf16)
    cosine, sine = cosine_ref[...], sine_ref[...]
    allowed = allowed_pairs(own_ref, all_ref)

    def back(v):
        v = v.astype(bf16).astype(f32)
        return (v * cosine - pltpu.roll(v, HD // 2, 1) * sine).astype(bf16)

    for h in range(heads):
        queries, keys, values = (
            packed_ref[:, k * share + h * HD : k * share + (h + 1) * HD] for k in range(3)
        )
        own_grad = mixed_grad[:, h * HD : (h + 1) * HD]
        attend = attend_rows(queries, keys, allowed)
        attend_grad = dot_nt(own_grad, values)
        scores_grad = attend * (attend_grad - jnp.sum(attend * attend_grad, axis=1, keepdims=True))
        scores_grad = scores_grad.astype(bf16)
        grads = (
            back(dot(scores_grad, keys) * scale),
            back(dot_tn(scores_grad, queries) * scale),
            dot_tn(attend.astype(bf16), own_grad).astype(bf16),
        )
        for k, v in enumerate(grads):
            packed_grad_ref[:, k * share + h * HD : k * share + (h + 1) * HD] = v
    packed_grad = packed_grad_ref[...]
    bias_ref[...] = jnp.broadcast_to(jnp.sum(packed_grad.astype(f32), axis=0, keepdims=True), bias_ref.shape)
    half = near_ref.shape[0]
    for s, piece in enumerate(pieces[:rings]):
        rows_grad = dot_nt(packed_grad, piece[...]).astype(bf16)
        columns = piece_at(where_ref, s, piece)
        near_ref[:, columns] = rows_grad[:half]
        far_ref[:, columns] = rows_grad[half:]


def group_call(kernel, group_len, where, operands, specs, pieces, out_widths, out_types, flops):
    def spec(kind, shape):
        if kind == "rows":
            return pl.BlockSpec((group_len, shape[1]), lambda i, where: (i, 0))
        if kind == "pair":
            return pl.BlockSpec((1,) + shape[1:], lambda i, where: (i, 0, 0))
        return pl.BlockSpec(shape, lambda i, where: (0, 0), pipeline_mode=pl.Buffered(1))

    operands = tuple(operands) + tuple(pieces)
    specs = tuple(specs) + ("all",) * len(pieces)
    return pl.pallas_call(
        kernel,
        grid_spec=pltpu.PrefetchScalarGridSpec(
            num_scalar_prefetch=1,
            grid=(2,),
            in_specs=[spec(k, v.shape) for k, v in zip(specs, operands)],
            out_specs=[pl.BlockSpec((r, w), lambda i, where: (i, 0)) for r, w in out_widths],
        ),
        out_shape=[jax.ShapeDtypeStruct((2 * r, w), t) for (r, w), t in zip(out_widths, out_types)],
        compiler_params=pltpu.CompilerParams(vmem_limit_bytes=48 * 1024 * 1024),
        cost_estimate=pl.CostEstimate(flops=flops, bytes_accessed=sum(2 * v.size for v in operands), transcendentals=0),
    )(where, *operands)


def body(lay, tokens, dense_weights, expert_weights, gain_attn, gain_ffn, qkv_bias, router_weight, routes, doc_ids, out_grad):
    row_count, model_width = tokens.shape
    rings = lay.rings
    ring = lax.axis_index("ring")
    pair = lax.axis_index("pair")
    ep = lax.axis_index("ep")
    local_experts = expert_weights.shape[1]
    expert_count = router_weight.shape[1] - 1
    owners = expert_count // local_experts
    dp_count = rings * 2
    ring_place = jnp.asarray(lay.place, jnp.int32)[ring]
    behind = [jnp.asarray(lay.order, jnp.int32)[(ring_place - s) % rings] for s in range(rings)]
    ring_order = jnp.stack(behind)
    own_expert = ep * local_experts
    where = []
    for dx in range(2):
        for dc in range(2):
            for dy in range(2):
                where.append((pair ^ dy) * 4 + (ep ^ (2 * dx + dc)))
    where = jnp.stack(where + [own_expert]).astype(jnp.int32)

    stream = tokens.astype(f32)
    gain_one = gain_attn.astype(f32)
    gain_two = gain_ffn.astype(f32)
    heads = H // 8
    share = heads * HD
    unit_share = SFF // owners
    units = FF // dp_count
    wide = 3 * units
    pad = (wide + expert_count + 1 + 127) // 128 * 128
    n = row_count

    mine, shared = deal_columns(dense_weights, share, owners)
    bits = jnp.sum(jnp.left_shift(jnp.int32(1), routes), axis=1, keepdims=True).astype(bf16)
    cot_blocks = [jnp.concatenate([out_grad, jnp.broadcast_to(bits, (row_count, 128))], axis=1)]
    mine, shared, cot_blocks[0] = together(mine, shared, cot_blocks[0])
    plane_part = lax.all_to_all(mine, PLANE, split_axis=0, concat_axis=0, tiled=True)
    plane_part = plane_part.reshape(-1, 4 * share)
    for _ in range(rings - 2):
        cot_blocks.append(permute(cot_blocks[-1], lay.onward))

    inverse_one = lax.rsqrt(jnp.mean(stream * stream, axis=1, keepdims=True) + norm_eps)
    normed = (stream * inverse_one * gain_one).astype(bf16)
    doc_pair = jnp.stack([doc_ids, permute(doc_ids, lay.up)])
    group_len = doc_ids.shape[0]
    before = jnp.sum((doc_pair[:, None, :] < doc_pair[:, :, None]).astype(jnp.int32), axis=2)
    spot = jnp.arange(group_len, dtype=jnp.int32)
    near_blocks = jnp.stack([ep, ep ^ 2, ep ^ 1, ep ^ 3])

    def in_order(values):
        return values.reshape(2, 4, row_count)[:, near_blocks].reshape(2, group_len)

    places = in_order(spot[None, :] - before)
    docs = in_order(doc_pair)
    spots = in_order(jnp.stack([spot, spot]))
    cosine, sine = rope_tables(places.reshape(-1))
    sine = jnp.where(jnp.arange(HD) < HD // 2, -sine, sine)
    spots_all = jnp.stack([docs, spots], axis=1)
    spots_own = jnp.stack([docs.reshape(-1), spots.reshape(-1)], axis=1)
    routed = expert_weights.reshape(expert_weights.shape[0], -1)
    router = router_weight.T
    turn = (own_expert + jnp.arange(expert_count, dtype=jnp.int32)) % expert_count
    router = stack(
        jnp.take(router, turn, axis=0),
        router[expert_count:],
        jnp.zeros((pad - wide - expert_count - 1, model_width), bf16),
    )
    slot = pair * 4 + ep
    bias_share = lax.dynamic_slice_in_dim(qkv_bias.astype(f32).reshape(3, 8, share), slot, 1, 1).reshape(1, 3 * share)
    plane_part, cot_blocks[-1], routed, normed, shared = together(plane_part, cot_blocks[-1], routed, normed, shared)

    qkv = [plane_part[:, : 3 * share]]
    qkv.append(permute(qkv[0], lay.onward))
    cot_blocks.append(permute(cot_blocks[-1], lay.onward))
    shared = lax.all_to_all(shared, "ep", split_axis=0, concat_axis=0, tiled=True)
    side, up = permute(normed, lay.side), permute(normed, lay.up)
    qkv[-1], cot_blocks[-1], side, up, cosine, sine = together(qkv[-1], cot_blocks[-1], side, up, cosine, sine)
    cross = permute(up, lay.side)
    near = stack(normed, side)
    near_core = permute(near, lay.core)
    for s in range(2, rings):
        qkv.append(permute(qkv[-1], lay.onward))
        if s == 2:
            gate_ffn, down_ffn = turn_weights(shared.reshape(routed.shape[0], 3 * unit_share), routed, dp_count)
            far = stack(up, cross)
            qkv[-1], near_core, far, gate_ffn, down_ffn = together(qkv[-1], near_core, far, gate_ffn, down_ffn)
            cots = lax.all_gather(after(jnp.stack(cot_blocks), qkv[-1]), PLANE, axis=0, tiled=False)
            far_core = permute(far, lay.core)
    normed_group = stack(near, near_core, far, far_core)
    qkv[-1], normed_group = together(qkv[-1], normed_group)

    outs = [plane_part[:, 3 * share :]]
    for _ in range(rings - 1):
        outs.append(permute(outs[-1] if len(outs) > 1 else after(outs[0], qkv[-1]), lay.onward))
    heads_flops = 8 * heads * group_len * group_len * HD
    packed, mixed = group_call(
        functools.partial(attend_kernel, heads),
        group_len,
        ring_order,
        (normed_group, bias_share, cosine, sine, spots_own, spots_all),
        ("rows", "all", "rows", "rows", "rows", "pair"),
        qkv,
        [(group_len, 3 * share), (group_len, share)],
        [bf16, bf16],
        4 * group_len * model_width * 3 * share + heads_flops,
    )
    down_ffn = lax.all_to_all(after(down_ffn, outs[-1]), ("ring", "pair"), split_axis=0, concat_axis=0, tiled=True)
    branch_parts = group_call(
        project_kernel,
        group_len,
        ring_order,
        (mixed,),
        ("rows",),
        outs,
        [(group_len // 2, model_width)] * 2,
        [bf16, bf16],
        4 * group_len * model_width * share,
    )
    branch = plane_sums(lay, *branch_parts)
    residual = stream + branch
    inverse_two = lax.rsqrt(jnp.mean(residual * residual, axis=1, keepdims=True) + norm_eps)
    normed_two = (residual * inverse_two * gain_two).astype(bf16)
    normed_two = after(normed_two, down_ffn)

    blocks, ups, sides, crosses = [normed_two], [], [], []
    for s in range(rings):
        up, side = permute(blocks[s], lay.up), permute(blocks[s], lay.side)
        sides.append(side)
        if s > 0:
            crosses.append(permute(ups[-1], lay.side))
        if s < rings - 1:
            onward = permute(blocks[s], lay.onward)
            onward, up = together(onward, up)
            blocks.append(onward)
        else:
            up = after(up, blocks[-1])
        ups.append(up)
    gate_ffn = lax.all_to_all(after(gate_ffn, ups[-1]), ("ring", "pair"), split_axis=0, concat_axis=0, tiled=True)
    crosses.append(permute(ups[-1], lay.side))
    down_rows = place_weights(down_ffn, wide, pad)
    rows = []
    for s in range(rings):
        for pieces in ((blocks[s], ups[s]), (sides[s], crosses[s])):
            rows += pieces
            rows += [permute(piece, lay.core) for piece in pieces]
    rows = stack(*rows)
    gate_rows = place_weights(gate_ffn, wide, pad, router)

    chunk, half = 4 * n, 2 * n
    order = list(range(rings))[::-1]
    late = rings // 2
    first_half, last_half = order[: rings - late], order[rings - late :]

    def cut_chunk(which, s, at):
        begin = (s % late if s < late else s - late) * chunk + at
        return which[begin : begin + half]

    def crossed(part, there, some):
        keep = {s: plus(cut_chunk(part, s, 0), cut_chunk(there, s, 0)) for s in some}
        send = {s: plus(cut_chunk(part, s, half), cut_chunk(there, s, half)) for s in some}
        return keep, send

    def all_there(*groups):
        flat, tree = jax.tree.flatten(groups)
        return jax.tree.unflatten(tree, lax.optimization_barrier(tuple(flat)))

    def ffn_half(first, chunks, kept):
        return ffn_chunks(first, chunks, where, rows, cots, gate_rows, down_rows, kept, units, expert_count)

    out_own_a, out_far_a, own_a, far_a, hidden, gate_up_grad = ffn_half(late, rings - late, ())

    keep, send = crossed(own_a, permute(far_a, lay.core), first_half)
    keep, send, hidden, gate_up_grad = all_there(keep, send, hidden, gate_up_grad)
    sided = {s: permute(send[s], lay.side) for s in first_half}
    out_own_b, out_far_b, own_b, far_b, hidden, gate_up_grad = ffn_half(0, late, (hidden, gate_up_grad))
    sided, own_b, far_b, hidden, gate_up_grad = all_there(sided, own_b, far_b, hidden, gate_up_grad)

    far_there = permute(far_b, lay.core)
    halves = {s: plus(keep[s], sided[s]) for s in first_half}
    keep, send = crossed(own_b, far_there, last_half)
    keep, send, halves, hidden = all_there(keep, send, halves, hidden)

    few = (len(last_half) + 1) // 2
    sided = {s: permute(send[s], lay.side) for s in last_half[:few]}
    upped = {s: permute(halves[s][n:], lay.up) for s in first_half}
    ffn_grad = down_grad(where, hidden, cots, model_width, wide, dp_count)
    sided, upped, ffn_grad, gate_up_grad = all_there(sided, upped, ffn_grad, gate_up_grad)

    own_sums = {s: halves[s][:n].astype(f32) + upped[s].astype(f32) for s in first_half}
    total = own_sums[order[0]]
    queue = list(order[1:])

    def step_on(total):
        return permute(total.astype(bf16), lay.backward)

    def step_in(arrived):
        return own_sums[queue.pop(0)] + arrived.astype(f32)

    halves = {s: plus(keep[s], sided[s]) for s in last_half[:few]}
    sided = {s: permute(send[s], lay.side) for s in last_half[few:]}
    upped = {s: permute(halves[s][n:], lay.up) for s in last_half[:few]}
    moving = step_on(total)
    ffn_grad, router_part = gate_grad(gate_up_grad, rows, ffn_grad, wide, dp_count)
    sided, upped, moving, ffn_grad = all_there(sided, upped, moving, ffn_grad)
    total = step_in(moving)
    own_sums.update({s: halves[s][:n].astype(f32) + upped[s].astype(f32) for s in last_half[:few]})

    halves = {s: plus(keep[s], sided[s]) for s in last_half[few:]}
    upped = {s: permute(halves[s][n:], lay.up) for s in last_half[few:]}
    moving = step_on(total)
    upped, moving = all_there(upped, moving)
    total = step_in(moving)
    own_sums.update({s: halves[s][:n].astype(f32) + upped[s].astype(f32) for s in last_half[few:]})
    while queue:
        total = step_in(step_on(total))
    normed_two_grad = total

    start = wide - wide // 8 * 8
    router_part = router_part[start : start + expert_count + 1]
    turn_back = (jnp.arange(expert_count, dtype=jnp.int32) - own_expert) % expert_count
    router_part = stack(jnp.take(router_part[:expert_count], turn_back, axis=0), router_part[expert_count:])

    cotangent = out_grad.astype(f32)
    scaled_two = normed_two_grad * gain_two
    gain_two_grad = jnp.sum(normed_two_grad * residual * inverse_two, axis=0)
    residual_grad = (
        cotangent
        + inverse_two * scaled_two
        - residual * inverse_two**3 * jnp.mean(scaled_two * residual, axis=1, keepdims=True)
    )
    branch_grad = residual_grad.astype(bf16)

    side, up = permute(branch_grad, lay.side), permute(branch_grad, lay.up)
    side, up, ffn_grad = together(side, up, ffn_grad)
    ffn_grad = lax.all_to_all(ffn_grad, ("ring", "pair"), split_axis=0, concat_axis=0, tiled=True)
    near, far = stack(branch_grad, side), stack(up, permute(up, lay.side))
    branch_grad_group = stack(near, permute(near, lay.core), far, permute(far, lay.core))
    packed_grad, near, far, bias_part = group_call(
        functools.partial(attend_back_kernel, heads),
        group_len,
        ring_order,
        (branch_grad_group, packed, cosine, sine, spots_own, spots_all),
        ("rows", "rows", "rows", "rows", "rows", "pair"),
        qkv + outs,
        [(group_len, 3 * share), (group_len // 2, model_width), (group_len // 2, model_width), (8, 3 * share)],
        [bf16, bf16, bf16, f32],
        4 * group_len * model_width * 4 * share + 3 * heads_flops,
    )
    normed_grad = plane_sums(lay, near, far)

    out_there = [permute(after(v, up), lay.core) for v in (out_far_a, out_far_b)]
    keep, send = crossed(out_own_a, out_there[0], first_half)
    more_keep, more_send = crossed(out_own_b, out_there[1], last_half)
    keep.update(more_keep)
    send.update(more_send)
    sided = {s: permute(after(send[s], branch_grad_group), lay.side) for s in first_half}
    sided.update({s: permute(after(send[s], far), lay.side) for s in last_half})
    halves = {s: plus(keep[s], sided[s]) for s in order}
    upped = {s: permute(halves[s][n:], lay.up) for s in order}
    out_sums = {s: halves[s][:n].astype(f32) + upped[s].astype(f32) for s in order}

    scaled_one = normed_grad * gain_one
    gain_one_grad = jnp.sum(normed_grad * stream * inverse_one, axis=0)
    input_grad = (
        residual_grad
        + inverse_one * scaled_one
        - stream * inverse_one**3 * jnp.mean(scaled_one * stream, axis=1, keepdims=True)
    )
    bias_part = (bias_part[0] + bias_part[8]).reshape(3, 1, share)
    bias_part = lax.dynamic_update_slice(jnp.zeros((3, 8, share), f32), bias_part, (0, slot, 0))
    small = stack(router_part, gain_two_grad[None], gain_one_grad[None], bias_part.reshape(3, model_width))
    doubling = lay.doubling()
    for step in doubling[:3]:
        small = small + permute(small, step)

    attn_grads = jnp.concatenate([dot_over(normed_group, packed_grad), dot_over(branch_grad_group, mixed)], axis=1)
    attn_grads = attn_grads.astype(bf16).reshape(rings, -1, 4 * share)
    shared_grad, expert_grad = turn_grads(after(ffn_grad, attn_grads), local_experts)
    shared_grad = lax.all_to_all(
        shared_grad.reshape(owners, -1, 3 * unit_share), "ep", split_axis=0, concat_axis=0, tiled=True
    )
    attn_grads, out_sums, small, shared_grad = all_there(attn_grads, out_sums, small, shared_grad)
    total, output_sum, more = None, None, doubling[3:]
    for i, s in enumerate(order):
        here = lax.dynamic_index_in_dim(attn_grads, behind[s], 0, keepdims=False).astype(f32)
        if i > 0:
            total, out_moving, small = together(total.astype(bf16), output_sum.astype(bf16), small)
            if i == rings - 1:
                total, shared_grad, expert_grad = together(total, shared_grad, expert_grad)
            here = here + permute(total, lay.backward).astype(f32)
            output_sum = out_sums[s] + permute(out_moving, lay.backward).astype(f32)
            if more:
                small = small + permute(small, more.pop(0))
        else:
            output_sum = out_sums[s]
        total = here
    output = (residual + output_sum).astype(bf16)
    total = total.astype(bf16).reshape(8, -1, 4 * share)
    total = lax.all_to_all(total, PLANE, split_axis=0, concat_axis=0, tiled=True)
    dense_grad = collect_columns(total, shared_grad, share)

    router_sum, gain_two_sum, gain_one_sum, bias_sum = jnp.split(small, [expert_count + 1, expert_count + 2, expert_count + 3])
    return (
        output,
        input_grad,
        dense_grad,
        expert_grad,
        gain_one_sum[0],
        gain_two_sum[0],
        bias_sum.reshape(-1),
        router_sum.T,
    )


def solution(mesh):
    devices = mesh.devices
    lay = Layout(devices.shape[0] // 2)
    inner = Mesh(devices.reshape(lay.rings, 2, devices.shape[1]), AXES)
    rows = P(AXES, None)
    experts = P(("ring", "pair"), "ep", None)
    in_specs = (rows, rows, experts, P(), P(), P(), P(), rows, P(("ring", "pair")), rows)
    out_specs = (rows, rows, rows, experts, P(), P(), P(), P())

    def run(*arguments):
        return body(lay, *arguments)

    return jax.shard_map(run, mesh=inner, in_specs=in_specs, out_specs=out_specs, check_vma=False)
```

time: 1360 us -> 962 us (0.71)
  matrix products: 209 us -> 7.69 us
  Pallas kernels: 0 us -> 188 us
  local copies, waits for them, and re-layouts: 243 us -> 80.8 us
  waiting for transfers between devices: 562 us -> 451 us
  blocking collectives: 58.4 us -> 0 us
  starting transfers between devices: 147 us -> 109 us
  other arithmetic: 113 us -> 87 us
    pallas_call x0 -> x13, Pallas kernels: none -> 188 us  [the longest x2 89.9 us: ffn_chunks(): pl.pallas_call(functools.partial(ffn_kernel, units, pad, experts), grid_s...]
    dot_general x25 -> x0, matrix products: 134 us -> none  [the longest x10 70.9 us: dot(): return jnp.dot(a, b, preferred_element_type=f32)]
    ppermute x129 -> x93, waiting for transfers between devices: 562 us -> 428 us  [permute(): return lax.ppermute(rows, AXES, pairs)]
    dot_general x4 -> x2, matrix products: 69.5 us -> 7.69 us  [dot_over(): return jnp.einsum('tc,tf->cf', a, b, preferred_element_type=f32)]
    all_gather x1 -> x0, blocking collectives: 58.4 us -> none  [body(): bits = lax.all_gather(bits, AXES, axis=0, tiled=False)]
    unnamed x393 -> x181, local copies, waits for them, and re-layouts: 122 us -> 63.5 us
    ppermute x129 -> x93, starting transfers between devices: 121 us -> 80.5 us  [permute(): return lax.ppermute(rows, AXES, pairs)]
    reshape x19 -> x1, local copies, waits for them, and re-layouts: 39.2 us -> 0.63 us  [body(): bias_sum.reshape(-1)]
  transfers between devices with their start and end apart: 135 -> 101, of which waited for: 42 -> 48; matrix products, arithmetic and copies ran while one was open for 31% -> 15% of each run, Pallas kernels for 0% -> 15%
where the time goes in v2:
time: 962 us; the launch traced here: 951 us
  waiting for transfers between devices  451 us (47%)
  Pallas kernels  188 us (20%)
  starting transfers between devices  109 us (11%)
  other arithmetic  87 us (9%)
  local copies, waits for them, and re-layouts  80.8 us (8%)
  between operations  27.3 us (3%)
    ppermute x93, waiting for transfers between devices, permute(): return lax.ppermute(rows, AXES, pairs)  428 us
    pallas_call x2, Pallas kernels, ffn_chunks(): pl.pallas_call(functools.partial(ffn_kernel, units, pad, experts), grid_s...  89.9 us
    ppermute x93, starting transfers between devices, permute(): return lax.ppermute(rows, AXES, pairs)  80.5 us
    unnamed x181, local copies, waits for them, and re-layouts  63.5 us
    convert_element_type x16, other arithmetic, plus(): return (a.astype(f32) + b.astype(f32)).astype(bf16)  31.1 us
    pallas_call x3, Pallas kernels, group_call(): pl.pallas_call(kernel, grid_spec=pltpu.PrefetchScalarGridSpec(num_scalar_...  29.2 us
    pallas_call x1, Pallas kernels, gate_grad(): pl.pallas_call(functools.partial(gate_grad_kernel, wide), grid=(total //...  28.9 us
  transfers between devices with their start and end apart: 101, of which 48 were waited for; matrix products, arithmetic and copies ran while one was open for 15% of the time, Pallas kernels for 15%

profile of v2, /device:TPU:0, one launch (start us, length us, event | category | flops | bytes accessed | tf_op | source)
XLA Modules:
  0.0 950.9 jit_solution(11594001511564714759)
XLA Ops:
  24.6 6.3 collective-permute-done
  34.3 4.7 copy.58
  39.5 5.4 collective-permute-done.1
  57.8 5.5 collective-permute-done.4
  63.4 11.9 %collective-permute-done.3 = bf16[128,2176]{1,0:T(8,128)(2,1)} collective-permute-done((bf16[128,2176]{1,0:T(8,128)(2,1)}, bf16[128,2176]{1,0:T(8,128)(2,1)}, u32[]{:S(2)}, u32[]{:S(2)}) %collective-permute-start.3) | collective-permute-done | bytes 557088 | tf_op jit(solution)/shard_map/ppermute | solution.py:55
  85.7 9.6 %collective-permute-done.9 = bf16[128,2048]{1,0:T(8,128)(2,1)} collective-permute-done((bf16[128,2048]{1,0:T(8,128)(2,1)}, bf16[128,2048]{1,0:T(8,128)(2,1)}, u32[]{:S(2)}, u32[]{:S(2)}) %collective-permute-start.9) | collective-permute-done | bytes 524320 | tf_op jit(solution)/shard_map/ppermute | solution.py:55
  113.8 15.7 %collective-permute-done.10.refs_3_ = bf16[512,768]{1,0:T(8,128)(2,1)S(1)} collective-permute-done((bf16[512,768]{1,0:T(8,128)(2,1)}, bf16[512,768]{1,0:T(8,128)(2,1)S(1)}, u32[]{:S(2)}, u32[]{:S(2)}) %collective-permute-start.10) | collective-permute-done | bytes 786464 | tf_op jit(solution)/shard_map/ppermute | solution.py:55
  140.8 6.4 collective-permute-done.13.refs_2_.refs_6_
  148.9 10.5 %shard_map.208 = (bf16[1024,768]{1,0:T(8,128)(2,1)}, bf16[1024,256]{1,0:T(8,128)(2,1)S(1)}) custom-call(s32[4]{0:T(128)S(1)} %pad_add_fusion.4.where_ref, bf16[1024,2048]{1,0:T(8,128)(2,1)} %copy-done.59, f32[1,768]{1,0:T(1,128)S(1)} %bitcast.82, f32[1024,128]{1,0:T(8,128)S(1)} %copy-done.10, f32[1024,128]{1,0:T(8,128)S(1)} %get-tuple-element.148.sine_ref, ...), custom_call_target="tpu_custom_call" | custom-call | flops 3758096384 | bytes 7874048 | tf_op jit(solution)/shard_map/pallas_call | solution.py:574
  164.8 5.3 all-to-all-start.2
  175.5 24.0 %collective-permute-done.17 = bf16[128,2048]{1,0:T(8,128)(2,1)S(1)} collective-permute-done((bf16[128,2048]{1,0:T(8,128)(2,1)S(1)}, bf16[128,2048]{1,0:T(8,128)(2,1)S(1)}, u32[]{:S(2)}, u32[]{:S(2)}) %collective-permute-start.17) | collective-permute-done | bytes 524320 | tf_op jit(solution)/shard_map/ppermute | solution.py:55
  201.6 17.7 %collective-permute-done.16 = bf16[128,2048]{1,0:T(8,128)(2,1)S(1)} collective-permute-done((bf16[128,2048]{1,0:T(8,128)(2,1)S(1)}, bf16[128,2048]{1,0:T(8,128)(2,1)S(1)}, u32[]{:S(2)}, u32[]{:S(2)}) %collective-permute-start.16) | collective-permute-done | bytes 524320 | tf_op jit(solution)/shard_map/ppermute | solution.py:55
  219.3 9.8 %collective-permute-done.18 = bf16[128,2048]{1,0:T(8,128)(2,1)S(1)} collective-permute-done((bf16[128,2048]{1,0:T(8,128)(2,1)S(1)}, bf16[128,2048]{1,0:T(8,128)(2,1)S(1)}, u32[]{:S(2)}, u32[]{:S(2)}) %collective-permute-start.18) | collective-permute-done | bytes 524320 | tf_op jit(solution)/shard_map/ppermute | solution.py:55
  235.4 11.0 %collective-permute-done.19 = bf16[128,2048]{1,0:T(8,128)(2,1)S(1)} collective-permute-done((bf16[128,2048]{1,0:T(8,128)(2,1)}, bf16[128,2048]{1,0:T(8,128)(2,1)S(1)}, u32[]{:S(2)}, u32[]{:S(2)}) %collective-permute-start.19) | collective-permute-done | bytes 524320 | tf_op jit(solution)/shard_map/ppermute | solution.py:55
  250.7 9.2 collective-permute-done.27
  264.3 8.2 collective-permute-done.35
  278.2 6.7 collective-permute-done.43
  284.9 4.6 all-to-all-start.3
  314.3 9.6 %collective-permute-done.32 = bf16[128,2048]{1,0:T(8,128)(2,1)S(1)} collective-permute-done((bf16[128,2048]{1,0:T(8,128)(2,1)S(1)}, bf16[128,2048]{1,0:T(8,128)(2,1)S(1)}, u32[]{:S(2)}, u32[]{:S(2)}) %collective-permute-start.32) | collective-permute-done | bytes 524320 | tf_op jit(solution)/shard_map/ppermute | solution.py:55
  336.5 9.9 %collective-permute-done.40 = bf16[128,2048]{1,0:T(8,128)(2,1)S(1)} collective-permute-done((bf16[128,2048]{1,0:T(8,128)(2,1)}, bf16[128,2048]{1,0:T(8,128)(2,1)S(1)}, u32[]{:S(2)}, u32[]{:S(2)}) %collective-permute-start.40) | collective-permute-done | bytes 524320 | tf_op jit(solution)/shard_map/ppermute | solution.py:55
  350.4 7.2 collective-permute-done.46
  361.2 7.2 collective-permute-done.47
  375.3 5.7 all-to-all-done.3.refs_0_
  381.0 5.0 shard_map.210.gate_ref
  388.4 44.9 %shard_map.212 = (bf16[1024,2048]{1,0:T(8,128)(2,1)}, bf16[1024,2048]{1,0:T(8,128)(2,1)}, bf16[1024,2048]{1,0:T(8,128)(2,1)}, bf16[1024,2048]{1,0:T(8,128)(2,1)}...) custom-call(s32[9]{0:T(128)} %stack.113.where_ref, ...), custom_call_target="tpu_custom_call" | custom-call | flops 32212254720 | bytes 33554432 | tf_op jit(solution)/shard_map/pallas_call | solution.py:199
  433.4 7.4 collective-permute-done.50
  446.0 45.0 %shard_map.213 = (bf16[1024,2048]{1,0:T(8,128)(2,1)}, bf16[1024,2048]{1,0:T(8,128)(2,1)}, bf16[1024,2048]{1,0:T(8,128)(2,1)}, bf16[1024,2048]{1,0:T(8,128)(2,1)}...) custom-call(s32[9]{0:T(128)} %stack.113.where_ref, ...), custom_call_target="tpu_custom_call", output_to_operand_aliasing={{4}: (8, {}), {5}: (9, {})} | custom-call | flops 32212254720 | bytes 33554432 | tf_op jit(solution)/shard_map/pallas_call | solution.py:199
  494.2 5.0 collective-permute-done.53
  507.3 17.7 %shard_map.214.held_ref = bf16[8,1584,256]{2,1,0:T(8,128)(2,1)} custom-call(s32[9]{0:T(128)} %stack.113.where_ref, bf16[4096,640]{1,0:T(8,128)(2,1)} %get-tuple-element.193.hidden_ref, bf16[8,4,128,2176]{3,2,1,0:T(8,128)(2,1)} %bitcast.91, bf16[8,4,128,2176]{3,2,1,0:T(8,128)(2,1)} %bitcast.92, bf16[8,4,128,2176]{3,2,1,0:T(8,128)(2,1)} %bitcast.93, ...), custom_call_target="tpu_custom_call" | custom-call | flops 10737418240 | bytes 22020096 | tf_op jit(solution)/shard_map/pallas_call | solution.py:245
  534.8 28.9 %shard_map.215 = (bf16[8,1584,256]{2,1,0:T(8,128)(2,1)}, f32[24,2048]{1,0:T(8,128)}) custom-call(bf16[4096,1280]{1,0:T(8,128)(2,1)} %get-tuple-element.197.grad_ref, bf16[4096,2048]{1,0:T(8,128)(2,1)} %constant_dynamic-update-slice_fusion.5.rows_ref, bf16[8,1584,256]{2,1,0:T(8,128)(2,1)} %shard_map.214.held_ref), custom_call_target="tpu_custom_call", output_to_operand_aliasing={{0}: (2, {})} | custom-call | flops 21474836480 | bytes 27262976 | tf_op jit(solution)/shard_map/pallas_call | solution.py:293
  568.0 10.6 %collective-permute-done.61 = bf16[128,2048]{1,0:T(8,128)(2,1)S(1)} collective-permute-done((bf16[128,2048]{1,0:T(8,128)(2,1)S(1)}, bf16[128,2048]{1,0:T(8,128)(2,1)S(1)}, u32[]{:S(2)}, u32[]{:S(2)}) %collective-permute-start.61) | collective-permute-done | bytes 524320 | tf_op jit(solution)/shard_map/ppermute | solution.py:55
  580.2 11.7 %collective-permute-done.62 = bf16[128,2048]{1,0:T(8,128)(2,1)S(1)} collective-permute-done((bf16[128,2048]{1,0:T(8,128)(2,1)S(1)}, bf16[128,2048]{1,0:T(8,128)(2,1)S(1)}, u32[]{:S(2)}, u32[]{:S(2)}) %collective-permute-start.62) | collective-permute-done | bytes 524320 | tf_op jit(solution)/shard_map/ppermute | solution.py:55
  594.9 11.2 %collective-permute-done.63 = bf16[128,2048]{1,0:T(8,128)(2,1)S(1)} collective-permute-done((bf16[128,2048]{1,0:T(8,128)(2,1)S(1)}, bf16[128,2048]{1,0:T(8,128)(2,1)S(1)}, u32[]{:S(2)}, u32[]{:S(2)}) %collective-permute-start.63) | collective-permute-done | bytes 524320 | tf_op jit(solution)/shard_map/ppermute | solution.py:55
  606.1 4.8 all-to-all-start.4
  621.1 14.7 %shard_map.216 = (bf16[1024,768]{1,0:T(8,128)(2,1)}, bf16[512,2048]{1,0:T(8,128)(2,1)}, bf16[512,2048]{1,0:T(8,128)(2,1)}, f32[16,768]{1,0:T(8,128)S(1)}) custom-call(s32[4]{0:T(128)S(1)} %copy-done.19, bf16[1024,2048]{1,0:T(8,128)(2,1)} %copy-done.57, bf16[1024,768]{1,0:T(8,128)(2,1)} %get-tuple-element.209.packed_ref, f32[1024,128]{1,0:T(8,128)S(1)} %copy-done.11, ...), custom_call_target="tpu_custom_call" | custom-call | flops 5905580032 | bytes 10493952 | tf_op jit(solution)/shard_map/pallas_call | solution.py:574
  649.0 10.2 %collective-permute-done.80 = bf16[128,2048]{1,0:T(8,128)(2,1)S(1)} collective-permute-done((bf16[128,2048]{1,0:T(8,128)(2,1)S(1)}, bf16[128,2048]{1,0:T(8,128)(2,1)S(1)}, u32[]{:S(2)}, u32[]{:S(2)}) %collective-permute-start.80) | collective-permute-done | bytes 524320 | tf_op jit(solution)/shard_map/ppermute | solution.py:55
  663.1 7.3 collective-permute-done.79
  670.4 29.0 %collective-permute-done.81 = bf16[128,2048]{1,0:T(8,128)(2,1)S(1)} collective-permute-done((bf16[128,2048]{1,0:T(8,128)(2,1)S(1)}, bf16[128,2048]{1,0:T(8,128)(2,1)S(1)}, u32[]{:S(2)}, u32[]{:S(2)}) %collective-permute-start.81) | collective-permute-done | bytes 524320 | tf_op jit(solution)/shard_map/ppermute | solution.py:55
  700.3 6.3 convolution_convert_fusion
  725.5 18.1 %collective-permute-done.84 = f32[14,2048]{1,0:T(8,128)S(1)} collective-permute-done((f32[14,2048]{1,0:T(8,128)S(1)}, f32[14,2048]{1,0:T(8,128)S(1)}, u32[]{:S(2)}, u32[]{:S(2)}) %collective-permute-start.84) | collective-permute-done | bytes 114720 | tf_op jit(solution)/shard_map/ppermute | solution.py:55
  751.7 8.6 shard_map.217
  763.8 9.5 collective-permute-done.69
  780.0 6.8 collective-permute-done.70
  787.9 7.0 all-to-all-done.5.shared_ref
  802.7 33.4 %collective-permute-done.87 = f32[14,2048]{1,0:T(8,128)} collective-permute-done((f32[14,2048]{1,0:T(8,128)S(1)}, f32[14,2048]{1,0:T(8,128)}, u32[]{:S(2)}, u32[]{:S(2)}) %collective-permute-start.87) | collective-permute-done | bytes 114720 | tf_op jit(solution)/shard_map/ppermute | solution.py:55
  849.5 35.9 %collective-permute-done.90 = f32[14,2048]{1,0:T(8,128)} collective-permute-done((f32[14,2048]{1,0:T(8,128)S(1)}, f32[14,2048]{1,0:T(8,128)}, u32[]{:S(2)}, u32[]{:S(2)}) %collective-permute-start.90) | collective-permute-done | bytes 114720 | tf_op jit(solution)/shard_map/ppermute | solution.py:55
  897.9 20.9 %collective-permute-done.92 = bf16[512,1024]{1,0:T(8,128)(2,1)} collective-permute-done((bf16[512,1024]{1,0:T(8,128)(2,1)}, bf16[512,1024]{1,0:T(8,128)(2,1)}, u32[]{:S(2)}, u32[]{:S(2)}) %collective-permute-start.92) | collective-permute-done | bytes 1048608 | tf_op jit(solution)/shard_map/ppermute | solution.py:55
  930.8 9.9 %all-to-all-done.6.attn_ref = bf16[8,64,1024]{2,1,0:T(8,128)(2,1)S(1)} async-done(((bf16[8,64,1024]{2,1,0:T(8,128)(2,1)}), bf16[8,64,1024]{2,1,0:T(8,128)(2,1)S(1)}, u32[]{:S(2)}, u32[]{:S(2)}) %all-to-all-start.6) | async-done | bytes 1048608 | tf_op jit(solution)/shard_map/all_to_all | solution.py:886
  (477 shorter events, 302.0 us)
Async XLA Ops:
  7.2 31.9 %collective-permute-start.6 = (s32[512]{0:T(512)}, s32[512]{0:T(512)S(1)}, u32[]{:S(2)}, u32[]{:S(2)}) collective-permute-start(s32[512]{0:T(512)} %param.23), channel_id=1, source_target_pairs={{0,4},{1,5},{2,6},{3,7},{4,0},{5,1},{6,2},{7,3},{8,12},{9,13},{10,... | collective-permute-start | bytes 6152 | tf_op jit(solution)/shard_map/ppermute | solution.py:55
  45.0 30.3 %collective-permute-start.2 = (bf16[512,768]{1,0:T(8,128)(2,1)S(1)}, bf16[512,768]{1,0:T(8,128)(2,1)}, u32[]{:S(2)}, u32[]{:S(2)}) collective-permute-start(bf16[512,768]{1,0:T(8,128)(2,1)S(1)} %slice.192.refs_0_), channel_id=1, source_target_pairs={{0,16},{1,17},{2,18},{3,19},{4,20},{5,21},{6,22},{7,23},{8,0},{9,1... | collective-permute-start | bytes 2359304 | tf_op jit(solution)/shard_map/ppermute | solution.py:55
  51.2 24.1 %collective-permute-start.3 = (bf16[128,2176]{1,0:T(8,128)(2,1)}, bf16[128,2176]{1,0:T(8,128)(2,1)}, u32[]{:S(2)}, u32[]{:S(2)}) collective-permute-start(bf16[128,2176]{1,0:T(8,128)(2,1)} %collective-permute-done.1), channel_id=1, source_target_pairs={{0,16},{1,17},{2,18},{3,19},{4,20},{5,21},{6,22},{7,23},{8,0},{9,1... | collective-permute-start | bytes 1671176 | tf_op jit(solution)/shard_map/ppermute | solution.py:55
  51.2 46.5 %all-to-all-start.1 = ((bf16[4,64,4224]{2,1,0:T(8,128)(2,1)}), bf16[4,64,4224]{2,1,0:T(8,128)(2,1)S(1)}, u32[]{:S(2)}, u32[]{:S(2)}) async-start(bf16[4,64,4224]{2,1,0:T(8,128)(2,1)} %copy-done.6), calls=%async_computation.1 | async-start | bytes 4325376 | tf_op jit(solution)/shard_map/all_to_all | solution.py:662
  54.8 333.6 %all-gather.3.cloned.1.call-start = ((), (), s32[]{:S(2)}) async-start(), calls=%async_computation.7 | async-start | bytes 20054016 | tf_op jit(solution)/shard_map/all_gather | solution.py:674
  77.6 29.4 %collective-permute-start.8 = (bf16[256,2048]{1,0:T(8,128)(2,1)}, bf16[256,2048]{1,0:T(8,128)(2,1)}, u32[]{:S(2)}, u32[]{:S(2)}) collective-permute-start(bf16[256,2048]{1,0:T(8,128)(2,1)} %pad_maximum_fusion.2), channel_id=1, source_target_pairs={{0,1},{1,0},{2,3},{3,2},{4,5},{5,4},{6,7},{7,6},{8,9},{9,8},{10,11... | collective-permute-start | bytes 3145736 | tf_op jit(solution)/shard_map/ppermute | solution.py:55
  77.6 29.4 %collective-permute-start.7 = (bf16[512,768]{1,0:T(8,128)(2,1)}, bf16[512,768]{1,0:T(8,128)(2,1)}, u32[]{:S(2)}, u32[]{:S(2)}) collective-permute-start(bf16[512,768]{1,0:T(8,128)(2,1)} %collective-permute-done.2.refs_1_), channel_id=1, source_target_pairs={{0,16},{1,17},{2,18},{3,19},{4,20},{5,21},{6,22},{7,23},{8,0},{9,1... | collective-permute-start | bytes 2359304 | tf_op jit(solution)/shard_map/ppermute | solution.py:55
  164.8 66.6 %all-to-all-start.2 = ((bf16[8,528,256]{2,1,0:T(8,128)(2,1)}), bf16[8,528,256]{2,1,0:T(8,128)(2,1)S(1)}, u32[]{:S(2)}, u32[]{:S(2)}) async-start(bf16[8,528,256]{2,1,0:T(8,128)(2,1)} %copy-done.5), calls=%async_computation.2 | async-start | bytes 4325376 | tf_op jit(solution)/shard_map/all_to_all | solution.py:694
  173.4 26.1 %collective-permute-start.17 = (bf16[128,2048]{1,0:T(8,128)(2,1)S(1)}, bf16[128,2048]{1,0:T(8,128)(2,1)S(1)}, u32[]{:S(2)}, u32[]{:S(2)}) collective-permute-start(bf16[128,2048]{1,0:T(8,128)(2,1)S(1)} %get-tuple-element.272), channel_id=1, source_target_pairs={{0,2},{1,3},{2,0},{3,1},{4,6},{5,7},{6,4},{7,5},{8,10},{9,11},{10,... | collective-permute-start | bytes 1572872 | tf_op jit(solution)/shard_map/ppermute | solution.py:55
  174.9 44.4 %collective-permute-start.16 = (bf16[128,2048]{1,0:T(8,128)(2,1)S(1)}, bf16[128,2048]{1,0:T(8,128)(2,1)S(1)}, u32[]{:S(2)}, u32[]{:S(2)}) collective-permute-start(bf16[128,2048]{1,0:T(8,128)(2,1)S(1)} %get-tuple-element.271), channel_id=1, source_target_pairs={{0,2},{1,3},{2,0},{3,1},{4,6},{5,7},{6,4},{7,5},{8,10},{9,11},{10,... | collective-permute-start | bytes 1572872 | tf_op jit(solution)/shard_map/ppermute | solution.py:55
  199.5 29.5 %collective-permute-start.18 = (bf16[128,2048]{1,0:T(8,128)(2,1)S(1)}, bf16[128,2048]{1,0:T(8,128)(2,1)S(1)}, u32[]{:S(2)}, u32[]{:S(2)}) collective-permute-start(bf16[128,2048]{1,0:T(8,128)(2,1)S(1)} %add_convert_fusion.33), channel_id=1, source_target_pairs={{0,4},{1,5},{2,6},{3,7},{4,0},{5,1},{6,2},{7,3},{8,12},{9,13},{10,... | collective-permute-start | bytes 1572872 | tf_op jit(solution)/shard_map/ppermute | solution.py:55
  277.6 23.9 %collective-permute-start.24 = (bf16[128,2048]{1,0:T(8,128)(2,1)}, bf16[128,2048]{1,0:T(8,128)(2,1)}, u32[]{:S(2)}, u32[]{:S(2)}) collective-permute-start(bf16[128,2048]{1,0:T(8,128)(2,1)} %collective-permute-done.20), channel_id=1, source_target_pairs={{0,2},{1,3},{2,0},{3,1},{4,6},{5,7},{6,4},{7,5},{8,10},{9,11},{10,... | collective-permute-start | bytes 1572872 | tf_op jit(solution)/shard_map/ppermute | solution.py:55
  284.9 96.1 %all-to-all-start.3 = ((bf16[8,1056,256]{2,1,0:T(8,128)(2,1)}), bf16[8,1056,256]{2,1,0:T(8,128)(2,1)}, u32[]{:S(2)}, u32[]{:S(2)}) async-start(bf16[8,1056,256]{2,1,0:T(8,128)(2,1)} %copy-done.2), calls=%async_computation.3 | async-start | bytes 8650752 | tf_op jit(solution)/shard_map/all_to_all | solution.py:725
  309.6 23.0 %collective-permute-start.37 = (bf16[128,2048]{1,0:T(8,128)(2,1)S(1)}, bf16[128,2048]{1,0:T(8,128)(2,1)S(1)}, u32[]{:S(2)}, u32[]{:S(2)}) collective-permute-start(bf16[128,2048]{1,0:T(8,128)(2,1)S(1)} %copy-done.49), channel_id=1, source_target_pairs={{0,1},{1,0},{2,3},{3,2},{4,5},{5,4},{6,7},{7,6},{8,9},{9,8},{10,11... | collective-permute-start | bytes 1572872 | tf_op jit(solution)/shard_map/ppermute | solution.py:55
  312.4 22.7 %collective-permute-start.39 = (bf16[128,2048]{1,0:T(8,128)(2,1)S(1)}, bf16[128,2048]{1,0:T(8,128)(2,1)S(1)}, u32[]{:S(2)}, u32[]{:S(2)}) collective-permute-start(bf16[128,2048]{1,0:T(8,128)(2,1)S(1)} %copy-done.49), channel_id=1, source_target_pairs={{0,2},{1,3},{2,0},{3,1},{4,6},{5,7},{6,4},{7,5},{8,10},{9,11},{10,... | collective-permute-start | bytes 1572872 | tf_op jit(solution)/shard_map/ppermute | solution.py:55
  313.8 22.2 %collective-permute-start.38 = (bf16[128,2048]{1,0:T(8,128)(2,1)}, bf16[128,2048]{1,0:T(8,128)(2,1)S(1)}, u32[]{:S(2)}, u32[]{:S(2)}) collective-permute-start(bf16[128,2048]{1,0:T(8,128)(2,1)} %collective-permute-done.36), channel_id=1, source_target_pairs={{0,1},{1,0},{2,3},{3,2},{4,5},{5,4},{6,7},{7,6},{8,9},{9,8},{10,11... | collective-permute-start | bytes 1572872 | tf_op jit(solution)/shard_map/ppermute | solution.py:55
  328.7 41.5 %collective-permute-start.44 = (bf16[128,2048]{1,0:T(8,128)(2,1)}, bf16[128,2048]{1,0:T(8,128)(2,1)S(1)}, u32[]{:S(2)}, u32[]{:S(2)}) collective-permute-start(bf16[128,2048]{1,0:T(8,128)(2,1)} %collective-permute-done.35), channel_id=1, source_target_pairs={{0,1},{1,0},{2,3},{3,2},{4,5},{5,4},{6,7},{7,6},{8,9},{9,8},{10,11... | collective-permute-start | bytes 1572872 | tf_op jit(solution)/shard_map/ppermute | solution.py:55
  332.6 25.0 %collective-permute-start.46 = (bf16[128,2048]{1,0:T(8,128)(2,1)}, bf16[128,2048]{1,0:T(8,128)(2,1)S(1)}, u32[]{:S(2)}, u32[]{:S(2)}) collective-permute-start(bf16[128,2048]{1,0:T(8,128)(2,1)} %collective-permute-done.35), channel_id=1, source_target_pairs={{0,2},{1,3},{2,0},{3,1},{4,6},{5,7},{6,4},{7,5},{8,10},{9,11},{10,... | collective-permute-start | bytes 1572872 | tf_op jit(solution)/shard_map/ppermute | solution.py:55
  336.0 35.1 %collective-permute-start.45 = (bf16[128,2048]{1,0:T(8,128)(2,1)}, bf16[128,2048]{1,0:T(8,128)(2,1)S(1)}, u32[]{:S(2)}, u32[]{:S(2)}) collective-permute-start(bf16[128,2048]{1,0:T(8,128)(2,1)} %collective-permute-done.43), channel_id=1, source_target_pairs={{0,1},{1,0},{2,3},{3,2},{4,5},{5,4},{6,7},{7,6},{8,9},{9,8},{10,11... | collective-permute-start | bytes 1572872 | tf_op jit(solution)/shard_map/ppermute | solution.py:55
  443.9 47.1 %collective-permute-start.51 = (bf16[256,2048]{1,0:T(8,128)(2,1)S(1)}, bf16[256,2048]{1,0:T(8,128)(2,1)S(1)}, u32[]{:S(2)}, u32[]{:S(2)}) collective-permute-start(bf16[256,2048]{1,0:T(8,128)(2,1)S(1)} %get-tuple-element.172), channel_id=1, source_target_pairs={{0,2},{1,3},{2,0},{3,1},{4,6},{5,7},{6,4},{7,5},{8,10},{9,11},{10,... | collective-permute-start | bytes 3145736 | tf_op jit(solution)/shard_map/ppermute | solution.py:55
  445.5 46.3 %collective-permute-start.52 = (bf16[256,2048]{1,0:T(8,128)(2,1)S(1)}, bf16[256,2048]{1,0:T(8,128)(2,1)}, u32[]{:S(2)}, u32[]{:S(2)}) collective-permute-start(bf16[256,2048]{1,0:T(8,128)(2,1)S(1)} %get-tuple-element.173), channel_id=1, source_target_pairs={{0,2},{1,3},{2,0},{3,1},{4,6},{5,7},{6,4},{7,5},{8,10},{9,11},{10,... | collective-permute-start | bytes 3145736 | tf_op jit(solution)/shard_map/ppermute | solution.py:55
  501.6 27.6 %collective-permute-start.55 = (bf16[256,2048]{1,0:T(8,128)(2,1)}, bf16[256,2048]{1,0:T(8,128)(2,1)S(1)}, u32[]{:S(2)}, u32[]{:S(2)}) collective-permute-start(bf16[256,2048]{1,0:T(8,128)(2,1)} %get-tuple-element.190), channel_id=1, source_target_pairs={{0,2},{1,3},{2,0},{3,1},{4,6},{5,7},{6,4},{7,5},{8,10},{9,11},{10,... | collective-permute-start | bytes 3145736 | tf_op jit(solution)/shard_map/ppermute | solution.py:55
  506.2 23.0 %collective-permute-start.57 = (bf16[128,2048]{1,0:T(8,128)(2,1)}, bf16[128,2048]{1,0:T(8,128)(2,1)}, u32[]{:S(2)}, u32[]{:S(2)}) collective-permute-start(bf16[128,2048]{1,0:T(8,128)(2,1)} %slice.216), channel_id=1, source_target_pairs={{0,4},{1,5},{2,6},{3,7},{4,0},{5,1},{6,2},{7,3},{8,12},{9,13},{10,... | collective-permute-start | bytes 1572872 | tf_op jit(solution)/shard_map/ppermute | solution.py:55
  506.8 56.9 %collective-permute-start.54 = (bf16[256,2048]{1,0:T(8,128)(2,1)S(1)}, bf16[256,2048]{1,0:T(8,128)(2,1)S(1)}, u32[]{:S(2)}, u32[]{:S(2)}) collective-permute-start(bf16[256,2048]{1,0:T(8,128)(2,1)S(1)} %get-tuple-element.188), channel_id=1, source_target_pairs={{0,2},{1,3},{2,0},{3,1},{4,6},{5,7},{6,4},{7,5},{8,10},{9,11},{10,... | collective-permute-start | bytes 3145736 | tf_op jit(solution)/shard_map/ppermute | solution.py:55
  531.5 32.2 %collective-permute-start.59 = (bf16[128,2048]{1,0:T(8,128)(2,1)}, bf16[128,2048]{1,0:T(8,128)(2,1)S(1)}, u32[]{:S(2)}, u32[]{:S(2)}) collective-permute-start(bf16[128,2048]{1,0:T(8,128)(2,1)} %add_convert_fusion.32), channel_id=1, source_target_pairs={{0,8},{1,9},{2,10},{3,11},{4,12},{5,13},{6,14},{7,15},{8,24},{9,25... | collective-permute-start | bytes 1572872 | tf_op jit(solution)/shard_map/ppermute | solution.py:55
  533.4 30.4 %collective-permute-start.58 = (bf16[128,2048]{1,0:T(8,128)(2,1)S(1)}, bf16[128,2048]{1,0:T(8,128)(2,1)S(1)}, u32[]{:S(2)}, u32[]{:S(2)}) collective-permute-start(bf16[128,2048]{1,0:T(8,128)(2,1)S(1)} %slice.278), channel_id=1, source_target_pairs={{0,4},{1,5},{2,6},{3,7},{4,0},{5,1},{6,2},{7,3},{8,12},{9,13},{10,... | collective-permute-start | bytes 1572872 | tf_op jit(solution)/shard_map/ppermute | solution.py:55
  606.1 145.5 %all-to-all-start.4 = ((bf16[8,1584,256]{2,1,0:T(8,128)(2,1)}), bf16[8,1584,256]{2,1,0:T(8,128)(2,1)}, u32[]{:S(2)}, u32[]{:S(2)}) async-start(bf16[8,1584,256]{2,1,0:T(8,128)(2,1)} %get-tuple-element.225), calls=%async_computation.4 | async-start | bytes 12976128 | tf_op jit(solution)/shard_map/all_to_all | solution.py:822
  615.6 30.8 %collective-permute-start.73 = (bf16[1024,2048]{1,0:T(8,128)(2,1)}, bf16[1024,2048]{1,0:T(8,128)(2,1)}, u32[]{:S(2)}, u32[]{:S(2)}) collective-permute-start(bf16[1024,2048]{1,0:T(8,128)(2,1)} %get-tuple-element.219), channel_id=1, source_target_pairs={{0,1},{1,0},{2,3},{3,2},{4,5},{5,4},{6,7},{7,6},{8,9},{9,8},{10,11... | collective-permute-start | bytes 12582920 | tf_op jit(solution)/shard_map/ppermute | solution.py:55
  635.9 23.8 %collective-permute-start.68 = (bf16[1024,2048]{1,0:T(8,128)(2,1)}, bf16[1024,2048]{1,0:T(8,128)(2,1)}, u32[]{:S(2)}, u32[]{:S(2)}) collective-permute-start(bf16[1024,2048]{1,0:T(8,128)(2,1)} %get-tuple-element.213), channel_id=1, source_target_pairs={{0,1},{1,0},{2,3},{3,2},{4,5},{5,4},{6,7},{7,6},{8,9},{9,8},{10,11... | collective-permute-start | bytes 12582920 | tf_op jit(solution)/shard_map/ppermute | solution.py:55
  644.9 25.5 %collective-permute-start.79 = (bf16[128,2048]{1,0:T(8,128)(2,1)S(1)}, bf16[128,2048]{1,0:T(8,128)(2,1)S(1)}, u32[]{:S(2)}, u32[]{:S(2)}) collective-permute-start(bf16[128,2048]{1,0:T(8,128)(2,1)S(1)} %get-tuple-element.269), channel_id=1, source_target_pairs={{0,2},{1,3},{2,0},{3,1},{4,6},{5,7},{6,4},{7,5},{8,10},{9,11},{10,... | collective-permute-start | bytes 1572872 | tf_op jit(solution)/shard_map/ppermute | solution.py:55
  648.4 58.4 %collective-permute-start.76 = (bf16[256,2048]{1,0:T(8,128)(2,1)S(1)}, bf16[256,2048]{1,0:T(8,128)(2,1)S(1)}, u32[]{:S(2)}, u32[]{:S(2)}) collective-permute-start(bf16[256,2048]{1,0:T(8,128)(2,1)S(1)} %add_convert_fusion.3), channel_id=1, source_target_pairs={{0,2},{1,3},{2,0},{3,1},{4,6},{5,7},{6,4},{7,5},{8,10},{9,11},{10,... | collective-permute-start | bytes 3145736 | tf_op jit(solution)/shard_map/ppermute | solution.py:55
  659.3 40.1 %collective-permute-start.81 = (bf16[128,2048]{1,0:T(8,128)(2,1)S(1)}, bf16[128,2048]{1,0:T(8,128)(2,1)S(1)}, u32[]{:S(2)}, u32[]{:S(2)}) collective-permute-start(bf16[128,2048]{1,0:T(8,128)(2,1)S(1)} %add_convert_fusion.29), channel_id=1, source_target_pairs={{0,4},{1,5},{2,6},{3,7},{4,0},{5,1},{6,2},{7,3},{8,12},{9,13},{10,... | collective-permute-start | bytes 1572872 | tf_op jit(solution)/shard_map/ppermute | solution.py:55
  662.6 52.8 %collective-permute-start.71 = (bf16[256,2048]{1,0:T(8,128)(2,1)}, bf16[256,2048]{1,0:T(8,128)(2,1)}, u32[]{:S(2)}, u32[]{:S(2)}) collective-permute-start(bf16[256,2048]{1,0:T(8,128)(2,1)} %add_convert_fusion.9), channel_id=1, source_target_pairs={{0,2},{1,3},{2,0},{3,1},{4,6},{5,7},{6,4},{7,5},{8,10},{9,11},{10,... | collective-permute-start | bytes 3145736 | tf_op jit(solution)/shard_map/ppermute | solution.py:55
  709.6 38.5 %collective-permute-start.74 = (bf16[256,2048]{1,0:T(8,128)(2,1)S(1)}, bf16[256,2048]{1,0:T(8,128)(2,1)S(1)}, u32[]{:S(2)}, u32[]{:S(2)}) collective-permute-start(bf16[256,2048]{1,0:T(8,128)(2,1)S(1)} %get-tuple-element.220), channel_id=1, source_target_pairs={{0,2},{1,3},{2,0},{3,1},{4,6},{5,7},{6,4},{7,5},{8,10},{9,11},{10,... | collective-permute-start | bytes 3145736 | tf_op jit(solution)/shard_map/ppermute | solution.py:55
  719.3 27.6 %collective-permute-start.72 = (bf16[128,2048]{1,0:T(8,128)(2,1)S(1)}, bf16[128,2048]{1,0:T(8,128)(2,1)S(1)}, u32[]{:S(2)}, u32[]{:S(2)}) collective-permute-start(bf16[128,2048]{1,0:T(8,128)(2,1)S(1)} %slice.289), channel_id=1, source_target_pairs={{0,4},{1,5},{2,6},{3,7},{4,0},{5,1},{6,2},{7,3},{8,12},{9,13},{10,... | collective-permute-start | bytes 1572872 | tf_op jit(solution)/shard_map/ppermute | solution.py:55
  721.1 22.5 %collective-permute-start.84 = (f32[14,2048]{1,0:T(8,128)S(1)}, f32[14,2048]{1,0:T(8,128)S(1)}, u32[]{:S(2)}, u32[]{:S(2)}) collective-permute-start(f32[14,2048]{1,0:T(8,128)S(1)} %add.460), channel_id=1, source_target_pairs={{0,4},{1,5},{2,6},{3,7},{4,0},{5,1},{6,2},{7,3},{8,12},{9,13},{10,... | collective-permute-start | bytes 344072 | tf_op jit(solution)/shard_map/ppermute | solution.py:55
  744.4 31.4 %collective-permute-start.77 = (bf16[128,2048]{1,0:T(8,128)(2,1)}, bf16[128,2048]{1,0:T(8,128)(2,1)}, u32[]{:S(2)}, u32[]{:S(2)}) collective-permute-start(bf16[128,2048]{1,0:T(8,128)(2,1)} %slice.297), channel_id=1, source_target_pairs={{0,4},{1,5},{2,6},{3,7},{4,0},{5,1},{6,2},{7,3},{8,12},{9,13},{10,... | collective-permute-start | bytes 1572872 | tf_op jit(solution)/shard_map/ppermute | solution.py:55
  746.9 26.4 %collective-permute-start.69 = (bf16[256,2048]{1,0:T(8,128)(2,1)}, bf16[256,2048]{1,0:T(8,128)(2,1)}, u32[]{:S(2)}, u32[]{:S(2)}) collective-permute-start(bf16[256,2048]{1,0:T(8,128)(2,1)} %get-tuple-element.215), channel_id=1, source_target_pairs={{0,2},{1,3},{2,0},{3,1},{4,6},{5,7},{6,4},{7,5},{8,10},{9,11},{10,... | collective-permute-start | bytes 3145736 | tf_op jit(solution)/shard_map/ppermute | solution.py:55
  751.6 26.2 %collective-permute-start.75 = (bf16[128,2048]{1,0:T(8,128)(2,1)}, bf16[128,2048]{1,0:T(8,128)(2,1)}, u32[]{:S(2)}, u32[]{:S(2)}) collective-permute-start(bf16[128,2048]{1,0:T(8,128)(2,1)} %slice.293), channel_id=1, source_target_pairs={{0,4},{1,5},{2,6},{3,7},{4,0},{5,1},{6,2},{7,3},{8,12},{9,13},{10,... | collective-permute-start | bytes 1572872 | tf_op jit(solution)/shard_map/ppermute | solution.py:55
  760.2 34.7 %all-to-all-start.5 = ((bf16[4,64,4224]{2,1,0:T(8,128)(2,1)}), bf16[4,64,4224]{2,1,0:T(8,128)(2,1)S(1)}, u32[]{:S(2)}, u32[]{:S(2)}) async-start(bf16[4,64,4224]{2,1,0:T(8,128)(2,1)} %bitcast.101), calls=%async_computation.5 | async-start | bytes 4325376 | tf_op jit(solution)/shard_map/all_to_all | solution.py:866
  797.2 42.1 %collective-permute-start.85 = (bf16[512,1024]{1,0:T(8,128)(2,1)}, bf16[512,1024]{1,0:T(8,128)(2,1)}, u32[]{:S(2)}, u32[]{:S(2)}) collective-permute-start(bf16[512,1024]{1,0:T(8,128)(2,1)} %dynamic-slice_bitcast_fusion), channel_id=1, source_target_pairs={{0,8},{1,9},{2,10},{3,11},{4,12},{5,13},{6,14},{7,15},{8,24},{9,25... | collective-permute-start | bytes 3145736 | tf_op jit(solution)/shard_map/ppermute | solution.py:55
  797.9 39.1 %collective-permute-start.86 = (bf16[128,2048]{1,0:T(8,128)(2,1)}, bf16[128,2048]{1,0:T(8,128)(2,1)}, u32[]{:S(2)}, u32[]{:S(2)}) collective-permute-start(bf16[128,2048]{1,0:T(8,128)(2,1)} %convert_add_fusion.5), channel_id=1, source_target_pairs={{0,8},{1,9},{2,10},{3,11},{4,12},{5,13},{6,14},{7,15},{8,24},{9,25... | collective-permute-start | bytes 1572872 | tf_op jit(solution)/shard_map/ppermute | solution.py:55
  800.7 35.4 %collective-permute-start.87 = (f32[14,2048]{1,0:T(8,128)S(1)}, f32[14,2048]{1,0:T(8,128)}, u32[]{:S(2)}, u32[]{:S(2)}) collective-permute-start(f32[14,2048]{1,0:T(8,128)S(1)} %add.461), channel_id=1, source_target_pairs={{0,8},{1,9},{2,10},{3,11},{4,12},{5,13},{6,14},{7,15},{8,0},{9,1},... | collective-permute-start | bytes 344072 | tf_op jit(solution)/shard_map/ppermute | solution.py:55
  842.2 46.3 %collective-permute-start.88 = (bf16[512,1024]{1,0:T(8,128)(2,1)}, bf16[512,1024]{1,0:T(8,128)(2,1)}, u32[]{:S(2)}, u32[]{:S(2)}) collective-permute-start(bf16[512,1024]{1,0:T(8,128)(2,1)} %fusion.1), channel_id=1, source_target_pairs={{0,8},{1,9},{2,10},{3,11},{4,12},{5,13},{6,14},{7,15},{8,24},{9,25... | collective-permute-start | bytes 3145736 | tf_op jit(solution)/shard_map/ppermute | solution.py:55
  842.7 43.6 %collective-permute-start.89 = (bf16[128,2048]{1,0:T(8,128)(2,1)}, bf16[128,2048]{1,0:T(8,128)(2,1)}, u32[]{:S(2)}, u32[]{:S(2)}) collective-permute-start(bf16[128,2048]{1,0:T(8,128)(2,1)} %add_convert_fusion.28), channel_id=1, source_target_pairs={{0,8},{1,9},{2,10},{3,11},{4,12},{5,13},{6,14},{7,15},{8,24},{9,25... | collective-permute-start | bytes 1572872 | tf_op jit(solution)/shard_map/ppermute | solution.py:55
  845.5 39.9 %collective-permute-start.90 = (f32[14,2048]{1,0:T(8,128)S(1)}, f32[14,2048]{1,0:T(8,128)}, u32[]{:S(2)}, u32[]{:S(2)}) collective-permute-start(f32[14,2048]{1,0:T(8,128)S(1)} %add.467), channel_id=1, source_target_pairs={{0,16},{1,17},{2,18},{3,19},{4,20},{5,21},{6,22},{7,23},{8,24},{9,... | collective-permute-start | bytes 344072 | tf_op jit(solution)/shard_map/ppermute | solution.py:55
  891.5 27.3 %collective-permute-start.92 = (bf16[512,1024]{1,0:T(8,128)(2,1)}, bf16[512,1024]{1,0:T(8,128)(2,1)}, u32[]{:S(2)}, u32[]{:S(2)}) collective-permute-start(bf16[512,1024]{1,0:T(8,128)(2,1)} %fusion.2), channel_id=1, source_target_pairs={{0,8},{1,9},{2,10},{3,11},{4,12},{5,13},{6,14},{7,15},{8,24},{9,25... | collective-permute-start | bytes 3145736 | tf_op jit(solution)/shard_map/ppermute | solution.py:55
  894.0 34.2 %collective-permute-start.91 = (bf16[128,2048]{1,0:T(8,128)(2,1)}, bf16[128,2048]{1,0:T(8,128)(2,1)}, u32[]{:S(2)}, u32[]{:S(2)}) collective-permute-start(bf16[128,2048]{1,0:T(8,128)(2,1)} %add_convert_fusion.27), channel_id=1, source_target_pairs={{0,8},{1,9},{2,10},{3,11},{4,12},{5,13},{6,14},{7,15},{8,24},{9,25... | collective-permute-start | bytes 1572872 | tf_op jit(solution)/shard_map/ppermute | solution.py:55
  (123 other events, 2021.3 us)
Sparse Core Ops, SparseCore 0:
  107.1 126.7 all-gather.2

commit v3 on v2

v3 whole, which is shorter than its diff:
```python
import functools

import jax
import jax.numpy as jnp
from jax import lax
from jax.experimental import pallas as pl
from jax.experimental.pallas import tpu as pltpu
from jax.sharding import Mesh, PartitionSpec as P

H = 16
HD = 128
FF = 1408
SFF = 5632

norm_eps = 1e-06
rope_base = 1000000.0
AXES = ("ring", "pair", "ep")
PLANE = ("pair", "ep")
SHARED = -1
f32 = jnp.float32
bf16 = jnp.bfloat16


class Layout:
    def __init__(self, rings):
        self.rings = rings
        self.order = list(range(0, rings, 2)) + list(range(1, rings, 2))[::-1]
        place = {r: i for i, r in enumerate(self.order)}
        self.place = [place[r] for r in range(rings)]
        self.core = self.pairs(lambda r, y, x, c: (r, y, x, 1 - c))
        self.side = self.pairs(lambda r, y, x, c: (r, y, 1 - x, c))
        self.side_core = self.pairs(lambda r, y, x, c: (r, y, 1 - x, 1 - c))
        self.up = self.pairs(lambda r, y, x, c: (r, 1 - y, x, c))
        self.cross = self.pairs(lambda r, y, x, c: (r, 1 - y, 1 - x, c))
        self.onward = self.pairs(lambda r, y, x, c: (self.order[(place[r] + 1) % rings], y, x, c))
        self.backward = self.pairs(lambda r, y, x, c: (self.order[(place[r] - 1) % rings], y, x, c))

    def pairs(self, move):
        found = []
        for r in range(self.rings):
            for y in range(2):
                for x in range(2):
                    for c in range(2):
                        u, v, w, q = move(r, y, x, c)
                        found.append((((r * 2 + y) * 2 + x) * 2 + c, ((u * 2 + v) * 2 + w) * 2 + q))
        return found

    def doubling(self):
        steps = []
        bit = 1
        while bit < self.rings * 8:
            steps.append([(i, i ^ bit) for i in range(self.rings * 8)])
            bit *= 2
        return steps


def permute(rows, pairs):
    return lax.ppermute(rows, AXES, pairs)


def stack(*parts):
    return jnp.concatenate(parts, axis=0)


def plus(a, b):
    return (a.astype(f32) + b.astype(f32)).astype(bf16)


def assemble_kernel(*refs):
    parts, out_ref, sems = refs[:-2], refs[-2], refs[-1]
    copies, at = [], 0
    for i, part in enumerate(parts):
        size = part.shape[0]
        copies.append(pltpu.make_async_copy(part, out_ref.at[pl.ds(at, size)], sems.at[i]))
        copies[-1].start()
        at += size
    for copy in copies:
        copy.wait()


def assemble(parts):
    rows = sum(part.shape[0] for part in parts)
    width = parts[0].shape[1]
    if rows * width > 1 << 24:
        return stack(*parts)
    return pl.pallas_call(
        assemble_kernel,
        in_specs=[pl.BlockSpec(memory_space=pltpu.VMEM)] * len(parts),
        out_specs=pl.BlockSpec(memory_space=pl.ANY),
        out_shape=jax.ShapeDtypeStruct((rows, width), bf16),
        scratch_shapes=[pltpu.SemaphoreType.DMA((len(parts),))],
        compiler_params=pltpu.CompilerParams(vmem_limit_bytes=48 * 1024 * 1024),
        cost_estimate=pl.CostEstimate(flops=0, bytes_accessed=4 * rows * width, transcendentals=0),
    )(*parts)


def rope_tables(places):
    steps_along = jnp.arange(HD // 2, dtype=f32) * (2.0 / HD)
    inverse = jnp.power(jnp.float32(rope_base), -steps_along)
    angles = places.astype(f32)[..., None] * inverse
    angles = jnp.concatenate([angles, angles], axis=-1)
    return jnp.cos(angles), jnp.sin(angles)


def dot(a, b):
    return jnp.dot(a, b, preferred_element_type=f32)


def dot_over(a, b):
    return jnp.einsum("tc,tf->cf", a, b, preferred_element_type=f32)


def after(value, *others):
    return lax.optimization_barrier((value,) + others)[0]


def together(*values):
    return lax.optimization_barrier(values)


def dot_nt(a, b):
    return lax.dot_general(a, b, (((1,), (1,)), ((), ())), preferred_element_type=f32)


def dot_tn(a, b):
    return lax.dot_general(a, b, (((0,), (0,)), ((), ())), preferred_element_type=f32)


def units_pass(gate_up, hidden_grad, gates):
    pad = hidden_grad.shape[1]
    g, u = gate_up[:, :pad], gate_up[:, pad:]
    sig = jax.nn.sigmoid(g)
    silu = g * sig
    hidden = (silu * u).astype(bf16).astype(f32)
    gated_grad = hidden_grad * gates
    up_grad = gated_grad * silu
    gate_grad = gated_grad * u * (sig + silu * (1.0 - sig))
    return (gates * hidden).astype(bf16), gate_grad, up_grad, hidden_grad * hidden


def with_logits(gate_grad, logit_grad, up_grad, base, at):
    lane = lax.broadcasted_iota(jnp.int32, logit_grad.shape, 1)
    parts = [gate_grad[:, :base]] if base else []
    parts.append(jnp.where(lane < at, gate_grad[:, base : base + 128], logit_grad))
    if base + 128 < gate_grad.shape[1]:
        parts.append(gate_grad[:, base + 128 :])
    return jnp.concatenate(parts + [up_grad], axis=1).astype(bf16)


def hand_out(wide, gate_sums, down_sums, out_ref, router_ref):
    pad = down_sums.shape[0]
    first = wide // 8 * 8
    router_ref[...] = gate_sums[first : first + router_ref.shape[0]]
    if len(out_ref.shape) == 2:
        out_ref[: 2 * pad] = gate_sums[...].astype(bf16)
        out_ref[2 * pad :] = down_sums[...].astype(bf16)
        return
    count, _, block = out_ref.shape
    for d in range(count):
        lanes = slice(d * block, (d + 1) * block)
        out_ref[d, :wide] = gate_sums[:wide, lanes].astype(bf16)
        out_ref[d, wide : 2 * wide] = gate_sums[pad : pad + wide, lanes].astype(bf16)
        out_ref[d, 2 * wide :] = down_sums[:wide, lanes].astype(bf16)


def add_grads(grad, rows, hidden, cots, gate_sums, down_sums):
    @pl.when(pl.program_id(0) == 0)
    def _():
        gate_sums[...] = jnp.zeros_like(gate_sums)
        down_sums[...] = jnp.zeros_like(down_sums)

    gate_sums[...] += dot_tn(grad, rows)
    down_sums[...] += dot_tn(hidden, cots)


def group_pass(groups, units, experts, where_ref, rows_ref, cots_ref, gate_ref, down_ref):
    n, width = rows_ref.shape
    pad = down_ref.shape[0]
    wide = units * len(groups)
    base = wide // 128 * 128
    at = wide - base
    gate_up = dot_nt(rows_ref[...], gate_ref[...])
    hidden_grad = dot_nt(cots_ref[:, :width], down_ref[...])
    logits = gate_up[:, base : base + 128]
    place = lax.broadcasted_iota(jnp.int32, (n, 128), 1) - at
    routed = (place >= 0) & (place < experts)
    bits = cots_ref[:, width : width + 128].astype(f32).astype(jnp.int32)
    turn = jnp.where(routed, lax.rem(where_ref[0] + place, experts), 0)
    chosen = (jnp.right_shift(bits, turn) & 1).astype(f32)
    peak = jnp.max(jnp.where(routed, logits, -jnp.inf), axis=1, keepdims=True)
    weights = jnp.where(routed, jnp.exp(logits - peak), 0.0)
    probs = weights / jnp.sum(weights, axis=1, keepdims=True)
    shared = jax.nn.sigmoid(logits)
    spot = lax.broadcasted_iota(jnp.int32, (128, pad), 1)
    lane = lax.broadcasted_iota(jnp.int32, (128, pad), 0) - at
    spread = jnp.zeros((128, pad), f32)
    for i, group in enumerate(groups):
        own = (spot >= i * units) & (spot < (i + 1) * units) & (lane == (experts if group == SHARED else group))
        spread = jnp.where(own, 1.0, spread)
    spread = spread.astype(bf16)
    gates = dot(jnp.where(place == experts, shared, probs * chosen).astype(bf16), spread)
    gated, gate_grad, up_grad, products = units_pass(gate_up, hidden_grad, gates)
    sums = dot_nt(products.astype(bf16), spread)
    own = sums * chosen
    mean = jnp.sum(jnp.where(routed, probs * own, 0.0), axis=1, keepdims=True)
    logit_grad = jnp.where(routed, probs * (own - mean), jnp.where(place == experts, sums * shared * (1.0 - shared), 0.0))
    return gated, with_logits(gate_grad, logit_grad, up_grad, base, at)


def first_kernel(
    groups, units, experts, where_ref, rows_ref, cots_ref, gate_ref, down_ref, hidden_ref, grad_ref, out_ref, router_ref, gate_sums, down_sums
):
    gated, grad = group_pass(groups, units, experts, where_ref, rows_ref, cots_ref, gate_ref, down_ref)
    hidden_ref[...] = gated
    grad_ref[...] = grad
    add_grads(grad, rows_ref[...], gated, cots_ref[:, : rows_ref.shape[1]], gate_sums, down_sums)

    @pl.when(pl.program_id(0) == pl.num_programs(0) - 1)
    def _():
        hand_out(units * len(groups), gate_sums, down_sums, out_ref, router_ref)


def grads_kernel(wide, where_ref, rows_ref, cots_ref, hidden_ref, grad_ref, out_ref, router_ref, gate_sums, down_sums):
    cots = cots_ref[:, : rows_ref.shape[1]]
    add_grads(grad_ref[...], rows_ref[...], hidden_ref[...], cots, gate_sums, down_sums)

    @pl.when(pl.program_id(0) == pl.num_programs(0) - 1)
    def _():
        hand_out(wide, gate_sums, down_sums, out_ref, router_ref)


def second_kernel(
    groups, units, experts, where_ref, rows_ref, cots_ref, hidden_in_ref, grad_in_ref, gate_in_ref, down_in_ref, gate_ref, down_ref, *refs
):
    out_own_ref, out_far_ref, own_ref, far_ref, hidden_ref, grad_ref = refs[-6:]
    half = own_ref.shape[0]
    gated, grad = group_pass(groups, units, experts, where_ref, rows_ref, cots_ref, gate_ref, down_ref)
    hidden_ref[...] = gated
    grad_ref[...] = grad
    rows_grad = (dot(grad_in_ref[...], gate_in_ref[...]) + dot(grad, gate_ref[...])).astype(bf16)
    own_ref[...] = rows_grad[:half]
    far_ref[...] = rows_grad[half:]
    out_part = (dot(hidden_in_ref[...], down_in_ref[...]) + dot(gated, down_ref[...])).astype(bf16)
    out_own_ref[...] = out_part[:half]
    out_far_ref[...] = out_part[half:]


def among_all(w, tile, first=0):
    return pl.BlockSpec((tile, w), lambda i, where: (first + i, 0))


def all_of(shape):
    return pl.BlockSpec(shape, lambda i, where: (0,) * len(shape), pipeline_mode=pl.Buffered(1))


def grads_out(wide, pad, width, count):
    direct = whole_tiles(wide, width // count)
    return (count, 3 * wide, width // count) if direct else (3 * pad, width), (24, width)


def to_owners(grad, wide, count):
    if len(grad.shape) == 3:
        return grad
    grad = grad.reshape(3, -1, grad.shape[1])[:, :wide]
    return grad.reshape(3 * wide, count, -1).transpose(1, 0, 2)


def token_grid(cots, rows, tile=512):
    return rows.shape[0] // tile, tile, [among_all(rows.shape[1], tile), among_all(cots.shape[1], tile)]


def first_units(groups, where, rows, cots, gate_rows, down_rows, units, experts, count):
    total, width = rows.shape
    pad = down_rows.shape[0]
    wide = units * len(groups)
    steps, tile, token_specs = token_grid(cots, rows)
    shapes = grads_out(wide, pad, width, count)
    hidden, grad, weights, router = pl.pallas_call(
        functools.partial(first_kernel, groups, units, experts),
        grid_spec=pltpu.PrefetchScalarGridSpec(
            num_scalar_prefetch=1,
            grid=(steps,),
            in_specs=token_specs + [all_of(gate_rows.shape), all_of(down_rows.shape)],
            out_specs=[among_all(pad, tile), among_all(2 * pad, tile), all_of(shapes[0]), all_of(shapes[1])],
            scratch_shapes=[pltpu.VMEM((2 * pad, width), f32), pltpu.VMEM((pad, width), f32)],
        ),
        out_shape=[
            jax.ShapeDtypeStruct((total, pad), bf16),
            jax.ShapeDtypeStruct((total, 2 * pad), bf16),
            jax.ShapeDtypeStruct(shapes[0], bf16),
            jax.ShapeDtypeStruct(shapes[1], f32),
        ],
        compiler_params=pltpu.CompilerParams(vmem_limit_bytes=60 * 1024 * 1024),
        cost_estimate=pl.CostEstimate(flops=12 * total * width * pad, bytes_accessed=4 * total * width, transcendentals=0),
    )(where, rows, cots, gate_rows, down_rows)
    return hidden, grad, to_owners(weights, wide, count), router


def weight_grads(where, rows, cots, hidden, grad, wide, count):
    total, width = rows.shape
    pad = hidden.shape[1]
    steps, tile, token_specs = token_grid(cots, rows)
    shapes = grads_out(wide, pad, width, count)
    weights, router = pl.pallas_call(
        functools.partial(grads_kernel, wide),
        grid_spec=pltpu.PrefetchScalarGridSpec(
            num_scalar_prefetch=1,
            grid=(steps,),
            in_specs=token_specs + [among_all(pad, tile), among_all(2 * pad, tile)],
            out_specs=[all_of(shapes[0]), all_of(shapes[1])],
            scratch_shapes=[pltpu.VMEM((2 * pad, width), f32), pltpu.VMEM((pad, width), f32)],
        ),
        out_shape=[jax.ShapeDtypeStruct(shapes[0], bf16), jax.ShapeDtypeStruct(shapes[1], f32)],
        compiler_params=pltpu.CompilerParams(vmem_limit_bytes=58 * 1024 * 1024),
        cost_estimate=pl.CostEstimate(flops=6 * total * width * pad, bytes_accessed=4 * total * width, transcendentals=0),
    )(where, rows, cots, hidden, grad)
    return to_owners(weights, wide, count), router


def second_units(groups, first, chunks, where, rows, cots, before, own, kept, units, experts):
    total, width = rows.shape
    steps, tile = chunks * 2, 512
    hidden_in, grad_in, gate_in, down_in = before
    gate_rows, down_rows = own
    pad = down_rows.shape[0]

    def half(w):
        return pl.BlockSpec((tile // 2, w), lambda i, where: (i, 0))

    def tokens_of(v):
        return among_all(v if isinstance(v, int) else v.shape[1], tile, first * 2)

    kept = list(kept)
    shapes = [(steps * tile // 2, width)] * 4 + [(total, pad), (total, 2 * pad)]
    return pl.pallas_call(
        functools.partial(second_kernel, groups, units, experts),
        grid_spec=pltpu.PrefetchScalarGridSpec(
            num_scalar_prefetch=1,
            grid=(steps,),
            in_specs=[tokens_of(rows), tokens_of(cots)]
            + [tokens_of(hidden_in), tokens_of(grad_in)]
            + [all_of(v.shape) for v in (gate_in, down_in, gate_rows, down_rows)]
            + [pl.BlockSpec(memory_space=pl.ANY)] * len(kept),
            out_specs=[half(width)] * 4 + [tokens_of(pad), tokens_of(2 * pad)],
        ),
        out_shape=[jax.ShapeDtypeStruct(shape, bf16) for shape in shapes],
        input_output_aliases={9 + i: 4 + i for i in range(len(kept))},
        compiler_params=pltpu.CompilerParams(vmem_limit_bytes=58 * 1024 * 1024),
        cost_estimate=pl.CostEstimate(flops=10 * steps * tile * width * pad, bytes_accessed=8 * steps * tile * width, transcendentals=0),
    )(where, rows, cots, hidden_in, grad_in, gate_in, down_in, gate_rows, down_rows, *kept)


def whole_tiles(units, rows):
    return units % 16 == 0 and rows % 128 == 0


def turn_kernel(columns_ref, out_ref):
    count, units, rows = out_ref.shape
    out_ref[...] = columns_ref[...].T.reshape(count, units, rows)


def turn_weights(columns, who, count, which=0):
    rows, width = columns.shape
    span = width // (3 * who)
    units = span // count
    if not whole_tiles(units, rows):
        columns = columns.reshape(rows, who, 3, count, units)[:, which]
        return columns.transpose(2, 1, 3, 0).reshape(count, -1, rows)
    return pl.pallas_call(
        turn_kernel,
        grid=(3,),
        in_specs=[pl.BlockSpec((rows, span), lambda k: (0, which * 3 + k))],
        out_specs=pl.BlockSpec((count, units, rows), lambda k: (0, k, 0)),
        out_shape=jax.ShapeDtypeStruct((count, 3 * units, rows), bf16),
        compiler_params=pltpu.CompilerParams(vmem_limit_bytes=32 * 1024 * 1024),
        cost_estimate=pl.CostEstimate(flops=0, bytes_accessed=4 * rows * 3 * span, transcendentals=0),
    )(columns)


def turn_back_kernel(first_ref, second_ref, shared_ref, routed_ref):
    count, units, rows = first_ref.shape

    def turned(block):
        return block.reshape(count * units, rows).T

    routed_ref[:, 0, :] = turned(first_ref[...]).astype(f32)
    routed_ref[:, 1, :] = turned(second_ref[:, :units]).astype(f32)
    shared_ref[...] = turned(second_ref[:, units:])


def turn_grads(first, second):
    count, units, rows = first.shape
    units = units // 3
    span = units * count
    if not whole_tiles(units, rows):
        second = second.reshape(count, 3, 2, units, rows)
        first = first.reshape(count, 3, units, rows)
        three = jnp.stack([first, second[:, :, 0], second[:, :, 1]]).transpose(0, 4, 2, 1, 3).reshape(3, rows, 3 * span)
        return three[2], jnp.moveaxis(three[:2], 0, 1).astype(f32)
    return pl.pallas_call(
        turn_back_kernel,
        grid=(3,),
        in_specs=[
            pl.BlockSpec((count, units, rows), lambda k: (0, k, 0)),
            pl.BlockSpec((count, 2 * units, rows), lambda k: (0, k, 0)),
        ],
        out_specs=[
            pl.BlockSpec((rows, span), lambda k: (0, k)),
            pl.BlockSpec((rows, 2, span), lambda k: (0, 0, k)),
        ],
        out_shape=[jax.ShapeDtypeStruct((rows, 3 * span), bf16), jax.ShapeDtypeStruct((rows, 2, 3 * span), f32)],
        compiler_params=pltpu.CompilerParams(vmem_limit_bytes=56 * 1024 * 1024),
        cost_estimate=pl.CostEstimate(flops=0, bytes_accessed=48 * rows * span, transcendentals=0),
    )(first, second)


def deal_kernel(share, dense_ref, attn_ref, shared_ref):
    width = share * 8
    for o in range(8):
        for k in range(4):
            at = k * width + o * share
            attn_ref[o, :, k * share : (k + 1) * share] = dense_ref[:, at : at + share]
    owners, _, columns = shared_ref.shape
    span = columns // 3
    for o in range(owners):
        for k in range(3):
            at = 4 * width + (k * owners + o) * span
            shared_ref[o, :, k * span : (k + 1) * span] = dense_ref[:, at : at + span]


def deal_columns(dense, share, owners):
    rows, columns = dense.shape
    shapes = [(8, rows, 4 * share), (owners, rows, (columns - 32 * share) // owners)]
    return pl.pallas_call(
        functools.partial(deal_kernel, share),
        out_shape=[jax.ShapeDtypeStruct(shape, bf16) for shape in shapes],
        compiler_params=pltpu.CompilerParams(vmem_limit_bytes=32 * 1024 * 1024),
        cost_estimate=pl.CostEstimate(flops=0, bytes_accessed=4 * rows * columns, transcendentals=0),
    )(dense)


def collect_kernel(share, attn_ref, shared_ref, dense_ref):
    width = share * 8
    for o in range(8):
        for k in range(4):
            at = k * width + o * share
            dense_ref[:, at : at + share] = attn_ref[o, :, k * share : (k + 1) * share].astype(f32)
    owners, _, columns = shared_ref.shape
    span = columns // 3
    for o in range(owners):
        for k in range(3):
            at = 4 * width + (k * owners + o) * span
            dense_ref[:, at : at + span] = shared_ref[o, :, k * span : (k + 1) * span].astype(f32)


def collect_columns(attn, shared, share):
    rows = attn.shape[1]
    columns = 32 * share + shared.shape[0] * shared.shape[2]
    return pl.pallas_call(
        functools.partial(collect_kernel, share),
        out_shape=jax.ShapeDtypeStruct((rows, columns), f32),
        compiler_params=pltpu.CompilerParams(vmem_limit_bytes=32 * 1024 * 1024),
        cost_estimate=pl.CostEstimate(flops=0, bytes_accessed=6 * rows * columns, transcendentals=0),
    )(attn, shared)


def place_kernel(units, *refs):
    parts, (router_ref, gate_ref, down_ref) = refs[:-3], refs[-3:]
    pad = down_ref.shape[0]
    wide = units * len(parts)
    blank = jnp.zeros((pad - wide, down_ref.shape[1]), bf16)
    for w, part in enumerate(parts):
        for k, (out_ref, at) in enumerate(((gate_ref, 0), (gate_ref, pad), (down_ref, 0))):
            out_ref[at + w * units : at + (w + 1) * units] = part[0, k * units : (k + 1) * units]
    gate_ref[wide:pad] = router_ref[...]
    gate_ref[pad + wide :] = blank
    down_ref[wide:] = blank


def place_weights(ffn, router):
    count, _, block = ffn.shape
    units = FF // count
    who = ffn.shape[1] // (3 * units)
    wide = units * who
    width = count * block
    pad = (wide + router.shape[0] + 127) // 128 * 128
    router = stack(router, jnp.zeros((pad - wide - router.shape[0], width), bf16))
    if not whole_tiles(units, block):
        gate, up, down = ffn.transpose(1, 0, 2).reshape(who, 3, units, width).transpose(1, 0, 2, 3).reshape(3, wide, width)
        blank = jnp.zeros((pad - wide, width), bf16)
        return stack(gate, router, up, blank), stack(down, blank)

    def column(r):
        return pl.BlockSpec((r, block), lambda i: (0, i))

    return pl.pallas_call(
        functools.partial(place_kernel, units),
        grid=(count,),
        in_specs=[pl.BlockSpec((1, 3 * units, block), lambda i, w=w: (i, w, 0)) for w in range(who)] + [column(pad - wide)],
        out_specs=[column(2 * pad), column(pad)],
        out_shape=[jax.ShapeDtypeStruct((r, width), bf16) for r in (2 * pad, pad)],
        compiler_params=pltpu.CompilerParams(vmem_limit_bytes=32 * 1024 * 1024),
        cost_estimate=pl.CostEstimate(flops=0, bytes_accessed=12 * wide * width, transcendentals=0),
    )(*[ffn] * who, router)


def attend_rows(queries, keys, allowed):
    scores = jnp.where(allowed, dot_nt(queries, keys) * HD ** (-0.5), -1e30)
    raw = jnp.exp(scores - jnp.max(scores, axis=1, keepdims=True))
    return raw / jnp.sum(raw, axis=1, keepdims=True)


def allowed_pairs(own_ref, all_ref):
    return (own_ref[:, :1] == all_ref[0, :1]) & (all_ref[0, 1:2] <= own_ref[:, 1:2])


def piece_at(where_ref, s, piece_ref):
    size = piece_ref.shape[0]
    return pl.ds(pl.multiple_of(where_ref[s] * size, size), size)


def attend_kernel(heads, where_ref, rows_ref, bias_ref, cosine_ref, sine_ref, own_ref, all_ref, *refs):
    pieces, (packed_ref, mixed_ref) = refs[:-2], refs[-2:]
    share = heads * HD
    packed = bias_ref[...]
    for s, piece in enumerate(pieces):
        packed = packed + dot(rows_ref[:, piece_at(where_ref, s, piece)], piece[:, : 3 * share])
    cosine, sine = cosine_ref[...], sine_ref[...]
    allowed = allowed_pairs(own_ref, all_ref)

    def turned(at):
        v = packed[:, at : at + HD]
        return (v * cosine + pltpu.roll(v, HD // 2, 1) * sine).astype(bf16)

    for h in range(heads):
        queries, keys = turned(h * HD), turned(share + h * HD)
        values = packed[:, 2 * share + h * HD : 2 * share + (h + 1) * HD].astype(bf16)
        attend = attend_rows(queries, keys, allowed)
        mixed_ref[:, h * HD : (h + 1) * HD] = dot(attend.astype(bf16), values).astype(bf16)
        for k, v in enumerate((queries, keys, values)):
            packed_ref[:, k * share + h * HD : k * share + (h + 1) * HD] = v


def project_kernel(where_ref, mixed_ref, *refs):
    pieces, (near_ref, far_ref) = refs[:-2], refs[-2:]
    half = near_ref.shape[0]
    for s, piece in enumerate(pieces):
        rows = dot_nt(mixed_ref[...], piece[:, piece.shape[1] * 3 // 4 :]).astype(bf16)
        columns = piece_at(where_ref, s, piece)
        near_ref[:, columns] = rows[:half]
        far_ref[:, columns] = rows[half:]


def attend_back_kernel(heads, where_ref, grad_ref, packed_ref, cosine_ref, sine_ref, own_ref, all_ref, *refs):
    pieces, (packed_grad_ref, near_ref, far_ref, bias_ref) = refs[:-4], refs[-4:]
    share = heads * HD
    scale = HD ** (-0.5)
    mixed_grad = 0.0
    for s, piece in enumerate(pieces):
        mixed_grad = mixed_grad + dot(grad_ref[:, piece_at(where_ref, s, piece)], piece[:, 3 * share :])
    mixed_grad = mixed_grad.astype(bf16)
    cosine, sine = cosine_ref[...], sine_ref[...]
    allowed = allowed_pairs(own_ref, all_ref)

    def back(v):
        v = v.astype(bf16).astype(f32)
        return (v * cosine - pltpu.roll(v, HD // 2, 1) * sine).astype(bf16)

    for h in range(heads):
        queries, keys, values = (
            packed_ref[:, k * share + h * HD : k * share + (h + 1) * HD] for k in range(3)
        )
        own_grad = mixed_grad[:, h * HD : (h + 1) * HD]
        attend = attend_rows(queries, keys, allowed)
        attend_grad = dot_nt(own_grad, values)
        scores_grad = attend * (attend_grad - jnp.sum(attend * attend_grad, axis=1, keepdims=True))
        scores_grad = scores_grad.astype(bf16)
        grads = (
            back(dot(scores_grad, keys) * scale),
            back(dot_tn(scores_grad, queries) * scale),
            dot_tn(attend.astype(bf16), own_grad).astype(bf16),
        )
        for k, v in enumerate(grads):
            packed_grad_ref[:, k * share + h * HD : k * share + (h + 1) * HD] = v
    packed_grad = packed_grad_ref[...]
    bias_ref[...] = jnp.broadcast_to(jnp.sum(packed_grad.astype(f32), axis=0, keepdims=True), bias_ref.shape)
    half = near_ref.shape[0]
    for s, piece in enumerate(pieces):
        rows_grad = dot_nt(packed_grad, piece[:, : 3 * share]).astype(bf16)
        columns = piece_at(where_ref, s, piece)
        near_ref[:, columns] = rows_grad[:half]
        far_ref[:, columns] = rows_grad[half:]


def group_call(kernel, group_len, where, operands, specs, pieces, out_widths, out_types, flops):
    def spec(kind, shape):
        if kind == "rows":
            return pl.BlockSpec((group_len, shape[1]), lambda i, where: (i, 0))
        if kind == "pair":
            return pl.BlockSpec((1,) + shape[1:], lambda i, where: (i, 0, 0))
        return pl.BlockSpec(shape, lambda i, where: (0, 0), pipeline_mode=pl.Buffered(1))

    operands = tuple(operands) + tuple(pieces)
    specs = tuple(specs) + ("all",) * len(pieces)
    return pl.pallas_call(
        kernel,
        grid_spec=pltpu.PrefetchScalarGridSpec(
            num_scalar_prefetch=1,
            grid=(2,),
            in_specs=[spec(k, v.shape) for k, v in zip(specs, operands)],
            out_specs=[pl.BlockSpec((r, w), lambda i, where: (i, 0)) for r, w in out_widths],
        ),
        out_shape=[jax.ShapeDtypeStruct((2 * r, w), t) for (r, w), t in zip(out_widths, out_types)],
        compiler_params=pltpu.CompilerParams(vmem_limit_bytes=48 * 1024 * 1024),
        cost_estimate=pl.CostEstimate(flops=flops, bytes_accessed=sum(2 * v.size for v in operands), transcendentals=0),
    )(where, *operands)


def body(lay, tokens, dense_weights, expert_weights, gain_attn, gain_ffn, qkv_bias, router_weight, routes, doc_ids, out_grad):
    row_count, model_width = tokens.shape
    rings = lay.rings
    ring = lax.axis_index("ring")
    pair = lax.axis_index("pair")
    ep = lax.axis_index("ep")
    local_experts = expert_weights.shape[1]
    expert_count = router_weight.shape[1] - 1
    owners = expert_count // local_experts
    dp_count = rings * 2
    ring_place = jnp.asarray(lay.place, jnp.int32)[ring]
    behind = [jnp.asarray(lay.order, jnp.int32)[(ring_place - s) % rings] for s in range(rings)]
    ring_order = jnp.stack(behind)
    own_expert = ep * local_experts
    where = own_expert[None].astype(jnp.int32)

    stream = tokens.astype(f32)
    gain_one = gain_attn.astype(f32)
    gain_two = gain_ffn.astype(f32)
    heads = H // 8
    share = heads * HD
    unit_share = SFF // owners
    units = FF // dp_count
    n = row_count

    bits = jnp.sum(jnp.left_shift(jnp.int32(1), routes), axis=1, keepdims=True).astype(bf16)
    cot_blocks = [jnp.concatenate([out_grad, jnp.broadcast_to(bits, (row_count, 128))], axis=1)]
    mine, shared = deal_columns(after(dense_weights, cot_blocks[0]), share, owners)
    plane_part = lax.all_to_all(mine, PLANE, split_axis=0, concat_axis=0, tiled=True)
    plane_part = plane_part.reshape(-1, 4 * share)
    cot_blocks.append(permute(cot_blocks[0], lay.onward))
    mine, cot_blocks[1] = together(mine, cot_blocks[1])
    for _ in range(rings - 3):
        cot_blocks.append(permute(cot_blocks[-1], lay.onward))

    inverse_one = lax.rsqrt(jnp.mean(stream * stream, axis=1, keepdims=True) + norm_eps)
    normed = (stream * inverse_one * gain_one).astype(bf16)
    doc_pair = jnp.stack([doc_ids, permute(doc_ids, lay.up)])
    group_len = doc_ids.shape[0]
    before = jnp.sum((doc_pair[:, None, :] < doc_pair[:, :, None]).astype(jnp.int32), axis=2)
    spot = jnp.arange(group_len, dtype=jnp.int32)
    near_blocks = jnp.stack([ep, ep ^ 2, ep ^ 1, ep ^ 3])

    def in_order(values):
        return values.reshape(2, 4, row_count)[:, near_blocks].reshape(2, group_len)

    places = in_order(spot[None, :] - before)
    docs = in_order(doc_pair)
    spots = in_order(jnp.stack([spot, spot]))
    cosine, sine = rope_tables(places.reshape(-1))
    sine = jnp.where(jnp.arange(HD) < HD // 2, -sine, sine)
    spots_all = jnp.stack([docs, spots], axis=1)
    spots_own = jnp.stack([docs.reshape(-1), spots.reshape(-1)], axis=1)
    routed = expert_weights.reshape(expert_weights.shape[0], -1)
    router = router_weight.T
    turn = (own_expert + jnp.arange(expert_count, dtype=jnp.int32)) % expert_count
    router = stack(jnp.take(router, turn, axis=0), router[expert_count:])
    slot = pair * 4 + ep
    bias_share = lax.dynamic_slice_in_dim(qkv_bias.astype(f32).reshape(3, 8, share), slot, 1, 1).reshape(1, 3 * share)
    plane_part, cot_blocks[-1], routed, normed = together(plane_part, cot_blocks[-1], routed, normed)

    qkv = [plane_part, permute(plane_part, lay.onward)]
    cot_blocks.append(permute(cot_blocks[-1], lay.onward))
    side, up = permute(normed, lay.side), permute(normed, lay.up)

    def between_cores(*pieces):
        return [permute(piece, lay.core) for piece in pieces]

    def over(pairs, pieces):
        return [permute(piece, pairs) for piece in pieces]

    cot_sides, cot_ups = over(lay.side, cot_blocks[:1]), over(lay.up, cot_blocks[:1])
    cot_cores = between_cores(*cot_blocks)
    first_ffn, second_ffn = (turn_weights(routed, local_experts, dp_count, w) for w in range(local_experts))
    qkv[-1], cot_blocks[-1], side, up, cot_sides, cot_ups, cosine, sine, first_ffn, second_ffn = lax.optimization_barrier(
        (qkv[-1], cot_blocks[-1], side, up, cot_sides, cot_ups, cosine, sine, first_ffn, second_ffn)
    )
    for s in range(2, rings):
        qkv.append(permute(qkv[-1], lay.onward))
        sides, ups = [], []
        if s == 2:
            cross = permute(up, lay.side)
            cores = between_cores(normed, side, up)
            sides, ups = over(lay.side, cot_blocks[1:2]), over(lay.up, cot_blocks[1:3])
            cross, cores = lax.optimization_barrier((cross, cores))
        elif s == 3:
            cores += between_cores(cross)
            normed_group = assemble((normed, side, *cores[:2], up, cross, *cores[2:]))
            sides, ups = over(lay.side, cot_blocks[2:]), over(lay.up, cot_blocks[3:])
        sides, ups, qkv[-1] = lax.optimization_barrier((sides, ups, qkv[-1]))
        cot_sides, cot_ups = cot_sides + sides, cot_ups + ups
    qkv[-1], normed_group = together(qkv[-1], normed_group)

    cot_crosses = [
        permute(cot_sides[s], lay.up) if s % 2 else permute(cot_ups[s], lay.side) for s in range(rings)
    ]
    heads_flops = 8 * heads * group_len * group_len * HD
    packed, mixed = group_call(
        functools.partial(attend_kernel, heads),
        group_len,
        ring_order,
        (normed_group, bias_share, cosine, sine, spots_own, spots_all),
        ("rows", "all", "rows", "rows", "rows", "pair"),
        qkv,
        [(group_len, 3 * share), (group_len, share)],
        [bf16, bf16],
        4 * group_len * model_width * 3 * share + heads_flops,
    )
    received = [lax.dynamic_index_in_dim(shared, ep ^ k, 0, keepdims=False) for k in range(4)]
    received[1:3] = [permute(v, pairs) for v, pairs in zip(received[1:3], (lay.core, lay.side))]
    branch_parts = group_call(
        project_kernel,
        group_len,
        ring_order,
        (mixed,),
        ("rows",),
        qkv,
        [(group_len // 2, model_width)] * 2,
        [bf16, bf16],
        4 * group_len * model_width * share,
    )
    *branch_parts, cot_crosses, first_ffn = lax.optimization_barrier((*branch_parts, cot_crosses, first_ffn))

    def to_units(ffn):
        return lax.all_to_all(ffn, ("ring", "pair"), split_axis=0, concat_axis=0, tiled=True)

    first_ffn = to_units(first_ffn)
    here = plus(branch_parts[0], permute(branch_parts[1], lay.core))
    cross, side = permute(here[3 * n :], lay.side), permute(here[n : 2 * n], lay.side)
    cots = []
    for s in range(rings):
        cores = [cot_cores[s]] + between_cores(cot_ups[s], cot_sides[s], cot_crosses[s])
        cots += [cot_blocks[s], cot_ups[s], *cores[:2], cot_sides[s], cot_crosses[s], *cores[2:]]
    cots = assemble(cots)
    cross, side, cots = together(cross, side, cots)
    received[3] = permute(after(received[3], cross), lay.side_core)
    up = permute(plus(here[2 * n : 3 * n], cross), lay.up)
    branch = here[:n].astype(f32) + side.astype(f32) + after(up, first_ffn, *received).astype(f32)
    residual = stream + branch
    inverse_two = lax.rsqrt(jnp.mean(residual * residual, axis=1, keepdims=True) + norm_eps)
    normed_two = (residual * inverse_two * gain_two).astype(bf16)

    blocks, ups, sides, crosses, inner = [normed_two], [], [], [], []

    for s in range(rings - 1):
        onward = permute(blocks[s], lay.onward)
        up, side = permute(blocks[s], lay.up), permute(blocks[s], lay.side)
        more, last = [], s == rings - 2
        if s >= 2:
            more.append(permute(ups[s - 2], lay.side))
            inner.append(between_cores(blocks[s - 2], ups[s - 2], sides[s - 2]))
        if last:
            more.append(permute(sides[s - 1], lay.up))
            inner.append(between_cores(blocks[s - 1], ups[s - 1], sides[s - 1]))
        if s == 1:
            shared_ffn = jnp.stack(received)[jnp.arange(4, dtype=jnp.int32) ^ ep].reshape(-1, 3 * unit_share)
            shared_ffn = turn_weights(shared_ffn, 1, dp_count)
            second_ffn = jnp.concatenate([second_ffn, shared_ffn], axis=1)
            second_ffn, onward = together(second_ffn, onward)
        onward, up, side, *more = together(onward, up, side, *more)
        blocks.append(onward)
        ups.append(up)
        sides.append(side)
        crosses += more
    up, side = permute(blocks[-1], lay.up), permute(blocks[-1], lay.side)
    inner.append(between_cores(blocks[-2], ups[-1], sides[-1]))
    up, side, crossing = together(up, side, ups[-1])
    ups.append(up)
    sides.append(side)
    second_ffn = to_units(after(second_ffn, up))
    inner.append(between_cores(blocks[-1], up, side))
    crossing, crossed_too = permute(crossing, lay.side), permute(up, lay.side)

    crosses += together(crossing, crossed_too)
    rows = []
    for s in range(rings):
        cores = inner[s] + between_cores(crosses[s])
        rows += [blocks[s], ups[s], *cores[:2], sides[s], crosses[s], *cores[2:]]
    rows = assemble(rows)

    first_rows = place_weights(first_ffn, router)
    late = rings // 2
    first_hidden, first_grad, first_weights_grad, first_router = first_units(
        (0,), where, rows, cots, *first_rows, units, expert_count, dp_count
    )
    first_weights_grad = to_units(first_weights_grad)
    second_rows = place_weights(after(second_ffn, first_hidden), router)

    chunk, half = 4 * n, 2 * n
    order = list(range(rings))[::-1]
    first_half, last_half = order[: rings - late], order[rings - late :]

    def cut_chunk(which, s, at):
        begin = (s % late if s < late else s - late) * chunk + at
        return which[begin : begin + half]

    def crossed(part, there, some):
        keep = {s: plus(cut_chunk(part, s, 0), cut_chunk(there, s, 0)) for s in some}
        send = {s: plus(cut_chunk(part, s, half), cut_chunk(there, s, half)) for s in some}
        return keep, send

    def all_there(*groups):
        flat, tree = jax.tree.flatten(groups)
        return jax.tree.unflatten(tree, lax.optimization_barrier(tuple(flat)))

    def ffn_half(first, chunks, kept):
        return second_units(
            (1, SHARED), first, chunks, where, rows, cots, (first_hidden, first_grad) + tuple(first_rows), second_rows, kept, units, expert_count
        )

    out_own_a, out_far_a, own_a, far_a, hidden, gate_up_grad = ffn_half(late, rings - late, ())

    keep, send = crossed(own_a, permute(far_a, lay.core), first_half)
    keep, send, hidden, gate_up_grad = all_there(keep, send, hidden, gate_up_grad)
    out_there_a = permute(after(out_far_a, hidden), lay.core)
    sided = {s: permute(send[s], lay.side) for s in first_half}
    out_own_b, out_far_b, own_b, far_b, hidden, gate_up_grad = ffn_half(0, late, (hidden, gate_up_grad))
    sided, own_b, far_b, hidden, gate_up_grad, first_weights_grad, out_there_a = all_there(
        sided, own_b, far_b, hidden, gate_up_grad, first_weights_grad, out_there_a
    )

    far_there = permute(far_b, lay.core)
    halves = {s: plus(keep[s], sided[s]) for s in first_half}
    upped = {order[0]: permute(halves[order[0]][n:], lay.up)}
    keep, send = crossed(own_b, far_there, last_half)
    keep, send, halves, hidden, upped = all_there(keep, send, halves, hidden, upped)
    own_sums = {order[0]: halves[order[0]][:n].astype(f32) + upped[order[0]].astype(f32)}
    total = own_sums[order[0]]
    queue = list(order[1:])

    def step_on(total):
        return permute(total.astype(bf16), lay.backward)

    def step_in(arrived):
        return own_sums[queue.pop(0)] + arrived.astype(f32)

    few = (len(last_half) + 1) // 2
    sided = {s: permute(send[s], lay.side) for s in last_half[:few]}
    upped = {s: permute(halves[s][n:], lay.up) for s in first_half[1:]}
    moving = step_on(total)
    ffn_grad, second_router = weight_grads(where, rows, cots, hidden, gate_up_grad, 2 * units, dp_count)
    out_there_b = permute(out_far_b, lay.core)
    sided, upped, moving, ffn_grad, out_there_b = all_there(sided, upped, moving, ffn_grad, out_there_b)
    own_sums.update({s: halves[s][:n].astype(f32) + upped[s].astype(f32) for s in first_half[1:]})
    total = step_in(moving)

    halves = {s: plus(keep[s], sided[s]) for s in last_half[:few]}
    sided = {s: permute(send[s], lay.side) for s in last_half[few:]}
    upped = {s: permute(halves[s][n:], lay.up) for s in last_half[:few]}
    moving = step_on(total)
    out_keep, out_send = crossed(out_own_a, out_there_a, first_half)
    sided, upped, moving, out_keep, out_send = all_there(sided, upped, moving, out_keep, out_send)
    own_sums.update({s: halves[s][:n].astype(f32) + upped[s].astype(f32) for s in last_half[:few]})
    total = step_in(moving)

    halves = {s: plus(keep[s], sided[s]) for s in last_half[few:]}
    upped = {s: permute(halves[s][n:], lay.up) for s in last_half[few:]}
    moving = step_on(total)
    more_keep, more_send = crossed(out_own_b, out_there_b, last_half)
    upped, moving, more_keep, more_send = all_there(upped, moving, more_keep, more_send)
    out_keep.update(more_keep)
    out_send.update(more_send)
    own_sums.update({s: halves[s][:n].astype(f32) + upped[s].astype(f32) for s in last_half[few:]})
    total = step_in(moving)
    while queue:
        total = step_in(step_on(total))
    normed_two_grad = total

    def router_rows(part, wide):
        start = wide - wide // 8 * 8
        return part[start : start + expert_count + 1]

    router_part = router_rows(first_router, units) + router_rows(second_router, 2 * units)
    turn_back = (jnp.arange(expert_count, dtype=jnp.int32) - own_expert) % expert_count
    router_part = stack(jnp.take(router_part[:expert_count], turn_back, axis=0), router_part[expert_count:])

    cotangent = out_grad.astype(f32)
    scaled_two = normed_two_grad * gain_two
    gain_two_grad = jnp.sum(normed_two_grad * residual * inverse_two, axis=0)
    residual_grad = (
        cotangent
        + inverse_two * scaled_two
        - residual * inverse_two**3 * jnp.mean(scaled_two * residual, axis=1, keepdims=True)
    )
    branch_grad = residual_grad.astype(bf16)

    side, up = permute(branch_grad, lay.side), permute(branch_grad, lay.up)
    core = permute(branch_grad, lay.core)
    side, up, core, ffn_grad = together(side, up, core, ffn_grad)
    ffn_grad = lax.all_to_all(ffn_grad, ("ring", "pair"), split_axis=0, concat_axis=0, tiled=True)
    cross = permute(up, lay.side)
    cores = [core, *between_cores(side, up)]
    cores.append(permute(cross, lay.core))
    branch_grad_group = assemble((branch_grad, side, *cores[:2], up, cross, *cores[2:]))
    keep, send = out_keep, out_send
    branch_grad_group = together(branch_grad_group)[0]

    quarter = [order[k :: 4] for k in range(4)] if rings > 4 else [[s] for s in order]
    sided = {s: permute(send[s], lay.side) for s in quarter[0]}
    packed_grad, near, far, bias_part = group_call(
        functools.partial(attend_back_kernel, heads),
        group_len,
        ring_order,
        (branch_grad_group, packed, cosine, sine, spots_own, spots_all),
        ("rows", "rows", "rows", "rows", "rows", "pair"),
        qkv,
        [(group_len, 3 * share), (group_len // 2, model_width), (group_len // 2, model_width), (8, 3 * share)],
        [bf16, bf16, bf16, f32],
        4 * group_len * model_width * 4 * share + 3 * heads_flops,
    )
    sided, packed_grad, near, far = all_there(sided, packed_grad, near, far)

    halves = {s: plus(keep[s], sided[s]) for s in quarter[0]}
    sided = {s: permute(send[s], lay.side) for s in quarter[1]}
    here = plus(near, permute(far, lay.core))
    attn_grads = jnp.concatenate([dot_over(normed_group, packed_grad), dot_over(branch_grad_group, mixed)], axis=1)
    attn_grads = attn_grads.astype(bf16).reshape(rings, -1, 4 * share)
    sided, attn_grads, here, halves = all_there(sided, attn_grads, here, halves)

    out_halves = {s: plus(keep[s], sided[s]) for s in quarter[1]}
    out_halves.update(halves)
    side, cross = permute(here[n : 2 * n], lay.side), permute(here[3 * n :], lay.side)
    def grads_at(s):
        return lax.dynamic_index_in_dim(attn_grads, behind[s], 0, keepdims=False).astype(f32)

    moving = permute(grads_at(order[0]).astype(bf16), lay.backward)
    side, cross, ffn_grad = together(side, cross, ffn_grad)

    up = permute(plus(here[2 * n : 3 * n], cross), lay.up)
    sided = {s: permute(send[s], lay.side) for s in quarter[2]}
    first_up = permute(out_halves[order[0]][n:], lay.up)
    sided, up, moving, first_up = all_there(sided, up, moving, first_up)
    output_sum = out_halves[order[0]][:n].astype(f32) + first_up.astype(f32)
    normed_grad = here[:n].astype(f32) + side.astype(f32) + up.astype(f32)
    scaled_one = normed_grad * gain_one
    gain_one_grad = jnp.sum(normed_grad * stream * inverse_one, axis=0)
    input_grad = (
        residual_grad
        + inverse_one * scaled_one
        - stream * inverse_one**3 * jnp.mean(scaled_one * stream, axis=1, keepdims=True)
    )
    bias_part = (bias_part[0] + bias_part[8]).reshape(3, 1, share)
    bias_part = lax.dynamic_update_slice(jnp.zeros((3, 8, share), f32), bias_part, (0, slot, 0))
    small = stack(router_part, gain_two_grad[None], gain_one_grad[None], bias_part.reshape(3, model_width))
    doubling = lay.doubling()

    total = grads_at(order[1]) + moving.astype(f32)
    out_halves.update({s: plus(keep[s], sided[s]) for s in quarter[2]})
    out_sums, out_queue = {}, list(order[1:])

    def outs_on(output_sum):
        return permute(output_sum.astype(bf16), lay.backward)

    def outs_over(some):
        return {s: permute(out_halves[s][n:], lay.up) for s in some}

    def outs_in(outs_up):
        out_sums.update({s: out_halves[s][:n].astype(f32) + outs_up[s].astype(f32) for s in outs_up})

    for i, s in enumerate(order[2:]):
        moving = permute(total.astype(bf16), lay.backward)
        if i == 0:
            outs_up = outs_over((quarter[0] + quarter[1])[1:])
            outgoing = outs_on(output_sum)
            sided = {s: permute(send[s], lay.side) for s in quarter[3]}
            for step in doubling[:2]:
                small = small + permute(small, step)
            shared_columns_grad, expert_grad = turn_grads(first_weights_grad, ffn_grad)
            moving, outs_up, sided, small, shared_columns_grad, expert_grad, outgoing = all_there(
                moving, outs_up, sided, small, shared_columns_grad, expert_grad, outgoing
            )
            outs_in(outs_up)
            output_sum = out_sums[out_queue.pop(0)] + outgoing.astype(f32)
            out_halves.update({s: plus(keep[s], sided[s]) for s in quarter[3]})
            outs_up = outs_over(quarter[2] + quarter[3])
            shared_columns_grad = lax.all_to_all(
                shared_columns_grad.reshape(owners, -1, 3 * unit_share),
                "ep",
                split_axis=0,
                concat_axis=0,
                tiled=True,
            )
        else:
            if i == 1:
                small = small + permute(small, doubling[2])
            if i == rings - 3:
                moving, small, shared_columns_grad = together(moving, small, shared_columns_grad)
            if i == 1:
                outs_in(outs_up)
            if i >= 1:
                output_sum = out_sums[out_queue.pop(0)] + outs_on(output_sum).astype(f32)
        total = grads_at(s) + moving.astype(f32)
    total = total.astype(bf16).reshape(8, -1, 4 * share)
    total = lax.all_to_all(total, PLANE, split_axis=0, concat_axis=0, tiled=True)
    for step in doubling[3:]:
        small = small + permute(small, step)
    while out_queue:
        output_sum = out_sums[out_queue.pop(0)] + outs_on(output_sum).astype(f32)
    output = (residual + output_sum).astype(bf16)
    dense_grad = collect_columns(total, shared_columns_grad, share)

    router_sum, gain_two_sum, gain_one_sum, bias_sum = jnp.split(small, [expert_count + 1, expert_count + 2, expert_count + 3])
    return (
        output,
        input_grad,
        dense_grad,
        expert_grad,
        gain_one_sum[0],
        gain_two_sum[0],
        bias_sum.reshape(-1),
        router_sum.T,
    )


def solution(mesh):
    devices = mesh.devices
    lay = Layout(devices.shape[0] // 2)
    inner = Mesh(devices.reshape(lay.rings, 2, devices.shape[1]), AXES)
    rows = P(AXES, None)
    experts = P(("ring", "pair"), "ep", None)
    in_specs = (rows, rows, experts, P(), P(), P(), P(), rows, P(("ring", "pair")), rows)
    out_specs = (rows, rows, rows, experts, P(), P(), P(), P())

    def run(*arguments):
        return body(lay, *arguments)

    return jax.shard_map(run, mesh=inner, in_specs=in_specs, out_specs=out_specs, check_vma=False)
```

time: 962 us -> 849 us (0.88)
  waiting for transfers between devices: 451 us -> 305 us
  Pallas kernels: 188 us -> 248 us
  local copies, waits for them, and re-layouts: 80.8 us -> 46.2 us
  starting transfers between devices: 109 us -> 136 us
  between operations: 27.3 us -> 14.6 us
    ppermute x93 -> x125, waiting for transfers between devices: 428 us -> 282 us  [permute(): return lax.ppermute(rows, AXES, pairs)]
    pallas_call x7 -> x13, Pallas kernels: 146 us -> 203 us  [the longest x2 81.6 us: second_units(): pl.pallas_call(functools.partial(second_kernel, groups, units, experts),...]
    unnamed x181 -> x200, local copies, waits for them, and re-layouts: 63.5 us -> 25 us
    ppermute x93 -> x125, starting transfers between devices: 80.5 us -> 104 us  [permute(): return lax.ppermute(rows, AXES, pairs)]
  transfers between devices with their start and end apart: 101 -> 132, of which waited for: 48 -> 57; matrix products, arithmetic and copies ran while one was open for 15% -> 12% of each run, Pallas kernels for 15% -> 24%
where the time goes in v3:
time: 849 us; the launch traced here: 840 us
  waiting for transfers between devices  305 us (36%)
  Pallas kernels  248 us (29%)
  starting transfers between devices  136 us (16%)
  other arithmetic  82.3 us (10%)
  local copies, waits for them, and re-layouts  46.2 us (5%)
  between operations  14.6 us (2%)
    ppermute x125, waiting for transfers between devices, permute(): return lax.ppermute(rows, AXES, pairs)  282 us
    ppermute x125, starting transfers between devices, permute(): return lax.ppermute(rows, AXES, pairs)  104 us
    pallas_call x2, Pallas kernels, second_units(): pl.pallas_call(functools.partial(second_kernel, groups, units, experts),...  81.6 us
    pallas_call x1, Pallas kernels, first_units(): pl.pallas_call(functools.partial(first_kernel, groups, units, experts), g...  47.1 us
    convert_element_type x16, other arithmetic, plus(): return (a.astype(f32) + b.astype(f32)).astype(bf16)  37.4 us
    pallas_call x3, Pallas kernels, group_call(): pl.pallas_call(kernel, grid_spec=pltpu.PrefetchScalarGridSpec(num_scalar_...  31.2 us
    pallas_call x4, Pallas kernels, assemble(): pl.pallas_call(assemble_kernel, in_specs=[pl.BlockSpec(memory_space=pltpu...  30.9 us
    pallas_call x1, Pallas kernels, weight_grads(): pl.pallas_call(functools.partial(grads_kernel, wide), grid_spec=pltpu.Pre...  30.2 us
  transfers between devices with their start and end apart: 132, of which 57 were waited for; matrix products, arithmetic and copies ran while one was open for 12% of the time, Pallas kernels for 24%

profile of v3, /device:TPU:0, one launch (start us, length us, event | category | flops | bytes accessed | tf_op | source)
XLA Modules:
  0.0 839.7 jit_solution(765182457570539949)
XLA Ops:
  24.0 4.7 copy.57
  28.8 5.5 all-to-all-done
  51.9 19.7 %collective-permute-done.4.refs_24_ = bf16[128,2176]{1,0:T(8,128)(2,1)} collective-permute-done((bf16[128,2176]{1,0:T(8,128)(2,1)}, bf16[128,2176]{1,0:T(8,128)(2,1)}, u32[]{:S(2)}, u32[]{:S(2)}) %collective-permute-start.4) | collective-permute-done | bytes 557088 | tf_op jit(solution)/shard_map/ppermute | solution.py:58
  77.4 9.2 %collective-permute-done.12.refs_12_ = bf16[128,2176]{1,0:T(8,128)(2,1)} collective-permute-done((bf16[128,2176]{1,0:T(8,128)(2,1)}, bf16[128,2176]{1,0:T(8,128)(2,1)}, u32[]{:S(2)}, u32[]{:S(2)}) %collective-permute-start.12) | collective-permute-done | bytes 557088 | tf_op jit(solution)/shard_map/ppermute | solution.py:58
  91.2 7.5 collective-permute-done.14.refs_17_
  112.7 6.6 collective-permute-done.2.refs_20_
  119.8 11.5 %collective-permute-done.10.refs_28_ = bf16[128,2176]{1,0:T(8,128)(2,1)} collective-permute-done((bf16[128,2176]{1,0:T(8,128)(2,1)}, bf16[128,2176]{1,0:T(8,128)(2,1)}, u32[]{:S(2)}, u32[]{:S(2)}) %collective-permute-start.10) | collective-permute-done | bytes 557088 | tf_op jit(solution)/shard_map/ppermute | solution.py:58
  133.8 4.4 shard_map.209.rows_ref
  138.2 11.0 %shard_map.210 = (bf16[1024,768]{1,0:T(8,128)(2,1)}, bf16[1024,256]{1,0:T(8,128)(2,1)S(1)}) custom-call(s32[4]{0:T(128)S(1)} %pad_add_fusion.4.where_ref, bf16[1024,2048]{1,0:T(8,128)(2,1)} %shard_map.209.rows_ref, f32[1,768]{1,0:T(1,128)S(1)} %bitcast.85, f32[1024,128]{1,0:T(8,128)S(1)} %copy-done.24, f32[1024,128]{1,0:T(8,128)S(1)} %copy-done.22, ...), custom_call_target="tpu_custom_call" | custom-call | flops 3758096384 | bytes 8922624 | tf_op jit(solution)/shard_map/pallas_call | solution.py:605
  149.3 5.2 shard_map.211
  158.4 5.7 all-to-all-start.1
  180.7 12.1 %shard_map.212.cots_ref = bf16[4096,2176]{1,0:T(8,128)(2,1)} custom-call(bf16[128,2176]{1,0:T(8,128)(2,1)} %pad_maximum_fusion.3.refs_0_, bf16[128,2176]{1,0:T(8,128)(2,1)} %collective-permute-done.8.refs_1_, bf16[128,2176]{1,0:T(8,128)(2,1)} %collective-permute-done.29.refs_2_, bf16[128,2176]{1,0:T(8,128)(2,1)} %collective-permute-done.30.refs_3_, ...), custom_call_target="tpu_custom_call" | custom-call | bytes 35651584 | tf_op jit(solution)/shard_map/pallas_call | solution.py:86
  192.8 9.0 %collective-permute-done.28 = bf16[128,2048]{1,0:T(8,128)(2,1)} collective-permute-done((bf16[128,2048]{1,0:T(8,128)(2,1)}, bf16[128,2048]{1,0:T(8,128)(2,1)}, u32[]{:S(2)}, u32[]{:S(2)}) %collective-permute-start.28) | collective-permute-done | bytes 524320 | tf_op jit(solution)/shard_map/ppermute | solution.py:58
  205.0 8.3 collective-permute-done.47
  213.4 5.5 collective-permute-done.45
  231.0 9.7 %collective-permute-done.49.refs_8_ = bf16[128,2048]{1,0:T(8,128)(2,1)} collective-permute-done((bf16[128,2048]{1,0:T(8,128)(2,1)S(1)}, bf16[128,2048]{1,0:T(8,128)(2,1)}, u32[]{:S(2)}, u32[]{:S(2)}) %collective-permute-start.49) | collective-permute-done | bytes 524320 | tf_op jit(solution)/shard_map/ppermute | solution.py:58
  264.0 9.9 %collective-permute-done.60.refs_5_ = bf16[128,2048]{1,0:T(8,128)(2,1)S(1)} collective-permute-done((bf16[128,2048]{1,0:T(8,128)(2,1)S(1)}, bf16[128,2048]{1,0:T(8,128)(2,1)S(1)}, u32[]{:S(2)}, u32[]{:S(2)}) %collective-permute-start.60) | collective-permute-done | bytes 524320 | tf_op jit(solution)/shard_map/ppermute | solution.py:58
  276.5 6.2 collective-permute-done.59.refs_20_
  286.3 9.8 %collective-permute-done.70.refs_25_ = bf16[128,2048]{1,0:T(8,128)(2,1)S(1)} collective-permute-done((bf16[128,2048]{1,0:T(8,128)(2,1)S(1)}, bf16[128,2048]{1,0:T(8,128)(2,1)S(1)}, u32[]{:S(2)}, u32[]{:S(2)}) %collective-permute-start.70) | collective-permute-done | bytes 524320 | tf_op jit(solution)/shard_map/ppermute | solution.py:58
  297.0 4.8 all-to-all-start.2
  310.3 10.9 %collective-permute-done.72.refs_21_ = bf16[128,2048]{1,0:T(8,128)(2,1)} collective-permute-done((bf16[128,2048]{1,0:T(8,128)(2,1)}, bf16[128,2048]{1,0:T(8,128)(2,1)}, u32[]{:S(2)}, u32[]{:S(2)}) %collective-permute-start.72) | collective-permute-done | bytes 524320 | tf_op jit(solution)/shard_map/ppermute | solution.py:58
  321.2 10.4 %collective-permute-done.73.refs_29_ = bf16[128,2048]{1,0:T(8,128)(2,1)} collective-permute-done((bf16[128,2048]{1,0:T(8,128)(2,1)}, bf16[128,2048]{1,0:T(8,128)(2,1)}, u32[]{:S(2)}, u32[]{:S(2)}) %collective-permute-start.73) | collective-permute-done | bytes 524320 | tf_op jit(solution)/shard_map/ppermute | solution.py:58
  334.1 4.3 shard_map.215
  341.9 10.8 %shard_map.214.rows_ref = bf16[4096,2048]{1,0:T(8,128)(2,1)} custom-call(bf16[128,2048]{1,0:T(8,128)(2,1)S(1)} %copy-done.6, bf16[128,2048]{1,0:T(8,128)(2,1)S(1)} %copy-done.11, bf16[128,2048]{1,0:T(8,128)(2,1)S(1)} %copy-done.15, bf16[128,2048]{1,0:T(8,128)(2,1)S(1)} %copy-done.17, bf16[128,2048]{1,0:T(8,128)(2,1)S(1)} %copy-done.13, ...), custom_call_target="tpu_custom_call" | custom-call | bytes 33554432 | tf_op jit(solution)/shard_map/pallas_call | solution.py:86
  352.7 47.1 %shard_map.216 = (bf16[4096,256]{1,0:T(8,128)(2,1)}, bf16[4096,512]{1,0:T(8,128)(2,1)}, bf16[8,528,256]{2,1,0:T(8,128)(2,1)}, f32[24,2048]{1,0:T(8,128)}) custom-call(s32[1]{0:T(128)} %bitcast.25.where_ref, bf16[4096,2048]{1,0:T(8,128)(2,1)} %shard_map.214.rows_ref, bf16[4096,2176]{1,0:T(8,128)(2,1)} %shard_map.212.cots_ref, bf16[512,2048]{1,0:T(8,128)(2,1)} %copy-done.29, ...), custom_call_target="tpu_custom_call" | custom-call | flops 25769803776 | bytes 33554432 | tf_op jit(solution)/shard_map/pallas_call | solution.py:278
  399.8 4.9 shard_map.217
  407.5 41.3 %shard_map.218 = (bf16[1024,2048]{1,0:T(8,128)(2,1)}, bf16[1024,2048]{1,0:T(8,128)(2,1)}, bf16[1024,2048]{1,0:T(8,128)(2,1)}, bf16[1024,2048]{1,0:T(8,128)(2,1)}...) custom-call(s32[1]{0:T(128)} %bitcast.25.where_ref, bf16[4096,2048]{1,0:T(8,128)(2,1)} %shard_map.214.rows_ref, ...), custom_call_target="tpu_custom_call" | custom-call | flops 16106127360 | bytes 33554432 | tf_op jit(solution)/shard_map/pallas_call | solution.py:335
  449.2 7.0 collective-permute-done.80
  460.6 6.2 all-to-all-start.3
  468.8 40.4 %shard_map.219 = (bf16[1024,2048]{1,0:T(8,128)(2,1)}, bf16[1024,2048]{1,0:T(8,128)(2,1)}, bf16[1024,2048]{1,0:T(8,128)(2,1)}, bf16[1024,2048]{1,0:T(8,128)(2,1)}...) custom-call(s32[1]{0:T(128)} %bitcast.25.where_ref, ...), custom_call_target="tpu_custom_call", output_to_operand_aliasing={{4}: (9, {}), {5}: (10, {})} | custom-call | flops 16106127360 | bytes 33554432 | tf_op jit(solution)/shard_map/pallas_call | solution.py:335
  509.2 7.4 all-to-all-done.3.first_ref
  522.8 6.4 collective-permute-done.84
  537.9 30.2 %shard_map.220 = (bf16[8,1056,256]{2,1,0:T(8,128)(2,1)}, f32[24,2048]{1,0:T(8,128)}) custom-call(s32[1]{0:T(128)} %bitcast.25.where_ref, bf16[4096,2048]{1,0:T(8,128)(2,1)} %shard_map.214.rows_ref, bf16[4096,2176]{1,0:T(8,128)(2,1)} %shard_map.212.cots_ref, bf16[4096,384]{1,0:T(8,128)(2,1)} %get-tuple-element.276.hidden_ref, ...), custom_call_target="tpu_custom_call" | custom-call | flops 19327352832 | bytes 33554432 | tf_op jit(solution)/shard_map/pallas_call | solution.py:304
  602.0 7.8 collective-permute-done.97.refs_1_
  610.1 4.8 all-to-all-start.4
  616.9 7.3 collective-permute-done.101.refs_5_
  637.4 15.0 %shard_map.222 = (bf16[1024,768]{1,0:T(8,128)(2,1)}, bf16[512,2048]{1,0:T(8,128)(2,1)}, bf16[512,2048]{1,0:T(8,128)(2,1)}, f32[16,768]{1,0:T(8,128)S(1)}) custom-call(s32[4]{0:T(128)S(1)} %pad_add_fusion.4.where_ref, bf16[1024,2048]{1,0:T(8,128)(2,1)} %shard_map.221.grad_ref, bf16[1024,768]{1,0:T(8,128)(2,1)} %get-tuple-element.299.packed_ref, ...), custom_call_target="tpu_custom_call" | custom-call | flops 5905580032 | bytes 10493952 | tf_op jit(solution)/shard_map/pallas_call | solution.py:605
  668.8 10.1 %collective-permute-done.95 = bf16[256,2048]{1,0:T(8,128)(2,1)S(1)} collective-permute-done((bf16[256,2048]{1,0:T(8,128)(2,1)}, bf16[256,2048]{1,0:T(8,128)(2,1)S(1)}, u32[]{:S(2)}, u32[]{:S(2)}) %collective-permute-start.95) | collective-permute-done | bytes 1048608 | tf_op jit(solution)/shard_map/ppermute | solution.py:58
  689.3 5.9 collective-permute-done.106
  697.2 9.3 %collective-permute-done.107 = bf16[128,2048]{1,0:T(8,128)(2,1)} collective-permute-done((bf16[128,2048]{1,0:T(8,128)(2,1)}, bf16[128,2048]{1,0:T(8,128)(2,1)}, u32[]{:S(2)}, u32[]{:S(2)}) %collective-permute-start.107) | collective-permute-done | bytes 524320 | tf_op jit(solution)/shard_map/ppermute | solution.py:58
  706.5 5.8 all-to-all-done.4.second_ref
  715.9 8.7 %shard_map.223 = (bf16[256,4224]{1,0:T(8,128)(2,1)}, f32[256,2,4224]{2,1,0:T(2,128)}) custom-call(bf16[8,528,256]{2,1,0:T(8,128)(2,1)} %copy-done.38, bf16[8,1056,256]{2,1,0:T(8,128)(2,1)} %all-to-all-done.4.second_ref), custom_call_target="tpu_custom_call" | custom-call | bytes 17301504 | tf_op jit(solution)/shard_map/pallas_call | solution.py:400
  724.6 4.3 collective-permute-done.105
  744.5 8.1 collective-permute-done.115
  754.6 13.7 %collective-permute-done.116 = bf16[128,2048]{1,0:T(8,128)(2,1)} collective-permute-done((bf16[128,2048]{1,0:T(8,128)(2,1)S(1)}, bf16[128,2048]{1,0:T(8,128)(2,1)}, u32[]{:S(2)}, u32[]{:S(2)}) %collective-permute-start.116) | collective-permute-done | bytes 524320 | tf_op jit(solution)/shard_map/ppermute | solution.py:58
  784.8 21.4 %collective-permute-done.119 = bf16[128,2048]{1,0:T(8,128)(2,1)S(1)} collective-permute-done((bf16[128,2048]{1,0:T(8,128)(2,1)S(1)}, bf16[128,2048]{1,0:T(8,128)(2,1)S(1)}, u32[]{:S(2)}, u32[]{:S(2)}) %collective-permute-start.119) | collective-permute-done | bytes 524320 | tf_op jit(solution)/shard_map/ppermute | solution.py:58
  824.6 5.5 collective-permute-done.124
  832.0 4.1 all-to-all-done.6.attn_ref
  (559 shorter events, 299.6 us)
Async XLA Ops:
  7.5 34.3 %collective-permute-start.7 = (bf16[128,2176]{1,0:T(8,128)(2,1)}, bf16[128,2176]{1,0:T(8,128)(2,1)S(1)}, u32[]{:S(2)}, u32[]{:S(2)}) collective-permute-start(bf16[128,2176]{1,0:T(8,128)(2,1)} %pad_maximum_fusion.3.refs_0_), channel_id=1, source_target_pairs={{0,2},{1,3},{2,0},{3,1},{4,6},{5,7},{6,4},{7,5},{8,10},{9,11},{10,... | collective-permute-start | bytes 1671176 | tf_op jit(solution)/shard_map/ppermute | solution.py:58
  9.0 41.7 %collective-permute-start.8 = (bf16[128,2176]{1,0:T(8,128)(2,1)}, bf16[128,2176]{1,0:T(8,128)(2,1)}, u32[]{:S(2)}, u32[]{:S(2)}) collective-permute-start(bf16[128,2176]{1,0:T(8,128)(2,1)} %pad_maximum_fusion.3.refs_0_), channel_id=1, source_target_pairs={{0,4},{1,5},{2,6},{3,7},{4,0},{5,1},{6,2},{7,3},{8,12},{9,13},{10,... | collective-permute-start | bytes 1671176 | tf_op jit(solution)/shard_map/ppermute | solution.py:58
  35.1 36.6 %collective-permute-start.3 = (bf16[512,1024]{1,0:T(8,128)(2,1)S(1)}, bf16[512,1024]{1,0:T(8,128)(2,1)}, u32[]{:S(2)}, u32[]{:S(2)}) collective-permute-start(bf16[512,1024]{1,0:T(8,128)(2,1)S(1)} %bitcast.81), channel_id=1, source_target_pairs={{0,16},{1,17},{2,18},{3,19},{4,20},{5,21},{6,22},{7,23},{8,0},{9,1... | collective-permute-start | bytes 3145736 | tf_op jit(solution)/shard_map/ppermute | solution.py:58
  41.8 29.9 %collective-permute-start.4 = (bf16[128,2176]{1,0:T(8,128)(2,1)}, bf16[128,2176]{1,0:T(8,128)(2,1)}, u32[]{:S(2)}, u32[]{:S(2)}) collective-permute-start(bf16[128,2176]{1,0:T(8,128)(2,1)} %collective-permute-done.1.refs_16_), channel_id=1, source_target_pairs={{0,16},{1,17},{2,18},{3,19},{4,20},{5,21},{6,22},{7,23},{8,0},{9,1... | collective-permute-start | bytes 1671176 | tf_op jit(solution)/shard_map/ppermute | solution.py:58
  71.7 27.0 %collective-permute-start.15 = (bf16[512,1024]{1,0:T(8,128)(2,1)}, bf16[512,1024]{1,0:T(8,128)(2,1)}, u32[]{:S(2)}, u32[]{:S(2)}) collective-permute-start(bf16[512,1024]{1,0:T(8,128)(2,1)} %collective-permute-done.3.refs_1_), channel_id=1, source_target_pairs={{0,16},{1,17},{2,18},{3,19},{4,20},{5,21},{6,22},{7,23},{8,0},{9,1... | collective-permute-start | bytes 3145736 | tf_op jit(solution)/shard_map/ppermute | solution.py:58
  77.4 26.2 %collective-permute-start.18 = (bf16[128,2048]{1,0:T(8,128)(2,1)}, bf16[128,2048]{1,0:T(8,128)(2,1)}, u32[]{:S(2)}, u32[]{:S(2)}) collective-permute-start(bf16[128,2048]{1,0:T(8,128)(2,1)} %fusion.5.refs_0_), channel_id=1, source_target_pairs={{0,1},{1,0},{2,3},{3,2},{4,5},{5,4},{6,7},{7,6},{8,9},{9,8},{10,11... | collective-permute-start | bytes 1572872 | tf_op jit(solution)/shard_map/ppermute | solution.py:58
  98.7 34.6 %collective-permute-start.16 = (bf16[512,1024]{1,0:T(8,128)(2,1)}, bf16[512,1024]{1,0:T(8,128)(2,1)}, u32[]{:S(2)}, u32[]{:S(2)}) collective-permute-start(bf16[512,1024]{1,0:T(8,128)(2,1)} %collective-permute-done.15.refs_2_), channel_id=1, source_target_pairs={{0,16},{1,17},{2,18},{3,19},{4,20},{5,21},{6,22},{7,23},{8,0},{9,1... | collective-permute-start | bytes 3145736 | tf_op jit(solution)/shard_map/ppermute | solution.py:58
  104.1 27.2 %collective-permute-start.10 = (bf16[128,2176]{1,0:T(8,128)(2,1)}, bf16[128,2176]{1,0:T(8,128)(2,1)}, u32[]{:S(2)}, u32[]{:S(2)}) collective-permute-start(bf16[128,2176]{1,0:T(8,128)(2,1)} %collective-permute-done.4.refs_24_), channel_id=1, source_target_pairs={{0,2},{1,3},{2,0},{3,1},{4,6},{5,7},{6,4},{7,5},{8,10},{9,11},{10,... | collective-permute-start | bytes 1671176 | tf_op jit(solution)/shard_map/ppermute | solution.py:58
  105.6 27.1 %collective-permute-start.11 = (bf16[128,2176]{1,0:T(8,128)(2,1)}, bf16[128,2176]{1,0:T(8,128)(2,1)}, u32[]{:S(2)}, u32[]{:S(2)}) collective-permute-start(bf16[128,2176]{1,0:T(8,128)(2,1)} %collective-permute-done.4.refs_24_), channel_id=1, source_target_pairs={{0,4},{1,5},{2,6},{3,7},{4,0},{5,1},{6,2},{7,3},{8,12},{9,13},{10,... | collective-permute-start | bytes 1671176 | tf_op jit(solution)/shard_map/ppermute | solution.py:58
  108.4 25.4 %collective-permute-start.21 = (bf16[128,2048]{1,0:T(8,128)(2,1)}, bf16[128,2048]{1,0:T(8,128)(2,1)}, u32[]{:S(2)}, u32[]{:S(2)}) collective-permute-start(bf16[128,2048]{1,0:T(8,128)(2,1)} %collective-permute-done.17.refs_5_), channel_id=1, source_target_pairs={{0,1},{1,0},{2,3},{3,2},{4,5},{5,4},{6,7},{7,6},{8,9},{9,8},{10,11... | collective-permute-start | bytes 1572872 | tf_op jit(solution)/shard_map/ppermute | solution.py:58
  119.3 35.1 %collective-permute-start.22 = (bf16[128,2176]{1,0:T(8,128)(2,1)}, bf16[128,2176]{1,0:T(8,128)(2,1)}, u32[]{:S(2)}, u32[]{:S(2)}) collective-permute-start(bf16[128,2176]{1,0:T(8,128)(2,1)} %collective-permute-done.8.refs_1_), channel_id=1, source_target_pairs={{0,2},{1,3},{2,0},{3,1},{4,6},{5,7},{6,4},{7,5},{8,10},{9,11},{10,... | collective-permute-start | bytes 1671176 | tf_op jit(solution)/shard_map/ppermute | solution.py:58
  131.3 23.2 %collective-permute-start.23 = (bf16[128,2176]{1,0:T(8,128)(2,1)}, bf16[128,2176]{1,0:T(8,128)(2,1)}, u32[]{:S(2)}, u32[]{:S(2)}) collective-permute-start(bf16[128,2176]{1,0:T(8,128)(2,1)} %collective-permute-done.12.refs_12_), channel_id=1, source_target_pairs={{0,4},{1,5},{2,6},{3,7},{4,0},{5,1},{6,2},{7,3},{8,12},{9,13},{10,... | collective-permute-start | bytes 1671176 | tf_op jit(solution)/shard_map/ppermute | solution.py:58
  133.3 24.1 %collective-permute-start.25 = (bf16[128,2176]{1,0:T(8,128)(2,1)}, bf16[128,2176]{1,0:T(8,128)(2,1)}, u32[]{:S(2)}, u32[]{:S(2)}) collective-permute-start(bf16[128,2176]{1,0:T(8,128)(2,1)} %collective-permute-done.10.refs_28_), channel_id=1, source_target_pairs={{0,4},{1,5},{2,6},{3,7},{4,0},{5,1},{6,2},{7,3},{8,12},{9,13},{10,... | collective-permute-start | bytes 1671176 | tf_op jit(solution)/shard_map/ppermute | solution.py:58
  158.4 65.2 %all-to-all-start.1 = ((bf16[8,528,256]{2,1,0:T(8,128)(2,1)}), bf16[8,528,256]{2,1,0:T(8,128)(2,1)}, u32[]{:S(2)}, u32[]{:S(2)}) async-start(bf16[8,528,256]{2,1,0:T(8,128)(2,1)} %shard_map.207), calls=%async_computation.1 | async-start | bytes 4325376 | tf_op jit(solution)/shard_map/all_to_all | solution.py:743
  176.0 25.8 %collective-permute-start.28 = (bf16[128,2048]{1,0:T(8,128)(2,1)}, bf16[128,2048]{1,0:T(8,128)(2,1)}, u32[]{:S(2)}, u32[]{:S(2)}) collective-permute-start(bf16[128,2048]{1,0:T(8,128)(2,1)} %get-tuple-element.370), channel_id=1, source_target_pairs={{0,2},{1,3},{2,0},{3,1},{4,6},{5,7},{6,4},{7,5},{8,10},{9,11},{10,... | collective-permute-start | bytes 1572872 | tf_op jit(solution)/shard_map/ppermute | solution.py:58
  178.8 26.2 %collective-permute-start.46 = (bf16[64,4224]{1,0:T(8,128)(2,1)}, bf16[64,4224]{1,0:T(8,128)(2,1)}, u32[]{:S(2)}, u32[]{:S(2)}) collective-permute-start(bf16[64,4224]{1,0:T(8,128)(2,1)} %get-tuple-element.367), channel_id=1, source_target_pairs={{0,1},{1,0},{2,3},{3,2},{4,5},{5,4},{6,7},{7,6},{8,9},{9,8},{10,11... | collective-permute-start | bytes 1622024 | tf_op jit(solution)/shard_map/ppermute | solution.py:58
  178.9 34.4 %collective-permute-start.47 = (bf16[64,4224]{1,0:T(8,128)(2,1)}, bf16[64,4224]{1,0:T(8,128)(2,1)}, u32[]{:S(2)}, u32[]{:S(2)}) collective-permute-start(bf16[64,4224]{1,0:T(8,128)(2,1)} %get-tuple-element.366), channel_id=1, source_target_pairs={{0,2},{1,3},{2,0},{3,1},{4,6},{5,7},{6,4},{7,5},{8,10},{9,11},{10,... | collective-permute-start | bytes 1622024 | tf_op jit(solution)/shard_map/ppermute | solution.py:58
  297.0 102.8 %all-to-all-start.2 = ((bf16[8,1056,256]{2,1,0:T(8,128)(2,1)}), bf16[8,1056,256]{2,1,0:T(8,128)(2,1)}, u32[]{:S(2)}, u32[]{:S(2)}) async-start(bf16[8,1056,256]{2,1,0:T(8,128)(2,1)} %pad_maximum_fusion), calls=%async_computation.2 | async-start | bytes 8650752 | tf_op jit(solution)/shard_map/all_to_all | solution.py:743
  307.6 24.0 %collective-permute-start.73 = (bf16[128,2048]{1,0:T(8,128)(2,1)}, bf16[128,2048]{1,0:T(8,128)(2,1)}, u32[]{:S(2)}, u32[]{:S(2)}) collective-permute-start(bf16[128,2048]{1,0:T(8,128)(2,1)} %copy-done.73), channel_id=1, source_target_pairs={{0,2},{1,3},{2,0},{3,1},{4,6},{5,7},{6,4},{7,5},{8,10},{9,11},{10,... | collective-permute-start | bytes 1572872 | tf_op jit(solution)/shard_map/ppermute | solution.py:58
  309.7 22.0 %collective-permute-start.68 = (bf16[128,2048]{1,0:T(8,128)(2,1)}, bf16[128,2048]{1,0:T(8,128)(2,1)S(1)}, u32[]{:S(2)}, u32[]{:S(2)}) collective-permute-start(bf16[128,2048]{1,0:T(8,128)(2,1)} %collective-permute-done.54.refs_16_), channel_id=1, source_target_pairs={{0,1},{1,0},{2,3},{3,2},{4,5},{5,4},{6,7},{7,6},{8,9},{9,8},{10,11... | collective-permute-start | bytes 1572872 | tf_op jit(solution)/shard_map/ppermute | solution.py:58
  309.7 23.1 %collective-permute-start.69 = (bf16[128,2048]{1,0:T(8,128)(2,1)}, bf16[128,2048]{1,0:T(8,128)(2,1)S(1)}, u32[]{:S(2)}, u32[]{:S(2)}) collective-permute-start(bf16[128,2048]{1,0:T(8,128)(2,1)} %copy-done.70), channel_id=1, source_target_pairs={{0,1},{1,0},{2,3},{3,2},{4,5},{5,4},{6,7},{7,6},{8,9},{9,8},{10,11... | collective-permute-start | bytes 1572872 | tf_op jit(solution)/shard_map/ppermute | solution.py:58
  310.2 22.1 %collective-permute-start.63 = (bf16[128,2048]{1,0:T(8,128)(2,1)S(1)}, bf16[128,2048]{1,0:T(8,128)(2,1)S(1)}, u32[]{:S(2)}, u32[]{:S(2)}) collective-permute-start(bf16[128,2048]{1,0:T(8,128)(2,1)S(1)} %collective-permute-done.60.refs_5_), channel_id=1, source_target_pairs={{0,1},{1,0},{2,3},{3,2},{4,5},{5,4},{6,7},{7,6},{8,9},{9,8},{10,11... | collective-permute-start | bytes 1572872 | tf_op jit(solution)/shard_map/ppermute | solution.py:58
  460.2 56.5 %collective-permute-start.83 = (bf16[1024,2048]{1,0:T(8,128)(2,1)}, bf16[1024,2048]{1,0:T(8,128)(2,1)}, u32[]{:S(2)}, u32[]{:S(2)}) collective-permute-start(bf16[1024,2048]{1,0:T(8,128)(2,1)} %get-tuple-element.261), channel_id=1, source_target_pairs={{0,1},{1,0},{2,3},{3,2},{4,5},{5,4},{6,7},{7,6},{8,9},{9,8},{10,11... | collective-permute-start | bytes 12582920 | tf_op jit(solution)/shard_map/ppermute | solution.py:58
  460.6 56.1 %all-to-all-start.3 = ((bf16[8,528,256]{2,1,0:T(8,128)(2,1)}), bf16[8,528,256]{2,1,0:T(8,128)(2,1)S(1)}, u32[]{:S(2)}, u32[]{:S(2)}) async-start(bf16[8,528,256]{2,1,0:T(8,128)(2,1)} %get-tuple-element.259), calls=%async_computation.3 | async-start | bytes 4325376 | tf_op jit(solution)/shard_map/all_to_all | solution.py:743
  466.7 49.9 %collective-permute-start.81 = (bf16[256,2048]{1,0:T(8,128)(2,1)}, bf16[256,2048]{1,0:T(8,128)(2,1)}, u32[]{:S(2)}, u32[]{:S(2)}) collective-permute-start(bf16[256,2048]{1,0:T(8,128)(2,1)} %get-tuple-element.251), channel_id=1, source_target_pairs={{0,2},{1,3},{2,0},{3,1},{4,6},{5,7},{6,4},{7,5},{8,10},{9,11},{10,... | collective-permute-start | bytes 3145736 | tf_op jit(solution)/shard_map/ppermute | solution.py:58
  467.3 49.3 %collective-permute-start.82 = (bf16[256,2048]{1,0:T(8,128)(2,1)}, bf16[256,2048]{1,0:T(8,128)(2,1)}, u32[]{:S(2)}, u32[]{:S(2)}) collective-permute-start(bf16[256,2048]{1,0:T(8,128)(2,1)} %get-tuple-element.252), channel_id=1, source_target_pairs={{0,2},{1,3},{2,0},{3,1},{4,6},{5,7},{6,4},{7,5},{8,10},{9,11},{10,... | collective-permute-start | bytes 3145736 | tf_op jit(solution)/shard_map/ppermute | solution.py:58
  516.7 51.4 %collective-permute-start.90 = (bf16[1024,2048]{1,0:T(8,128)(2,1)}, bf16[1024,2048]{1,0:T(8,128)(2,1)}, u32[]{:S(2)}, u32[]{:S(2)}) collective-permute-start(bf16[1024,2048]{1,0:T(8,128)(2,1)} %get-tuple-element.279), channel_id=1, source_target_pairs={{0,1},{1,0},{2,3},{3,2},{4,5},{5,4},{6,7},{7,6},{8,9},{9,8},{10,11... | collective-permute-start | bytes 12582920 | tf_op jit(solution)/shard_map/ppermute | solution.py:58
  533.5 34.6 %collective-permute-start.89 = (bf16[128,2048]{1,0:T(8,128)(2,1)S(1)}, bf16[128,2048]{1,0:T(8,128)(2,1)}, u32[]{:S(2)}, u32[]{:S(2)}) collective-permute-start(bf16[128,2048]{1,0:T(8,128)(2,1)S(1)} %add_convert_fusion.33), channel_id=1, source_target_pairs={{0,8},{1,9},{2,10},{3,11},{4,12},{5,13},{6,14},{7,15},{8,24},{9,25... | collective-permute-start | bytes 1572872 | tf_op jit(solution)/shard_map/ppermute | solution.py:58
  533.5 34.6 %collective-permute-start.87 = (bf16[256,2048]{1,0:T(8,128)(2,1)}, bf16[256,2048]{1,0:T(8,128)(2,1)}, u32[]{:S(2)}, u32[]{:S(2)}) collective-permute-start(bf16[256,2048]{1,0:T(8,128)(2,1)} %get-tuple-element.272), channel_id=1, source_target_pairs={{0,2},{1,3},{2,0},{3,1},{4,6},{5,7},{6,4},{7,5},{8,10},{9,11},{10,... | collective-permute-start | bytes 3145736 | tf_op jit(solution)/shard_map/ppermute | solution.py:58
  535.0 33.1 %collective-permute-start.88 = (bf16[128,2048]{1,0:T(8,128)(2,1)}, bf16[128,2048]{1,0:T(8,128)(2,1)}, u32[]{:S(2)}, u32[]{:S(2)}) collective-permute-start(bf16[128,2048]{1,0:T(8,128)(2,1)} %slice.211), channel_id=1, source_target_pairs={{0,4},{1,5},{2,6},{3,7},{4,0},{5,1},{6,2},{7,3},{8,12},{9,13},{10,... | collective-permute-start | bytes 1572872 | tf_op jit(solution)/shard_map/ppermute | solution.py:58
  536.5 43.8 %collective-permute-start.86 = (bf16[256,2048]{1,0:T(8,128)(2,1)S(1)}, bf16[256,2048]{1,0:T(8,128)(2,1)}, u32[]{:S(2)}, u32[]{:S(2)}) collective-permute-start(bf16[256,2048]{1,0:T(8,128)(2,1)S(1)} %get-tuple-element.270), channel_id=1, source_target_pairs={{0,2},{1,3},{2,0},{3,1},{4,6},{5,7},{6,4},{7,5},{8,10},{9,11},{10,... | collective-permute-start | bytes 3145736 | tf_op jit(solution)/shard_map/ppermute | solution.py:58
  610.1 102.2 %all-to-all-start.4 = ((bf16[8,1056,256]{2,1,0:T(8,128)(2,1)}), bf16[8,1056,256]{2,1,0:T(8,128)(2,1)}, u32[]{:S(2)}, u32[]{:S(2)}) async-start(bf16[8,1056,256]{2,1,0:T(8,128)(2,1)} %get-tuple-element.311), calls=%async_computation.4 | async-start | bytes 8650752 | tf_op jit(solution)/shard_map/all_to_all | solution.py:908
  624.2 28.1 %collective-permute-start.96 = (bf16[256,2048]{1,0:T(8,128)(2,1)}, bf16[256,2048]{1,0:T(8,128)(2,1)}, u32[]{:S(2)}, u32[]{:S(2)}) collective-permute-start(bf16[256,2048]{1,0:T(8,128)(2,1)} %get-tuple-element.292), channel_id=1, source_target_pairs={{0,2},{1,3},{2,0},{3,1},{4,6},{5,7},{6,4},{7,5},{8,10},{9,11},{10,... | collective-permute-start | bytes 3145736 | tf_op jit(solution)/shard_map/ppermute | solution.py:58
  653.3 25.6 %collective-permute-start.95 = (bf16[256,2048]{1,0:T(8,128)(2,1)}, bf16[256,2048]{1,0:T(8,128)(2,1)S(1)}, u32[]{:S(2)}, u32[]{:S(2)}) collective-permute-start(bf16[256,2048]{1,0:T(8,128)(2,1)} %get-tuple-element.291), channel_id=1, source_target_pairs={{0,2},{1,3},{2,0},{3,1},{4,6},{5,7},{6,4},{7,5},{8,10},{9,11},{10,... | collective-permute-start | bytes 3145736 | tf_op jit(solution)/shard_map/ppermute | solution.py:58
  680.6 25.9 %collective-permute-start.107 = (bf16[128,2048]{1,0:T(8,128)(2,1)}, bf16[128,2048]{1,0:T(8,128)(2,1)}, u32[]{:S(2)}, u32[]{:S(2)}) collective-permute-start(bf16[128,2048]{1,0:T(8,128)(2,1)} %get-tuple-element.368), channel_id=1, source_target_pairs={{0,2},{1,3},{2,0},{3,1},{4,6},{5,7},{6,4},{7,5},{8,10},{9,11},{10,... | collective-permute-start | bytes 1572872 | tf_op jit(solution)/shard_map/ppermute | solution.py:58
  682.2 46.8 %collective-permute-start.105 = (bf16[256,2048]{1,0:T(8,128)(2,1)}, bf16[256,2048]{1,0:T(8,128)(2,1)}, u32[]{:S(2)}, u32[]{:S(2)}) collective-permute-start(bf16[256,2048]{1,0:T(8,128)(2,1)} %get-tuple-element.309), channel_id=1, source_target_pairs={{0,2},{1,3},{2,0},{3,1},{4,6},{5,7},{6,4},{7,5},{8,10},{9,11},{10,... | collective-permute-start | bytes 3145736 | tf_op jit(solution)/shard_map/ppermute | solution.py:58
  682.8 71.8 %collective-permute-start.113 = (bf16[256,2048]{1,0:T(8,128)(2,1)}, bf16[256,2048]{1,0:T(8,128)(2,1)}, u32[]{:S(2)}, u32[]{:S(2)}) collective-permute-start(bf16[256,2048]{1,0:T(8,128)(2,1)} %get-tuple-element.317), channel_id=1, source_target_pairs={{0,2},{1,3},{2,0},{3,1},{4,6},{5,7},{6,4},{7,5},{8,10},{9,11},{10,... | collective-permute-start | bytes 3145736 | tf_op jit(solution)/shard_map/ppermute | solution.py:58
  685.3 45.6 %collective-permute-start.109 = (bf16[512,1024]{1,0:T(8,128)(2,1)}, bf16[512,1024]{1,0:T(8,128)(2,1)}, u32[]{:S(2)}, u32[]{:S(2)}) collective-permute-start(bf16[512,1024]{1,0:T(8,128)(2,1)} %dynamic-slice_bitcast_fusion), channel_id=1, source_target_pairs={{0,8},{1,9},{2,10},{3,11},{4,12},{5,13},{6,14},{7,15},{8,24},{9,25... | collective-permute-start | bytes 3145736 | tf_op jit(solution)/shard_map/ppermute | solution.py:58
  695.2 35.7 %collective-permute-start.110 = (bf16[128,2048]{1,0:T(8,128)(2,1)}, bf16[128,2048]{1,0:T(8,128)(2,1)}, u32[]{:S(2)}, u32[]{:S(2)}) collective-permute-start(bf16[128,2048]{1,0:T(8,128)(2,1)} %slice.237), channel_id=1, source_target_pairs={{0,4},{1,5},{2,6},{3,7},{4,0},{5,1},{6,2},{7,3},{8,12},{9,13},{10,... | collective-permute-start | bytes 1572872 | tf_op jit(solution)/shard_map/ppermute | solution.py:58
  728.9 25.6 %collective-permute-start.112 = (bf16[128,2048]{1,0:T(8,128)(2,1)}, bf16[128,2048]{1,0:T(8,128)(2,1)}, u32[]{:S(2)}, u32[]{:S(2)}) collective-permute-start(bf16[128,2048]{1,0:T(8,128)(2,1)} %slice.282), channel_id=1, source_target_pairs={{0,4},{1,5},{2,6},{3,7},{4,0},{5,1},{6,2},{7,3},{8,12},{9,13},{10,... | collective-permute-start | bytes 1572872 | tf_op jit(solution)/shard_map/ppermute | solution.py:58
  734.1 34.2 %collective-permute-start.111 = (bf16[512,1024]{1,0:T(8,128)(2,1)}, bf16[512,1024]{1,0:T(8,128)(2,1)}, u32[]{:S(2)}, u32[]{:S(2)}) collective-permute-start(bf16[512,1024]{1,0:T(8,128)(2,1)} %fusion.2), channel_id=1, source_target_pairs={{0,8},{1,9},{2,10},{3,11},{4,12},{5,13},{6,14},{7,15},{8,24},{9,25... | collective-permute-start | bytes 3145736 | tf_op jit(solution)/shard_map/ppermute | solution.py:58
  736.7 31.6 %collective-permute-start.116 = (bf16[128,2048]{1,0:T(8,128)(2,1)S(1)}, bf16[128,2048]{1,0:T(8,128)(2,1)}, u32[]{:S(2)}, u32[]{:S(2)}) collective-permute-start(bf16[128,2048]{1,0:T(8,128)(2,1)S(1)} %add_convert_fusion.29), channel_id=1, source_target_pairs={{0,8},{1,9},{2,10},{3,11},{4,12},{5,13},{6,14},{7,15},{8,24},{9,25... | collective-permute-start | bytes 1572872 | tf_op jit(solution)/shard_map/ppermute | solution.py:58
  752.7 32.2 %collective-permute-start.118 = (bf16[128,2048]{1,0:T(8,128)(2,1)}, bf16[128,2048]{1,0:T(8,128)(2,1)}, u32[]{:S(2)}, u32[]{:S(2)}) collective-permute-start(bf16[128,2048]{1,0:T(8,128)(2,1)} %slice.288), channel_id=1, source_target_pairs={{0,4},{1,5},{2,6},{3,7},{4,0},{5,1},{6,2},{7,3},{8,12},{9,13},{10,... | collective-permute-start | bytes 1572872 | tf_op jit(solution)/shard_map/ppermute | solution.py:58
  768.3 42.7 %collective-permute-start.122 = (f32[14,2048]{1,0:T(8,128)S(1)}, f32[14,2048]{1,0:T(8,128)}, u32[]{:S(2)}, u32[]{:S(2)}) collective-permute-start(f32[14,2048]{1,0:T(8,128)S(1)} %add.460), channel_id=1, source_target_pairs={{0,4},{1,5},{2,6},{3,7},{4,0},{5,1},{6,2},{7,3},{8,12},{9,13},{10,... | collective-permute-start | bytes 344072 | tf_op jit(solution)/shard_map/ppermute | solution.py:58
  772.3 39.6 %collective-permute-start.121 = (bf16[512,1024]{1,0:T(8,128)(2,1)}, bf16[512,1024]{1,0:T(8,128)(2,1)}, u32[]{:S(2)}, u32[]{:S(2)}) collective-permute-start(bf16[512,1024]{1,0:T(8,128)(2,1)} %fusion), channel_id=1, source_target_pairs={{0,8},{1,9},{2,10},{3,11},{4,12},{5,13},{6,14},{7,15},{8,24},{9,25... | collective-permute-start | bytes 3145736 | tf_op jit(solution)/shard_map/ppermute | solution.py:58
  772.6 39.3 %all-to-all-start.5 = ((bf16[4,64,4224]{2,1,0:T(8,128)(2,1)}), bf16[4,64,4224]{2,1,0:T(8,128)(2,1)S(1)}, u32[]{:S(2)}, u32[]{:S(2)}) async-start(bf16[4,64,4224]{2,1,0:T(8,128)(2,1)} %bitcast.89), calls=%async_computation.5 | async-start | bytes 4325376 | tf_op jit(solution)/shard_map/all_to_all | solution.py:994
  777.9 28.4 %collective-permute-start.119 = (bf16[128,2048]{1,0:T(8,128)(2,1)S(1)}, bf16[128,2048]{1,0:T(8,128)(2,1)S(1)}, u32[]{:S(2)}, u32[]{:S(2)}) collective-permute-start(bf16[128,2048]{1,0:T(8,128)(2,1)S(1)} %add_convert_fusion.28), channel_id=1, source_target_pairs={{0,8},{1,9},{2,10},{3,11},{4,12},{5,13},{6,14},{7,15},{8,24},{9,25... | collective-permute-start | bytes 1572872 | tf_op jit(solution)/shard_map/ppermute | solution.py:58
  783.4 38.4 %collective-permute-start.117 = (bf16[128,2048]{1,0:T(8,128)(2,1)}, bf16[128,2048]{1,0:T(8,128)(2,1)}, u32[]{:S(2)}, u32[]{:S(2)}) collective-permute-start(bf16[128,2048]{1,0:T(8,128)(2,1)} %slice.286), channel_id=1, source_target_pairs={{0,4},{1,5},{2,6},{3,7},{4,0},{5,1},{6,2},{7,3},{8,12},{9,13},{10,... | collective-permute-start | bytes 1572872 | tf_op jit(solution)/shard_map/ppermute | solution.py:58
  (184 other events, 2222.5 us)

commit v4 on v3

--- a/solution.py
+++ b/solution.py
@@ -207,15 +207,32 @@
     return gated, with_logits(gate_grad, logit_grad, up_grad, base, at)
 
 
-def first_kernel(
-    groups, units, experts, where_ref, rows_ref, cots_ref, gate_ref, down_ref, hidden_ref, grad_ref, out_ref, router_ref, gate_sums, down_sums
-):
+def first_kernel(groups, units, experts, count, where_ref, *refs):
+    pieces, refs = refs[:count], refs[count:]
+    cots_ref, gate_ref, down_ref, rows_ref, hidden_ref, grad_ref, out_ref, router_ref, gate_sums, down_sums, held, sems = refs
+    step, steps = pl.program_id(0), pl.num_programs(0)
+    each, size = held.shape[1] // pieces[0].shape[0], pieces[0].shape[0]
+
+    def copy(piece, slot, t):
+        return pltpu.make_async_copy(piece, held.at[slot, pl.ds(t * size, size)], sems.at[slot, t])
+
+    for j in range(count // each):
+
+        @pl.when(step == max(j - 1, 0))
+        def _(j=j):
+            for t in range(each):
+                copy(pieces[j * each + t], j % 2, t).start()
+
+    slot = lax.rem(step, 2)
+    for t in range(each):
+        copy(pieces[t], slot, t).wait()
+    rows_ref[...] = held[slot]
     gated, grad = group_pass(groups, units, experts, where_ref, rows_ref, cots_ref, gate_ref, down_ref)
     hidden_ref[...] = gated
     grad_ref[...] = grad
     add_grads(grad, rows_ref[...], gated, cots_ref[:, : rows_ref.shape[1]], gate_sums, down_sums)
 
-    @pl.when(pl.program_id(0) == pl.num_programs(0) - 1)
+    @pl.when(step == steps - 1)
     def _():
         hand_out(units * len(groups), gate_sums, down_sums, out_ref, router_ref)
 
@@ -269,22 +286,30 @@
     return rows.shape[0] // tile, tile, [among_all(rows.shape[1], tile), among_all(cots.shape[1], tile)]
 
 
-def first_units(groups, where, rows, cots, gate_rows, down_rows, units, experts, count):
-    total, width = rows.shape
+def first_units(groups, where, pieces, cots, gate_rows, down_rows, units, experts, count):
+    total, width = cots.shape[0], gate_rows.shape[1]
     pad = down_rows.shape[0]
     wide = units * len(groups)
-    steps, tile, token_specs = token_grid(cots, rows)
+    tile = 512
     shapes = grads_out(wide, pad, width, count)
-    hidden, grad, weights, router = pl.pallas_call(
-        functools.partial(first_kernel, groups, units, experts),
+    rows, hidden, grad, weights, router = pl.pallas_call(
+        functools.partial(first_kernel, groups, units, experts, len(pieces)),
         grid_spec=pltpu.PrefetchScalarGridSpec(
             num_scalar_prefetch=1,
-            grid=(steps,),
-            in_specs=token_specs + [all_of(gate_rows.shape), all_of(down_rows.shape)],
-            out_specs=[among_all(pad, tile), among_all(2 * pad, tile), all_of(shapes[0]), all_of(shapes[1])],
-            scratch_shapes=[pltpu.VMEM((2 * pad, width), f32), pltpu.VMEM((pad, width), f32)],
+            grid=(total // tile,),
+            in_specs=[pl.BlockSpec(memory_space=pl.ANY)] * len(pieces)
+            + [among_all(cots.shape[1], tile), all_of(gate_rows.shape), all_of(down_rows.shape)],
+            out_specs=[among_all(width, tile), among_all(pad, tile), among_all(2 * pad, tile)]
+            + [all_of(shape) for shape in shapes],
+            scratch_shapes=[
+                pltpu.VMEM((2 * pad, width), f32),
+                pltpu.VMEM((pad, width), f32),
+                pltpu.VMEM((2, tile, width), bf16),
+                pltpu.SemaphoreType.DMA((2, tile // pieces[0].shape[0])),
+            ],
         ),
         out_shape=[
+            jax.ShapeDtypeStruct((total, width), bf16),
             jax.ShapeDtypeStruct((total, pad), bf16),
             jax.ShapeDtypeStruct((total, 2 * pad), bf16),
             jax.ShapeDtypeStruct(shapes[0], bf16),
@@ -292,8 +317,8 @@
         ],
         compiler_params=pltpu.CompilerParams(vmem_limit_bytes=60 * 1024 * 1024),
         cost_estimate=pl.CostEstimate(flops=12 * total * width * pad, bytes_accessed=4 * total * width, transcendentals=0),
-    )(where, rows, cots, gate_rows, down_rows)
-    return hidden, grad, to_owners(weights, wide, count), router
+    )(where, *pieces, cots, gate_rows, down_rows)
+    return rows, hidden, grad, to_owners(weights, wide, count), router
 
 
 def weight_grads(where, rows, cots, hidden, grad, wide, count):
@@ -750,55 +775,57 @@
         cores = [cot_cores[s]] + between_cores(cot_ups[s], cot_sides[s], cot_crosses[s])
         cots += [cot_blocks[s], cot_ups[s], *cores[:2], cot_sides[s], cot_crosses[s], *cores[2:]]
     cots = assemble(cots)
-    cross, side, cots = together(cross, side, cots)
+    cross, cots = together(cross, cots)
     received[3] = permute(after(received[3], cross), lay.side_core)
     up = permute(plus(here[2 * n : 3 * n], cross), lay.up)
-    branch = here[:n].astype(f32) + side.astype(f32) + after(up, first_ffn, *received).astype(f32)
+    branch = here[:n].astype(f32) + side.astype(f32) + after(up, first_ffn, *received[:3]).astype(f32)
     residual = stream + branch
     inverse_two = lax.rsqrt(jnp.mean(residual * residual, axis=1, keepdims=True) + norm_eps)
     normed_two = (residual * inverse_two * gain_two).astype(bf16)
 
     blocks, ups, sides, crosses, inner = [normed_two], [], [], [], []
 
-    for s in range(rings - 1):
-        onward = permute(blocks[s], lay.onward)
-        up, side = permute(blocks[s], lay.up), permute(blocks[s], lay.side)
-        more, last = [], s == rings - 2
-        if s >= 2:
-            more.append(permute(ups[s - 2], lay.side))
-            inner.append(between_cores(blocks[s - 2], ups[s - 2], sides[s - 2]))
-        if last:
-            more.append(permute(sides[s - 1], lay.up))
-            inner.append(between_cores(blocks[s - 1], ups[s - 1], sides[s - 1]))
-        if s == 1:
+    for s in range(rings):
+        up = permute(blocks[s], lay.up)
+        going = {}
+        if s < rings - 1:
+            going["onward"] = permute(blocks[s], lay.onward)
+        if s == 0:
+            going["received"] = received[3]
+        else:
+            going["side"] = permute(blocks[s - 1], lay.side)
+        if s == rings - 2:
+            first_rows = place_weights(first_ffn, router)
+            going["first_rows"] = first_rows
+        if s == rings - 1:
+            crosses = {k: permute(sides[k], lay.up) for k in range(1, rings - 2, 2)}
+            crosses[0] = permute(ups[0], lay.side)
             shared_ffn = jnp.stack(received)[jnp.arange(4, dtype=jnp.int32) ^ ep].reshape(-1, 3 * unit_share)
-            shared_ffn = turn_weights(shared_ffn, 1, dp_count)
-            second_ffn = jnp.concatenate([second_ffn, shared_ffn], axis=1)
-            second_ffn, onward = together(second_ffn, onward)
-        onward, up, side, *more = together(onward, up, side, *more)
-        blocks.append(onward)
+            second_ffn = jnp.concatenate([second_ffn, turn_weights(shared_ffn, 1, dp_count)], axis=1)
+            going["crosses"], going["second_ffn"] = crosses, second_ffn
+        up, going = lax.optimization_barrier((up, going))
         ups.append(up)
-        sides.append(side)
-        crosses += more
-    up, side = permute(blocks[-1], lay.up), permute(blocks[-1], lay.side)
-    inner.append(between_cores(blocks[-2], ups[-1], sides[-1]))
-    up, side, crossing = together(up, side, ups[-1])
-    ups.append(up)
-    sides.append(side)
-    second_ffn = to_units(after(second_ffn, up))
-    inner.append(between_cores(blocks[-1], up, side))
-    crossing, crossed_too = permute(crossing, lay.side), permute(up, lay.side)
-
-    crosses += together(crossing, crossed_too)
+        if "onward" in going:
+            blocks.append(going["onward"])
+        if "side" in going:
+            sides.append(going["side"])
+        if "received" in going:
+            received[3] = going["received"]
+        if "first_rows" in going:
+            first_rows = going["first_rows"]
+        if "crosses" in going:
+            crosses, second_ffn = going["crosses"], going["second_ffn"]
+    second_ffn = to_units(second_ffn)
+    sides.append(permute(blocks[-1], lay.side))
+    crosses.update({k: permute(ups[k], lay.side) for k in range(rings) if k not in crosses})
+    inner = [between_cores(blocks[s], ups[s], sides[s]) for s in range(rings)]
     rows = []
     for s in range(rings):
         cores = inner[s] + between_cores(crosses[s])
         rows += [blocks[s], ups[s], *cores[:2], sides[s], crosses[s], *cores[2:]]
-    rows = assemble(rows)
-
-    first_rows = place_weights(first_ffn, router)
+
     late = rings // 2
-    first_hidden, first_grad, first_weights_grad, first_router = first_units(
+    rows, first_hidden, first_grad, first_weights_grad, first_router = first_units(
         (0,), where, rows, cots, *first_rows, units, expert_count, dp_count
     )
     first_weights_grad = to_units(first_weights_grad)
@@ -827,14 +854,15 @@
         )
 
     out_own_a, out_far_a, own_a, far_a, hidden, gate_up_grad = ffn_half(late, rings - late, ())
+    own_a, far_a, first_weights_grad = all_there(own_a, far_a, first_weights_grad)
 
     keep, send = crossed(own_a, permute(far_a, lay.core), first_half)
     keep, send, hidden, gate_up_grad = all_there(keep, send, hidden, gate_up_grad)
     out_there_a = permute(after(out_far_a, hidden), lay.core)
     sided = {s: permute(send[s], lay.side) for s in first_half}
     out_own_b, out_far_b, own_b, far_b, hidden, gate_up_grad = ffn_half(0, late, (hidden, gate_up_grad))
-    sided, own_b, far_b, hidden, gate_up_grad, first_weights_grad, out_there_a = all_there(
-        sided, own_b, far_b, hidden, gate_up_grad, first_weights_grad, out_there_a
+    sided, own_b, far_b, hidden, gate_up_grad, out_there_a = all_there(
+        sided, own_b, far_b, hidden, gate_up_grad, out_there_a
     )
 
     far_there = permute(far_b, lay.core)
@@ -975,45 +1003,39 @@
     def outs_in(outs_up):
         out_sums.update({s: out_halves[s][:n].astype(f32) + outs_up[s].astype(f32) for s in outs_up})
 
-    for i, s in enumerate(order[2:]):
-        moving = permute(total.astype(bf16), lay.backward)
-        if i == 0:
-            outs_up = outs_over((quarter[0] + quarter[1])[1:])
-            outgoing = outs_on(output_sum)
-            sided = {s: permute(send[s], lay.side) for s in quarter[3]}
-            for step in doubling[:2]:
-                small = small + permute(small, step)
-            shared_columns_grad, expert_grad = turn_grads(first_weights_grad, ffn_grad)
-            moving, outs_up, sided, small, shared_columns_grad, expert_grad, outgoing = all_there(
-                moving, outs_up, sided, small, shared_columns_grad, expert_grad, outgoing
-            )
-            outs_in(outs_up)
-            output_sum = out_sums[out_queue.pop(0)] + outgoing.astype(f32)
-            out_halves.update({s: plus(keep[s], sided[s]) for s in quarter[3]})
-            outs_up = outs_over(quarter[2] + quarter[3])
-            shared_columns_grad = lax.all_to_all(
-                shared_columns_grad.reshape(owners, -1, 3 * unit_share),
-                "ep",
-                split_axis=0,
-                concat_axis=0,
-                tiled=True,
-            )
-        else:
-            if i == 1:
-                small = small + permute(small, doubling[2])
-            if i == rings - 3:
-                moving, small, shared_columns_grad = together(moving, small, shared_columns_grad)
-            if i == 1:
-                outs_in(outs_up)
-            if i >= 1:
-                output_sum = out_sums[out_queue.pop(0)] + outs_on(output_sum).astype(f32)
-        total = grads_at(s) + moving.astype(f32)
-    total = total.astype(bf16).reshape(8, -1, 4 * share)
+    moving = permute(total.astype(bf16), lay.backward)
+    outs_up = outs_over((quarter[0] + quarter[1])[1:])
+    sided = {s: permute(send[s], lay.side) for s in quarter[3]}
+    small = small + permute(small, doubling[0])
+    shared_columns_grad, expert_grad = turn_grads(first_weights_grad, ffn_grad)
+    shared_columns_grad = lax.all_to_all(
+        shared_columns_grad.reshape(owners, -1, 3 * unit_share), "ep", split_axis=0, concat_axis=0, tiled=True
+    )
+    moving, outs_up, sided, small, expert_grad = all_there(moving, outs_up, sided, small, expert_grad)
+    outs_in(outs_up)
+    out_halves.update({s: plus(keep[s], sided[s]) for s in quarter[3]})
+
+    total = grads_at(order[2]) + moving.astype(f32)
+    moving = permute(total.astype(bf16), lay.backward)
+    outs_up = outs_over(quarter[2] + quarter[3])
+    output_sum = after(output_sum, outs_up[order[2]])
+    outgoing = [outs_on(v) for v in (output_sum[: n // 2], output_sum[n // 2 :])]
+    for step in doubling[1:3]:
+        small = small + permute(small, step)
+    moving, shared_columns_grad, outs_up, small = all_there(moving, shared_columns_grad, outs_up, small)
+    outs_in(outs_up)
+    total = grads_at(order[3]) + moving.astype(f32)
+    for s in order[4:]:
+        total = grads_at(s) + permute(total.astype(bf16), lay.backward).astype(f32)
+
+    total, small = all_there(total.astype(bf16), small)
+    total = total.reshape(8, -1, 4 * share)
     total = lax.all_to_all(total, PLANE, split_axis=0, concat_axis=0, tiled=True)
+    for s in out_queue[:-1]:
+        outgoing = [outs_on(out_sums[s][k * n // 2 : (k + 1) * n // 2] + v.astype(f32)) for k, v in enumerate(outgoing)]
+    output_sum = out_sums[out_queue[-1]] + stack(*outgoing).astype(f32)
     for step in doubling[3:]:
         small = small + permute(small, step)
-    while out_queue:
-        output_sum = out_sums[out_queue.pop(0)] + outs_on(output_sum).astype(f32)
     output = (residual + output_sum).astype(bf16)
     dense_grad = collect_columns(total, shared_columns_grad, share)
 

time: 849 us -> 826 us (0.973)
  Pallas kernels: 248 us -> 238 us
  waiting for transfers between devices: 305 us -> 296 us
    pallas_call x4 -> x3, Pallas kernels: 30.9 us -> 20.2 us  [assemble(): pl.pallas_call(assemble_kernel, in_specs=[pl.BlockSpec(memory_space=pltpu...]
    ppermute x125 -> x128, waiting for transfers between devices: 282 us -> 281 us  [permute(): return lax.ppermute(rows, AXES, pairs)]
    ppermute x125 -> x128, starting transfers between devices: 104 us -> 103 us  [permute(): return lax.ppermute(rows, AXES, pairs)]
    unnamed x200 -> x190, local copies, waits for them, and re-layouts: 25 us -> 24.6 us
  transfers between devices with their start and end apart: 132 -> 135, of which waited for: 57 -> 60; matrix products, arithmetic and copies ran while one was open for 12% -> 13% of each run, Pallas kernels for 24% -> 29%
where the time goes in v4:
time: 826 us; the launch traced here: 817 us
  waiting for transfers between devices  296 us (36%)
  Pallas kernels  238 us (29%)
  starting transfers between devices  137 us (17%)
  other arithmetic  79.9 us (10%)
  local copies, waits for them, and re-layouts  44.9 us (5%)
  between operations  14.3 us (2%)
    ppermute x128, waiting for transfers between devices, permute(): return lax.ppermute(rows, AXES, pairs)  281 us
    ppermute x128, starting transfers between devices, permute(): return lax.ppermute(rows, AXES, pairs)  103 us
    pallas_call x2, Pallas kernels, second_units(): pl.pallas_call(functools.partial(second_kernel, groups, units, experts),...  81.4 us
    pallas_call x1, Pallas kernels, first_units(): pl.pallas_call(functools.partial(first_kernel, groups, units, experts, le...  48.3 us
    convert_element_type x16, other arithmetic, plus(): return (a.astype(f32) + b.astype(f32)).astype(bf16)  34.6 us
    pallas_call x3, Pallas kernels, group_call(): pl.pallas_call(kernel, grid_spec=pltpu.PrefetchScalarGridSpec(num_scalar_...  31.2 us
    pallas_call x1, Pallas kernels, weight_grads(): pl.pallas_call(functools.partial(grads_kernel, wide), grid_spec=pltpu.Pre...  30.2 us
    unnamed x190, local copies, waits for them, and re-layouts  24.6 us
  transfers between devices with their start and end apart: 135, of which 60 were waited for; matrix products, arithmetic and copies ran while one was open for 13% of the time, Pallas kernels for 29%

profile of v4, /device:TPU:0, one launch (start us, length us, event | category | flops | bytes accessed | tf_op | source)
XLA Modules:
  0.0 817.0 jit_solution(17749533737763017072)
XLA Ops:
  3.4 4.0 collective-permute-start
  24.0 4.7 copy.57
  28.8 5.5 all-to-all-done
  52.0 19.6 %collective-permute-done.4.refs_24_ = bf16[128,2176]{1,0:T(8,128)(2,1)S(1)} collective-permute-done((bf16[128,2176]{1,0:T(8,128)(2,1)}, bf16[128,2176]{1,0:T(8,128)(2,1)S(1)}, u32[]{:S(2)}, u32[]{:S(2)}) %collective-permute-start.4) | collective-permute-done | bytes 557088 | tf_op jit(solution)/shard_map/ppermute | solution.py:58
  78.1 9.2 %collective-permute-done.12.refs_12_ = bf16[128,2176]{1,0:T(8,128)(2,1)} collective-permute-done((bf16[128,2176]{1,0:T(8,128)(2,1)}, bf16[128,2176]{1,0:T(8,128)(2,1)}, u32[]{:S(2)}, u32[]{:S(2)}) %collective-permute-start.12) | collective-permute-done | bytes 557088 | tf_op jit(solution)/shard_map/ppermute | solution.py:58
  92.0 7.5 collective-permute-done.14.refs_17_
  113.4 6.7 collective-permute-done.2.refs_20_
  120.6 11.5 %collective-permute-done.10.refs_28_ = bf16[128,2176]{1,0:T(8,128)(2,1)} collective-permute-done((bf16[128,2176]{1,0:T(8,128)(2,1)}, bf16[128,2176]{1,0:T(8,128)(2,1)}, u32[]{:S(2)}, u32[]{:S(2)}) %collective-permute-start.10) | collective-permute-done | bytes 557088 | tf_op jit(solution)/shard_map/ppermute | solution.py:58
  134.6 4.4 shard_map.209.rows_ref
  139.0 11.1 %shard_map.210 = (bf16[1024,768]{1,0:T(8,128)(2,1)}, bf16[1024,256]{1,0:T(8,128)(2,1)S(1)}) custom-call(s32[4]{0:T(128)S(1)} %pad_add_fusion.4.where_ref, bf16[1024,2048]{1,0:T(8,128)(2,1)} %shard_map.209.rows_ref, f32[1,768]{1,0:T(1,128)S(1)} %bitcast.85, f32[1024,128]{1,0:T(8,128)S(1)} %copy-done.11, f32[1024,128]{1,0:T(8,128)S(1)} %copy-done.9, ...), custom_call_target="tpu_custom_call" | custom-call | flops 3758096384 | bytes 8922624 | tf_op jit(solution)/shard_map/pallas_call | solution.py:630
  150.0 5.2 shard_map.211
  159.2 5.7 all-to-all-start.1
  180.8 12.1 %shard_map.212.refs_32_.cots_ref = bf16[4096,2176]{1,0:T(8,128)(2,1)} custom-call(bf16[128,2176]{1,0:T(8,128)(2,1)} %pad_maximum_fusion.3.refs_0_, bf16[128,2176]{1,0:T(8,128)(2,1)} %collective-permute-done.8.refs_1_, bf16[128,2176]{1,0:T(8,128)(2,1)} %collective-permute-done.29.refs_2_, bf16[128,2176]{1,0:T(8,128)(2,1)} %collective-permute-done.30.refs_3_, ...), custom_call_target="tpu_custom_call" | custom-call | bytes 35651584 | tf_op jit(solution)/shard_map/pallas_call | solution.py:86
  197.6 5.6 collective-permute-done.47
  203.2 9.2 %collective-permute-done.45 = bf16[128,2048]{1,0:T(8,128)(2,1)} collective-permute-done((bf16[128,2048]{1,0:T(8,128)(2,1)S(1)}, bf16[128,2048]{1,0:T(8,128)(2,1)}, u32[]{:S(2)}, u32[]{:S(2)}) %collective-permute-start.45) | collective-permute-done | bytes 524320 | tf_op jit(solution)/shard_map/ppermute | solution.py:58
  224.4 7.3 collective-permute-done.48.refs_1_
  237.6 7.3 collective-permute-done.53.refs_9_
  250.4 4.3 shard_map.213
  272.9 5.7 collective-permute-done.62.refs_20_
  280.2 5.5 all-to-all-start.2
  293.8 10.5 %collective-permute-done.71.refs_21_ = bf16[128,2048]{1,0:T(8,128)(2,1)S(1)} collective-permute-done((bf16[128,2048]{1,0:T(8,128)(2,1)}, bf16[128,2048]{1,0:T(8,128)(2,1)S(1)}, u32[]{:S(2)}, u32[]{:S(2)}) %collective-permute-start.71) | collective-permute-done | bytes 524320 | tf_op jit(solution)/shard_map/ppermute | solution.py:58
  304.4 11.2 %collective-permute-done.76.refs_28_ = bf16[128,2048]{1,0:T(8,128)(2,1)S(1)} collective-permute-done((bf16[128,2048]{1,0:T(8,128)(2,1)}, bf16[128,2048]{1,0:T(8,128)(2,1)S(1)}, u32[]{:S(2)}, u32[]{:S(2)}) %collective-permute-start.76) | collective-permute-done | bytes 524320 | tf_op jit(solution)/shard_map/ppermute | solution.py:58
  316.6 9.4 %collective-permute-done.77.refs_29_ = bf16[128,2048]{1,0:T(8,128)(2,1)S(1)} collective-permute-done((bf16[128,2048]{1,0:T(8,128)(2,1)}, bf16[128,2048]{1,0:T(8,128)(2,1)S(1)}, u32[]{:S(2)}, u32[]{:S(2)}) %collective-permute-start.77) | collective-permute-done | bytes 524320 | tf_op jit(solution)/shard_map/ppermute | solution.py:58
  330.3 48.3 %shard_map.215 = (bf16[4096,2048]{1,0:T(8,128)(2,1)}, bf16[4096,256]{1,0:T(8,128)(2,1)}, bf16[4096,512]{1,0:T(8,128)(2,1)}, bf16[8,528,256]{2,1,0:T(8,128)(2,1)}, f32[24,2048]{1,0:T(8,128)}) custom-call(s32[1]{0:T(128)} %bitcast.24.where_ref, bf16[128,2048]{1,0:T(8,128)(2,1)} %multiply_convert_fusion.refs_0_, ...), custom_call_target="tpu_custom_call" | custom-call | flops 25769803776 | bytes 33554432 | tf_op jit(solution)/shard_map/pallas_call | solution.py:295
  378.6 6.5 all-to-all-start.3
  385.3 4.9 shard_map.216
  393.0 40.8 %shard_map.217 = (bf16[1024,2048]{1,0:T(8,128)(2,1)}, bf16[1024,2048]{1,0:T(8,128)(2,1)}, bf16[1024,2048]{1,0:T(8,128)(2,1)}, bf16[1024,2048]{1,0:T(8,128)(2,1)}...) custom-call(s32[1]{0:T(128)} %bitcast.24.where_ref, bf16[4096,2048]{1,0:T(8,128)(2,1)} %get-tuple-element.239.rows_ref, ...), custom_call_target="tpu_custom_call" | custom-call | flops 16106127360 | bytes 33554432 | tf_op jit(solution)/shard_map/pallas_call | solution.py:360
  435.0 7.4 collective-permute-done.80
  448.4 40.6 %shard_map.218 = (bf16[1024,2048]{1,0:T(8,128)(2,1)}, bf16[1024,2048]{1,0:T(8,128)(2,1)}, bf16[1024,2048]{1,0:T(8,128)(2,1)}, bf16[1024,2048]{1,0:T(8,128)(2,1)}...) custom-call(s32[1]{0:T(128)} %bitcast.24.where_ref, ...), custom_call_target="tpu_custom_call", output_to_operand_aliasing={{4}: (9, {}), {5}: (10, {})} | custom-call | flops 16106127360 | bytes 33554432 | tf_op jit(solution)/shard_map/pallas_call | solution.py:360
  489.0 5.5 collective-permute-done.82
  497.4 10.4 %collective-permute-done.84 = bf16[1024,2048]{1,0:T(8,128)(2,1)S(1)} collective-permute-done((bf16[1024,2048]{1,0:T(8,128)(2,1)}, bf16[1024,2048]{1,0:T(8,128)(2,1)S(1)}, u32[]{:S(2)}, u32[]{:S(2)}) %collective-permute-start.84) | collective-permute-done | bytes 4194336 | tf_op jit(solution)/shard_map/ppermute | solution.py:58
  515.7 30.2 %shard_map.219 = (bf16[8,1056,256]{2,1,0:T(8,128)(2,1)}, f32[24,2048]{1,0:T(8,128)}) custom-call(s32[1]{0:T(128)} %bitcast.24.where_ref, bf16[4096,2048]{1,0:T(8,128)(2,1)} %get-tuple-element.239.rows_ref, bf16[4096,2176]{1,0:T(8,128)(2,1)} %shard_map.212.refs_32_.cots_ref, bf16[4096,384]{1,0:T(8,128)(2,1)} %get-tuple-element.277.hidden_ref, ...), custom_call_target="tpu_custom_call" | custom-call | flops 19327352832 | bytes 33554432 | tf_op jit(solution)/shard_map/pallas_call | solution.py:329
  571.8 5.1 collective-permute-done.94
  581.1 9.2 %collective-permute-done.97.refs_1_ = bf16[128,2048]{1,0:T(8,128)(2,1)S(1)} collective-permute-done((bf16[128,2048]{1,0:T(8,128)(2,1)S(1)}, bf16[128,2048]{1,0:T(8,128)(2,1)S(1)}, u32[]{:S(2)}, u32[]{:S(2)}) %collective-permute-start.97) | collective-permute-done | bytes 524320 | tf_op jit(solution)/shard_map/ppermute | solution.py:58
  590.3 4.8 all-to-all-start.4
  597.5 7.0 collective-permute-done.101.refs_5_
  617.7 15.0 %shard_map.221 = (bf16[1024,768]{1,0:T(8,128)(2,1)}, bf16[512,2048]{1,0:T(8,128)(2,1)}, bf16[512,2048]{1,0:T(8,128)(2,1)}, f32[16,768]{1,0:T(8,128)S(1)}) custom-call(s32[4]{0:T(128)S(1)} %pad_add_fusion.4.where_ref, bf16[1024,2048]{1,0:T(8,128)(2,1)} %shard_map.220.grad_ref, bf16[1024,768]{1,0:T(8,128)(2,1)} %get-tuple-element.300.packed_ref, ...), custom_call_target="tpu_custom_call" | custom-call | flops 5905580032 | bytes 10493952 | tf_op jit(solution)/shard_map/pallas_call | solution.py:630
  648.7 10.5 %collective-permute-done.95 = bf16[256,2048]{1,0:T(8,128)(2,1)S(1)} collective-permute-done((bf16[256,2048]{1,0:T(8,128)(2,1)}, bf16[256,2048]{1,0:T(8,128)(2,1)S(1)}, u32[]{:S(2)}, u32[]{:S(2)}) %collective-permute-start.95) | collective-permute-done | bytes 1048608 | tf_op jit(solution)/shard_map/ppermute | solution.py:58
  670.1 5.5 collective-permute-done.106
  677.5 9.3 %collective-permute-done.107 = bf16[128,2048]{1,0:T(8,128)(2,1)} collective-permute-done((bf16[128,2048]{1,0:T(8,128)(2,1)}, bf16[128,2048]{1,0:T(8,128)(2,1)}, u32[]{:S(2)}, u32[]{:S(2)}) %collective-permute-start.107) | collective-permute-done | bytes 524320 | tf_op jit(solution)/shard_map/ppermute | solution.py:58
  686.8 5.9 all-to-all-done.4.second_ref
  697.0 8.7 %shard_map.222 = (bf16[256,4224]{1,0:T(8,128)(2,1)}, f32[256,2,4224]{2,1,0:T(2,128)}) custom-call(bf16[8,528,256]{2,1,0:T(8,128)(2,1)} %copy-done.25, bf16[8,1056,256]{2,1,0:T(8,128)(2,1)} %all-to-all-done.4.second_ref), custom_call_target="tpu_custom_call" | custom-call | bytes 17301504 | tf_op jit(solution)/shard_map/pallas_call | solution.py:425
  723.8 11.7 %collective-permute-done.117 = bf16[128,2048]{1,0:T(8,128)(2,1)S(1)} collective-permute-done((bf16[128,2048]{1,0:T(8,128)(2,1)S(1)}, bf16[128,2048]{1,0:T(8,128)(2,1)S(1)}, u32[]{:S(2)}, u32[]{:S(2)}) %collective-permute-start.117) | collective-permute-done | bytes 524320 | tf_op jit(solution)/shard_map/ppermute | solution.py:58
  736.0 6.8 collective-permute-done.111
  751.0 5.1 collective-permute-done.118
  765.4 11.2 %collective-permute-done.115 = bf16[512,1024]{1,0:T(8,128)(2,1)} collective-permute-done((bf16[512,1024]{1,0:T(8,128)(2,1)}, bf16[512,1024]{1,0:T(8,128)(2,1)}, u32[]{:S(2)}, u32[]{:S(2)}) %collective-permute-start.115) | collective-permute-done | bytes 1048608 | tf_op jit(solution)/shard_map/ppermute | solution.py:58
  784.6 5.4 collective-permute-done.126
  805.4 5.2 collective-permute-done.125
  (557 shorter events, 298.5 us)
Async XLA Ops:
  7.5 34.3 %collective-permute-start.7 = (bf16[128,2176]{1,0:T(8,128)(2,1)}, bf16[128,2176]{1,0:T(8,128)(2,1)S(1)}, u32[]{:S(2)}, u32[]{:S(2)}) collective-permute-start(bf16[128,2176]{1,0:T(8,128)(2,1)} %pad_maximum_fusion.3.refs_0_), channel_id=1, source_target_pairs={{0,2},{1,3},{2,0},{3,1},{4,6},{5,7},{6,4},{7,5},{8,10},{9,11},{10,... | collective-permute-start | bytes 1671176 | tf_op jit(solution)/shard_map/ppermute | solution.py:58
  8.9 41.7 %collective-permute-start.8 = (bf16[128,2176]{1,0:T(8,128)(2,1)}, bf16[128,2176]{1,0:T(8,128)(2,1)}, u32[]{:S(2)}, u32[]{:S(2)}) collective-permute-start(bf16[128,2176]{1,0:T(8,128)(2,1)} %pad_maximum_fusion.3.refs_0_), channel_id=1, source_target_pairs={{0,4},{1,5},{2,6},{3,7},{4,0},{5,1},{6,2},{7,3},{8,12},{9,13},{10,... | collective-permute-start | bytes 1671176 | tf_op jit(solution)/shard_map/ppermute | solution.py:58
  35.1 36.5 %collective-permute-start.3 = (bf16[512,1024]{1,0:T(8,128)(2,1)S(1)}, bf16[512,1024]{1,0:T(8,128)(2,1)}, u32[]{:S(2)}, u32[]{:S(2)}) collective-permute-start(bf16[512,1024]{1,0:T(8,128)(2,1)S(1)} %bitcast.81), channel_id=1, source_target_pairs={{0,16},{1,17},{2,18},{3,19},{4,20},{5,21},{6,22},{7,23},{8,0},{9,1... | collective-permute-start | bytes 3145736 | tf_op jit(solution)/shard_map/ppermute | solution.py:58
  41.8 29.8 %collective-permute-start.4 = (bf16[128,2176]{1,0:T(8,128)(2,1)}, bf16[128,2176]{1,0:T(8,128)(2,1)S(1)}, u32[]{:S(2)}, u32[]{:S(2)}) collective-permute-start(bf16[128,2176]{1,0:T(8,128)(2,1)} %collective-permute-done.1.refs_16_), channel_id=1, source_target_pairs={{0,16},{1,17},{2,18},{3,19},{4,20},{5,21},{6,22},{7,23},{8,0},{9,1... | collective-permute-start | bytes 1671176 | tf_op jit(solution)/shard_map/ppermute | solution.py:58
  72.4 27.0 %collective-permute-start.15 = (bf16[512,1024]{1,0:T(8,128)(2,1)}, bf16[512,1024]{1,0:T(8,128)(2,1)}, u32[]{:S(2)}, u32[]{:S(2)}) collective-permute-start(bf16[512,1024]{1,0:T(8,128)(2,1)} %collective-permute-done.3.refs_1_), channel_id=1, source_target_pairs={{0,16},{1,17},{2,18},{3,19},{4,20},{5,21},{6,22},{7,23},{8,0},{9,1... | collective-permute-start | bytes 3145736 | tf_op jit(solution)/shard_map/ppermute | solution.py:58
  78.1 26.2 %collective-permute-start.18 = (bf16[128,2048]{1,0:T(8,128)(2,1)}, bf16[128,2048]{1,0:T(8,128)(2,1)}, u32[]{:S(2)}, u32[]{:S(2)}) collective-permute-start(bf16[128,2048]{1,0:T(8,128)(2,1)} %fusion.5.refs_0_), channel_id=1, source_target_pairs={{0,1},{1,0},{2,3},{3,2},{4,5},{5,4},{6,7},{7,6},{8,9},{9,8},{10,11... | collective-permute-start | bytes 1572872 | tf_op jit(solution)/shard_map/ppermute | solution.py:58
  99.4 34.6 %collective-permute-start.16 = (bf16[512,1024]{1,0:T(8,128)(2,1)}, bf16[512,1024]{1,0:T(8,128)(2,1)}, u32[]{:S(2)}, u32[]{:S(2)}) collective-permute-start(bf16[512,1024]{1,0:T(8,128)(2,1)} %collective-permute-done.15.refs_2_), channel_id=1, source_target_pairs={{0,16},{1,17},{2,18},{3,19},{4,20},{5,21},{6,22},{7,23},{8,0},{9,1... | collective-permute-start | bytes 3145736 | tf_op jit(solution)/shard_map/ppermute | solution.py:58
  104.8 27.2 %collective-permute-start.10 = (bf16[128,2176]{1,0:T(8,128)(2,1)}, bf16[128,2176]{1,0:T(8,128)(2,1)}, u32[]{:S(2)}, u32[]{:S(2)}) collective-permute-start(bf16[128,2176]{1,0:T(8,128)(2,1)} %copy-done.47), channel_id=1, source_target_pairs={{0,2},{1,3},{2,0},{3,1},{4,6},{5,7},{6,4},{7,5},{8,10},{9,11},{10,... | collective-permute-start | bytes 1671176 | tf_op jit(solution)/shard_map/ppermute | solution.py:58
  106.4 27.1 %collective-permute-start.11 = (bf16[128,2176]{1,0:T(8,128)(2,1)}, bf16[128,2176]{1,0:T(8,128)(2,1)}, u32[]{:S(2)}, u32[]{:S(2)}) collective-permute-start(bf16[128,2176]{1,0:T(8,128)(2,1)} %copy-done.47), channel_id=1, source_target_pairs={{0,4},{1,5},{2,6},{3,7},{4,0},{5,1},{6,2},{7,3},{8,12},{9,13},{10,... | collective-permute-start | bytes 1671176 | tf_op jit(solution)/shard_map/ppermute | solution.py:58
  109.1 25.5 %collective-permute-start.21 = (bf16[128,2048]{1,0:T(8,128)(2,1)}, bf16[128,2048]{1,0:T(8,128)(2,1)}, u32[]{:S(2)}, u32[]{:S(2)}) collective-permute-start(bf16[128,2048]{1,0:T(8,128)(2,1)} %collective-permute-done.17.refs_5_), channel_id=1, source_target_pairs={{0,1},{1,0},{2,3},{3,2},{4,5},{5,4},{6,7},{7,6},{8,9},{9,8},{10,11... | collective-permute-start | bytes 1572872 | tf_op jit(solution)/shard_map/ppermute | solution.py:58
  120.1 35.1 %collective-permute-start.22 = (bf16[128,2176]{1,0:T(8,128)(2,1)}, bf16[128,2176]{1,0:T(8,128)(2,1)}, u32[]{:S(2)}, u32[]{:S(2)}) collective-permute-start(bf16[128,2176]{1,0:T(8,128)(2,1)} %collective-permute-done.8.refs_1_), channel_id=1, source_target_pairs={{0,2},{1,3},{2,0},{3,1},{4,6},{5,7},{6,4},{7,5},{8,10},{9,11},{10,... | collective-permute-start | bytes 1671176 | tf_op jit(solution)/shard_map/ppermute | solution.py:58
  132.0 23.2 %collective-permute-start.23 = (bf16[128,2176]{1,0:T(8,128)(2,1)}, bf16[128,2176]{1,0:T(8,128)(2,1)}, u32[]{:S(2)}, u32[]{:S(2)}) collective-permute-start(bf16[128,2176]{1,0:T(8,128)(2,1)} %collective-permute-done.12.refs_12_), channel_id=1, source_target_pairs={{0,4},{1,5},{2,6},{3,7},{4,0},{5,1},{6,2},{7,3},{8,12},{9,13},{10,... | collective-permute-start | bytes 1671176 | tf_op jit(solution)/shard_map/ppermute | solution.py:58
  133.5 22.0 %collective-permute-start.24 = (bf16[128,2176]{1,0:T(8,128)(2,1)}, bf16[128,2176]{1,0:T(8,128)(2,1)}, u32[]{:S(2)}, u32[]{:S(2)}) collective-permute-start(bf16[128,2176]{1,0:T(8,128)(2,1)} %collective-permute-done.14.refs_17_), channel_id=1, source_target_pairs={{0,2},{1,3},{2,0},{3,1},{4,6},{5,7},{6,4},{7,5},{8,10},{9,11},{10,... | collective-permute-start | bytes 1671176 | tf_op jit(solution)/shard_map/ppermute | solution.py:58
  134.0 24.1 %collective-permute-start.25 = (bf16[128,2176]{1,0:T(8,128)(2,1)}, bf16[128,2176]{1,0:T(8,128)(2,1)}, u32[]{:S(2)}, u32[]{:S(2)}) collective-permute-start(bf16[128,2176]{1,0:T(8,128)(2,1)} %collective-permute-done.10.refs_28_), channel_id=1, source_target_pairs={{0,4},{1,5},{2,6},{3,7},{4,0},{5,1},{6,2},{7,3},{8,12},{9,13},{10,... | collective-permute-start | bytes 1671176 | tf_op jit(solution)/shard_map/ppermute | solution.py:58
  159.2 55.6 %all-to-all-start.1 = ((bf16[8,528,256]{2,1,0:T(8,128)(2,1)}), bf16[8,528,256]{2,1,0:T(8,128)(2,1)}, u32[]{:S(2)}, u32[]{:S(2)}) async-start(bf16[8,528,256]{2,1,0:T(8,128)(2,1)} %shard_map.207), calls=%async_computation.1 | async-start | bytes 4325376 | tf_op jit(solution)/shard_map/all_to_all | solution.py:768
  179.2 23.9 %collective-permute-start.47 = (bf16[64,4224]{1,0:T(8,128)(2,1)S(1)}, bf16[64,4224]{1,0:T(8,128)(2,1)}, u32[]{:S(2)}, u32[]{:S(2)}) collective-permute-start(bf16[64,4224]{1,0:T(8,128)(2,1)S(1)} %get-tuple-element.370), channel_id=1, source_target_pairs={{0,2},{1,3},{2,0},{3,1},{4,6},{5,7},{6,4},{7,5},{8,10},{9,11},{10,... | collective-permute-start | bytes 1622024 | tf_op jit(solution)/shard_map/ppermute | solution.py:58
  197.5 26.8 %collective-permute-start.50 = (bf16[64,4224]{1,0:T(8,128)(2,1)}, bf16[64,4224]{1,0:T(8,128)(2,1)}, u32[]{:S(2)}, u32[]{:S(2)}) collective-permute-start(bf16[64,4224]{1,0:T(8,128)(2,1)} %get-tuple-element.219), channel_id=1, source_target_pairs={{0,3},{1,2},{2,1},{3,0},{4,7},{5,6},{6,5},{7,4},{8,11},{9,10},{10,... | collective-permute-start | bytes 1622024 | tf_op jit(solution)/shard_map/ppermute | solution.py:58
  280.2 98.4 %all-to-all-start.2 = ((bf16[8,1056,256]{2,1,0:T(8,128)(2,1)}), bf16[8,1056,256]{2,1,0:T(8,128)(2,1)}, u32[]{:S(2)}, u32[]{:S(2)}) async-start(bf16[8,1056,256]{2,1,0:T(8,128)(2,1)} %pad_maximum_fusion), calls=%async_computation.2 | async-start | bytes 8650752 | tf_op jit(solution)/shard_map/all_to_all | solution.py:768
  290.9 24.7 %collective-permute-start.76 = (bf16[128,2048]{1,0:T(8,128)(2,1)}, bf16[128,2048]{1,0:T(8,128)(2,1)S(1)}, u32[]{:S(2)}, u32[]{:S(2)}) collective-permute-start(bf16[128,2048]{1,0:T(8,128)(2,1)} %collective-permute-done.57.refs_24_), channel_id=1, source_target_pairs={{0,2},{1,3},{2,0},{3,1},{4,6},{5,7},{6,4},{7,5},{8,10},{9,11},{10,... | collective-permute-start | bytes 1572872 | tf_op jit(solution)/shard_map/ppermute | solution.py:58
  291.4 24.2 %collective-permute-start.67 = (bf16[128,2048]{1,0:T(8,128)(2,1)}, bf16[128,2048]{1,0:T(8,128)(2,1)S(1)}, u32[]{:S(2)}, u32[]{:S(2)}) collective-permute-start(bf16[128,2048]{1,0:T(8,128)(2,1)} %collective-permute-done.58.refs_12_), channel_id=1, source_target_pairs={{0,1},{1,0},{2,3},{3,2},{4,5},{5,4},{6,7},{7,6},{8,9},{9,8},{10,11... | collective-permute-start | bytes 1572872 | tf_op jit(solution)/shard_map/ppermute | solution.py:58
  292.2 23.9 %collective-permute-start.70 = (bf16[128,2048]{1,0:T(8,128)(2,1)}, bf16[128,2048]{1,0:T(8,128)(2,1)S(1)}, u32[]{:S(2)}, u32[]{:S(2)}) collective-permute-start(bf16[128,2048]{1,0:T(8,128)(2,1)} %collective-permute-done.56.refs_17_), channel_id=1, source_target_pairs={{0,1},{1,0},{2,3},{3,2},{4,5},{5,4},{6,7},{7,6},{8,9},{9,8},{10,11... | collective-permute-start | bytes 1572872 | tf_op jit(solution)/shard_map/ppermute | solution.py:58
  293.8 22.4 %collective-permute-start.74 = (bf16[128,2048]{1,0:T(8,128)(2,1)}, bf16[128,2048]{1,0:T(8,128)(2,1)S(1)}, u32[]{:S(2)}, u32[]{:S(2)}) collective-permute-start(bf16[128,2048]{1,0:T(8,128)(2,1)} %collective-permute-done.57.refs_24_), channel_id=1, source_target_pairs={{0,1},{1,0},{2,3},{3,2},{4,5},{5,4},{6,7},{7,6},{8,9},{9,8},{10,11... | collective-permute-start | bytes 1572872 | tf_op jit(solution)/shard_map/ppermute | solution.py:58
  378.6 56.4 %all-to-all-start.3 = ((bf16[8,528,256]{2,1,0:T(8,128)(2,1)}), bf16[8,528,256]{2,1,0:T(8,128)(2,1)S(1)}, u32[]{:S(2)}, u32[]{:S(2)}) async-start(bf16[8,528,256]{2,1,0:T(8,128)(2,1)} %get-tuple-element.248), calls=%async_computation.3 | async-start | bytes 4325376 | tf_op jit(solution)/shard_map/all_to_all | solution.py:768
  446.2 48.3 %collective-permute-start.83 = (bf16[1024,2048]{1,0:T(8,128)(2,1)}, bf16[1024,2048]{1,0:T(8,128)(2,1)}, u32[]{:S(2)}, u32[]{:S(2)}) collective-permute-start(bf16[1024,2048]{1,0:T(8,128)(2,1)} %get-tuple-element.262), channel_id=1, source_target_pairs={{0,1},{1,0},{2,3},{3,2},{4,5},{5,4},{6,7},{7,6},{8,9},{9,8},{10,11... | collective-permute-start | bytes 12582920 | tf_op jit(solution)/shard_map/ppermute | solution.py:58
  446.4 42.6 %collective-permute-start.81 = (bf16[256,2048]{1,0:T(8,128)(2,1)}, bf16[256,2048]{1,0:T(8,128)(2,1)S(1)}, u32[]{:S(2)}, u32[]{:S(2)}) collective-permute-start(bf16[256,2048]{1,0:T(8,128)(2,1)} %get-tuple-element.253), channel_id=1, source_target_pairs={{0,2},{1,3},{2,0},{3,1},{4,6},{5,7},{6,4},{7,5},{8,10},{9,11},{10,... | collective-permute-start | bytes 3145736 | tf_op jit(solution)/shard_map/ppermute | solution.py:58
  446.7 47.8 %collective-permute-start.82 = (bf16[256,2048]{1,0:T(8,128)(2,1)}, bf16[256,2048]{1,0:T(8,128)(2,1)S(1)}, u32[]{:S(2)}, u32[]{:S(2)}) collective-permute-start(bf16[256,2048]{1,0:T(8,128)(2,1)} %get-tuple-element.254), channel_id=1, source_target_pairs={{0,2},{1,3},{2,0},{3,1},{4,6},{5,7},{6,4},{7,5},{8,10},{9,11},{10,... | collective-permute-start | bytes 3145736 | tf_op jit(solution)/shard_map/ppermute | solution.py:58
  494.5 51.4 %collective-permute-start.90 = (bf16[1024,2048]{1,0:T(8,128)(2,1)}, bf16[1024,2048]{1,0:T(8,128)(2,1)}, u32[]{:S(2)}, u32[]{:S(2)}) collective-permute-start(bf16[1024,2048]{1,0:T(8,128)(2,1)} %get-tuple-element.280), channel_id=1, source_target_pairs={{0,1},{1,0},{2,3},{3,2},{4,5},{5,4},{6,7},{7,6},{8,9},{9,8},{10,11... | collective-permute-start | bytes 12582920 | tf_op jit(solution)/shard_map/ppermute | solution.py:58
  510.4 35.5 %collective-permute-start.89 = (bf16[128,2048]{1,0:T(8,128)(2,1)S(1)}, bf16[128,2048]{1,0:T(8,128)(2,1)}, u32[]{:S(2)}, u32[]{:S(2)}) collective-permute-start(bf16[128,2048]{1,0:T(8,128)(2,1)S(1)} %add_convert_fusion.30), channel_id=1, source_target_pairs={{0,8},{1,9},{2,10},{3,11},{4,12},{5,13},{6,14},{7,15},{8,24},{9,25... | collective-permute-start | bytes 1572872 | tf_op jit(solution)/shard_map/ppermute | solution.py:58
  511.4 34.5 %collective-permute-start.87 = (bf16[256,2048]{1,0:T(8,128)(2,1)}, bf16[256,2048]{1,0:T(8,128)(2,1)}, u32[]{:S(2)}, u32[]{:S(2)}) collective-permute-start(bf16[256,2048]{1,0:T(8,128)(2,1)} %get-tuple-element.273), channel_id=1, source_target_pairs={{0,2},{1,3},{2,0},{3,1},{4,6},{5,7},{6,4},{7,5},{8,10},{9,11},{10,... | collective-permute-start | bytes 3145736 | tf_op jit(solution)/shard_map/ppermute | solution.py:58
  512.5 33.4 %collective-permute-start.88 = (bf16[128,2048]{1,0:T(8,128)(2,1)}, bf16[128,2048]{1,0:T(8,128)(2,1)}, u32[]{:S(2)}, u32[]{:S(2)}) collective-permute-start(bf16[128,2048]{1,0:T(8,128)(2,1)} %slice.231), channel_id=1, source_target_pairs={{0,4},{1,5},{2,6},{3,7},{4,0},{5,1},{6,2},{7,3},{8,12},{9,13},{10,... | collective-permute-start | bytes 1572872 | tf_op jit(solution)/shard_map/ppermute | solution.py:58
  514.0 45.1 %collective-permute-start.86 = (bf16[256,2048]{1,0:T(8,128)(2,1)S(1)}, bf16[256,2048]{1,0:T(8,128)(2,1)}, u32[]{:S(2)}, u32[]{:S(2)}) collective-permute-start(bf16[256,2048]{1,0:T(8,128)(2,1)S(1)} %get-tuple-element.271), channel_id=1, source_target_pairs={{0,2},{1,3},{2,0},{3,1},{4,6},{5,7},{6,4},{7,5},{8,10},{9,11},{10,... | collective-permute-start | bytes 3145736 | tf_op jit(solution)/shard_map/ppermute | solution.py:58
  590.3 102.4 %all-to-all-start.4 = ((bf16[8,1056,256]{2,1,0:T(8,128)(2,1)}), bf16[8,1056,256]{2,1,0:T(8,128)(2,1)}, u32[]{:S(2)}, u32[]{:S(2)}) async-start(bf16[8,1056,256]{2,1,0:T(8,128)(2,1)} %get-tuple-element.312), calls=%async_computation.4 | async-start | bytes 8650752 | tf_op jit(solution)/shard_map/all_to_all | solution.py:936
  604.5 28.2 %collective-permute-start.96 = (bf16[256,2048]{1,0:T(8,128)(2,1)}, bf16[256,2048]{1,0:T(8,128)(2,1)}, u32[]{:S(2)}, u32[]{:S(2)}) collective-permute-start(bf16[256,2048]{1,0:T(8,128)(2,1)} %get-tuple-element.293), channel_id=1, source_target_pairs={{0,2},{1,3},{2,0},{3,1},{4,6},{5,7},{6,4},{7,5},{8,10},{9,11},{10,... | collective-permute-start | bytes 3145736 | tf_op jit(solution)/shard_map/ppermute | solution.py:58
  633.7 25.6 %collective-permute-start.95 = (bf16[256,2048]{1,0:T(8,128)(2,1)}, bf16[256,2048]{1,0:T(8,128)(2,1)S(1)}, u32[]{:S(2)}, u32[]{:S(2)}) collective-permute-start(bf16[256,2048]{1,0:T(8,128)(2,1)} %get-tuple-element.292), channel_id=1, source_target_pairs={{0,2},{1,3},{2,0},{3,1},{4,6},{5,7},{6,4},{7,5},{8,10},{9,11},{10,... | collective-permute-start | bytes 3145736 | tf_op jit(solution)/shard_map/ppermute | solution.py:58
  660.7 26.1 %collective-permute-start.107 = (bf16[128,2048]{1,0:T(8,128)(2,1)}, bf16[128,2048]{1,0:T(8,128)(2,1)}, u32[]{:S(2)}, u32[]{:S(2)}) collective-permute-start(bf16[128,2048]{1,0:T(8,128)(2,1)} %get-tuple-element.372), channel_id=1, source_target_pairs={{0,2},{1,3},{2,0},{3,1},{4,6},{5,7},{6,4},{7,5},{8,10},{9,11},{10,... | collective-permute-start | bytes 1572872 | tf_op jit(solution)/shard_map/ppermute | solution.py:58
  662.5 47.0 %collective-permute-start.105 = (bf16[256,2048]{1,0:T(8,128)(2,1)}, bf16[256,2048]{1,0:T(8,128)(2,1)}, u32[]{:S(2)}, u32[]{:S(2)}) collective-permute-start(bf16[256,2048]{1,0:T(8,128)(2,1)} %get-tuple-element.310), channel_id=1, source_target_pairs={{0,2},{1,3},{2,0},{3,1},{4,6},{5,7},{6,4},{7,5},{8,10},{9,11},{10,... | collective-permute-start | bytes 3145736 | tf_op jit(solution)/shard_map/ppermute | solution.py:58
  662.9 73.1 %collective-permute-start.113 = (bf16[256,2048]{1,0:T(8,128)(2,1)}, bf16[256,2048]{1,0:T(8,128)(2,1)}, u32[]{:S(2)}, u32[]{:S(2)}) collective-permute-start(bf16[256,2048]{1,0:T(8,128)(2,1)} %get-tuple-element.318), channel_id=1, source_target_pairs={{0,2},{1,3},{2,0},{3,1},{4,6},{5,7},{6,4},{7,5},{8,10},{9,11},{10,... | collective-permute-start | bytes 3145736 | tf_op jit(solution)/shard_map/ppermute | solution.py:58
  665.7 45.9 %collective-permute-start.109 = (bf16[512,1024]{1,0:T(8,128)(2,1)}, bf16[512,1024]{1,0:T(8,128)(2,1)}, u32[]{:S(2)}, u32[]{:S(2)}) collective-permute-start(bf16[512,1024]{1,0:T(8,128)(2,1)} %dynamic-slice_bitcast_fusion), channel_id=1, source_target_pairs={{0,8},{1,9},{2,10},{3,11},{4,12},{5,13},{6,14},{7,15},{8,24},{9,25... | collective-permute-start | bytes 3145736 | tf_op jit(solution)/shard_map/ppermute | solution.py:58
  675.6 36.0 %collective-permute-start.110 = (bf16[128,2048]{1,0:T(8,128)(2,1)}, bf16[128,2048]{1,0:T(8,128)(2,1)}, u32[]{:S(2)}, u32[]{:S(2)}) collective-permute-start(bf16[128,2048]{1,0:T(8,128)(2,1)} %slice.257), channel_id=1, source_target_pairs={{0,4},{1,5},{2,6},{3,7},{4,0},{5,1},{6,2},{7,3},{8,12},{9,13},{10,... | collective-permute-start | bytes 1572872 | tf_op jit(solution)/shard_map/ppermute | solution.py:58
  705.7 59.7 %all-to-all-start.5 = ((bf16[4,64,4224]{2,1,0:T(8,128)(2,1)}), bf16[4,64,4224]{2,1,0:T(8,128)(2,1)S(1)}, u32[]{:S(2)}, u32[]{:S(2)}) async-start(bf16[4,64,4224]{2,1,0:T(8,128)(2,1)} %bitcast.89), calls=%async_computation.5 | async-start | bytes 4325376 | tf_op jit(solution)/shard_map/all_to_all | solution.py:1011
  709.5 26.5 %collective-permute-start.112 = (bf16[128,2048]{1,0:T(8,128)(2,1)}, bf16[128,2048]{1,0:T(8,128)(2,1)}, u32[]{:S(2)}, u32[]{:S(2)}) collective-permute-start(bf16[128,2048]{1,0:T(8,128)(2,1)} %slice.308), channel_id=1, source_target_pairs={{0,4},{1,5},{2,6},{3,7},{4,0},{5,1},{6,2},{7,3},{8,12},{9,13},{10,... | collective-permute-start | bytes 1572872 | tf_op jit(solution)/shard_map/ppermute | solution.py:58
  715.9 26.9 %collective-permute-start.111 = (bf16[512,1024]{1,0:T(8,128)(2,1)S(1)}, bf16[512,1024]{1,0:T(8,128)(2,1)S(1)}, u32[]{:S(2)}, u32[]{:S(2)}) collective-permute-start(bf16[512,1024]{1,0:T(8,128)(2,1)S(1)} %fusion.2), channel_id=1, source_target_pairs={{0,8},{1,9},{2,10},{3,11},{4,12},{5,13},{6,14},{7,15},{8,24},{9,25... | collective-permute-start | bytes 3145736 | tf_op jit(solution)/shard_map/ppermute | solution.py:58
  735.5 22.6 %collective-permute-start.120 = (bf16[64,2048]{1,0:T(8,128)(2,1)S(1)}, bf16[64,2048]{1,0:T(8,128)(2,1)S(1)}, u32[]{:S(2)}, u32[]{:S(2)}) collective-permute-start(bf16[64,2048]{1,0:T(8,128)(2,1)S(1)} %get-tuple-element.380), channel_id=1, source_target_pairs={{0,8},{1,9},{2,10},{3,11},{4,12},{5,13},{6,14},{7,15},{8,24},{9,25... | collective-permute-start | bytes 786440 | tf_op jit(solution)/shard_map/ppermute | solution.py:58
  735.6 22.5 %collective-permute-start.123 = (bf16[64,2048]{1,0:T(8,128)(2,1)S(1)}, bf16[64,2048]{1,0:T(8,128)(2,1)S(1)}, u32[]{:S(2)}, u32[]{:S(2)}) collective-permute-start(bf16[64,2048]{1,0:T(8,128)(2,1)S(1)} %get-tuple-element.381), channel_id=1, source_target_pairs={{0,8},{1,9},{2,10},{3,11},{4,12},{5,13},{6,14},{7,15},{8,24},{9,25... | collective-permute-start | bytes 786440 | tf_op jit(solution)/shard_map/ppermute | solution.py:58
  747.1 29.5 %collective-permute-start.115 = (bf16[512,1024]{1,0:T(8,128)(2,1)}, bf16[512,1024]{1,0:T(8,128)(2,1)}, u32[]{:S(2)}, u32[]{:S(2)}) collective-permute-start(bf16[512,1024]{1,0:T(8,128)(2,1)} %fusion.1), channel_id=1, source_target_pairs={{0,8},{1,9},{2,10},{3,11},{4,12},{5,13},{6,14},{7,15},{8,24},{9,25... | collective-permute-start | bytes 3145736 | tf_op jit(solution)/shard_map/ppermute | solution.py:58
  759.0 32.2 %collective-permute-start.121 = (bf16[64,2048]{1,0:T(8,128)(2,1)}, bf16[64,2048]{1,0:T(8,128)(2,1)}, u32[]{:S(2)}, u32[]{:S(2)}) collective-permute-start(bf16[64,2048]{1,0:T(8,128)(2,1)} %get-tuple-element.378), channel_id=1, source_target_pairs={{0,8},{1,9},{2,10},{3,11},{4,12},{5,13},{6,14},{7,15},{8,24},{9,25... | collective-permute-start | bytes 786440 | tf_op jit(solution)/shard_map/ppermute | solution.py:58
  760.6 30.6 %collective-permute-start.124 = (bf16[64,2048]{1,0:T(8,128)(2,1)}, bf16[64,2048]{1,0:T(8,128)(2,1)}, u32[]{:S(2)}, u32[]{:S(2)}) collective-permute-start(bf16[64,2048]{1,0:T(8,128)(2,1)} %get-tuple-element.379), channel_id=1, source_target_pairs={{0,8},{1,9},{2,10},{3,11},{4,12},{5,13},{6,14},{7,15},{8,24},{9,25... | collective-permute-start | bytes 786440 | tf_op jit(solution)/shard_map/ppermute | solution.py:58
  779.7 33.6 %all-to-all-start.6 = ((bf16[8,64,1024]{2,1,0:T(8,128)(2,1)}), bf16[8,64,1024]{2,1,0:T(8,128)(2,1)S(1)}, u32[]{:S(2)}, u32[]{:S(2)}) async-start(bf16[8,64,1024]{2,1,0:T(8,128)(2,1)} %bitcast.87), calls=%async_computation.6 | async-start | bytes 2097152 | tf_op jit(solution)/shard_map/all_to_all | solution.py:1033
  (182 other events, 1994.4 us)

commit v5 on v4

--- a/solution.py
+++ b/solution.py
@@ -208,25 +208,33 @@
 
 
 def first_kernel(groups, units, experts, count, where_ref, *refs):
-    pieces, refs = refs[:count], refs[count:]
-    cots_ref, gate_ref, down_ref, rows_ref, hidden_ref, grad_ref, out_ref, router_ref, gate_sums, down_sums, held, sems = refs
+    pieces, cot_pieces, refs = refs[:count], refs[count : 2 * count], refs[2 * count :]
+    gate_ref, down_ref, rows_ref, cots_ref, hidden_ref, grad_ref, out_ref, router_ref, *scratch = refs
+    gate_sums, down_sums, held, held_cots, sems = scratch
     step, steps = pl.program_id(0), pl.num_programs(0)
     each, size = held.shape[1] // pieces[0].shape[0], pieces[0].shape[0]
 
-    def copy(piece, slot, t):
-        return pltpu.make_async_copy(piece, held.at[slot, pl.ds(t * size, size)], sems.at[slot, t])
+    def copies(at, slot, t):
+        place = pl.ds(t * size, size)
+        return (
+            pltpu.make_async_copy(pieces[at], held.at[slot, place], sems.at[slot, t]),
+            pltpu.make_async_copy(cot_pieces[at], held_cots.at[slot, place], sems.at[slot, each + t]),
+        )
 
     for j in range(count // each):
 
         @pl.when(step == max(j - 1, 0))
         def _(j=j):
             for t in range(each):
-                copy(pieces[j * each + t], j % 2, t).start()
+                for copy in copies(j * each + t, j % 2, t):
+                    copy.start()
 
     slot = lax.rem(step, 2)
     for t in range(each):
-        copy(pieces[t], slot, t).wait()
+        for copy in copies(t, slot, t):
+            copy.wait()
     rows_ref[...] = held[slot]
+    cots_ref[...] = held_cots[slot]
     gated, grad = group_pass(groups, units, experts, where_ref, rows_ref, cots_ref, gate_ref, down_ref)
     hidden_ref[...] = gated
     grad_ref[...] = grad
@@ -286,30 +294,32 @@
     return rows.shape[0] // tile, tile, [among_all(rows.shape[1], tile), among_all(cots.shape[1], tile)]
 
 
-def first_units(groups, where, pieces, cots, gate_rows, down_rows, units, experts, count):
-    total, width = cots.shape[0], gate_rows.shape[1]
+def first_units(groups, where, pieces, cot_pieces, gate_rows, down_rows, units, experts, count):
+    total, width, wider = sum(v.shape[0] for v in pieces), gate_rows.shape[1], cot_pieces[0].shape[1]
     pad = down_rows.shape[0]
     wide = units * len(groups)
     tile = 512
     shapes = grads_out(wide, pad, width, count)
-    rows, hidden, grad, weights, router = pl.pallas_call(
+    rows, cots, hidden, grad, weights, router = pl.pallas_call(
         functools.partial(first_kernel, groups, units, experts, len(pieces)),
         grid_spec=pltpu.PrefetchScalarGridSpec(
             num_scalar_prefetch=1,
             grid=(total // tile,),
-            in_specs=[pl.BlockSpec(memory_space=pl.ANY)] * len(pieces)
-            + [among_all(cots.shape[1], tile), all_of(gate_rows.shape), all_of(down_rows.shape)],
-            out_specs=[among_all(width, tile), among_all(pad, tile), among_all(2 * pad, tile)]
+            in_specs=[pl.BlockSpec(memory_space=pl.ANY)] * (2 * len(pieces))
+            + [all_of(gate_rows.shape), all_of(down_rows.shape)],
+            out_specs=[among_all(width, tile), among_all(wider, tile), among_all(pad, tile), among_all(2 * pad, tile)]
             + [all_of(shape) for shape in shapes],
             scratch_shapes=[
                 pltpu.VMEM((2 * pad, width), f32),
                 pltpu.VMEM((pad, width), f32),
                 pltpu.VMEM((2, tile, width), bf16),
-                pltpu.SemaphoreType.DMA((2, tile // pieces[0].shape[0])),
+                pltpu.VMEM((2, tile, wider), bf16),
+                pltpu.SemaphoreType.DMA((2, 2 * tile // pieces[0].shape[0])),
             ],
         ),
         out_shape=[
             jax.ShapeDtypeStruct((total, width), bf16),
+            jax.ShapeDtypeStruct((total, wider), bf16),
             jax.ShapeDtypeStruct((total, pad), bf16),
             jax.ShapeDtypeStruct((total, 2 * pad), bf16),
             jax.ShapeDtypeStruct(shapes[0], bf16),
@@ -317,8 +327,8 @@
         ],
         compiler_params=pltpu.CompilerParams(vmem_limit_bytes=60 * 1024 * 1024),
         cost_estimate=pl.CostEstimate(flops=12 * total * width * pad, bytes_accessed=4 * total * width, transcendentals=0),
-    )(where, *pieces, cots, gate_rows, down_rows)
-    return rows, hidden, grad, to_owners(weights, wide, count), router
+    )(where, *pieces, *cot_pieces, gate_rows, down_rows)
+    return rows, cots, hidden, grad, to_owners(weights, wide, count), router
 
 
 def weight_grads(where, rows, cots, hidden, grad, wide, count):
@@ -699,11 +709,10 @@
     turn = (own_expert + jnp.arange(expert_count, dtype=jnp.int32)) % expert_count
     router = stack(jnp.take(router, turn, axis=0), router[expert_count:])
     slot = pair * 4 + ep
-    bias_share = lax.dynamic_slice_in_dim(qkv_bias.astype(f32).reshape(3, 8, share), slot, 1, 1).reshape(1, 3 * share)
+    bias_share = lax.dynamic_slice_in_dim(qkv_bias.astype(f32).reshape(3, 8, share), slot, 1, 1, allow_negative_indices=False).reshape(1, 3 * share)
     plane_part, cot_blocks[-1], routed, normed = together(plane_part, cot_blocks[-1], routed, normed)
 
     qkv = [plane_part, permute(plane_part, lay.onward)]
-    cot_blocks.append(permute(cot_blocks[-1], lay.onward))
     side, up = permute(normed, lay.side), permute(normed, lay.up)
 
     def between_cores(*pieces):
@@ -713,11 +722,15 @@
         return [permute(piece, pairs) for piece in pieces]
 
     cot_sides, cot_ups = over(lay.side, cot_blocks[:1]), over(lay.up, cot_blocks[:1])
-    cot_cores = between_cores(*cot_blocks)
     first_ffn, second_ffn = (turn_weights(routed, local_experts, dp_count, w) for w in range(local_experts))
-    qkv[-1], cot_blocks[-1], side, up, cot_sides, cot_ups, cosine, sine, first_ffn, second_ffn = lax.optimization_barrier(
-        (qkv[-1], cot_blocks[-1], side, up, cot_sides, cot_ups, cosine, sine, first_ffn, second_ffn)
+    qkv[-1], side, up, cot_sides, cot_ups, cosine, sine, first_ffn, second_ffn = lax.optimization_barrier(
+        (qkv[-1], side, up, cot_sides, cot_ups, cosine, sine, first_ffn, second_ffn)
     )
+    cot_crosses = []
+
+    def crossing(s):
+        return permute(cot_sides[s], lay.up) if s % 2 else permute(cot_ups[s], lay.side)
+
     for s in range(2, rings):
         qkv.append(permute(qkv[-1], lay.onward))
         sides, ups = [], []
@@ -730,13 +743,13 @@
             cores += between_cores(cross)
             normed_group = assemble((normed, side, *cores[:2], up, cross, *cores[2:]))
             sides, ups = over(lay.side, cot_blocks[2:]), over(lay.up, cot_blocks[3:])
-        sides, ups, qkv[-1] = lax.optimization_barrier((sides, ups, qkv[-1]))
+            cot_crosses = [crossing(0), crossing(1)]
+        sides, ups, qkv[-1], cot_crosses = lax.optimization_barrier((sides, ups, qkv[-1], cot_crosses))
         cot_sides, cot_ups = cot_sides + sides, cot_ups + ups
     qkv[-1], normed_group = together(qkv[-1], normed_group)
 
-    cot_crosses = [
-        permute(cot_sides[s], lay.up) if s % 2 else permute(cot_ups[s], lay.side) for s in range(rings)
-    ]
+    cot_blocks.append(permute(after(cot_blocks[-1], qkv[-1]), lay.onward))
+    cot_crosses += [crossing(s) for s in range(2, rings - 1)]
     heads_flops = 8 * heads * group_len * group_len * HD
     packed, mixed = group_call(
         functools.partial(attend_kernel, heads),
@@ -749,7 +762,10 @@
         [bf16, bf16],
         4 * group_len * model_width * 3 * share + heads_flops,
     )
-    received = [lax.dynamic_index_in_dim(shared, ep ^ k, 0, keepdims=False) for k in range(4)]
+    packed, mixed, cot_crosses, cot_blocks = lax.optimization_barrier((packed, mixed, cot_crosses, cot_blocks))
+    cot_sides += over(lay.side, cot_blocks[-1:])
+    cot_ups += over(lay.up, cot_blocks[-1:])
+    received = [lax.dynamic_index_in_dim(shared, ep ^ k, 0, keepdims=False, allow_negative_indices=False) for k in range(4)]
     received[1:3] = [permute(v, pairs) for v, pairs in zip(received[1:3], (lay.core, lay.side))]
     branch_parts = group_call(
         project_kernel,
@@ -762,23 +778,18 @@
         [bf16, bf16],
         4 * group_len * model_width * share,
     )
-    *branch_parts, cot_crosses, first_ffn = lax.optimization_barrier((*branch_parts, cot_crosses, first_ffn))
 
     def to_units(ffn):
         return lax.all_to_all(ffn, ("ring", "pair"), split_axis=0, concat_axis=0, tiled=True)
 
-    first_ffn = to_units(first_ffn)
+    first_ffn = to_units(after(first_ffn, packed))
     here = plus(branch_parts[0], permute(branch_parts[1], lay.core))
     cross, side = permute(here[3 * n :], lay.side), permute(here[n : 2 * n], lay.side)
-    cots = []
-    for s in range(rings):
-        cores = [cot_cores[s]] + between_cores(cot_ups[s], cot_sides[s], cot_crosses[s])
-        cots += [cot_blocks[s], cot_ups[s], *cores[:2], cot_sides[s], cot_crosses[s], *cores[2:]]
-    cots = assemble(cots)
-    cross, cots = together(cross, cots)
     received[3] = permute(after(received[3], cross), lay.side_core)
     up = permute(plus(here[2 * n : 3 * n], cross), lay.up)
+    up, cot_sides, cot_ups = lax.optimization_barrier((up, cot_sides, cot_ups))
     branch = here[:n].astype(f32) + side.astype(f32) + after(up, first_ffn, *received[:3]).astype(f32)
+    cot_crosses.append(permute(cot_ups[-1], lay.side))
     residual = stream + branch
     inverse_two = lax.rsqrt(jnp.mean(residual * residual, axis=1, keepdims=True) + norm_eps)
     normed_two = (residual * inverse_two * gain_two).astype(bf16)
@@ -794,6 +805,8 @@
             going["received"] = received[3]
         else:
             going["side"] = permute(blocks[s - 1], lay.side)
+        if s == 1:
+            going["crosses_too"] = cot_crosses
         if s == rings - 2:
             first_rows = place_weights(first_ffn, router)
             going["first_rows"] = first_rows
@@ -809,6 +822,8 @@
             blocks.append(going["onward"])
         if "side" in going:
             sides.append(going["side"])
+        if "crosses_too" in going:
+            cot_crosses = going["crosses_too"]
         if "received" in going:
             received[3] = going["received"]
         if "first_rows" in going:
@@ -817,16 +832,24 @@
             crosses, second_ffn = going["crosses"], going["second_ffn"]
     second_ffn = to_units(second_ffn)
     sides.append(permute(blocks[-1], lay.side))
-    crosses.update({k: permute(ups[k], lay.side) for k in range(rings) if k not in crosses})
-    inner = [between_cores(blocks[s], ups[s], sides[s]) for s in range(rings)]
+    crosses.update({k: permute(ups[k], lay.side) for k in range(2, rings - 1) if k not in crosses})
+    cots = list(zip(cot_blocks, cot_ups, cot_sides, cot_crosses))
+    cot_cores = [between_cores(*v) for v in cots]
+    inner = [between_cores(blocks[s], ups[s], sides[s]) for s in range(rings - 1)]
+    sides[-1], ups[-1], crosses, cot_cores, inner = lax.optimization_barrier((sides[-1], ups[-1], crosses, cot_cores, inner))
+    crosses[rings - 1] = permute(ups[-1], lay.side)
+    inner.append(between_cores(blocks[-1], ups[-1], sides[-1]))
+    cot_pieces = []
+    for (block, up, side, cross), cores in zip(cots, cot_cores):
+        cot_pieces += [block, up, *cores[:2], side, cross, *cores[2:]]
     rows = []
     for s in range(rings):
         cores = inner[s] + between_cores(crosses[s])
         rows += [blocks[s], ups[s], *cores[:2], sides[s], crosses[s], *cores[2:]]
 
     late = rings // 2
-    rows, first_hidden, first_grad, first_weights_grad, first_router = first_units(
-        (0,), where, rows, cots, *first_rows, units, expert_count, dp_count
+    rows, cots, first_hidden, first_grad, first_weights_grad, first_router = first_units(
+        (0,), where, rows, cot_pieces, *first_rows, units, expert_count, dp_count
     )
     first_weights_grad = to_units(first_weights_grad)
     second_rows = place_weights(after(second_ffn, first_hidden), router)
@@ -856,21 +879,43 @@
     out_own_a, out_far_a, own_a, far_a, hidden, gate_up_grad = ffn_half(late, rings - late, ())
     own_a, far_a, first_weights_grad = all_there(own_a, far_a, first_weights_grad)
 
-    keep, send = crossed(own_a, permute(far_a, lay.core), first_half)
+    pair_first = order[1::2]
+
+    def link(s, second):
+        return lay.side if (s in pair_first) == second else lay.up
+
+    def split(part, there, some):
+        keep, send = crossed(part, there, [s for s in some if s not in pair_first])
+        for s in some:
+            if s in pair_first:
+                pieces = [plus(*(cut_chunk(v, s, t * n)[:n] for v in (part, there))) for t in range(4)]
+                keep[s], send[s] = stack(pieces[0], pieces[2]), stack(pieces[1], pieces[3])
+        return keep, send
+
+    def start(send, some):
+        return {s: permute(send[s], link(s, False)) for s in some}
+
+    def go_on(keep, arrived, some):
+        halves = {s: plus(keep[s], arrived[s]) for s in some}
+        return halves, {s: permute(halves[s][n:], link(s, True)) for s in some}
+
+    def finish(halves, arrived):
+        return {s: halves[s][:n].astype(f32) + arrived[s].astype(f32) for s in halves}
+
+    keep, send = split(own_a, permute(far_a, lay.core), first_half)
     keep, send, hidden, gate_up_grad = all_there(keep, send, hidden, gate_up_grad)
     out_there_a = permute(after(out_far_a, hidden), lay.core)
-    sided = {s: permute(send[s], lay.side) for s in first_half}
+    arrived = start(send, first_half)
     out_own_b, out_far_b, own_b, far_b, hidden, gate_up_grad = ffn_half(0, late, (hidden, gate_up_grad))
-    sided, own_b, far_b, hidden, gate_up_grad, out_there_a = all_there(
-        sided, own_b, far_b, hidden, gate_up_grad, out_there_a
+    arrived, own_b, far_b, hidden, gate_up_grad, out_there_a = all_there(
+        arrived, own_b, far_b, hidden, gate_up_grad, out_there_a
     )
 
     far_there = permute(far_b, lay.core)
-    halves = {s: plus(keep[s], sided[s]) for s in first_half}
-    upped = {order[0]: permute(halves[order[0]][n:], lay.up)}
-    keep, send = crossed(own_b, far_there, last_half)
-    keep, send, halves, hidden, upped = all_there(keep, send, halves, hidden, upped)
-    own_sums = {order[0]: halves[order[0]][:n].astype(f32) + upped[order[0]].astype(f32)}
+    halves, arrived = go_on(keep, arrived, first_half)
+    keep, send = split(own_b, far_there, last_half)
+    keep, send, halves, arrived, hidden = all_there(keep, send, halves, arrived, hidden)
+    own_sums = finish(halves, arrived)
     total = own_sums[order[0]]
     queue = list(order[1:])
 
@@ -880,33 +925,25 @@
     def step_in(arrived):
         return own_sums[queue.pop(0)] + arrived.astype(f32)
 
-    few = (len(last_half) + 1) // 2
-    sided = {s: permute(send[s], lay.side) for s in last_half[:few]}
-    upped = {s: permute(halves[s][n:], lay.up) for s in first_half[1:]}
+    arrived = start(send, last_half)
     moving = step_on(total)
     ffn_grad, second_router = weight_grads(where, rows, cots, hidden, gate_up_grad, 2 * units, dp_count)
     out_there_b = permute(out_far_b, lay.core)
-    sided, upped, moving, ffn_grad, out_there_b = all_there(sided, upped, moving, ffn_grad, out_there_b)
-    own_sums.update({s: halves[s][:n].astype(f32) + upped[s].astype(f32) for s in first_half[1:]})
+    arrived, moving, ffn_grad, out_there_b = all_there(arrived, moving, ffn_grad, out_there_b)
     total = step_in(moving)
 
-    halves = {s: plus(keep[s], sided[s]) for s in last_half[:few]}
-    sided = {s: permute(send[s], lay.side) for s in last_half[few:]}
-    upped = {s: permute(halves[s][n:], lay.up) for s in last_half[:few]}
+    halves, arrived = go_on(keep, arrived, last_half)
     moving = step_on(total)
     out_keep, out_send = crossed(out_own_a, out_there_a, first_half)
-    sided, upped, moving, out_keep, out_send = all_there(sided, upped, moving, out_keep, out_send)
-    own_sums.update({s: halves[s][:n].astype(f32) + upped[s].astype(f32) for s in last_half[:few]})
+    halves, arrived, moving, out_keep, out_send = all_there(halves, arrived, moving, out_keep, out_send)
+    own_sums.update(finish(halves, arrived))
     total = step_in(moving)
 
-    halves = {s: plus(keep[s], sided[s]) for s in last_half[few:]}
-    upped = {s: permute(halves[s][n:], lay.up) for s in last_half[few:]}
     moving = step_on(total)
     more_keep, more_send = crossed(out_own_b, out_there_b, last_half)
-    upped, moving, more_keep, more_send = all_there(upped, moving, more_keep, more_send)
+    moving, more_keep, more_send = all_there(moving, more_keep, more_send)
     out_keep.update(more_keep)
     out_send.update(more_send)
-    own_sums.update({s: halves[s][:n].astype(f32) + upped[s].astype(f32) for s in last_half[few:]})
     total = step_in(moving)
     while queue:
         total = step_in(step_on(total))
@@ -967,7 +1004,7 @@
     out_halves.update(halves)
     side, cross = permute(here[n : 2 * n], lay.side), permute(here[3 * n :], lay.side)
     def grads_at(s):
-        return lax.dynamic_index_in_dim(attn_grads, behind[s], 0, keepdims=False).astype(f32)
+        return lax.dynamic_index_in_dim(attn_grads, behind[s], 0, keepdims=False, allow_negative_indices=False).astype(f32)
 
     moving = permute(grads_at(order[0]).astype(bf16), lay.backward)
     side, cross, ffn_grad = together(side, cross, ffn_grad)
@@ -986,7 +1023,7 @@
         - stream * inverse_one**3 * jnp.mean(scaled_one * stream, axis=1, keepdims=True)
     )
     bias_part = (bias_part[0] + bias_part[8]).reshape(3, 1, share)
-    bias_part = lax.dynamic_update_slice(jnp.zeros((3, 8, share), f32), bias_part, (0, slot, 0))
+    bias_part = lax.dynamic_update_slice(jnp.zeros((3, 8, share), f32), bias_part, (0, slot, 0), allow_negative_indices=False)
     small = stack(router_part, gain_two_grad[None], gain_one_grad[None], bias_part.reshape(3, model_width))
     doubling = lay.doubling()
 
@@ -1006,7 +1043,7 @@
     moving = permute(total.astype(bf16), lay.backward)
     outs_up = outs_over((quarter[0] + quarter[1])[1:])
     sided = {s: permute(send[s], lay.side) for s in quarter[3]}
-    small = small + permute(small, doubling[0])
+    small = small + permute(small, doubling[3])
     shared_columns_grad, expert_grad = turn_grads(first_weights_grad, ffn_grad)
     shared_columns_grad = lax.all_to_all(
         shared_columns_grad.reshape(owners, -1, 3 * unit_share), "ep", split_axis=0, concat_axis=0, tiled=True
@@ -1020,7 +1057,7 @@
     outs_up = outs_over(quarter[2] + quarter[3])
     output_sum = after(output_sum, outs_up[order[2]])
     outgoing = [outs_on(v) for v in (output_sum[: n // 2], output_sum[n // 2 :])]
-    for step in doubling[1:3]:
+    for step in doubling[:3]:
         small = small + permute(small, step)
     moving, shared_columns_grad, outs_up, small = all_there(moving, shared_columns_grad, outs_up, small)
     outs_in(outs_up)
@@ -1033,11 +1070,13 @@
     total = lax.all_to_all(total, PLANE, split_axis=0, concat_axis=0, tiled=True)
     for s in out_queue[:-1]:
         outgoing = [outs_on(out_sums[s][k * n // 2 : (k + 1) * n // 2] + v.astype(f32)) for k, v in enumerate(outgoing)]
+    total, small = together(total, small)
+    dense_grad = collect_columns(total, shared_columns_grad, share)
+    dense_grad, *outgoing = together(dense_grad, *outgoing)
     output_sum = out_sums[out_queue[-1]] + stack(*outgoing).astype(f32)
-    for step in doubling[3:]:
+    for step in doubling[4:]:
         small = small + permute(small, step)
     output = (residual + output_sum).astype(bf16)
-    dense_grad = collect_columns(total, shared_columns_grad, share)
 
     router_sum, gain_two_sum, gain_one_sum, bias_sum = jnp.split(small, [expert_count + 1, expert_count + 2, expert_count + 3])
     return (

time: 826 us -> 819 us (level)
  Pallas kernels: 238 us -> 224 us
  local copies, waits for them, and re-layouts: 44.9 us -> 58.4 us
    pallas_call x3 -> x2, Pallas kernels: 20.2 us -> 5.58 us  [assemble(): pl.pallas_call(assemble_kernel, in_specs=[pl.BlockSpec(memory_space=pltpu...]
    unnamed x190 -> x246, local copies, waits for them, and re-layouts: 24.6 us -> 38.3 us
    convert_element_type x16 -> x18, other arithmetic: 34.6 us -> 30.6 us  [plus(): return (a.astype(f32) + b.astype(f32)).astype(bf16)]
  transfers between devices with their start and end apart: 135 -> 135, of which waited for: 60 -> 60; matrix products, arithmetic and copies ran while one was open for 13% -> 12% of each run, Pallas kernels for 29% -> 27%
where the time goes in v5:
time: 819 us; the launch traced here: 809 us
  waiting for transfers between devices  296 us (36%)
  Pallas kernels  224 us (27%)
  starting transfers between devices  137 us (17%)
  other arithmetic  80.4 us (10%)
  local copies, waits for them, and re-layouts  58.4 us (7%)
    ppermute x128, waiting for transfers between devices, permute(): return lax.ppermute(rows, AXES, pairs)  276 us
    ppermute x128, starting transfers between devices, permute(): return lax.ppermute(rows, AXES, pairs)  105 us
    pallas_call x2, Pallas kernels, second_units(): pl.pallas_call(functools.partial(second_kernel, groups, units, experts),...  81.7 us
    pallas_call x1, Pallas kernels, first_units(): pl.pallas_call(functools.partial(first_kernel, groups, units, experts, le...  48.4 us
    unnamed x246, local copies, waits for them, and re-layouts  38.3 us
    pallas_call x3, Pallas kernels, group_call(): pl.pallas_call(kernel, grid_spec=pltpu.PrefetchScalarGridSpec(num_scalar_...  31.1 us
    convert_element_type x18, other arithmetic, plus(): return (a.astype(f32) + b.astype(f32)).astype(bf16)  30.6 us
    pallas_call x1, Pallas kernels, weight_grads(): pl.pallas_call(functools.partial(grads_kernel, wide), grid_spec=pltpu.Pre...  30.2 us
  transfers between devices with their start and end apart: 135, of which 60 were waited for; matrix products, arithmetic and copies ran while one was open for 12% of the time, Pallas kernels for 27%

profile of v5, /device:TPU:0, one launch (start us, length us, event | category | flops | bytes accessed | tf_op | source)
XLA Modules:
  0.0 809.4 jit_solution(18354830997690831784)
XLA Ops:
  3.4 4.0 collective-permute-start
  23.9 4.7 copy.57
  28.7 5.6 all-to-all-done
  51.7 7.9 collective-permute-done.6.refs_1_
  65.3 9.0 %collective-permute-done.3.refs_44_ = bf16[128,2176]{1,0:T(8,128)(2,1)} collective-permute-done((bf16[128,2176]{1,0:T(8,128)(2,1)S(1)}, bf16[128,2176]{1,0:T(8,128)(2,1)}, u32[]{:S(2)}, u32[]{:S(2)}) %collective-permute-start.3) | collective-permute-done | bytes 557088 | tf_op jit(solution)/shard_map/ppermute | solution.py:58
  79.8 6.8 collective-permute-done.5.refs_49_
  112.1 4.1 collective-permute-done.14.refs_37_
  121.6 11.0 %shard_map.210 = (bf16[1024,768]{1,0:T(8,128)(2,1)}, bf16[1024,256]{1,0:T(8,128)(2,1)S(1)}) custom-call(s32[4]{0:T(128)S(1)} %pad_add_fusion.4.where_ref, bf16[1024,2048]{1,0:T(8,128)(2,1)} %shard_map.209.rows_ref, f32[1,768]{1,0:T(1,128)S(1)} %bitcast.85, f32[1024,128]{1,0:T(8,128)S(1)} %copy-done.19, f32[1024,128]{1,0:T(8,128)S(1)} %copy-done.17, ...), custom_call_target="tpu_custom_call" | custom-call | flops 3758096384 | bytes 8922624 | tf_op jit(solution)/shard_map/pallas_call | solution.py:640
  132.6 5.2 shard_map.211
  137.8 5.3 all-to-all-start.1
  153.1 17.0 %collective-permute-done.25 = bf16[128,2048]{1,0:T(8,128)(2,1)S(1)} collective-permute-done((bf16[128,2048]{1,0:T(8,128)(2,1)S(1)}, bf16[128,2048]{1,0:T(8,128)(2,1)S(1)}, u32[]{:S(2)}, u32[]{:S(2)}) %collective-permute-start.25) | collective-permute-done | bytes 524320 | tf_op jit(solution)/shard_map/ppermute | solution.py:58
  173.0 9.1 %collective-permute-done.28.refs_57_ = bf16[128,2176]{1,0:T(8,128)(2,1)S(1)} collective-permute-done((bf16[128,2176]{1,0:T(8,128)(2,1)}, bf16[128,2176]{1,0:T(8,128)(2,1)S(1)}, u32[]{:S(2)}, u32[]{:S(2)}) %collective-permute-start.28) | collective-permute-done | bytes 557088 | tf_op jit(solution)/shard_map/ppermute | solution.py:58
  182.5 10.7 %collective-permute-done.26 = bf16[128,2048]{1,0:T(8,128)(2,1)S(1)} collective-permute-done((bf16[128,2048]{1,0:T(8,128)(2,1)S(1)}, bf16[128,2048]{1,0:T(8,128)(2,1)S(1)}, u32[]{:S(2)}, u32[]{:S(2)}) %collective-permute-start.26) | collective-permute-done | bytes 524320 | tf_op jit(solution)/shard_map/ppermute | solution.py:58
  204.2 8.0 collective-permute-done.31.refs_1_
  218.0 11.2 %collective-permute-done.37.refs_4_ = bf16[128,2048]{1,0:T(8,128)(2,1)S(1)} collective-permute-done((bf16[128,2048]{1,0:T(8,128)(2,1)}, bf16[128,2048]{1,0:T(8,128)(2,1)S(1)}, u32[]{:S(2)}, u32[]{:S(2)}) %collective-permute-start.37) | collective-permute-done | bytes 524320 | tf_op jit(solution)/shard_map/ppermute | solution.py:58
  233.4 4.3 shard_map.212
  256.0 5.0 collective-permute-done.45.refs_20_
  264.0 4.7 all-to-all-start.2
  290.1 12.2 %collective-permute-done.41.refs_28_ = bf16[128,2048]{1,0:T(8,128)(2,1)S(1)} collective-permute-done((bf16[128,2048]{1,0:T(8,128)(2,1)}, bf16[128,2048]{1,0:T(8,128)(2,1)S(1)}, u32[]{:S(2)}, u32[]{:S(2)}) %collective-permute-start.41) | collective-permute-done | bytes 524320 | tf_op jit(solution)/shard_map/ppermute | solution.py:58
  302.3 10.4 %collective-permute-done.46.refs_21_ = bf16[128,2048]{1,0:T(8,128)(2,1)S(1)} collective-permute-done((bf16[128,2048]{1,0:T(8,128)(2,1)}, bf16[128,2048]{1,0:T(8,128)(2,1)S(1)}, u32[]{:S(2)}, u32[]{:S(2)}) %collective-permute-start.46) | collective-permute-done | bytes 524320 | tf_op jit(solution)/shard_map/ppermute | solution.py:58
  314.4 11.9 %collective-permute-done.77.refs_29_ = bf16[128,2048]{1,0:T(8,128)(2,1)S(1)} collective-permute-done((bf16[128,2048]{1,0:T(8,128)(2,1)}, bf16[128,2048]{1,0:T(8,128)(2,1)S(1)}, u32[]{:S(2)}, u32[]{:S(2)}) %collective-permute-start.77) | collective-permute-done | bytes 524320 | tf_op jit(solution)/shard_map/ppermute | solution.py:58
  329.9 48.4 %shard_map.214 = (bf16[4096,2048]{1,0:T(8,128)(2,1)}, bf16[4096,2176]{1,0:T(8,128)(2,1)}, bf16[4096,256]{1,0:T(8,128)(2,1)}, bf16[4096,512]{1,0:T(8,128)(2,1)}, ...) custom-call(s32[1]{0:T(128)} %bitcast.24.where_ref, bf16[128,2048]{1,0:T(8,128)(2,1)} %multiply_convert_fusion.refs_0_, ...), custom_call_target="tpu_custom_call" | custom-call | flops 25769803776 | bytes 33554432 | tf_op jit(solution)/shard_map/pallas_call | solution.py:303
  378.3 6.2 all-to-all-start.3
  384.7 4.9 shard_map.215
  392.4 40.8 %shard_map.216 = (bf16[1024,2048]{1,0:T(8,128)(2,1)}, bf16[1024,2048]{1,0:T(8,128)(2,1)}, bf16[1024,2048]{1,0:T(8,128)(2,1)}, bf16[1024,2048]{1,0:T(8,128)(2,1)}...) custom-call(s32[1]{0:T(128)} %bitcast.24.where_ref, bf16[4096,2048]{1,0:T(8,128)(2,1)} %get-tuple-element.336.rows_ref, ...), custom_call_target="tpu_custom_call" | custom-call | flops 16106127360 | bytes 33554432 | tf_op jit(solution)/shard_map/pallas_call | solution.py:370
  434.4 7.4 collective-permute-done.80
  450.6 40.8 %shard_map.217 = (bf16[1024,2048]{1,0:T(8,128)(2,1)}, bf16[1024,2048]{1,0:T(8,128)(2,1)}, bf16[1024,2048]{1,0:T(8,128)(2,1)}, bf16[1024,2048]{1,0:T(8,128)(2,1)}...) custom-call(s32[1]{0:T(128)} %bitcast.24.where_ref, ...), custom_call_target="tpu_custom_call", output_to_operand_aliasing={{4}: (9, {}), {5}: (10, {})} | custom-call | flops 16106127360 | bytes 33554432 | tf_op jit(solution)/shard_map/pallas_call | solution.py:370
  495.2 9.0 %collective-permute-done.84 = bf16[1024,2048]{1,0:T(8,128)(2,1)S(1)} collective-permute-done((bf16[1024,2048]{1,0:T(8,128)(2,1)}, bf16[1024,2048]{1,0:T(8,128)(2,1)S(1)}, u32[]{:S(2)}, u32[]{:S(2)}) %collective-permute-start.84) | collective-permute-done | bytes 4194336 | tf_op jit(solution)/shard_map/ppermute | solution.py:58
  511.4 30.2 %shard_map.218 = (bf16[8,1056,256]{2,1,0:T(8,128)(2,1)}, f32[24,2048]{1,0:T(8,128)}) custom-call(s32[1]{0:T(128)} %bitcast.24.where_ref, bf16[4096,2048]{1,0:T(8,128)(2,1)} %get-tuple-element.336.rows_ref, bf16[4096,2176]{1,0:T(8,128)(2,1)} %get-tuple-element.337.cots_ref, bf16[4096,384]{1,0:T(8,128)(2,1)} %get-tuple-element.373.hidden_ref, ...), custom_call_target="tpu_custom_call" | custom-call | flops 19327352832 | bytes 33554432 | tf_op jit(solution)/shard_map/pallas_call | solution.py:339
  549.4 4.3 add_convert_fusion.10
  562.6 4.2 add_convert_fusion.6
  566.8 7.4 collective-permute-done.94
  577.0 9.9 %collective-permute-done.97.refs_1_ = bf16[128,2048]{1,0:T(8,128)(2,1)S(1)} collective-permute-done((bf16[128,2048]{1,0:T(8,128)(2,1)S(1)}, bf16[128,2048]{1,0:T(8,128)(2,1)S(1)}, u32[]{:S(2)}, u32[]{:S(2)}) %collective-permute-start.97) | collective-permute-done | bytes 524320 | tf_op jit(solution)/shard_map/ppermute | solution.py:58
  587.2 4.8 all-to-all-start.4
  594.0 7.6 collective-permute-done.101.refs_5_
  605.6 14.9 %shard_map.220 = (bf16[1024,768]{1,0:T(8,128)(2,1)}, bf16[512,2048]{1,0:T(8,128)(2,1)}, bf16[512,2048]{1,0:T(8,128)(2,1)}, f32[16,768]{1,0:T(8,128)S(1)}) custom-call(s32[4]{0:T(128)S(1)} %pad_add_fusion.4.where_ref, bf16[1024,2048]{1,0:T(8,128)(2,1)} %shard_map.219.grad_ref, bf16[1024,768]{1,0:T(8,128)(2,1)} %get-tuple-element.265.packed_ref, ...), custom_call_target="tpu_custom_call" | custom-call | flops 5905580032 | bytes 10493952 | tf_op jit(solution)/shard_map/pallas_call | solution.py:640
  620.5 6.8 collective-permute-done.96
  645.1 9.1 %collective-permute-done.95 = bf16[256,2048]{1,0:T(8,128)(2,1)S(1)} collective-permute-done((bf16[256,2048]{1,0:T(8,128)(2,1)}, bf16[256,2048]{1,0:T(8,128)(2,1)S(1)}, u32[]{:S(2)}, u32[]{:S(2)}) %collective-permute-start.95) | collective-permute-done | bytes 1048608 | tf_op jit(solution)/shard_map/ppermute | solution.py:58
  665.0 5.5 collective-permute-done.106
  672.2 9.6 %collective-permute-done.107 = bf16[128,2048]{1,0:T(8,128)(2,1)} collective-permute-done((bf16[128,2048]{1,0:T(8,128)(2,1)}, bf16[128,2048]{1,0:T(8,128)(2,1)}, u32[]{:S(2)}, u32[]{:S(2)}) %collective-permute-start.107) | collective-permute-done | bytes 524320 | tf_op jit(solution)/shard_map/ppermute | solution.py:58
  681.7 7.7 all-to-all-done.4.second_ref
  693.7 8.6 %shard_map.221 = (bf16[256,4224]{1,0:T(8,128)(2,1)}, f32[256,2,4224]{2,1,0:T(2,128)}) custom-call(bf16[8,528,256]{2,1,0:T(8,128)(2,1)} %copy-done.35, bf16[8,1056,256]{2,1,0:T(8,128)(2,1)} %all-to-all-done.4.second_ref), custom_call_target="tpu_custom_call" | custom-call | bytes 17301504 | tf_op jit(solution)/shard_map/pallas_call | solution.py:435
  718.4 13.7 %collective-permute-done.117 = bf16[128,2048]{1,0:T(8,128)(2,1)S(1)} collective-permute-done((bf16[128,2048]{1,0:T(8,128)(2,1)S(1)}, bf16[128,2048]{1,0:T(8,128)(2,1)S(1)}, u32[]{:S(2)}, u32[]{:S(2)}) %collective-permute-start.117) | collective-permute-done | bytes 524320 | tf_op jit(solution)/shard_map/ppermute | solution.py:58
  732.3 7.8 collective-permute-done.111
  757.1 7.0 collective-permute-done.120
  764.1 9.8 %collective-permute-done.115 = bf16[512,1024]{1,0:T(8,128)(2,1)} collective-permute-done((bf16[512,1024]{1,0:T(8,128)(2,1)}, bf16[512,1024]{1,0:T(8,128)(2,1)}, u32[]{:S(2)}, u32[]{:S(2)}) %collective-permute-start.115) | collective-permute-done | bytes 1048608 | tf_op jit(solution)/shard_map/ppermute | solution.py:58
  790.9 5.5 all-to-all-done.6.attn_ref
  800.2 4.5 collective-permute-done.126
  (618 shorter events, 298.3 us)
Async XLA Ops:
  7.4 43.0 %collective-permute-start.10 = (bf16[128,2176]{1,0:T(8,128)(2,1)}, bf16[128,2176]{1,0:T(8,128)(2,1)}, u32[]{:S(2)}, u32[]{:S(2)}) collective-permute-start(bf16[128,2176]{1,0:T(8,128)(2,1)} %pad_maximum_fusion.7.refs_32_), channel_id=1, source_target_pairs={{0,4},{1,5},{2,6},{3,7},{4,0},{5,1},{6,2},{7,3},{8,12},{9,13},{10,... | collective-permute-start | bytes 1671176 | tf_op jit(solution)/shard_map/ppermute | solution.py:58
  9.0 41.5 %collective-permute-start.9 = (bf16[128,2176]{1,0:T(8,128)(2,1)}, bf16[128,2176]{1,0:T(8,128)(2,1)}, u32[]{:S(2)}, u32[]{:S(2)}) collective-permute-start(bf16[128,2176]{1,0:T(8,128)(2,1)} %pad_maximum_fusion.7.refs_32_), channel_id=1, source_target_pairs={{0,2},{1,3},{2,0},{3,1},{4,6},{5,7},{6,4},{7,5},{8,10},{9,11},{10,... | collective-permute-start | bytes 1671176 | tf_op jit(solution)/shard_map/ppermute | solution.py:58
  34.9 24.7 %collective-permute-start.6 = (bf16[512,1024]{1,0:T(8,128)(2,1)S(1)}, bf16[512,1024]{1,0:T(8,128)(2,1)}, u32[]{:S(2)}, u32[]{:S(2)}) collective-permute-start(bf16[512,1024]{1,0:T(8,128)(2,1)S(1)} %bitcast.81), channel_id=1, source_target_pairs={{0,16},{1,17},{2,18},{3,19},{4,20},{5,21},{6,22},{7,23},{8,0},{9,1... | collective-permute-start | bytes 3145736 | tf_op jit(solution)/shard_map/ppermute | solution.py:58
  59.6 27.7 %collective-permute-start.12 = (bf16[512,1024]{1,0:T(8,128)(2,1)}, bf16[512,1024]{1,0:T(8,128)(2,1)}, u32[]{:S(2)}, u32[]{:S(2)}) collective-permute-start(bf16[512,1024]{1,0:T(8,128)(2,1)} %collective-permute-done.6.refs_1_), channel_id=1, source_target_pairs={{0,16},{1,17},{2,18},{3,19},{4,20},{5,21},{6,22},{7,23},{8,0},{9,1... | collective-permute-start | bytes 3145736 | tf_op jit(solution)/shard_map/ppermute | solution.py:58
  65.3 22.3 %collective-permute-start.17 = (bf16[128,2048]{1,0:T(8,128)(2,1)}, bf16[128,2048]{1,0:T(8,128)(2,1)S(1)}, u32[]{:S(2)}, u32[]{:S(2)}) collective-permute-start(bf16[128,2048]{1,0:T(8,128)(2,1)} %fusion.5.refs_0_), channel_id=1, source_target_pairs={{0,1},{1,0},{2,3},{3,2},{4,5},{5,4},{6,7},{7,6},{8,9},{9,8},{10,11... | collective-permute-start | bytes 1572872 | tf_op jit(solution)/shard_map/ppermute | solution.py:58
  87.4 28.8 %collective-permute-start.13 = (bf16[512,1024]{1,0:T(8,128)(2,1)}, bf16[512,1024]{1,0:T(8,128)(2,1)}, u32[]{:S(2)}, u32[]{:S(2)}) collective-permute-start(bf16[512,1024]{1,0:T(8,128)(2,1)} %collective-permute-done.12.refs_2_), channel_id=1, source_target_pairs={{0,16},{1,17},{2,18},{3,19},{4,20},{5,21},{6,22},{7,23},{8,0},{9,1... | collective-permute-start | bytes 3145736 | tf_op jit(solution)/shard_map/ppermute | solution.py:58
  88.5 23.6 %collective-permute-start.2 = (bf16[128,2176]{1,0:T(8,128)(2,1)}, bf16[128,2176]{1,0:T(8,128)(2,1)}, u32[]{:S(2)}, u32[]{:S(2)}) collective-permute-start(bf16[128,2176]{1,0:T(8,128)(2,1)} %collective-permute-done.1.refs_48_), channel_id=1, source_target_pairs={{0,2},{1,3},{2,0},{3,1},{4,6},{5,7},{6,4},{7,5},{8,10},{9,11},{10,... | collective-permute-start | bytes 1671176 | tf_op jit(solution)/shard_map/ppermute | solution.py:58
  88.9 27.4 %collective-permute-start.14 = (bf16[128,2176]{1,0:T(8,128)(2,1)}, bf16[128,2176]{1,0:T(8,128)(2,1)}, u32[]{:S(2)}, u32[]{:S(2)}) collective-permute-start(bf16[128,2176]{1,0:T(8,128)(2,1)} %collective-permute-done.10.refs_33_), channel_id=1, source_target_pairs={{0,2},{1,3},{2,0},{3,1},{4,6},{5,7},{6,4},{7,5},{8,10},{9,11},{10,... | collective-permute-start | bytes 1671176 | tf_op jit(solution)/shard_map/ppermute | solution.py:58
  91.3 24.9 %collective-permute-start.15 = (bf16[128,2176]{1,0:T(8,128)(2,1)}, bf16[128,2176]{1,0:T(8,128)(2,1)}, u32[]{:S(2)}, u32[]{:S(2)}) collective-permute-start(bf16[128,2176]{1,0:T(8,128)(2,1)} %collective-permute-done.3.refs_44_), channel_id=1, source_target_pairs={{0,4},{1,5},{2,6},{3,7},{4,0},{5,1},{6,2},{7,3},{8,12},{9,13},{10,... | collective-permute-start | bytes 1671176 | tf_op jit(solution)/shard_map/ppermute | solution.py:58
  102.8 29.8 %collective-permute-start.21 = (bf16[128,2176]{1,0:T(8,128)(2,1)}, bf16[128,2176]{1,0:T(8,128)(2,1)}, u32[]{:S(2)}, u32[]{:S(2)}) collective-permute-start(bf16[128,2176]{1,0:T(8,128)(2,1)} %collective-permute-done.5.refs_49_), channel_id=1, source_target_pairs={{0,2},{1,3},{2,0},{3,1},{4,6},{5,7},{6,4},{7,5},{8,10},{9,11},{10,... | collective-permute-start | bytes 1671176 | tf_op jit(solution)/shard_map/ppermute | solution.py:58
  137.8 56.2 %all-to-all-start.1 = ((bf16[8,528,256]{2,1,0:T(8,128)(2,1)}), bf16[8,528,256]{2,1,0:T(8,128)(2,1)}, u32[]{:S(2)}, u32[]{:S(2)}) async-start(bf16[8,528,256]{2,1,0:T(8,128)(2,1)} %shard_map.207), calls=%async_computation.1 | async-start | bytes 4325376 | tf_op jit(solution)/shard_map/all_to_all | solution.py:783
  143.1 29.2 %collective-permute-start.27 = (bf16[128,2176]{1,0:T(8,128)(2,1)}, bf16[128,2176]{1,0:T(8,128)(2,1)S(1)}, u32[]{:S(2)}, u32[]{:S(2)}) collective-permute-start(bf16[128,2176]{1,0:T(8,128)(2,1)} %collective-permute-done.22.refs_56_), channel_id=1, source_target_pairs={{0,2},{1,3},{2,0},{3,1},{4,6},{5,7},{6,4},{7,5},{8,10},{9,11},{10,... | collective-permute-start | bytes 1671176 | tf_op jit(solution)/shard_map/ppermute | solution.py:58
  150.5 42.7 %collective-permute-start.29 = (bf16[64,4224]{1,0:T(8,128)(2,1)S(1)}, bf16[64,4224]{1,0:T(8,128)(2,1)}, u32[]{:S(2)}, u32[]{:S(2)}) collective-permute-start(bf16[64,4224]{1,0:T(8,128)(2,1)S(1)} %get-tuple-element.479), channel_id=1, source_target_pairs={{0,1},{1,0},{2,3},{3,2},{4,5},{5,4},{6,7},{7,6},{8,9},{9,8},{10,11... | collective-permute-start | bytes 1622024 | tf_op jit(solution)/shard_map/ppermute | solution.py:58
  150.5 43.5 %collective-permute-start.30 = (bf16[64,4224]{1,0:T(8,128)(2,1)S(1)}, bf16[64,4224]{1,0:T(8,128)(2,1)}, u32[]{:S(2)}, u32[]{:S(2)}) collective-permute-start(bf16[64,4224]{1,0:T(8,128)(2,1)S(1)} %get-tuple-element.478), channel_id=1, source_target_pairs={{0,2},{1,3},{2,0},{3,1},{4,6},{5,7},{6,4},{7,5},{8,10},{9,11},{10,... | collective-permute-start | bytes 1622024 | tf_op jit(solution)/shard_map/ppermute | solution.py:58
  151.1 30.9 %collective-permute-start.28 = (bf16[128,2176]{1,0:T(8,128)(2,1)}, bf16[128,2176]{1,0:T(8,128)(2,1)S(1)}, u32[]{:S(2)}, u32[]{:S(2)}) collective-permute-start(bf16[128,2176]{1,0:T(8,128)(2,1)} %collective-permute-done.22.refs_56_), channel_id=1, source_target_pairs={{0,4},{1,5},{2,6},{3,7},{4,0},{5,1},{6,2},{7,3},{8,12},{9,13},{10,... | collective-permute-start | bytes 1671176 | tf_op jit(solution)/shard_map/ppermute | solution.py:58
  170.2 23.0 %collective-permute-start.26 = (bf16[128,2048]{1,0:T(8,128)(2,1)S(1)}, bf16[128,2048]{1,0:T(8,128)(2,1)S(1)}, u32[]{:S(2)}, u32[]{:S(2)}) collective-permute-start(bf16[128,2048]{1,0:T(8,128)(2,1)S(1)} %add_convert_fusion.35), channel_id=1, source_target_pairs={{0,4},{1,5},{2,6},{3,7},{4,0},{5,1},{6,2},{7,3},{8,12},{9,13},{10,... | collective-permute-start | bytes 1572872 | tf_op jit(solution)/shard_map/ppermute | solution.py:58
  182.1 22.2 %collective-permute-start.33 = (bf16[64,4224]{1,0:T(8,128)(2,1)}, bf16[64,4224]{1,0:T(8,128)(2,1)}, u32[]{:S(2)}, u32[]{:S(2)}) collective-permute-start(bf16[64,4224]{1,0:T(8,128)(2,1)} %get-tuple-element.269), channel_id=1, source_target_pairs={{0,3},{1,2},{2,1},{3,0},{4,7},{5,6},{6,5},{7,4},{8,11},{9,10},{10,... | collective-permute-start | bytes 1622024 | tf_op jit(solution)/shard_map/ppermute | solution.py:58
  202.8 26.4 %collective-permute-start.37 = (bf16[128,2048]{1,0:T(8,128)(2,1)}, bf16[128,2048]{1,0:T(8,128)(2,1)S(1)}, u32[]{:S(2)}, u32[]{:S(2)}) collective-permute-start(bf16[128,2048]{1,0:T(8,128)(2,1)} %multiply_convert_fusion.refs_0_), channel_id=1, source_target_pairs={{0,2},{1,3},{2,0},{3,1},{4,6},{5,7},{6,4},{7,5},{8,10},{9,11},{10,... | collective-permute-start | bytes 1572872 | tf_op jit(solution)/shard_map/ppermute | solution.py:58
  216.5 25.6 %collective-permute-start.40 = (bf16[128,2048]{1,0:T(8,128)(2,1)}, bf16[128,2048]{1,0:T(8,128)(2,1)}, u32[]{:S(2)}, u32[]{:S(2)}) collective-permute-start(bf16[128,2048]{1,0:T(8,128)(2,1)} %collective-permute-done.32.refs_8_), channel_id=1, source_target_pairs={{0,2},{1,3},{2,0},{3,1},{4,6},{5,7},{6,4},{7,5},{8,10},{9,11},{10,... | collective-permute-start | bytes 1572872 | tf_op jit(solution)/shard_map/ppermute | solution.py:58
  264.0 114.2 %all-to-all-start.2 = ((bf16[8,1056,256]{2,1,0:T(8,128)(2,1)}), bf16[8,1056,256]{2,1,0:T(8,128)(2,1)}, u32[]{:S(2)}, u32[]{:S(2)}) async-start(bf16[8,1056,256]{2,1,0:T(8,128)(2,1)} %pad_maximum_fusion), calls=%async_computation.2 | async-start | bytes 8650752 | tf_op jit(solution)/shard_map/all_to_all | solution.py:783
  287.9 24.9 %collective-permute-start.68 = (bf16[128,2048]{1,0:T(8,128)(2,1)}, bf16[128,2048]{1,0:T(8,128)(2,1)S(1)}, u32[]{:S(2)}, u32[]{:S(2)}) collective-permute-start(bf16[128,2048]{1,0:T(8,128)(2,1)} %collective-permute-done.40.refs_12_), channel_id=1, source_target_pairs={{0,1},{1,0},{2,3},{3,2},{4,5},{5,4},{6,7},{7,6},{8,9},{9,8},{10,11... | collective-permute-start | bytes 1572872 | tf_op jit(solution)/shard_map/ppermute | solution.py:58
  287.9 24.8 %collective-permute-start.46 = (bf16[128,2048]{1,0:T(8,128)(2,1)}, bf16[128,2048]{1,0:T(8,128)(2,1)S(1)}, u32[]{:S(2)}, u32[]{:S(2)}) collective-permute-start(bf16[128,2048]{1,0:T(8,128)(2,1)} %collective-permute-done.38.refs_17_), channel_id=1, source_target_pairs={{0,2},{1,3},{2,0},{3,1},{4,6},{5,7},{6,4},{7,5},{8,10},{9,11},{10,... | collective-permute-start | bytes 1572872 | tf_op jit(solution)/shard_map/ppermute | solution.py:58
  289.4 23.3 %collective-permute-start.70 = (bf16[128,2048]{1,0:T(8,128)(2,1)}, bf16[128,2048]{1,0:T(8,128)(2,1)S(1)}, u32[]{:S(2)}, u32[]{:S(2)}) collective-permute-start(bf16[128,2048]{1,0:T(8,128)(2,1)} %collective-permute-done.38.refs_17_), channel_id=1, source_target_pairs={{0,1},{1,0},{2,3},{3,2},{4,5},{5,4},{6,7},{7,6},{8,9},{9,8},{10,11... | collective-permute-start | bytes 1572872 | tf_op jit(solution)/shard_map/ppermute | solution.py:58
  289.7 23.0 %collective-permute-start.71 = (bf16[128,2048]{1,0:T(8,128)(2,1)}, bf16[128,2048]{1,0:T(8,128)(2,1)S(1)}, u32[]{:S(2)}, u32[]{:S(2)}) collective-permute-start(bf16[128,2048]{1,0:T(8,128)(2,1)} %collective-permute-done.45.refs_20_), channel_id=1, source_target_pairs={{0,1},{1,0},{2,3},{3,2},{4,5},{5,4},{6,7},{7,6},{8,9},{9,8},{10,11... | collective-permute-start | bytes 1572872 | tf_op jit(solution)/shard_map/ppermute | solution.py:58
  378.3 56.1 %all-to-all-start.3 = ((bf16[8,528,256]{2,1,0:T(8,128)(2,1)}), bf16[8,528,256]{2,1,0:T(8,128)(2,1)S(1)}, u32[]{:S(2)}, u32[]{:S(2)}) async-start(bf16[8,528,256]{2,1,0:T(8,128)(2,1)} %get-tuple-element.346), calls=%async_computation.3 | async-start | bytes 4325376 | tf_op jit(solution)/shard_map/all_to_all | solution.py:783
  448.5 43.1 %collective-permute-start.83 = (bf16[1024,2048]{1,0:T(8,128)(2,1)}, bf16[1024,2048]{1,0:T(8,128)(2,1)}, u32[]{:S(2)}, u32[]{:S(2)}) collective-permute-start(bf16[1024,2048]{1,0:T(8,128)(2,1)} %get-tuple-element.360), channel_id=1, source_target_pairs={{0,1},{1,0},{2,3},{3,2},{4,5},{5,4},{6,7},{7,6},{8,9},{9,8},{10,11... | collective-permute-start | bytes 12582920 | tf_op jit(solution)/shard_map/ppermute | solution.py:58
  448.6 42.9 %collective-permute-start.81 = (bf16[256,2048]{1,0:T(8,128)(2,1)}, bf16[256,2048]{1,0:T(8,128)(2,1)S(1)}, u32[]{:S(2)}, u32[]{:S(2)}) collective-permute-start(bf16[256,2048]{1,0:T(8,128)(2,1)} %pad_maximum_fusion.4), channel_id=1, source_target_pairs={{0,4},{1,5},{2,6},{3,7},{4,0},{5,1},{6,2},{7,3},{8,12},{9,13},{10,... | collective-permute-start | bytes 3145736 | tf_op jit(solution)/shard_map/ppermute | solution.py:58
  450.1 41.4 %collective-permute-start.82 = (bf16[256,2048]{1,0:T(8,128)(2,1)}, bf16[256,2048]{1,0:T(8,128)(2,1)S(1)}, u32[]{:S(2)}, u32[]{:S(2)}) collective-permute-start(bf16[256,2048]{1,0:T(8,128)(2,1)} %get-tuple-element.352), channel_id=1, source_target_pairs={{0,2},{1,3},{2,0},{3,1},{4,6},{5,7},{6,4},{7,5},{8,10},{9,11},{10,... | collective-permute-start | bytes 3145736 | tf_op jit(solution)/shard_map/ppermute | solution.py:58
  491.6 50.0 %collective-permute-start.90 = (bf16[1024,2048]{1,0:T(8,128)(2,1)}, bf16[1024,2048]{1,0:T(8,128)(2,1)}, u32[]{:S(2)}, u32[]{:S(2)}) collective-permute-start(bf16[1024,2048]{1,0:T(8,128)(2,1)} %get-tuple-element.376), channel_id=1, source_target_pairs={{0,1},{1,0},{2,3},{3,2},{4,5},{5,4},{6,7},{7,6},{8,9},{9,8},{10,11... | collective-permute-start | bytes 12582920 | tf_op jit(solution)/shard_map/ppermute | solution.py:58
  508.0 33.5 %collective-permute-start.89 = (bf16[128,2048]{1,0:T(8,128)(2,1)S(1)}, bf16[128,2048]{1,0:T(8,128)(2,1)}, u32[]{:S(2)}, u32[]{:S(2)}) collective-permute-start(bf16[128,2048]{1,0:T(8,128)(2,1)S(1)} %add_convert_fusion.26), channel_id=1, source_target_pairs={{0,8},{1,9},{2,10},{3,11},{4,12},{5,13},{6,14},{7,15},{8,24},{9,25... | collective-permute-start | bytes 1572872 | tf_op jit(solution)/shard_map/ppermute | solution.py:58
  509.0 32.6 %collective-permute-start.87 = (bf16[256,2048]{1,0:T(8,128)(2,1)}, bf16[256,2048]{1,0:T(8,128)(2,1)S(1)}, u32[]{:S(2)}, u32[]{:S(2)}) collective-permute-start(bf16[256,2048]{1,0:T(8,128)(2,1)} %pad_maximum_fusion.6), channel_id=1, source_target_pairs={{0,4},{1,5},{2,6},{3,7},{4,0},{5,1},{6,2},{7,3},{8,12},{9,13},{10,... | collective-permute-start | bytes 3145736 | tf_op jit(solution)/shard_map/ppermute | solution.py:58
  509.9 31.6 %collective-permute-start.88 = (bf16[256,2048]{1,0:T(8,128)(2,1)}, bf16[256,2048]{1,0:T(8,128)(2,1)}, u32[]{:S(2)}, u32[]{:S(2)}) collective-permute-start(bf16[256,2048]{1,0:T(8,128)(2,1)} %get-tuple-element.370), channel_id=1, source_target_pairs={{0,2},{1,3},{2,0},{3,1},{4,6},{5,7},{6,4},{7,5},{8,10},{9,11},{10,... | collective-permute-start | bytes 3145736 | tf_op jit(solution)/shard_map/ppermute | solution.py:58
  587.2 102.2 %all-to-all-start.4 = ((bf16[8,1056,256]{2,1,0:T(8,128)(2,1)}), bf16[8,1056,256]{2,1,0:T(8,128)(2,1)}, u32[]{:S(2)}, u32[]{:S(2)}) async-start(bf16[8,1056,256]{2,1,0:T(8,128)(2,1)} %get-tuple-element.411), calls=%async_computation.4 | async-start | bytes 8650752 | tf_op jit(solution)/shard_map/all_to_all | solution.py:973
  601.6 25.8 %collective-permute-start.96 = (bf16[256,2048]{1,0:T(8,128)(2,1)}, bf16[256,2048]{1,0:T(8,128)(2,1)S(1)}, u32[]{:S(2)}, u32[]{:S(2)}) collective-permute-start(bf16[256,2048]{1,0:T(8,128)(2,1)} %get-tuple-element.392), channel_id=1, source_target_pairs={{0,2},{1,3},{2,0},{3,1},{4,6},{5,7},{6,4},{7,5},{8,10},{9,11},{10,... | collective-permute-start | bytes 3145736 | tf_op jit(solution)/shard_map/ppermute | solution.py:58
  629.0 25.2 %collective-permute-start.95 = (bf16[256,2048]{1,0:T(8,128)(2,1)}, bf16[256,2048]{1,0:T(8,128)(2,1)S(1)}, u32[]{:S(2)}, u32[]{:S(2)}) collective-permute-start(bf16[256,2048]{1,0:T(8,128)(2,1)} %get-tuple-element.391), channel_id=1, source_target_pairs={{0,2},{1,3},{2,0},{3,1},{4,6},{5,7},{6,4},{7,5},{8,10},{9,11},{10,... | collective-permute-start | bytes 3145736 | tf_op jit(solution)/shard_map/ppermute | solution.py:58
  656.8 25.0 %collective-permute-start.107 = (bf16[128,2048]{1,0:T(8,128)(2,1)}, bf16[128,2048]{1,0:T(8,128)(2,1)}, u32[]{:S(2)}, u32[]{:S(2)}) collective-permute-start(bf16[128,2048]{1,0:T(8,128)(2,1)} %get-tuple-element.480), channel_id=1, source_target_pairs={{0,2},{1,3},{2,0},{3,1},{4,6},{5,7},{6,4},{7,5},{8,10},{9,11},{10,... | collective-permute-start | bytes 1572872 | tf_op jit(solution)/shard_map/ppermute | solution.py:58
  657.4 48.7 %collective-permute-start.105 = (bf16[256,2048]{1,0:T(8,128)(2,1)}, bf16[256,2048]{1,0:T(8,128)(2,1)}, u32[]{:S(2)}, u32[]{:S(2)}) collective-permute-start(bf16[256,2048]{1,0:T(8,128)(2,1)} %get-tuple-element.409), channel_id=1, source_target_pairs={{0,2},{1,3},{2,0},{3,1},{4,6},{5,7},{6,4},{7,5},{8,10},{9,11},{10,... | collective-permute-start | bytes 3145736 | tf_op jit(solution)/shard_map/ppermute | solution.py:58
  658.9 73.4 %collective-permute-start.113 = (bf16[256,2048]{1,0:T(8,128)(2,1)}, bf16[256,2048]{1,0:T(8,128)(2,1)}, u32[]{:S(2)}, u32[]{:S(2)}) collective-permute-start(bf16[256,2048]{1,0:T(8,128)(2,1)} %get-tuple-element.417), channel_id=1, source_target_pairs={{0,2},{1,3},{2,0},{3,1},{4,6},{5,7},{6,4},{7,5},{8,10},{9,11},{10,... | collective-permute-start | bytes 3145736 | tf_op jit(solution)/shard_map/ppermute | solution.py:58
  661.3 47.0 %collective-permute-start.109 = (bf16[512,1024]{1,0:T(8,128)(2,1)}, bf16[512,1024]{1,0:T(8,128)(2,1)}, u32[]{:S(2)}, u32[]{:S(2)}) collective-permute-start(bf16[512,1024]{1,0:T(8,128)(2,1)} %dynamic-slice_bitcast_fusion), channel_id=1, source_target_pairs={{0,8},{1,9},{2,10},{3,11},{4,12},{5,13},{6,14},{7,15},{8,24},{9,25... | collective-permute-start | bytes 3145736 | tf_op jit(solution)/shard_map/ppermute | solution.py:58
  670.5 37.7 %collective-permute-start.110 = (bf16[128,2048]{1,0:T(8,128)(2,1)}, bf16[128,2048]{1,0:T(8,128)(2,1)}, u32[]{:S(2)}, u32[]{:S(2)}) collective-permute-start(bf16[128,2048]{1,0:T(8,128)(2,1)} %slice.321), channel_id=1, source_target_pairs={{0,4},{1,5},{2,6},{3,7},{4,0},{5,1},{6,2},{7,3},{8,12},{9,13},{10,... | collective-permute-start | bytes 1572872 | tf_op jit(solution)/shard_map/ppermute | solution.py:58
  702.3 61.8 %all-to-all-start.5 = ((bf16[4,64,4224]{2,1,0:T(8,128)(2,1)}), bf16[4,64,4224]{2,1,0:T(8,128)(2,1)S(1)}, u32[]{:S(2)}, u32[]{:S(2)}) async-start(bf16[4,64,4224]{2,1,0:T(8,128)(2,1)} %bitcast.89), calls=%async_computation.5 | async-start | bytes 4325376 | tf_op jit(solution)/shard_map/all_to_all | solution.py:1048
  706.1 26.2 %collective-permute-start.112 = (bf16[128,2048]{1,0:T(8,128)(2,1)}, bf16[128,2048]{1,0:T(8,128)(2,1)}, u32[]{:S(2)}, u32[]{:S(2)}) collective-permute-start(bf16[128,2048]{1,0:T(8,128)(2,1)} %slice.375), channel_id=1, source_target_pairs={{0,4},{1,5},{2,6},{3,7},{4,0},{5,1},{6,2},{7,3},{8,12},{9,13},{10,... | collective-permute-start | bytes 1572872 | tf_op jit(solution)/shard_map/ppermute | solution.py:58
  713.2 27.0 %collective-permute-start.111 = (bf16[512,1024]{1,0:T(8,128)(2,1)S(1)}, bf16[512,1024]{1,0:T(8,128)(2,1)S(1)}, u32[]{:S(2)}, u32[]{:S(2)}) collective-permute-start(bf16[512,1024]{1,0:T(8,128)(2,1)S(1)} %fusion.2), channel_id=1, source_target_pairs={{0,8},{1,9},{2,10},{3,11},{4,12},{5,13},{6,14},{7,15},{8,24},{9,25... | collective-permute-start | bytes 3145736 | tf_op jit(solution)/shard_map/ppermute | solution.py:58
  732.2 22.6 %collective-permute-start.121 = (bf16[64,2048]{1,0:T(8,128)(2,1)S(1)}, bf16[64,2048]{1,0:T(8,128)(2,1)S(1)}, u32[]{:S(2)}, u32[]{:S(2)}) collective-permute-start(bf16[64,2048]{1,0:T(8,128)(2,1)S(1)} %get-tuple-element.489), channel_id=1, source_target_pairs={{0,8},{1,9},{2,10},{3,11},{4,12},{5,13},{6,14},{7,15},{8,24},{9,25... | collective-permute-start | bytes 786440 | tf_op jit(solution)/shard_map/ppermute | solution.py:58
  732.2 22.5 %collective-permute-start.124 = (bf16[64,2048]{1,0:T(8,128)(2,1)S(1)}, bf16[64,2048]{1,0:T(8,128)(2,1)S(1)}, u32[]{:S(2)}, u32[]{:S(2)}) collective-permute-start(bf16[64,2048]{1,0:T(8,128)(2,1)S(1)} %get-tuple-element.488), channel_id=1, source_target_pairs={{0,8},{1,9},{2,10},{3,11},{4,12},{5,13},{6,14},{7,15},{8,24},{9,25... | collective-permute-start | bytes 786440 | tf_op jit(solution)/shard_map/ppermute | solution.py:58
  743.4 30.5 %collective-permute-start.115 = (bf16[512,1024]{1,0:T(8,128)(2,1)}, bf16[512,1024]{1,0:T(8,128)(2,1)}, u32[]{:S(2)}, u32[]{:S(2)}) collective-permute-start(bf16[512,1024]{1,0:T(8,128)(2,1)} %fusion.1), channel_id=1, source_target_pairs={{0,8},{1,9},{2,10},{3,11},{4,12},{5,13},{6,14},{7,15},{8,24},{9,25... | collective-permute-start | bytes 3145736 | tf_op jit(solution)/shard_map/ppermute | solution.py:58
  755.7 26.9 %collective-permute-start.122 = (bf16[64,2048]{1,0:T(8,128)(2,1)}, bf16[64,2048]{1,0:T(8,128)(2,1)}, u32[]{:S(2)}, u32[]{:S(2)}) collective-permute-start(bf16[64,2048]{1,0:T(8,128)(2,1)} %get-tuple-element.487), channel_id=1, source_target_pairs={{0,8},{1,9},{2,10},{3,11},{4,12},{5,13},{6,14},{7,15},{8,24},{9,25... | collective-permute-start | bytes 786440 | tf_op jit(solution)/shard_map/ppermute | solution.py:58
  756.5 27.8 %collective-permute-start.125 = (bf16[64,2048]{1,0:T(8,128)(2,1)}, bf16[64,2048]{1,0:T(8,128)(2,1)}, u32[]{:S(2)}, u32[]{:S(2)}) collective-permute-start(bf16[64,2048]{1,0:T(8,128)(2,1)} %get-tuple-element.486), channel_id=1, source_target_pairs={{0,8},{1,9},{2,10},{3,11},{4,12},{5,13},{6,14},{7,15},{8,24},{9,25... | collective-permute-start | bytes 786440 | tf_op jit(solution)/shard_map/ppermute | solution.py:58
  (210 other events, 2296.1 us)

commit v6 on v5

--- a/solution.py
+++ b/solution.py
@@ -163,11 +163,11 @@
         out_ref[d, 2 * wide :] = down_sums[:wide, lanes].astype(bf16)
 
 
-def add_grads(grad, rows, hidden, cots, gate_sums, down_sums):
+def add_grads(grad, rows, hidden, cots, gate_sums, down_sums, before=()):
     @pl.when(pl.program_id(0) == 0)
     def _():
-        gate_sums[...] = jnp.zeros_like(gate_sums)
-        down_sums[...] = jnp.zeros_like(down_sums)
+        gate_sums[...] = before[0][...] if before else jnp.zeros_like(gate_sums)
+        down_sums[...] = before[1][...] if before else jnp.zeros_like(down_sums)
 
     gate_sums[...] += dot_tn(grad, rows)
     down_sums[...] += dot_tn(hidden, cots)
@@ -207,10 +207,11 @@
     return gated, with_logits(gate_grad, logit_grad, up_grad, base, at)
 
 
-def first_kernel(groups, units, experts, count, where_ref, *refs):
+def first_kernel(groups, units, experts, count, last, where_ref, *refs):
     pieces, cot_pieces, refs = refs[:count], refs[count : 2 * count], refs[2 * count :]
-    gate_ref, down_ref, rows_ref, cots_ref, hidden_ref, grad_ref, out_ref, router_ref, *scratch = refs
-    gate_sums, down_sums, held, held_cots, sems = scratch
+    gate_ref, down_ref, *before = refs[: 4 if last else 2]
+    rows_ref, cots_ref, hidden_ref, grad_ref, *outs, held, held_cots, sems = refs[8 if last else 2 :]
+    gate_sums, down_sums = outs[-2:]
     step, steps = pl.program_id(0), pl.num_programs(0)
     each, size = held.shape[1] // pieces[0].shape[0], pieces[0].shape[0]
 
@@ -238,11 +239,13 @@
     gated, grad = group_pass(groups, units, experts, where_ref, rows_ref, cots_ref, gate_ref, down_ref)
     hidden_ref[...] = gated
     grad_ref[...] = grad
-    add_grads(grad, rows_ref[...], gated, cots_ref[:, : rows_ref.shape[1]], gate_sums, down_sums)
-
-    @pl.when(step == steps - 1)
-    def _():
-        hand_out(units * len(groups), gate_sums, down_sums, out_ref, router_ref)
+    add_grads(grad, rows_ref[...], gated, cots_ref[:, : rows_ref.shape[1]], gate_sums, down_sums, before)
+
+    if last:
+
+        @pl.when(step == steps - 1)
+        def _():
+            hand_out(units * len(groups), gate_sums, down_sums, *outs[:2])
 
 
 def grads_kernel(wide, where_ref, rows_ref, cots_ref, hidden_ref, grad_ref, out_ref, router_ref, gate_sums, down_sums):
@@ -294,41 +297,47 @@
     return rows.shape[0] // tile, tile, [among_all(rows.shape[1], tile), among_all(cots.shape[1], tile)]
 
 
-def first_units(groups, where, pieces, cot_pieces, gate_rows, down_rows, units, experts, count):
-    total, width, wider = sum(v.shape[0] for v in pieces), gate_rows.shape[1], cot_pieces[0].shape[1]
+def first_units(groups, where, pieces, cot_pieces, gate_rows, down_rows, units, experts, count, total, before=()):
+    width, wider = gate_rows.shape[1], cot_pieces[0].shape[1]
     pad = down_rows.shape[0]
     wide = units * len(groups)
     tile = 512
+    steps = sum(v.shape[0] for v in pieces) // tile
+    first = total // tile - steps if before else 0
+    sums = [(2 * pad, width), (pad, width)]
     shapes = grads_out(wide, pad, width, count)
-    rows, cots, hidden, grad, weights, router = pl.pallas_call(
-        functools.partial(first_kernel, groups, units, experts, len(pieces)),
+    widths = (width, wider, pad, 2 * pad)
+    whole = [jax.ShapeDtypeStruct((total, w), bf16) for w in widths]
+    outs = [among_all(w, tile, first) for w in widths]
+    held = [
+        pltpu.VMEM((2, tile, width), bf16),
+        pltpu.VMEM((2, tile, wider), bf16),
+        pltpu.SemaphoreType.DMA((2, 2 * tile // pieces[0].shape[0])),
+    ]
+    if before:
+        outs += [all_of(shape) for shape in shapes]
+        whole += [jax.ShapeDtypeStruct(shapes[0], bf16), jax.ShapeDtypeStruct(shapes[1], f32)]
+        held = [pltpu.VMEM(shape, f32) for shape in sums] + held
+    else:
+        outs += [all_of(shape) for shape in sums]
+        whole += [jax.ShapeDtypeStruct(shape, f32) for shape in sums]
+    kept = [pl.BlockSpec(memory_space=pl.ANY)] * 4
+    return pl.pallas_call(
+        functools.partial(first_kernel, groups, units, experts, len(pieces), bool(before)),
         grid_spec=pltpu.PrefetchScalarGridSpec(
             num_scalar_prefetch=1,
-            grid=(total // tile,),
+            grid=(steps,),
             in_specs=[pl.BlockSpec(memory_space=pl.ANY)] * (2 * len(pieces))
-            + [all_of(gate_rows.shape), all_of(down_rows.shape)],
-            out_specs=[among_all(width, tile), among_all(wider, tile), among_all(pad, tile), among_all(2 * pad, tile)]
-            + [all_of(shape) for shape in shapes],
-            scratch_shapes=[
-                pltpu.VMEM((2 * pad, width), f32),
-                pltpu.VMEM((pad, width), f32),
-                pltpu.VMEM((2, tile, width), bf16),
-                pltpu.VMEM((2, tile, wider), bf16),
-                pltpu.SemaphoreType.DMA((2, 2 * tile // pieces[0].shape[0])),
-            ],
+            + [all_of(gate_rows.shape), all_of(down_rows.shape)]
+            + ([all_of(shape) for shape in sums] + kept if before else []),
+            out_specs=outs,
+            scratch_shapes=held,
         ),
-        out_shape=[
-            jax.ShapeDtypeStruct((total, width), bf16),
-            jax.ShapeDtypeStruct((total, wider), bf16),
-            jax.ShapeDtypeStruct((total, pad), bf16),
-            jax.ShapeDtypeStruct((total, 2 * pad), bf16),
-            jax.ShapeDtypeStruct(shapes[0], bf16),
-            jax.ShapeDtypeStruct(shapes[1], f32),
-        ],
+        out_shape=whole,
+        input_output_aliases={2 * len(pieces) + 5 + i: i for i in range(4)} if before else {},
         compiler_params=pltpu.CompilerParams(vmem_limit_bytes=60 * 1024 * 1024),
-        cost_estimate=pl.CostEstimate(flops=12 * total * width * pad, bytes_accessed=4 * total * width, transcendentals=0),
-    )(where, *pieces, *cot_pieces, gate_rows, down_rows)
-    return rows, cots, hidden, grad, to_owners(weights, wide, count), router
+        cost_estimate=pl.CostEstimate(flops=12 * steps * tile * width * pad, bytes_accessed=4 * steps * tile * width, transcendentals=0),
+    )(where, *pieces, *cot_pieces, gate_rows, down_rows, *before)
 
 
 def weight_grads(where, rows, cots, hidden, grad, wide, count):
@@ -833,24 +842,23 @@
     second_ffn = to_units(second_ffn)
     sides.append(permute(blocks[-1], lay.side))
     crosses.update({k: permute(ups[k], lay.side) for k in range(2, rings - 1) if k not in crosses})
+    crosses[rings - 1] = permute(ups[-1], lay.side)
     cots = list(zip(cot_blocks, cot_ups, cot_sides, cot_crosses))
-    cot_cores = [between_cores(*v) for v in cots]
-    inner = [between_cores(blocks[s], ups[s], sides[s]) for s in range(rings - 1)]
-    sides[-1], ups[-1], crosses, cot_cores, inner = lax.optimization_barrier((sides[-1], ups[-1], crosses, cot_cores, inner))
-    crosses[rings - 1] = permute(ups[-1], lay.side)
-    inner.append(between_cores(blocks[-1], ups[-1], sides[-1]))
-    cot_pieces = []
-    for (block, up, side, cross), cores in zip(cots, cot_cores):
-        cot_pieces += [block, up, *cores[:2], side, cross, *cores[2:]]
-    rows = []
-    for s in range(rings):
-        cores = inner[s] + between_cores(crosses[s])
-        rows += [blocks[s], ups[s], *cores[:2], sides[s], crosses[s], *cores[2:]]
 
     late = rings // 2
-    rows, cots, first_hidden, first_grad, first_weights_grad, first_router = first_units(
-        (0,), where, rows, cot_pieces, *first_rows, units, expert_count, dp_count
-    )
+
+    def first_ffn_half(begin, end, *before):
+        rows, cot_rows = [], []
+        for s in range(begin, end):
+            for pieces, four in ((rows, (blocks[s], ups[s], sides[s], crosses[s])), (cot_rows, cots[s])):
+                there = between_cores(*four)
+                pieces += [*four[:2], *there[:2], *four[2:], *there[2:]]
+        return first_units((0,), where, rows, cot_rows, *first_rows, units, expert_count, dp_count, 8 * n * rings, *before)
+
+    filled = first_ffn_half(0, late)
+    filled, blocks, ups, sides, crosses, cots = lax.optimization_barrier((filled, blocks, ups, sides, crosses, cots))
+    rows, cots, first_hidden, first_grad, first_weights_grad, first_router = first_ffn_half(late, rings, (*filled[4:], *filled[:4]))
+    first_weights_grad = to_owners(first_weights_grad, units, dp_count)
     first_weights_grad = to_units(first_weights_grad)
     second_rows = place_weights(after(second_ffn, first_hidden), router)
 

time: 819 us -> 802 us (0.979)
  waiting for transfers between devices: 296 us -> 267 us
  Pallas kernels: 224 us -> 233 us
    ppermute x128, waiting for transfers between devices: 276 us -> 247 us  [permute(): return lax.ppermute(rows, AXES, pairs)]
    pallas_call x1 -> x2, Pallas kernels: 48.4 us -> 57.2 us  [first_units(): pl.pallas_call(functools.partial(first_kernel, groups, units, experts, le...]
    unnamed x246 -> x244, local copies, waits for them, and re-layouts: 38.3 us -> 40.6 us
  transfers between devices with their start and end apart: 135 -> 135, of which waited for: 60 -> 62; matrix products, arithmetic and copies ran while one was open for 12% -> 12% of each run, Pallas kernels for 27% -> 29%
where the time goes in v6:
time: 802 us; the launch traced here: 793 us
  waiting for transfers between devices  267 us (33%)
  Pallas kernels  233 us (29%)
  starting transfers between devices  140 us (17%)
  other arithmetic  79.8 us (10%)
  local copies, waits for them, and re-layouts  59.7 us (7%)
    ppermute x128, waiting for transfers between devices, permute(): return lax.ppermute(rows, AXES, pairs)  247 us
    ppermute x128, starting transfers between devices, permute(): return lax.ppermute(rows, AXES, pairs)  107 us
    pallas_call x2, Pallas kernels, second_units(): pl.pallas_call(functools.partial(second_kernel, groups, units, experts),...  81.5 us
    pallas_call x2, Pallas kernels, first_units(): pl.pallas_call(functools.partial(first_kernel, groups, units, experts, le...  57.2 us
    unnamed x244, local copies, waits for them, and re-layouts  40.6 us
    pallas_call x3, Pallas kernels, group_call(): pl.pallas_call(kernel, grid_spec=pltpu.PrefetchScalarGridSpec(num_scalar_...  31.3 us
    pallas_call x1, Pallas kernels, weight_grads(): pl.pallas_call(functools.partial(grads_kernel, wide), grid_spec=pltpu.Pre...  30.4 us
    convert_element_type x18, other arithmetic, plus(): return (a.astype(f32) + b.astype(f32)).astype(bf16)  29.8 us
  transfers between devices with their start and end apart: 135, of which 62 were waited for; matrix products, arithmetic and copies ran while one was open for 12% of the time, Pallas kernels for 29%

profile of v6, /device:TPU:0, one launch (start us, length us, event | category | flops | bytes accessed | tf_op | source)
XLA Modules:
  0.0 792.5 jit_solution(6917940283388093422)
XLA Ops:
  3.4 4.0 collective-permute-start
  23.9 4.7 copy.61
  28.7 5.6 all-to-all-done
  51.7 7.9 collective-permute-done.6.refs_1_
  65.3 9.0 %collective-permute-done.3.refs_28_ = bf16[128,2176]{1,0:T(8,128)(2,1)} collective-permute-done((bf16[128,2176]{1,0:T(8,128)(2,1)S(1)}, bf16[128,2176]{1,0:T(8,128)(2,1)}, u32[]{:S(2)}, u32[]{:S(2)}) %collective-permute-start.3) | collective-permute-done | bytes 557088 | tf_op jit(solution)/shard_map/ppermute | solution.py:58
  79.7 6.8 collective-permute-done.5.refs_17_
  111.8 4.3 collective-permute-done.14.refs_21_
  121.6 11.0 %shard_map.210 = (bf16[1024,768]{1,0:T(8,128)(2,1)}, bf16[1024,256]{1,0:T(8,128)(2,1)S(1)}) custom-call(s32[4]{0:T(128)S(1)} %pad_add_fusion.4.where_ref, bf16[1024,2048]{1,0:T(8,128)(2,1)} %shard_map.209.rows_ref, f32[1,768]{1,0:T(1,128)S(1)} %bitcast.85, f32[1024,128]{1,0:T(8,128)S(1)} %copy-done.21, f32[1024,128]{1,0:T(8,128)S(1)} %copy-done.19, ...), custom_call_target="tpu_custom_call" | custom-call | flops 3758096384 | bytes 8922624 | tf_op jit(solution)/shard_map/pallas_call | solution.py:649
  132.7 5.2 shard_map.211
  137.9 5.2 all-to-all-start.1
  153.1 17.0 %collective-permute-done.25 = bf16[128,2048]{1,0:T(8,128)(2,1)S(1)} collective-permute-done((bf16[128,2048]{1,0:T(8,128)(2,1)S(1)}, bf16[128,2048]{1,0:T(8,128)(2,1)S(1)}, u32[]{:S(2)}, u32[]{:S(2)}) %collective-permute-start.25) | collective-permute-done | bytes 524320 | tf_op jit(solution)/shard_map/ppermute | solution.py:58
  173.2 9.0 %collective-permute-done.28.refs_25_ = bf16[128,2176]{1,0:T(8,128)(2,1)} collective-permute-done((bf16[128,2176]{1,0:T(8,128)(2,1)}, bf16[128,2176]{1,0:T(8,128)(2,1)}, u32[]{:S(2)}, u32[]{:S(2)}) %collective-permute-start.28) | collective-permute-done | bytes 557088 | tf_op jit(solution)/shard_map/ppermute | solution.py:58
  182.5 10.7 %collective-permute-done.26 = bf16[128,2048]{1,0:T(8,128)(2,1)S(1)} collective-permute-done((bf16[128,2048]{1,0:T(8,128)(2,1)S(1)}, bf16[128,2048]{1,0:T(8,128)(2,1)S(1)}, u32[]{:S(2)}, u32[]{:S(2)}) %collective-permute-start.26) | collective-permute-done | bytes 524320 | tf_op jit(solution)/shard_map/ppermute | solution.py:58
  204.7 7.5 collective-permute-done.31.refs_1_
  218.5 11.2 %collective-permute-done.39.refs_4_ = bf16[128,2048]{1,0:T(8,128)(2,1)S(1)} collective-permute-done((bf16[128,2048]{1,0:T(8,128)(2,1)}, bf16[128,2048]{1,0:T(8,128)(2,1)S(1)}, u32[]{:S(2)}, u32[]{:S(2)}) %collective-permute-start.39) | collective-permute-done | bytes 524320 | tf_op jit(solution)/shard_map/ppermute | solution.py:58
  233.8 4.3 shard_map.212
  256.3 5.0 collective-permute-done.46.refs_4_
  263.2 5.9 all-to-all-start.2
  284.3 26.7 %shard_map.214 = (bf16[4096,2048]{1,0:T(8,128)(2,1)}, bf16[4096,2176]{1,0:T(8,128)(2,1)}, bf16[4096,256]{1,0:T(8,128)(2,1)}, bf16[4096,512]{1,0:T(8,128)(2,1)}, ...) custom-call(s32[1]{0:T(128)} %bitcast.24.where_ref, bf16[128,2048]{1,0:T(8,128)(2,1)} %multiply_convert_fusion.refs_0_, ...), custom_call_target="tpu_custom_call" | custom-call | flops 12884901888 | bytes 16777216 | tf_op jit(solution)/shard_map/pallas_call | solution.py:325
  311.0 5.4 collective-permute-done.63.refs_13_
  331.6 30.6 %shard_map.215 = (bf16[4096,2048]{1,0:T(8,128)(2,1)}, bf16[4096,2176]{1,0:T(8,128)(2,1)}, bf16[4096,256]{1,0:T(8,128)(2,1)}, bf16[4096,512]{1,0:T(8,128)(2,1)}, ...) custom-call(s32[1]{0:T(128)} %bitcast.24.where_ref, ...), custom_call_target="tpu_custom_call", output_to_operand_aliasing={{0}: (37, {}), {1}: (38, {}), {2}: (39, {}), {3}: (40, {})} | custom-call | flops 12884901888 | bytes 16777216 | tf_op jit(solution)/shard_map/pallas_call | solution.py:325
  362.2 6.2 all-to-all-start.3
  368.6 4.9 shard_map.216
  376.3 40.8 %shard_map.217 = (bf16[1024,2048]{1,0:T(8,128)(2,1)}, bf16[1024,2048]{1,0:T(8,128)(2,1)}, bf16[1024,2048]{1,0:T(8,128)(2,1)}, bf16[1024,2048]{1,0:T(8,128)(2,1)}...) custom-call(s32[1]{0:T(128)} %bitcast.24.where_ref, bf16[4096,2048]{1,0:T(8,128)(2,1)} %get-tuple-element.332.rows_ref, ...), custom_call_target="tpu_custom_call" | custom-call | flops 16106127360 | bytes 33554432 | tf_op jit(solution)/shard_map/pallas_call | solution.py:379
  418.3 7.4 collective-permute-done.80
  434.1 40.6 %shard_map.218 = (bf16[1024,2048]{1,0:T(8,128)(2,1)}, bf16[1024,2048]{1,0:T(8,128)(2,1)}, bf16[1024,2048]{1,0:T(8,128)(2,1)}, bf16[1024,2048]{1,0:T(8,128)(2,1)}...) custom-call(s32[1]{0:T(128)} %bitcast.24.where_ref, ...), custom_call_target="tpu_custom_call", output_to_operand_aliasing={{4}: (9, {}), {5}: (10, {})} | custom-call | flops 16106127360 | bytes 33554432 | tf_op jit(solution)/shard_map/pallas_call | solution.py:379
  478.7 8.7 %collective-permute-done.84 = bf16[1024,2048]{1,0:T(8,128)(2,1)S(1)} collective-permute-done((bf16[1024,2048]{1,0:T(8,128)(2,1)}, bf16[1024,2048]{1,0:T(8,128)(2,1)S(1)}, u32[]{:S(2)}, u32[]{:S(2)}) %collective-permute-start.84) | collective-permute-done | bytes 4194336 | tf_op jit(solution)/shard_map/ppermute | solution.py:58
  494.9 30.4 %shard_map.219 = (bf16[8,1056,256]{2,1,0:T(8,128)(2,1)}, f32[24,2048]{1,0:T(8,128)}) custom-call(s32[1]{0:T(128)} %bitcast.24.where_ref, bf16[4096,2048]{1,0:T(8,128)(2,1)} %get-tuple-element.332.rows_ref, bf16[4096,2176]{1,0:T(8,128)(2,1)} %get-tuple-element.333.cots_ref, bf16[4096,384]{1,0:T(8,128)(2,1)} %get-tuple-element.369.hidden_ref, ...), custom_call_target="tpu_custom_call" | custom-call | flops 19327352832 | bytes 33554432 | tf_op jit(solution)/shard_map/pallas_call | solution.py:348
  533.0 4.1 add_convert_fusion.10
  546.3 4.0 add_convert_fusion.6
  550.4 7.6 collective-permute-done.94
  560.4 10.2 %collective-permute-done.97.refs_1_ = bf16[128,2048]{1,0:T(8,128)(2,1)S(1)} collective-permute-done((bf16[128,2048]{1,0:T(8,128)(2,1)S(1)}, bf16[128,2048]{1,0:T(8,128)(2,1)S(1)}, u32[]{:S(2)}, u32[]{:S(2)}) %collective-permute-start.97) | collective-permute-done | bytes 524320 | tf_op jit(solution)/shard_map/ppermute | solution.py:58
  570.7 4.7 all-to-all-start.4
  577.7 7.5 collective-permute-done.101.refs_5_
  589.3 15.0 %shard_map.221 = (bf16[1024,768]{1,0:T(8,128)(2,1)}, bf16[512,2048]{1,0:T(8,128)(2,1)}, bf16[512,2048]{1,0:T(8,128)(2,1)}, f32[16,768]{1,0:T(8,128)S(1)}) custom-call(s32[4]{0:T(128)S(1)} %pad_add_fusion.4.where_ref, bf16[1024,2048]{1,0:T(8,128)(2,1)} %shard_map.220.grad_ref, bf16[1024,768]{1,0:T(8,128)(2,1)} %get-tuple-element.263.packed_ref, ...), custom_call_target="tpu_custom_call" | custom-call | flops 5905580032 | bytes 10493952 | tf_op jit(solution)/shard_map/pallas_call | solution.py:649
  604.3 6.8 collective-permute-done.96
  617.9 3.9 convolution_convert_fusion
  628.9 9.0 %collective-permute-done.95 = bf16[256,2048]{1,0:T(8,128)(2,1)S(1)} collective-permute-done((bf16[256,2048]{1,0:T(8,128)(2,1)}, bf16[256,2048]{1,0:T(8,128)(2,1)S(1)}, u32[]{:S(2)}, u32[]{:S(2)}) %collective-permute-start.95) | collective-permute-done | bytes 1048608 | tf_op jit(solution)/shard_map/ppermute | solution.py:58
  648.6 5.6 collective-permute-done.106
  655.8 9.6 %collective-permute-done.107 = bf16[128,2048]{1,0:T(8,128)(2,1)} collective-permute-done((bf16[128,2048]{1,0:T(8,128)(2,1)}, bf16[128,2048]{1,0:T(8,128)(2,1)}, u32[]{:S(2)}, u32[]{:S(2)}) %collective-permute-start.107) | collective-permute-done | bytes 524320 | tf_op jit(solution)/shard_map/ppermute | solution.py:58
  665.4 7.4 all-to-all-done.4.second_ref
  677.1 8.6 %shard_map.222 = (bf16[256,4224]{1,0:T(8,128)(2,1)}, f32[256,2,4224]{2,1,0:T(2,128)}) custom-call(bf16[8,528,256]{2,1,0:T(8,128)(2,1)} %copy-done.35, bf16[8,1056,256]{2,1,0:T(8,128)(2,1)} %all-to-all-done.4.second_ref), custom_call_target="tpu_custom_call" | custom-call | bytes 17301504 | tf_op jit(solution)/shard_map/pallas_call | solution.py:444
  701.6 13.9 %collective-permute-done.117 = bf16[128,2048]{1,0:T(8,128)(2,1)S(1)} collective-permute-done((bf16[128,2048]{1,0:T(8,128)(2,1)S(1)}, bf16[128,2048]{1,0:T(8,128)(2,1)S(1)}, u32[]{:S(2)}, u32[]{:S(2)}) %collective-permute-start.117) | collective-permute-done | bytes 524320 | tf_op jit(solution)/shard_map/ppermute | solution.py:58
  715.7 7.7 collective-permute-done.111
  740.7 5.5 collective-permute-done.120
  746.2 11.0 %collective-permute-done.115 = bf16[512,1024]{1,0:T(8,128)(2,1)} collective-permute-done((bf16[512,1024]{1,0:T(8,128)(2,1)}, bf16[512,1024]{1,0:T(8,128)(2,1)}, u32[]{:S(2)}, u32[]{:S(2)}) %collective-permute-start.115) | collective-permute-done | bytes 1048608 | tf_op jit(solution)/shard_map/ppermute | solution.py:58
  774.3 5.5 all-to-all-done.6.attn_ref
  783.8 4.3 collective-permute-done.126
  (617 shorter events, 298.1 us)
Async XLA Ops:
  7.5 42.9 %collective-permute-start.10 = (bf16[128,2176]{1,0:T(8,128)(2,1)}, bf16[128,2176]{1,0:T(8,128)(2,1)}, u32[]{:S(2)}, u32[]{:S(2)}) collective-permute-start(bf16[128,2176]{1,0:T(8,128)(2,1)} %pad_maximum_fusion.7.refs_16_), channel_id=1, source_target_pairs={{0,4},{1,5},{2,6},{3,7},{4,0},{5,1},{6,2},{7,3},{8,12},{9,13},{10,... | collective-permute-start | bytes 1671176 | tf_op jit(solution)/shard_map/ppermute | solution.py:58
  9.0 41.4 %collective-permute-start.9 = (bf16[128,2176]{1,0:T(8,128)(2,1)}, bf16[128,2176]{1,0:T(8,128)(2,1)}, u32[]{:S(2)}, u32[]{:S(2)}) collective-permute-start(bf16[128,2176]{1,0:T(8,128)(2,1)} %pad_maximum_fusion.7.refs_16_), channel_id=1, source_target_pairs={{0,2},{1,3},{2,0},{3,1},{4,6},{5,7},{6,4},{7,5},{8,10},{9,11},{10,... | collective-permute-start | bytes 1671176 | tf_op jit(solution)/shard_map/ppermute | solution.py:58
  34.9 24.7 %collective-permute-start.6 = (bf16[512,1024]{1,0:T(8,128)(2,1)S(1)}, bf16[512,1024]{1,0:T(8,128)(2,1)}, u32[]{:S(2)}, u32[]{:S(2)}) collective-permute-start(bf16[512,1024]{1,0:T(8,128)(2,1)S(1)} %bitcast.81), channel_id=1, source_target_pairs={{0,16},{1,17},{2,18},{3,19},{4,20},{5,21},{6,22},{7,23},{8,0},{9,1... | collective-permute-start | bytes 3145736 | tf_op jit(solution)/shard_map/ppermute | solution.py:58
  59.6 27.7 %collective-permute-start.12 = (bf16[512,1024]{1,0:T(8,128)(2,1)}, bf16[512,1024]{1,0:T(8,128)(2,1)}, u32[]{:S(2)}, u32[]{:S(2)}) collective-permute-start(bf16[512,1024]{1,0:T(8,128)(2,1)} %collective-permute-done.6.refs_1_), channel_id=1, source_target_pairs={{0,16},{1,17},{2,18},{3,19},{4,20},{5,21},{6,22},{7,23},{8,0},{9,1... | collective-permute-start | bytes 3145736 | tf_op jit(solution)/shard_map/ppermute | solution.py:58
  64.7 21.8 %collective-permute-start.5 = (bf16[128,2176]{1,0:T(8,128)(2,1)}, bf16[128,2176]{1,0:T(8,128)(2,1)}, u32[]{:S(2)}, u32[]{:S(2)}) collective-permute-start(bf16[128,2176]{1,0:T(8,128)(2,1)} %collective-permute-done.1.refs_16_), channel_id=1, source_target_pairs={{0,4},{1,5},{2,6},{3,7},{4,0},{5,1},{6,2},{7,3},{8,12},{9,13},{10,... | collective-permute-start | bytes 1671176 | tf_op jit(solution)/shard_map/ppermute | solution.py:58
  65.3 22.3 %collective-permute-start.17 = (bf16[128,2048]{1,0:T(8,128)(2,1)}, bf16[128,2048]{1,0:T(8,128)(2,1)S(1)}, u32[]{:S(2)}, u32[]{:S(2)}) collective-permute-start(bf16[128,2048]{1,0:T(8,128)(2,1)} %fusion.5.refs_0_), channel_id=1, source_target_pairs={{0,1},{1,0},{2,3},{3,2},{4,5},{5,4},{6,7},{7,6},{8,9},{9,8},{10,11... | collective-permute-start | bytes 1572872 | tf_op jit(solution)/shard_map/ppermute | solution.py:58
  87.3 28.8 %collective-permute-start.13 = (bf16[512,1024]{1,0:T(8,128)(2,1)}, bf16[512,1024]{1,0:T(8,128)(2,1)}, u32[]{:S(2)}, u32[]{:S(2)}) collective-permute-start(bf16[512,1024]{1,0:T(8,128)(2,1)} %collective-permute-done.12.refs_2_), channel_id=1, source_target_pairs={{0,16},{1,17},{2,18},{3,19},{4,20},{5,21},{6,22},{7,23},{8,0},{9,1... | collective-permute-start | bytes 3145736 | tf_op jit(solution)/shard_map/ppermute | solution.py:58
  88.3 23.4 %collective-permute-start.2 = (bf16[128,2176]{1,0:T(8,128)(2,1)}, bf16[128,2176]{1,0:T(8,128)(2,1)}, u32[]{:S(2)}, u32[]{:S(2)}) collective-permute-start(bf16[128,2176]{1,0:T(8,128)(2,1)} %collective-permute-done.1.refs_16_), channel_id=1, source_target_pairs={{0,2},{1,3},{2,0},{3,1},{4,6},{5,7},{6,4},{7,5},{8,10},{9,11},{10,... | collective-permute-start | bytes 1671176 | tf_op jit(solution)/shard_map/ppermute | solution.py:58
  88.7 27.4 %collective-permute-start.14 = (bf16[128,2176]{1,0:T(8,128)(2,1)}, bf16[128,2176]{1,0:T(8,128)(2,1)}, u32[]{:S(2)}, u32[]{:S(2)}) collective-permute-start(bf16[128,2176]{1,0:T(8,128)(2,1)} %collective-permute-done.10.refs_17_), channel_id=1, source_target_pairs={{0,2},{1,3},{2,0},{3,1},{4,6},{5,7},{6,4},{7,5},{8,10},{9,11},{10,... | collective-permute-start | bytes 1671176 | tf_op jit(solution)/shard_map/ppermute | solution.py:58
  91.2 24.9 %collective-permute-start.15 = (bf16[128,2176]{1,0:T(8,128)(2,1)}, bf16[128,2176]{1,0:T(8,128)(2,1)}, u32[]{:S(2)}, u32[]{:S(2)}) collective-permute-start(bf16[128,2176]{1,0:T(8,128)(2,1)} %collective-permute-done.3.refs_28_), channel_id=1, source_target_pairs={{0,4},{1,5},{2,6},{3,7},{4,0},{5,1},{6,2},{7,3},{8,12},{9,13},{10,... | collective-permute-start | bytes 1671176 | tf_op jit(solution)/shard_map/ppermute | solution.py:58
  102.4 30.3 %collective-permute-start.21 = (bf16[128,2176]{1,0:T(8,128)(2,1)}, bf16[128,2176]{1,0:T(8,128)(2,1)}, u32[]{:S(2)}, u32[]{:S(2)}) collective-permute-start(bf16[128,2176]{1,0:T(8,128)(2,1)} %collective-permute-done.5.refs_17_), channel_id=1, source_target_pairs={{0,2},{1,3},{2,0},{3,1},{4,6},{5,7},{6,4},{7,5},{8,10},{9,11},{10,... | collective-permute-start | bytes 1671176 | tf_op jit(solution)/shard_map/ppermute | solution.py:58
  137.9 56.1 %all-to-all-start.1 = ((bf16[8,528,256]{2,1,0:T(8,128)(2,1)}), bf16[8,528,256]{2,1,0:T(8,128)(2,1)}, u32[]{:S(2)}, u32[]{:S(2)}) async-start(bf16[8,528,256]{2,1,0:T(8,128)(2,1)} %shard_map.207), calls=%async_computation.1 | async-start | bytes 4325376 | tf_op jit(solution)/shard_map/all_to_all | solution.py:792
  143.2 29.2 %collective-permute-start.27 = (bf16[128,2176]{1,0:T(8,128)(2,1)}, bf16[128,2176]{1,0:T(8,128)(2,1)S(1)}, u32[]{:S(2)}, u32[]{:S(2)}) collective-permute-start(bf16[128,2176]{1,0:T(8,128)(2,1)} %collective-permute-done.22.refs_24_), channel_id=1, source_target_pairs={{0,2},{1,3},{2,0},{3,1},{4,6},{5,7},{6,4},{7,5},{8,10},{9,11},{10,... | collective-permute-start | bytes 1671176 | tf_op jit(solution)/shard_map/ppermute | solution.py:58
  147.9 22.2 %collective-permute-start.25 = (bf16[128,2048]{1,0:T(8,128)(2,1)S(1)}, bf16[128,2048]{1,0:T(8,128)(2,1)S(1)}, u32[]{:S(2)}, u32[]{:S(2)}) collective-permute-start(bf16[128,2048]{1,0:T(8,128)(2,1)S(1)} %get-tuple-element.479), channel_id=1, source_target_pairs={{0,2},{1,3},{2,0},{3,1},{4,6},{5,7},{6,4},{7,5},{8,10},{9,11},{10,... | collective-permute-start | bytes 1572872 | tf_op jit(solution)/shard_map/ppermute | solution.py:58
  150.5 42.7 %collective-permute-start.29 = (bf16[64,4224]{1,0:T(8,128)(2,1)S(1)}, bf16[64,4224]{1,0:T(8,128)(2,1)}, u32[]{:S(2)}, u32[]{:S(2)}) collective-permute-start(bf16[64,4224]{1,0:T(8,128)(2,1)S(1)} %get-tuple-element.475), channel_id=1, source_target_pairs={{0,1},{1,0},{2,3},{3,2},{4,5},{5,4},{6,7},{7,6},{8,9},{9,8},{10,11... | collective-permute-start | bytes 1622024 | tf_op jit(solution)/shard_map/ppermute | solution.py:58
  150.5 43.5 %collective-permute-start.30 = (bf16[64,4224]{1,0:T(8,128)(2,1)S(1)}, bf16[64,4224]{1,0:T(8,128)(2,1)}, u32[]{:S(2)}, u32[]{:S(2)}) collective-permute-start(bf16[64,4224]{1,0:T(8,128)(2,1)S(1)} %get-tuple-element.474), channel_id=1, source_target_pairs={{0,2},{1,3},{2,0},{3,1},{4,6},{5,7},{6,4},{7,5},{8,10},{9,11},{10,... | collective-permute-start | bytes 1622024 | tf_op jit(solution)/shard_map/ppermute | solution.py:58
  151.1 31.1 %collective-permute-start.28 = (bf16[128,2176]{1,0:T(8,128)(2,1)}, bf16[128,2176]{1,0:T(8,128)(2,1)}, u32[]{:S(2)}, u32[]{:S(2)}) collective-permute-start(bf16[128,2176]{1,0:T(8,128)(2,1)} %collective-permute-done.22.refs_24_), channel_id=1, source_target_pairs={{0,4},{1,5},{2,6},{3,7},{4,0},{5,1},{6,2},{7,3},{8,12},{9,13},{10,... | collective-permute-start | bytes 1671176 | tf_op jit(solution)/shard_map/ppermute | solution.py:58
  170.3 22.9 %collective-permute-start.26 = (bf16[128,2048]{1,0:T(8,128)(2,1)S(1)}, bf16[128,2048]{1,0:T(8,128)(2,1)S(1)}, u32[]{:S(2)}, u32[]{:S(2)}) collective-permute-start(bf16[128,2048]{1,0:T(8,128)(2,1)S(1)} %add_convert_fusion.35), channel_id=1, source_target_pairs={{0,4},{1,5},{2,6},{3,7},{4,0},{5,1},{6,2},{7,3},{8,12},{9,13},{10,... | collective-permute-start | bytes 1572872 | tf_op jit(solution)/shard_map/ppermute | solution.py:58
  172.4 21.6 %collective-permute-start.24 = (bf16[128,2048]{1,0:T(8,128)(2,1)}, bf16[128,2048]{1,0:T(8,128)(2,1)}, u32[]{:S(2)}, u32[]{:S(2)}) collective-permute-start(bf16[128,2048]{1,0:T(8,128)(2,1)} %get-tuple-element.478), channel_id=1, source_target_pairs={{0,2},{1,3},{2,0},{3,1},{4,6},{5,7},{6,4},{7,5},{8,10},{9,11},{10,... | collective-permute-start | bytes 1572872 | tf_op jit(solution)/shard_map/ppermute | solution.py:58
  182.2 22.5 %collective-permute-start.33 = (bf16[64,4224]{1,0:T(8,128)(2,1)}, bf16[64,4224]{1,0:T(8,128)(2,1)}, u32[]{:S(2)}, u32[]{:S(2)}) collective-permute-start(bf16[64,4224]{1,0:T(8,128)(2,1)} %get-tuple-element.267), channel_id=1, source_target_pairs={{0,3},{1,2},{2,1},{3,0},{4,7},{5,6},{6,5},{7,4},{8,11},{9,10},{10,... | collective-permute-start | bytes 1622024 | tf_op jit(solution)/shard_map/ppermute | solution.py:58
  203.3 26.4 %collective-permute-start.39 = (bf16[128,2048]{1,0:T(8,128)(2,1)}, bf16[128,2048]{1,0:T(8,128)(2,1)S(1)}, u32[]{:S(2)}, u32[]{:S(2)}) collective-permute-start(bf16[128,2048]{1,0:T(8,128)(2,1)} %multiply_convert_fusion.refs_0_), channel_id=1, source_target_pairs={{0,2},{1,3},{2,0},{3,1},{4,6},{5,7},{6,4},{7,5},{8,10},{9,11},{10,... | collective-permute-start | bytes 1572872 | tf_op jit(solution)/shard_map/ppermute | solution.py:58
  216.5 25.9 %collective-permute-start.42 = (bf16[128,2048]{1,0:T(8,128)(2,1)}, bf16[128,2048]{1,0:T(8,128)(2,1)}, u32[]{:S(2)}, u32[]{:S(2)}) collective-permute-start(bf16[128,2048]{1,0:T(8,128)(2,1)} %collective-permute-done.32.refs_8_), channel_id=1, source_target_pairs={{0,2},{1,3},{2,0},{3,1},{4,6},{5,7},{6,4},{7,5},{8,10},{9,11},{10,... | collective-permute-start | bytes 1572872 | tf_op jit(solution)/shard_map/ppermute | solution.py:58
  263.2 99.0 %all-to-all-start.2 = ((bf16[8,1056,256]{2,1,0:T(8,128)(2,1)}), bf16[8,1056,256]{2,1,0:T(8,128)(2,1)}, u32[]{:S(2)}, u32[]{:S(2)}) async-start(bf16[8,1056,256]{2,1,0:T(8,128)(2,1)} %pad_maximum_fusion), calls=%async_computation.2 | async-start | bytes 8650752 | tf_op jit(solution)/shard_map/all_to_all | solution.py:792
  279.8 31.2 %collective-permute-start.61 = (bf16[128,2048]{1,0:T(8,128)(2,1)}, bf16[128,2048]{1,0:T(8,128)(2,1)S(1)}, u32[]{:S(2)}, u32[]{:S(2)}) collective-permute-start(bf16[128,2048]{1,0:T(8,128)(2,1)} %collective-permute-done.41.refs_8_), channel_id=1, source_target_pairs={{0,2},{1,3},{2,0},{3,1},{4,6},{5,7},{6,4},{7,5},{8,10},{9,11},{10,... | collective-permute-start | bytes 1572872 | tf_op jit(solution)/shard_map/ppermute | solution.py:58
  280.6 30.4 %collective-permute-start.62 = (bf16[128,2048]{1,0:T(8,128)(2,1)}, bf16[128,2048]{1,0:T(8,128)(2,1)S(1)}, u32[]{:S(2)}, u32[]{:S(2)}) collective-permute-start(bf16[128,2048]{1,0:T(8,128)(2,1)} %collective-permute-done.40.refs_1_), channel_id=1, source_target_pairs={{0,2},{1,3},{2,0},{3,1},{4,6},{5,7},{6,4},{7,5},{8,10},{9,11},{10,... | collective-permute-start | bytes 1572872 | tf_op jit(solution)/shard_map/ppermute | solution.py:58
  281.9 34.5 %collective-permute-start.63 = (bf16[128,2048]{1,0:T(8,128)(2,1)}, bf16[128,2048]{1,0:T(8,128)(2,1)S(1)}, u32[]{:S(2)}, u32[]{:S(2)}) collective-permute-start(bf16[128,2048]{1,0:T(8,128)(2,1)} %collective-permute-done.43.refs_9_), channel_id=1, source_target_pairs={{0,2},{1,3},{2,0},{3,1},{4,6},{5,7},{6,4},{7,5},{8,10},{9,11},{10,... | collective-permute-start | bytes 1572872 | tf_op jit(solution)/shard_map/ppermute | solution.py:58
  362.2 56.1 %all-to-all-start.3 = ((bf16[8,528,256]{2,1,0:T(8,128)(2,1)}), bf16[8,528,256]{2,1,0:T(8,128)(2,1)S(1)}, u32[]{:S(2)}, u32[]{:S(2)}) async-start(bf16[8,528,256]{2,1,0:T(8,128)(2,1)} %get-tuple-element.342), calls=%async_computation.3 | async-start | bytes 4325376 | tf_op jit(solution)/shard_map/all_to_all | solution.py:792
  432.2 42.6 %collective-permute-start.83 = (bf16[1024,2048]{1,0:T(8,128)(2,1)}, bf16[1024,2048]{1,0:T(8,128)(2,1)}, u32[]{:S(2)}, u32[]{:S(2)}) collective-permute-start(bf16[1024,2048]{1,0:T(8,128)(2,1)} %get-tuple-element.356), channel_id=1, source_target_pairs={{0,1},{1,0},{2,3},{3,2},{4,5},{5,4},{6,7},{7,6},{8,9},{9,8},{10,11... | collective-permute-start | bytes 12582920 | tf_op jit(solution)/shard_map/ppermute | solution.py:58
  432.3 42.4 %collective-permute-start.81 = (bf16[256,2048]{1,0:T(8,128)(2,1)}, bf16[256,2048]{1,0:T(8,128)(2,1)S(1)}, u32[]{:S(2)}, u32[]{:S(2)}) collective-permute-start(bf16[256,2048]{1,0:T(8,128)(2,1)} %pad_maximum_fusion.4), channel_id=1, source_target_pairs={{0,4},{1,5},{2,6},{3,7},{4,0},{5,1},{6,2},{7,3},{8,12},{9,13},{10,... | collective-permute-start | bytes 3145736 | tf_op jit(solution)/shard_map/ppermute | solution.py:58
  433.8 41.0 %collective-permute-start.82 = (bf16[256,2048]{1,0:T(8,128)(2,1)}, bf16[256,2048]{1,0:T(8,128)(2,1)S(1)}, u32[]{:S(2)}, u32[]{:S(2)}) collective-permute-start(bf16[256,2048]{1,0:T(8,128)(2,1)} %get-tuple-element.348), channel_id=1, source_target_pairs={{0,2},{1,3},{2,0},{3,1},{4,6},{5,7},{6,4},{7,5},{8,10},{9,11},{10,... | collective-permute-start | bytes 3145736 | tf_op jit(solution)/shard_map/ppermute | solution.py:58
  474.9 50.5 %collective-permute-start.90 = (bf16[1024,2048]{1,0:T(8,128)(2,1)}, bf16[1024,2048]{1,0:T(8,128)(2,1)}, u32[]{:S(2)}, u32[]{:S(2)}) collective-permute-start(bf16[1024,2048]{1,0:T(8,128)(2,1)} %get-tuple-element.372), channel_id=1, source_target_pairs={{0,1},{1,0},{2,3},{3,2},{4,5},{5,4},{6,7},{7,6},{8,9},{9,8},{10,11... | collective-permute-start | bytes 12582920 | tf_op jit(solution)/shard_map/ppermute | solution.py:58
  491.3 34.0 %collective-permute-start.89 = (bf16[128,2048]{1,0:T(8,128)(2,1)S(1)}, bf16[128,2048]{1,0:T(8,128)(2,1)}, u32[]{:S(2)}, u32[]{:S(2)}) collective-permute-start(bf16[128,2048]{1,0:T(8,128)(2,1)S(1)} %add_convert_fusion.26), channel_id=1, source_target_pairs={{0,8},{1,9},{2,10},{3,11},{4,12},{5,13},{6,14},{7,15},{8,24},{9,25... | collective-permute-start | bytes 1572872 | tf_op jit(solution)/shard_map/ppermute | solution.py:58
  492.3 33.0 %collective-permute-start.87 = (bf16[256,2048]{1,0:T(8,128)(2,1)}, bf16[256,2048]{1,0:T(8,128)(2,1)S(1)}, u32[]{:S(2)}, u32[]{:S(2)}) collective-permute-start(bf16[256,2048]{1,0:T(8,128)(2,1)} %pad_maximum_fusion.6), channel_id=1, source_target_pairs={{0,4},{1,5},{2,6},{3,7},{4,0},{5,1},{6,2},{7,3},{8,12},{9,13},{10,... | collective-permute-start | bytes 3145736 | tf_op jit(solution)/shard_map/ppermute | solution.py:58
  493.2 32.2 %collective-permute-start.88 = (bf16[256,2048]{1,0:T(8,128)(2,1)}, bf16[256,2048]{1,0:T(8,128)(2,1)}, u32[]{:S(2)}, u32[]{:S(2)}) collective-permute-start(bf16[256,2048]{1,0:T(8,128)(2,1)} %get-tuple-element.366), channel_id=1, source_target_pairs={{0,2},{1,3},{2,0},{3,1},{4,6},{5,7},{6,4},{7,5},{8,10},{9,11},{10,... | collective-permute-start | bytes 3145736 | tf_op jit(solution)/shard_map/ppermute | solution.py:58
  570.7 102.2 %all-to-all-start.4 = ((bf16[8,1056,256]{2,1,0:T(8,128)(2,1)}), bf16[8,1056,256]{2,1,0:T(8,128)(2,1)}, u32[]{:S(2)}, u32[]{:S(2)}) async-start(bf16[8,1056,256]{2,1,0:T(8,128)(2,1)} %get-tuple-element.407), calls=%async_computation.4 | async-start | bytes 8650752 | tf_op jit(solution)/shard_map/all_to_all | solution.py:981
  585.2 25.8 %collective-permute-start.96 = (bf16[256,2048]{1,0:T(8,128)(2,1)}, bf16[256,2048]{1,0:T(8,128)(2,1)S(1)}, u32[]{:S(2)}, u32[]{:S(2)}) collective-permute-start(bf16[256,2048]{1,0:T(8,128)(2,1)} %get-tuple-element.388), channel_id=1, source_target_pairs={{0,2},{1,3},{2,0},{3,1},{4,6},{5,7},{6,4},{7,5},{8,10},{9,11},{10,... | collective-permute-start | bytes 3145736 | tf_op jit(solution)/shard_map/ppermute | solution.py:58
  612.7 25.2 %collective-permute-start.95 = (bf16[256,2048]{1,0:T(8,128)(2,1)}, bf16[256,2048]{1,0:T(8,128)(2,1)S(1)}, u32[]{:S(2)}, u32[]{:S(2)}) collective-permute-start(bf16[256,2048]{1,0:T(8,128)(2,1)} %get-tuple-element.387), channel_id=1, source_target_pairs={{0,2},{1,3},{2,0},{3,1},{4,6},{5,7},{6,4},{7,5},{8,10},{9,11},{10,... | collective-permute-start | bytes 3145736 | tf_op jit(solution)/shard_map/ppermute | solution.py:58
  640.5 24.9 %collective-permute-start.107 = (bf16[128,2048]{1,0:T(8,128)(2,1)}, bf16[128,2048]{1,0:T(8,128)(2,1)}, u32[]{:S(2)}, u32[]{:S(2)}) collective-permute-start(bf16[128,2048]{1,0:T(8,128)(2,1)} %get-tuple-element.476), channel_id=1, source_target_pairs={{0,2},{1,3},{2,0},{3,1},{4,6},{5,7},{6,4},{7,5},{8,10},{9,11},{10,... | collective-permute-start | bytes 1572872 | tf_op jit(solution)/shard_map/ppermute | solution.py:58
  641.1 48.4 %collective-permute-start.105 = (bf16[256,2048]{1,0:T(8,128)(2,1)}, bf16[256,2048]{1,0:T(8,128)(2,1)}, u32[]{:S(2)}, u32[]{:S(2)}) collective-permute-start(bf16[256,2048]{1,0:T(8,128)(2,1)} %get-tuple-element.405), channel_id=1, source_target_pairs={{0,2},{1,3},{2,0},{3,1},{4,6},{5,7},{6,4},{7,5},{8,10},{9,11},{10,... | collective-permute-start | bytes 3145736 | tf_op jit(solution)/shard_map/ppermute | solution.py:58
  642.6 73.1 %collective-permute-start.113 = (bf16[256,2048]{1,0:T(8,128)(2,1)}, bf16[256,2048]{1,0:T(8,128)(2,1)}, u32[]{:S(2)}, u32[]{:S(2)}) collective-permute-start(bf16[256,2048]{1,0:T(8,128)(2,1)} %get-tuple-element.413), channel_id=1, source_target_pairs={{0,2},{1,3},{2,0},{3,1},{4,6},{5,7},{6,4},{7,5},{8,10},{9,11},{10,... | collective-permute-start | bytes 3145736 | tf_op jit(solution)/shard_map/ppermute | solution.py:58
  644.9 46.7 %collective-permute-start.109 = (bf16[512,1024]{1,0:T(8,128)(2,1)}, bf16[512,1024]{1,0:T(8,128)(2,1)}, u32[]{:S(2)}, u32[]{:S(2)}) collective-permute-start(bf16[512,1024]{1,0:T(8,128)(2,1)} %dynamic-slice_bitcast_fusion), channel_id=1, source_target_pairs={{0,8},{1,9},{2,10},{3,11},{4,12},{5,13},{6,14},{7,15},{8,24},{9,25... | collective-permute-start | bytes 3145736 | tf_op jit(solution)/shard_map/ppermute | solution.py:58
  654.2 37.4 %collective-permute-start.110 = (bf16[128,2048]{1,0:T(8,128)(2,1)}, bf16[128,2048]{1,0:T(8,128)(2,1)}, u32[]{:S(2)}, u32[]{:S(2)}) collective-permute-start(bf16[128,2048]{1,0:T(8,128)(2,1)} %slice.321), channel_id=1, source_target_pairs={{0,4},{1,5},{2,6},{3,7},{4,0},{5,1},{6,2},{7,3},{8,12},{9,13},{10,... | collective-permute-start | bytes 1572872 | tf_op jit(solution)/shard_map/ppermute | solution.py:58
  685.7 60.5 %all-to-all-start.5 = ((bf16[4,64,4224]{2,1,0:T(8,128)(2,1)}), bf16[4,64,4224]{2,1,0:T(8,128)(2,1)S(1)}, u32[]{:S(2)}, u32[]{:S(2)}) async-start(bf16[4,64,4224]{2,1,0:T(8,128)(2,1)} %bitcast.89), calls=%async_computation.5 | async-start | bytes 4325376 | tf_op jit(solution)/shard_map/all_to_all | solution.py:1056
  689.5 26.2 %collective-permute-start.112 = (bf16[128,2048]{1,0:T(8,128)(2,1)}, bf16[128,2048]{1,0:T(8,128)(2,1)}, u32[]{:S(2)}, u32[]{:S(2)}) collective-permute-start(bf16[128,2048]{1,0:T(8,128)(2,1)} %slice.375), channel_id=1, source_target_pairs={{0,4},{1,5},{2,6},{3,7},{4,0},{5,1},{6,2},{7,3},{8,12},{9,13},{10,... | collective-permute-start | bytes 1572872 | tf_op jit(solution)/shard_map/ppermute | solution.py:58
  696.5 27.0 %collective-permute-start.111 = (bf16[512,1024]{1,0:T(8,128)(2,1)S(1)}, bf16[512,1024]{1,0:T(8,128)(2,1)S(1)}, u32[]{:S(2)}, u32[]{:S(2)}) collective-permute-start(bf16[512,1024]{1,0:T(8,128)(2,1)S(1)} %fusion.2), channel_id=1, source_target_pairs={{0,8},{1,9},{2,10},{3,11},{4,12},{5,13},{6,14},{7,15},{8,24},{9,25... | collective-permute-start | bytes 3145736 | tf_op jit(solution)/shard_map/ppermute | solution.py:58
  726.6 30.6 %collective-permute-start.115 = (bf16[512,1024]{1,0:T(8,128)(2,1)}, bf16[512,1024]{1,0:T(8,128)(2,1)}, u32[]{:S(2)}, u32[]{:S(2)}) collective-permute-start(bf16[512,1024]{1,0:T(8,128)(2,1)} %fusion.1), channel_id=1, source_target_pairs={{0,8},{1,9},{2,10},{3,11},{4,12},{5,13},{6,14},{7,15},{8,24},{9,25... | collective-permute-start | bytes 3145736 | tf_op jit(solution)/shard_map/ppermute | solution.py:58
  738.0 27.9 %collective-permute-start.122 = (bf16[64,2048]{1,0:T(8,128)(2,1)}, bf16[64,2048]{1,0:T(8,128)(2,1)}, u32[]{:S(2)}, u32[]{:S(2)}) collective-permute-start(bf16[64,2048]{1,0:T(8,128)(2,1)} %get-tuple-element.483), channel_id=1, source_target_pairs={{0,8},{1,9},{2,10},{3,11},{4,12},{5,13},{6,14},{7,15},{8,24},{9,25... | collective-permute-start | bytes 786440 | tf_op jit(solution)/shard_map/ppermute | solution.py:58
  738.9 28.7 %collective-permute-start.125 = (bf16[64,2048]{1,0:T(8,128)(2,1)}, bf16[64,2048]{1,0:T(8,128)(2,1)}, u32[]{:S(2)}, u32[]{:S(2)}) collective-permute-start(bf16[64,2048]{1,0:T(8,128)(2,1)} %get-tuple-element.482), channel_id=1, source_target_pairs={{0,8},{1,9},{2,10},{3,11},{4,12},{5,13},{6,14},{7,15},{8,24},{9,25... | collective-permute-start | bytes 786440 | tf_op jit(solution)/shard_map/ppermute | solution.py:58
  (209 other events, 1968.8 us)
